TPU v7x, 32 devices: a whole 2x2x4 slice. The times are simulated.
32 devices in a mesh: samp: 2 (over y), row: 2 (over x), col: 8 (over z, core).
Axes of the slice: x: 2, y: 2, z: 4, core: 2. Of those that a mesh axis runs over, the one named last changes fastest.
Arguments:
- tokens: bfloat16 [8, 512, 768], P('samp', 'col'), may hold values from -110 to 110
- restype: int32 [512], P('col'), may hold values from 0 to 31
- type_table: bfloat16 [32, 768], replicated, may hold values from -8 to 8
- key_mask: int32 [512], P('col'), may hold values 0 or 1
- pair: bfloat16 [512, 512, 128], P('row', 'col'), may hold values from -160 to 160
- w_bias: bfloat16 [128, 16], replicated, may hold values from -0.5 to 0.5
- w_query: bfloat16 [768, 768], replicated, may hold values from -2 to 2
- w_key: bfloat16 [768, 768], replicated, may hold values from -2 to 2
- w_value: bfloat16 [768, 768], replicated, may hold values from -0.21875 to 0.21875
- w_gate: bfloat16 [768, 768], replicated, may hold values from -0.21875 to 0.21875
- cotangent: bfloat16 [8, 512, 768], P('samp', 'col'), may hold values from -6 to 6
Outputs:
- token_grad: bfloat16 [8, 512, 768], P('samp', 'col')
- pair_grad: bfloat16 [512, 512, 128], P('row', 'col')
- bias_weight_grad: float32 [128, 16], replicated
All inputs are finite; a program needn't handle non-finite values. No bound on the sum of `key_mask` on one device may be relied on, other than what follows from the above.
Results may differ from a plain program's by a relative error of at most 0.034.
The roundings to bfloat16 on the way count: a program that leaves them out, or rounds other values in their place, can miss the bound.
Values may be sent and summed in bfloat16 or wider, within the bound.
No kernel may reach another device: no remote copies, remote signals or barrier semaphores. Data moves between devices by JAX's collectives and lax.ppermute only.
A program may use at most 128 MiB of HBM per device.

v0:
```python
import math

import jax
import jax.numpy as jnp
from jax import lax
from jax.sharding import PartitionSpec as P

D = 768
H = 16
CH = 48
NTYPE = 32


def broadcast(block, axis, source):
    block = jnp.where(lax.axis_index(axis) == source, block, jnp.zeros_like(block))
    return lax.psum(block, axis)


def token_norm(tokens, restype, type_table):
    onehot = (restype[:, None] == jnp.arange(NTYPE, dtype=jnp.int32)[None, :]).astype(jnp.bfloat16)
    embedded = tokens.astype(jnp.float32) + jnp.dot(
        onehot, type_table, preferred_element_type=jnp.float32
    )
    centred = embedded - jnp.mean(embedded, axis=-1, keepdims=True)
    inv_std = lax.rsqrt(jnp.mean(centred * centred, axis=-1, keepdims=True) + 1e-05)
    return (centred * inv_std, inv_std)


def pair_norm(block):
    values = block.astype(jnp.float32)
    centred = values - jnp.mean(values, axis=-1, keepdims=True)
    inv_std = lax.rsqrt(jnp.mean(centred * centred, axis=-1, keepdims=True) + 1e-05)
    return (centred * inv_std, inv_std)


def norm_back(grad_in, normed, inv_std):
    return inv_std * (
        grad_in
        - jnp.mean(grad_in, axis=-1, keepdims=True)
        - normed * jnp.mean(grad_in * normed, axis=-1, keepdims=True)
    )


def project(rows_in, weight):
    return jnp.einsum("std,de->ste", rows_in, weight, preferred_element_type=jnp.float32).astype(
        jnp.bfloat16
    )


def back_project(grads, weight):
    return jnp.einsum(
        "ste,de->std", grads, weight.astype(jnp.float32), precision=lax.Precision.HIGHEST
    )


def pair_back(grad_bias, pair_normed, pair_inv, bias_weight):
    grad_normed = jnp.einsum("hij,ch->ijc", grad_bias, bias_weight, precision=lax.Precision.HIGHEST)
    return norm_back(grad_normed, pair_normed, pair_inv)


def body(
    tokens, restype, type_table, key_mask, pair, w_bias, w_query, w_key, w_value, w_gate, cotangent
):
    n_row = lax.axis_size("row")
    n_col = lax.axis_size("col")
    n_samp = lax.axis_size("samp")
    samp_dev = tokens.shape[0]
    tok_col = tokens.shape[1]
    spread = n_col // n_row
    row_count = tok_col * spread
    total_tokens = tok_col * n_col
    row_index = lax.axis_index("row")
    col_index = lax.axis_index("col")
    is_owner = col_index // spread == row_index
    own_start = col_index % spread * tok_col
    normed, inv_std = token_norm(tokens, restype, type_table)
    own_act = normed.astype(jnp.bfloat16)
    key_proj = project(own_act, w_key)
    value_proj = project(own_act, w_value)
    stacked = jnp.stack([own_act, cotangent])
    pieces = [broadcast(stacked, "col", row_index * spread + member) for member in range(spread)]
    gathered = jnp.concatenate(pieces, axis=2)
    query_side = gathered[0]
    grad_rows = gathered[1]
    queries = project(query_side, w_query)
    gate_lin = project(query_side, w_gate)
    pair_normed, pair_inv = pair_norm(pair)
    bias_weight = w_bias.astype(jnp.float32)
    bias = jnp.einsum("ijc,ch->hij", pair_normed, bias_weight, precision=lax.Precision.HIGHEST)
    query_heads = queries.reshape(samp_dev, row_count, H, CH)
    key_heads = key_proj.reshape(samp_dev, tok_col, H, CH)
    value_heads = value_proj.reshape(samp_dev, tok_col, H, CH)
    scores = (
        jnp.einsum("sihc,sjhc->shij", query_heads, key_heads, preferred_element_type=jnp.float32)
        / math.sqrt(CH)
        + bias[None]
    )
    scores = jnp.where(key_mask[None, None, None, :] == 1, scores, -1000000000.0)
    top = lax.pmax(jnp.max(scores, axis=-1), "col")
    expo = jnp.exp(scores - top[..., None])
    partial_out = jnp.einsum(
        "shij,sjhc->sihc",
        expo.astype(jnp.bfloat16),
        value_heads,
        preferred_element_type=jnp.float32,
    )
    totals, summed = lax.psum(
        (jnp.sum(expo, axis=-1), partial_out.reshape(samp_dev, row_count, D)), "col"
    )
    attended = (
        summed.reshape(samp_dev, row_count, H, CH) / jnp.transpose(totals, (0, 2, 1))[..., None]
    )
    flat_out = attended.reshape(samp_dev, row_count, D)
    sig_gate = jax.nn.sigmoid(gate_lin.astype(jnp.float32))
    grad_f = grad_rows.astype(jnp.float32)
    grad_out = (grad_f * sig_gate).astype(jnp.bfloat16)
    grad_gate = (grad_f * flat_out * sig_gate * (1.0 - sig_gate)).astype(jnp.bfloat16)
    gate_piece = lax.dynamic_slice_in_dim(grad_gate, own_start, tok_col, 1)
    gate_term = jnp.where(
        is_owner,
        jnp.einsum("ste,de->std", gate_piece, w_gate, preferred_element_type=jnp.float32),
        0.0,
    )
    grad_heads = grad_out.reshape(samp_dev, row_count, H, CH)
    delta = jnp.transpose(jnp.sum(grad_heads.astype(jnp.float32) * attended, axis=-1), (0, 2, 1))
    probs = expo / totals[..., None]
    grad_pre = jnp.einsum(
        "sihc,sjhc->shij", grad_heads, value_heads, preferred_element_type=jnp.float32
    )
    grad_scores = probs * (grad_pre - delta[..., None])
    rounded = grad_scores.astype(jnp.bfloat16)
    grad_query = (
        jnp.einsum("shij,sjhc->sihc", rounded, key_heads, preferred_element_type=jnp.float32)
        / math.sqrt(CH)
    ).reshape(samp_dev, row_count, D)
    grad_key = (
        jnp.einsum("shij,sihc->sjhc", rounded, query_heads, preferred_element_type=jnp.float32)
        / math.sqrt(CH)
    ).reshape(samp_dev, tok_col, D)
    grad_value = jnp.einsum(
        "shij,sihc->sjhc",
        probs.astype(jnp.bfloat16),
        grad_heads,
        preferred_element_type=jnp.float32,
    ).reshape(samp_dev, tok_col, D)
    bias_local = jnp.sum(grad_scores, axis=0)
    blank = jnp.zeros((samp_dev, total_tokens, D), jnp.float32)
    mine = lax.psum_scatter(
        lax.dynamic_update_slice_in_dim(blank, grad_query, row_index * row_count, 1),
        "col",
        scatter_dimension=1,
        tiled=True,
    )
    query_all, key_all, value_all, gate_all = lax.psum(
        (mine, grad_key, grad_value, gate_term), "row"
    )
    grad_act = (
        back_project(query_all, w_query)
        + back_project(key_all, w_key)
        + back_project(value_all, w_value)
        + gate_all
    )
    token_grad = norm_back(grad_act, normed, inv_std).astype(jnp.bfloat16)
    samples = samp_dev * n_samp
    grad_bias = lax.psum(bias_local, "samp")
    grad_pair = pair_back(grad_bias, pair_normed, pair_inv, bias_weight)
    pair_grad = (grad_pair * (total_tokens / samples)).astype(jnp.bfloat16)
    weight_part = jnp.einsum("ijc,hij->ch", pair_normed, grad_bias, precision=lax.Precision.HIGHEST)
    weight_sum = lax.psum(weight_part, ("row", "col"))
    bias_weight_grad = weight_sum / samples
    return (token_grad, pair_grad, bias_weight_grad)


def solution(mesh):
    placed = (
        P("samp", "col", None),
        P("col"),
        P(),
        P("col"),
        P("row", "col", None),
        P(),
        P(),
        P(),
        P(),
        P(),
        P("samp", "col", None),
    )
    return jax.shard_map(
        body,
        mesh=mesh,
        in_specs=placed,
        out_specs=(P("samp", "col", None), P("row", "col", None), P()),
        check_vma=False,
    )
```

profile of v0, /device:TPU:0, one launch (start us, length us, event | category | flops | bytes accessed | tf_op | source)
XLA Modules:
  0.0 493.1 jit_solution(4723223414528472441)
XLA Ops:
  7.2 1.1 fusion.53
  8.4 1.2 fusion.48
  9.5 1.2 multiply_reduce_fusion.2
  10.8 1.2 fusion.61
  11.9 2.8 broadcast_select_fusion
  14.8 6.9 %copy.51 = bf16[256,64,128]{0,2,1:T(8,128)(2,1)} copy(bf16[256,64,128]{2,1,0:T(8,128)(2,1)} %param.15) | data formatting | bytes 8388608 | tf_op args[4]
  21.7 3.6 convert_reduce_fusion
  25.4 0.5 convolution_convert_fusion.3
  25.9 1.2 copy.69
  27.1 4.0 fusion.13
  31.1 3.6 fusion.24
  34.7 0.6 copy.53
  35.3 60.1 %all-reduce.17.cloned.1.call-done = (bf16[2,4,64,768]{3,2,1,0:T(8,128)(2,1)}, bf16[2,4,64,768]{3,2,1,0:T(8,128)(2,1)}, bf16[2,4,64,768]{3,2,1,0:T(8,128)(2,1)}, bf16[2,4,64,768]{3,2,1,0:T(8,128)(2,1)}) async-done(((bf16[2,4,64,768]{3,2,1,0:T(8,128)(2,1)}, bf16[2,4,64,768]{3,2,1,0:T(8,128)(2,1)}, bf16[2,4,64,768]{3,2,1,0:T(8,128)(2,1)}, bf16[2,4,64,768]{3,2,1,0:T(8,128)(2,1)}), ...) | async-done | bytes 3145744 | tf_op jit(solution)/shard_map/psum | solution.py:16
  95.4 1.3 constant_dynamic-update-slice_fusion.3
  96.8 1.2 constant_dynamic-update-slice_fusion.2
  98.0 0.1 constant_dynamic-update-slice_fusion.1
  98.1 0.1 constant_dynamic-update-slice_fusion
  98.1 1.7 copy-done.9
  99.8 2.5 convolution_convert_fusion.1
  102.3 2.6 copy.49
  105.0 5.4 %fusion.18 = (f32[4,16,256]{2,1,0:T(8,128)}, f32[4,16,256,64]{2,3,1,0:T(8,128)}) fusion(f32[16,256,64]{1,2,0:T(8,128)S(1)} %copy.53, pred[64]{0:T(512)(128)(4,1)S(1)} %broadcast_compare_fusion, bf16[4,256,16,48]{1,3,2,0:T(8,128)(2,1)} %bitcast.91, bf16[4,64,16,48]{1,3,2,0:T(8,128)(2,1)} %bitcast.97), kind=kOutput, calls=%fused_computation.21 | convolution fusion | flops 104841216 | bytes 7274560 | tf_op jit(solution)/shard_map/sihc,sjhc->shij/dot_general | solution.py:94
  110.4 0.2 all-reduce.13.cloned.1.call-start
  110.6 1.8 convolution_convert_fusion.2
  112.4 1.2 copy.70
  113.6 50.6 %all-reduce.9.cloned.1.call-done = f32[4,16,256]{2,1,0:T(8,128)} async-done(((f32[4,16,256]{2,1,0:T(8,128)}), f32[4,16,256]{2,1,0:T(8,128)}) %all-reduce.9.cloned.1.call-update) | async-done | bytes 65552 | tf_op jit(solution)/shard_map/pmax | solution.py:99
  164.2 5.6 %fusion.21 = f32[4,16,48,256]{3,2,1,0:T(8,128)} fusion(bf16[4,64,16,48]{1,3,2,0:T(8,128)(2,1)} %bitcast.103, f32[4,16,256,64]{2,3,1,0:T(8,128)} %get-tuple-element.31, f32[4,16,256]{2,1,0:T(8,128)} %all-reduce.9.cloned.1.call-done, f32[16,256,64]{1,2,0:T(8,128)S(1)} %copy.53, pred[64]{0:T(512)(128)(4,1)S(1)} %broadcast_compare_fusion), kind=kOutput, calls=%fused_computation.27 | convolution fusion | flops 105906176 | bytes 8847424 | tf_op jit(solution)/shard_map/shij,sjhc->sihc/dot_general | solution.py:101
  169.8 3.6 copy.57
  173.4 4.1 fusion.63
  177.6 5.7 %multiply_convert_fusion = (bf16[4,256,768]{2,1,0:T(8,128)(2,1)}, f32[4,256,768]{2,1,0:T(8,128)}) fusion(bf16[2,4,256,768]{3,2,1,0:T(8,128)(2,1)} %copy-done.9, bf16[768,768]{1,0:T(8,128)(2,1)S(1)} %copy-done), kind=kOutput, calls=%fused_computation.23 | convolution fusion | flops 1214251008 | bytes 9043968 | tf_op jit(solution)/shard_map/std,de->ste/dot_general | solution.py:45
  183.3 2.6 copy.54
  185.9 69.1 %all-reduce.13.cloned.1.call-done = (f32[4,16,256]{2,1,0:T(8,128)}, f32[4,256,768]{2,1,0:T(8,128)}) async-done(((f32[4,16,256]{2,1,0:T(8,128)}, f32[4,256,768]{2,1,0:T(8,128)}), (f32[4,16,256]{2,1,0:T(8,128)}, f32[4,256,768]{2,1,0:T(8,128)})) %all-reduce.13.cloned.1.call-update) | async-done | bytes 3211280 | tf_op jit(solution)/shard_map/psum | solution.py:107
  255.0 3.6 copy.58
  258.6 3.3 multiply_reduce_fusion
  261.9 0.3 copy-done.3
  262.2 4.9 fusion.66
  267.1 1.3 copy-done.7
  268.4 2.2 convolution_multiply_fusion
  270.6 3.6 copy.60
  274.2 3.2 broadcast_in_dim.13
  277.4 1.9 constant_dynamic-update-slice_fusion.4
  279.4 3.5 fusion.23
  282.9 1.6 copy.64
  284.5 0.3 all-reduce.15.cloned.1.call-start
  284.8 5.8 %fusion.19 = f32[4,16,48,64]{3,2,1,0:T(8,128)} fusion(bf16[4,256,16,48]{1,3,2,0:T(8,128)(2,1)} %bitcast.101, f32[4,16,256]{2,1,0:T(8,128)S(1)} %copy-done.21, f32[4,16,256,64]{2,3,1,0:T(8,128)} %get-tuple-element.31, f32[4,16,256]{2,1,0:T(8,128)S(1)} %copy-done.20, f32[16,256,64]{1,2,0:T(8,128)S(1)} %copy.53, pred[64]{0:T(512)(128)(4,1)S(1)} %broadcast_compare_fusion), kind=kOutput, calls=%fused_computation.25 | convolution fusion | flops 106954752 | bytes 7733312 | tf_op jit(solution)/shard_map/shij,sihc->sjhc/dot_general | solution.py:140
  290.6 2.7 copy.62
  293.3 0.2 div.93
  293.6 1.6 constant_dynamic-slice_fusion
  295.2 2.8 copy.71
  298.0 3.5 convolution_multiply_fusion.1
  301.5 2.7 copy.61
  304.2 3.4 convolution_select_fusion
  307.6 41.8 %reduce-scatter.2.cloned.1.call-done = f32[4,64,768]{2,1,0:T(8,128)} async-done(((f32[4,512,768]{2,1,0:T(8,128)}), f32[4,64,768]{2,1,0:T(8,128)}) %reduce-scatter.2.cloned.1.call-update) | async-done | bytes 786448 | tf_op jit(solution)/shard_map/reduce_scatter | solution.py:148
  349.4 40.6 %all-reduce.11.cloned.1.call-done = f32[16,256,64]{1,0,2:T(8,128)} async-done(((f32[16,256,64]{1,0,2:T(8,128)}), f32[16,256,64]{1,0,2:T(8,128)}) %all-reduce.11.cloned.1.call-update) | async-done | bytes 1048592 | tf_op jit(solution)/shard_map/psum | solution.py:165
  390.1 8.1 %fusion.64 = (f32[256,64]{0,1:T(8,128)S(1)}, f32[256,64]{0,1:T(8,128)S(1)}, f32[256,64,128]{0,2,1:T(8,128)S(1)}) fusion(f32[256,64]{0,1:T(8,128)S(1)} %add_rsqrt_fusion, f32[256,64]{0,1:T(8,128)S(1)} %broadcast_multiply_fusion.2, bf16[256,64,128]{0,2,1:T(8,128)(2,1)} %copy.51, f32[16,256,64]{1,0,2:T(8,128)} %all-reduce.11.cloned.1.call-done, ...), kind=kOutput, calls=%fused_computation.101 | convolution fusion | flops 415203328 | bytes 13897728 | tf_op jit(solution)/shard_map/hij,ch->ijc/dot_general | solution.py:57
  398.2 5.1 %fusion.12 = bf16[256,64,128]{0,2,1:T(8,128)(2,1)} fusion(bf16[256,64,128]{0,2,1:T(8,128)(2,1)S(1)} %copy-done.2, f32[256,64,128]{0,2,1:T(8,128)S(1)} %get-tuple-element.37, f32[256,64]{0,1:T(8,128)S(1)} %get-tuple-element.40, f32[256,64]{0,1:T(8,128)S(1)} %get-tuple-element.41, f32[256,64]{0,1:T(8,128)S(1)} %add_rsqrt_fusion, ...), kind=kLoop, calls=%fused_computation.12 | loop fusion | flops 18874368 | bytes 17039360 | tf_op jit(solution)/shard_map/convert_element_type | solution.py:167
  403.3 6.4 %copy.66 = bf16[256,64,128]{2,1,0:T(8,128)(2,1)} copy(bf16[256,64,128]{0,2,1:T(8,128)(2,1)} %fusion.12) | data formatting | bytes 8388608
  409.8 8.8 %fusion.37 = f32[128,16]{0,1:T(8,128)S(1)} fusion(f32[16,256,64]{1,0,2:T(8,128)} %all-reduce.11.cloned.1.call-done, bf16[256,64,128]{0,2,1:T(8,128)(2,1)} %copy.51, f32[256,64]{0,1:T(8,128)S(1)} %add_rsqrt_fusion, f32[256,64]{0,1:T(8,128)S(1)} %broadcast_multiply_fusion.2), kind=kOutput, calls=%fused_computation.53 | convolution fusion | flops 408944640 | bytes 5382144 | tf_op jit(solution)/shard_map/ijc,hij->ch/dot_general | solution.py:168
  418.6 34.2 %psum.95 = f32[128,16]{0,1:T(8,128)S(1)} all-reduce(f32[128,16]{0,1:T(8,128)S(1)} %fusion.37), channel_id=1, replica_groups=mesh['samp'=2,'row'=2,'col'=8] {'row','col'}, use_global_device_ids=true, to_apply=%region_25.26 | all-reduce | flops 2048 | bytes 16384 | tf_op jit(solution)/shard_map/psum | solution.py:169
  452.9 0.6 broadcast_multiply_fusion.3
  453.5 25.8 %all-reduce.15.cloned.1.call-done = (f32[4,64,768]{2,1,0:T(8,128)}, f32[4,64,768]{2,1,0:T(8,128)}, f32[4,64,768]{2,1,0:T(8,128)}, f32[4,64,768]{2,1,0:T(8,128)}) async-done(((f32[4,64,768]{2,1,0:T(8,128)}, f32[4,64,768]{2,1,0:T(8,128)}, f32[4,64,768]{2,1,0:T(8,128)}, f32[4,64,768]{2,1,0:T(8,128)}), (f32[4,64,768]{2,1,0:T(8,128)}, f32[4,64,768]{2,1,0:T(8,128)}, f32[4,64,768]{2,1,0:T(8,128)}, ...) | async-done | bytes 3145744 | tf_op jit(solution)/shard_map/psum | solution.py:154
  479.3 2.8 fusion.32
  482.1 1.2 convolution_add_fusion.1
  483.3 1.4 fusion.65
  484.8 1.0 multiply_convert_fusion.1
  (62 shorter events, 0.4 us)
Async XLA Ops:
  7.2 170.4 %copy-start = (bf16[768,768]{1,0:T(8,128)(2,1)S(1)}, bf16[768,768]{1,0:T(8,128)(2,1)}, u32[]{:S(2)}) copy-start(bf16[768,768]{1,0:T(8,128)(2,1)} %param.20) | copy-start | bytes 3538948
  7.2 88.3 %all-reduce.17.cloned.1.call-start = ((), (), s32[]{:S(2)}) async-start(), calls=%async_computation.6 | async-start | bytes 6291456 | tf_op jit(solution)/shard_map/psum | solution.py:16
  14.7 149.5 %all-reduce.9.cloned.1.call-start = ((), (), s32[]{:S(2)}) async-start(), calls=%async_computation.1 | async-start | bytes 131072 | tf_op jit(solution)/shard_map/pmax | solution.py:99
  21.7 3.6 copy-start.6
  21.7 3.6 copy-start.10
  25.9 5.2 %copy-start.22 = (bf16[128,16]{0,1:T(8,128)(2,1)S(1)}, bf16[128,16]{0,1:T(8,128)(2,1)}, u32[]{:S(2)}) copy-start(bf16[128,16]{0,1:T(8,128)(2,1)} %param.16) | copy-start | bytes 12292
  27.1 4.0 copy-start.1
  31.1 4.2 copy-start.23
  95.4 2.5 copy-start.19
  95.4 2.6 copy-start.18
  95.4 4.3 copy-start.12
  98.1 1.7 copy-start.9
  110.4 144.6 %all-reduce.13.cloned.1.call-start = ((), (), s32[]{:S(2)}) async-start(), calls=%async_computation.4 | async-start | bytes 6422528 | tf_op jit(solution)/shard_map/psum | solution.py:107
  169.8 3.6 copy-start.20
  177.5 171.9 %reduce-scatter.2.cloned.1.call-start = ((), (), s32[]{:S(2)}) async-start(), calls=%async_computation.2 | async-start | bytes 7077888 | tf_op jit(solution)/shard_map/reduce_scatter | solution.py:148
  255.0 3.6 copy-start.21
  258.6 3.6 copy-start.3
  262.2 6.2 %copy-start.8 = (bf16[4,64,768]{1,2,0:T(8,128)(2,1)S(1)}, bf16[4,64,768]{1,2,0:T(8,128)(2,1)}, u32[]{:S(2)}) copy-start(bf16[4,64,768]{1,2,0:T(8,128)(2,1)} %copy.69) | copy-start | bytes 1179652
  267.1 1.3 copy-start.7
  274.2 3.2 copy-start.5
  279.3 110.7 %all-reduce.11.cloned.1.call-start = ((), (), s32[]{:S(2)}) async-start(), calls=%async_computation.3 | async-start | bytes 2097152 | tf_op jit(solution)/shard_map/psum | solution.py:165
  279.4 3.5 copy-start.14
  284.5 194.8 %all-reduce.15.cloned.1.call-start = ((), (), s32[]{:S(2)}) async-start(), calls=%async_computation.5 | async-start | bytes 6291456 | tf_op jit(solution)/shard_map/psum | solution.py:154
  293.6 4.4 copy-start.4
  390.1 8.2 %copy-start.2 = (bf16[256,64,128]{0,2,1:T(8,128)(2,1)S(1)}, bf16[256,64,128]{0,2,1:T(8,128)(2,1)}, u32[]{:S(2)}) copy-start(bf16[256,64,128]{0,2,1:T(8,128)(2,1)} %copy.51) | copy-start | bytes 12582916
  409.8 72.3 %copy-start.11 = (bf16[768,768]{1,0:T(8,128)(2,1)S(1)}, bf16[768,768]{1,0:T(8,128)(2,1)}, u32[]{:S(2)}) copy-start(bf16[768,768]{1,0:T(8,128)(2,1)} %param.18) | copy-start | bytes 3538948
  479.3 2.8 copy-start.17
  479.3 4.0 copy-start.13
  479.3 4.0 copy-start.15
  479.3 4.0 copy-start.16
Sparse Core Ops, SparseCore 0:
  14.9 80.5 all-reduce.16
  110.5 53.6 all-reduce.8
  177.6 77.3 all-reduce.12
  279.5 69.8 reduce-scatter.1
  351.6 38.3 all-reduce.10
  392.4 86.8 all-reduce.14
where the time goes:
time: 502 us; the launch traced here: 493 us
  waiting for transfers between devices  288 us (57%)
  matrix products  68.4 us (14%)
  local copies, waits for them, and re-layouts  55.1 us (11%)
  blocking collectives  34.2 us (7%)
  other arithmetic  31.5 us (6%)
  between operations  15 us (3%)
    psum x1, waiting for transfers between devices, body(): lax.psum((jnp.sum(expo, axis=-1), partial_out.reshape(samp_dev, row_count...  69.1 us
    psum x1, waiting for transfers between devices, broadcast(): return lax.psum(block, axis)  60.1 us
    pmax x1, waiting for transfers between devices, body(): top = lax.pmax(jnp.max(scores, axis=-1), 'col')  50.6 us
    reduce_scatter x1, waiting for transfers between devices, body(): lax.psum_scatter(lax.dynamic_update_slice_in_dim(blank, grad_query, row_i...  41.8 us
    psum x1, waiting for transfers between devices, body(): grad_bias = lax.psum(bias_local, 'samp')  40.6 us
    psum x1, blocking collectives, body(): weight_sum = lax.psum(weight_part, ('row', 'col'))  34.2 us
    psum x1, waiting for transfers between devices, body(): lax.psum((mine, grad_key, grad_value, gate_term), 'row')  25.8 us
    unnamed x54, local copies, waits for them, and re-layouts  22.1 us
  transfers between devices with their start and end apart: 6, of which 6 were waited for; matrix products, arithmetic and copies ran while one was open for 18% of the time, Pallas kernels for 0%

commit v1 on v0

--- a/solution.py
+++ b/solution.py
@@ -3,6 +3,8 @@
 import jax
 import jax.numpy as jnp
 from jax import lax
+from jax.experimental import pallas as pl
+from jax.experimental.pallas import tpu as pltpu
 from jax.sharding import PartitionSpec as P
 
 D = 768
@@ -58,7 +60,7 @@
     return norm_back(grad_normed, pair_normed, pair_inv)
 
 
-def body(
+def body_any(
     tokens, restype, type_table, key_mask, pair, w_bias, w_query, w_key, w_value, w_gate, cotangent
 ):
     n_row = lax.axis_size("row")
@@ -171,6 +173,504 @@
     return (token_grad, pair_grad, bias_weight_grad)
 
 
+EPS = 1e-05
+SCALE = 1.0 / math.sqrt(CH)
+NT = (((1,), (1,)), ((), ()))
+TN = (((0,), (0,)), ((), ()))
+MASKED = -65504.0
+
+
+def params(megabytes):
+    return pltpu.CompilerParams(vmem_limit_bytes=megabytes * 1024 * 1024)
+
+
+def matmul(left, right):
+    return jnp.dot(left, right, preferred_element_type=jnp.float32)
+
+
+def matmul_nt(left, right):
+    return lax.dot_general(left, right, NT, preferred_element_type=jnp.float32)
+
+
+def matmul_tn(left, right):
+    return lax.dot_general(left, right, TN, preferred_element_type=jnp.float32)
+
+
+def halves(values):
+    high = values.astype(jnp.bfloat16)
+    low = (values - high.astype(jnp.float32)).astype(jnp.bfloat16)
+    return high, low
+
+
+def unit_rows(values):
+    centred = values - jnp.mean(values, axis=-1, keepdims=True)
+    inv_std = lax.rsqrt(jnp.mean(centred * centred, axis=-1, keepdims=True) + EPS)
+    return centred * inv_std, inv_std
+
+
+def embed_rows(tokens_ref, types_ref, table_ref):
+    count, length, width = tokens_ref.shape
+    index = lax.broadcasted_iota(jnp.int32, (NTYPE, length), 0)
+    onehot = jnp.where(types_ref[...] == index, 1.0, 0.0).astype(jnp.bfloat16)
+    added = matmul_tn(onehot, table_ref[...])
+    embedded = tokens_ref[...].astype(jnp.float32) + added[None]
+    return unit_rows(embedded.reshape(count * length, width))
+
+
+def token_kernel(
+    row_ref, tokens_ref, types_ref, table_ref, wq_ref, wk_ref, wv_ref, wg_ref, cot_ref, out_ref
+):
+    normed, _ = embed_rows(tokens_ref, types_ref, table_ref)
+    act = normed.astype(jnp.bfloat16)
+    heads, _, _, count = out_ref.shape
+
+    def store(slot, rounded):
+        out_ref[:, slot] = rounded.T.reshape(heads, CH, count)
+
+    for slot, ref in enumerate((wq_ref, wk_ref, wv_ref)):
+        store(slot, matmul(act, ref[...]).astype(jnp.bfloat16))
+    gate = matmul(act, wg_ref[...]).astype(jnp.bfloat16).astype(jnp.float32)
+    cot = cot_ref[...].reshape(gate.shape).astype(jnp.float32)
+    store(3, (cot * jax.nn.sigmoid(gate)).astype(jnp.bfloat16))
+
+
+def token_messages(row, tokens, types, table, weights, cotangent, n_row, n_col):
+    samp_dev, tok_col, _ = tokens.shape
+    width = D // n_row
+    whole3 = lambda i, r: (0, 0, 0)
+    whole2 = lambda i, r: (0, 0)
+    weight_spec = pl.BlockSpec((D, width), lambda i, r: (0, r[0]))
+    shape = (n_col, 4, CH, samp_dev * tok_col)
+    return pl.pallas_call(
+        token_kernel,
+        out_shape=jax.ShapeDtypeStruct(shape, jnp.bfloat16),
+        grid_spec=pltpu.PrefetchScalarGridSpec(
+            num_scalar_prefetch=1,
+            grid=(1,),
+            in_specs=[
+                pl.BlockSpec(tokens.shape, whole3),
+                pl.BlockSpec(types.shape, whole2),
+                pl.BlockSpec(table.shape, whole2),
+                weight_spec,
+                weight_spec,
+                weight_spec,
+                weight_spec,
+                pl.BlockSpec((samp_dev, tok_col, width), lambda i, r: (0, 0, r[0])),
+            ],
+            out_specs=pl.BlockSpec(shape, lambda i, r: (0, 0, 0, 0)),
+        ),
+        compiler_params=params(56),
+        cost_estimate=pl.CostEstimate(
+            flops=2 * samp_dev * tok_col * D * width * 4, bytes_accessed=4_000_000, transcendentals=0
+        ),
+        name="token_messages",
+    )(row, tokens, types, table, *weights, cotangent)
+
+
+def own_kernel(
+    row_ref, tokens_ref, types_ref, table_ref, wg_ref, cot_ref, slope_ref, normed_ref, inv_ref
+):
+    normed, inv_std = embed_rows(tokens_ref, types_ref, table_ref)
+    gate = matmul(normed.astype(jnp.bfloat16), wg_ref[...]).astype(jnp.bfloat16)
+    sig = jax.nn.sigmoid(gate.astype(jnp.float32))
+    cot = cot_ref[...].reshape(gate.shape).astype(jnp.float32)
+    slope_ref[...] = (cot * sig * (1.0 - sig)).T
+    normed_ref[...] = normed.T
+    inv_ref[...] = jnp.broadcast_to(inv_std, (inv_std.shape[0], 128)).T[:8]
+
+
+def own_rows(row, tokens, types, table, w_gate, cotangent, half):
+    _, tok_col, _ = tokens.shape
+    count = half * tok_col
+    part_spec = pl.BlockSpec((half, tok_col, D), lambda i, r: (r[0], 0, 0))
+    whole2 = lambda i, r: (0, 0)
+    return pl.pallas_call(
+        own_kernel,
+        out_shape=[
+            jax.ShapeDtypeStruct((D, count), jnp.float32),
+            jax.ShapeDtypeStruct((D, count), jnp.float32),
+            jax.ShapeDtypeStruct((8, count), jnp.float32),
+        ],
+        grid_spec=pltpu.PrefetchScalarGridSpec(
+            num_scalar_prefetch=1,
+            grid=(1,),
+            in_specs=[
+                part_spec,
+                pl.BlockSpec(types.shape, whole2),
+                pl.BlockSpec(table.shape, whole2),
+                pl.BlockSpec(w_gate.shape, whole2),
+                part_spec,
+            ],
+            out_specs=[
+                pl.BlockSpec((D, count), whole2),
+                pl.BlockSpec((D, count), whole2),
+                pl.BlockSpec((8, count), whole2),
+            ],
+        ),
+        compiler_params=params(56),
+        cost_estimate=pl.CostEstimate(
+            flops=2 * count * D * D, bytes_accessed=3_000_000, transcendentals=0
+        ),
+        name="own_rows",
+    )(row, tokens, types, table, w_gate, cotangent)
+
+
+def pair_columns(pair_ref, k, many):
+    _, _, length, width = pair_ref.shape
+    blocks = [pair_ref[p, pl.ds(k, many)] for p in range(2)]
+    rows = jnp.concatenate(blocks, axis=1).reshape(many * 2 * length, width)
+    values = rows.T.astype(jnp.float32)
+    centred = values - jnp.mean(values, axis=0, keepdims=True)
+    inv_std = lax.rsqrt(jnp.mean(centred * centred, axis=0, keepdims=True) + EPS)
+    return centred, inv_std
+
+
+def bias_kernel(pair_ref, weight_ref, mask_ref, out_ref, flat_ref):
+    _, count, length, width = pair_ref.shape
+    whole = flat_ref.shape[0] // H
+    weight = jnp.concatenate([weight_ref[...]] * 2, axis=1)
+    many = 4
+    base = pl.program_id(0) * count
+
+    def step(n, carry):
+        k = n * many
+        centred, inv_std = pair_columns(pair_ref, k, many)
+        bias = matmul(weight, jnp.concatenate(halves(centred), axis=0)) * inv_std
+        for m in range(many):
+            lanes = slice(m * 2 * length, (m + 1) * 2 * length)
+            flat_ref[pl.ds(base + k + m, H, stride=whole), :] = bias[:, lanes]
+        return carry
+
+    lax.fori_loop(0, count // many, step, 0, unroll=2)
+
+    @pl.when(pl.program_id(0) == pl.num_programs(0) - 1)
+    def _():
+        keep = jnp.broadcast_to(mask_ref[...].astype(jnp.float32), (128, length)).T
+        keep = jnp.concatenate([keep] * (2 * whole // 128), axis=1) == 1.0
+        for h in range(H):
+            turned = flat_ref[h * whole : (h + 1) * whole, :].T
+            bias = jnp.concatenate([turned[:length], turned[length:]], axis=1)
+            out_ref[h] = jnp.where(keep, bias, MASKED)
+
+
+def pair_bias(pair, weight_t, mask):
+    row_count, tok_col, width = pair.shape
+    steps = 4
+    whole = row_count // 2
+    count = whole // steps
+    return pl.pallas_call(
+        bias_kernel,
+        out_shape=jax.ShapeDtypeStruct((H, tok_col, row_count), jnp.float32),
+        grid=(steps,),
+        in_specs=[
+            pl.BlockSpec((2, count, tok_col, width), lambda i: (0, i, 0, 0)),
+            pl.BlockSpec(weight_t.shape, lambda i: (0, 0)),
+            pl.BlockSpec(mask.shape, lambda i: (0, 0)),
+        ],
+        out_specs=pl.BlockSpec((H, tok_col, row_count), lambda i: (0, 0, 0)),
+        scratch_shapes=[pltpu.VMEM((H * whole, 2 * tok_col), jnp.float32)],
+        compiler_params=params(24),
+        cost_estimate=pl.CostEstimate(
+            flops=row_count * tok_col * width * 3000, bytes_accessed=5_000_000, transcendentals=0
+        ),
+        name="pair_bias",
+    )(pair.reshape(2, whole, tok_col, width), weight_t, mask)
+
+
+def shift_of(top):
+    return jnp.floor(jnp.clip(14.0 - jnp.log2(top), -100.0, 100.0))
+
+
+def attention_kernel(tokens_ref, bias_ref, back_ref, grad_bias_ref, sum_ref):
+    n_col = tokens_ref.shape[0]
+    tok_col, row_count = bias_ref.shape[1:]
+    half = back_ref.shape[2] // tok_col
+    n_row = bias_ref.shape[0] // n_col
+    step = pl.program_id(0)
+
+    @pl.when(step == 0)
+    def _():
+        sum_ref[...] = jnp.zeros_like(sum_ref)
+
+    outs = []
+    for sample in range(half):
+        lanes = slice(sample * tok_col, (sample + 1) * tok_col)
+
+        def side(slot):
+            return jnp.concatenate([tokens_ref[c, slot, :, lanes] for c in range(n_col)], axis=1)
+
+        query_t, key_t, value_t, grad_t = [side(slot) for slot in range(4)]
+        key = key_t.T
+        value = value_t.T
+        attended_parts, grad_query_parts = [], []
+        grad_key = jnp.zeros(key_t.shape, jnp.float32)
+        grad_value = jnp.zeros(key_t.shape, jnp.float32)
+        for block in range(n_row):
+            cols = slice(block * row_count, (block + 1) * row_count)
+            heads = slice(block * n_col, (block + 1) * n_col)
+            bias = bias_ref[heads].reshape(n_col * tok_col, row_count)
+            query_b = query_t[:, cols]
+            grad_b = grad_t[:, cols]
+            scores = matmul(key, query_b) * SCALE + bias
+            scores = jnp.where(bias < -60000.0, -1000000000.0, scores)
+            expo = jnp.exp(scores - jnp.max(scores, axis=0, keepdims=True))
+            share = 1.0 / jnp.sum(expo, axis=0, keepdims=True)
+            attended = matmul(value_t, expo.astype(jnp.bfloat16)) * share
+            delta = jnp.sum(grad_b.astype(jnp.float32) * attended, axis=0, keepdims=True)
+            probs = expo * share
+            grad_scores = probs * (matmul(value, grad_b) - delta)
+            rounded = grad_scores.astype(jnp.bfloat16)
+            attended_parts.append(attended)
+            grad_query_parts.append(matmul(key_t, rounded) * SCALE)
+            grad_key = grad_key + matmul_nt(query_b, rounded)
+            grad_value = grad_value + matmul_nt(grad_b, probs.astype(jnp.bfloat16))
+            sum_ref[heads] += grad_scores.reshape(n_col, tok_col, row_count)
+        outs.append(
+            (
+                jnp.concatenate(grad_query_parts, axis=1),
+                grad_key * SCALE,
+                grad_value,
+                jnp.concatenate(attended_parts, axis=1),
+            )
+        )
+    spare = jnp.zeros((8 - 4, half * tok_col), jnp.float32)
+    tops = [jnp.max(jnp.abs(out[slot]), axis=0, keepdims=True) for slot in range(4) for out in outs]
+    shifts = shift_of(jnp.concatenate(tops, axis=0))
+    scales = jnp.exp2(shifts)
+    scaled = [
+        [out[slot] * scales[slot * half + n : slot * half + n + 1] for n, out in enumerate(outs)]
+        for slot in range(4)
+    ]
+    for c in range(n_col):
+        lanes = slice(c * tok_col, (c + 1) * tok_col)
+        for slot in range(4):
+            back_ref[c, slot * CH : (slot + 1) * CH, :] = jnp.concatenate(
+                [part[:, lanes] for part in scaled[slot]], axis=1
+            )
+        tails = [
+            jnp.concatenate([shifts[slot * half + n :, lanes][:1] for n in range(half)], axis=1)
+            for slot in range(4)
+        ]
+        back_ref[c, 4 * CH :, :] = jnp.concatenate(tails + [spare], axis=0)
+
+    @pl.when(step == pl.num_programs(0) - 1)
+    def _():
+        for head in range(n_row * n_col):
+            sums = sum_ref[head]
+            shift = shift_of(jnp.max(jnp.abs(sums), axis=0, keepdims=True))
+            grad_bias_ref[head, :tok_col, :] = sums * jnp.exp2(shift)
+            grad_bias_ref[head, tok_col:, :] = jnp.broadcast_to(shift, (8, row_count))
+
+
+def attention(arrived, bias, n_row):
+    n_col, _, _, held = arrived.shape
+    _, tok_col, row_count = bias.shape
+    half = held // tok_col // n_row
+    width = half * tok_col
+    back_shape = (n_row * n_col, 4 * CH + 8, width)
+    bias_shape = (n_row * n_col, tok_col + 8, row_count)
+    return pl.pallas_call(
+        attention_kernel,
+        out_shape=[
+            jax.ShapeDtypeStruct(back_shape, jnp.float32),
+            jax.ShapeDtypeStruct(bias_shape, jnp.float32),
+        ],
+        grid=(n_row,),
+        in_specs=[
+            pl.BlockSpec((n_col, 4, CH, width), lambda i: (0, 0, 0, i)),
+            pl.BlockSpec(bias.shape, lambda i: (0, 0, 0)),
+        ],
+        out_specs=[
+            pl.BlockSpec((n_col, 4 * CH + 8, width), lambda i: (i, 0, 0)),
+            pl.BlockSpec(bias_shape, lambda i: (0, 0, 0)),
+        ],
+        scratch_shapes=[pltpu.VMEM(bias.shape, jnp.float32)],
+        compiler_params=params(24),
+        cost_estimate=pl.CostEstimate(
+            flops=8_000_000_000, bytes_accessed=6_000_000, transcendentals=1_000_000
+        ),
+        name="attention",
+    )(arrived, bias)
+
+
+def back_kernel(
+    back_ref, slope_ref, normed_ref, inv_ref, wq_ref, wk_ref, wv_ref, wg_ref, out_ref
+):
+    count = back_ref.shape[-1]
+
+    def side(slot):
+        scale = jnp.exp2(-back_ref[:, 4 * CH + slot : 4 * CH + slot + 1, :])
+        return (back_ref[:, slot * CH : (slot + 1) * CH, :] * scale).reshape(D, count)
+
+    total = jnp.zeros((D, count), jnp.float32)
+    for slot, ref in enumerate((wq_ref, wk_ref, wv_ref)):
+        parts = matmul(ref[...], jnp.concatenate(halves(side(slot)), axis=1))
+        total = total + (parts[:, :count] + parts[:, count:])
+    total = total + matmul(wg_ref[...], (side(3) * slope_ref[...]).astype(jnp.bfloat16))
+    normed = normed_ref[...]
+    result = inv_ref[:1] * (
+        total
+        - jnp.mean(total, axis=0, keepdims=True)
+        - normed * jnp.mean(total * normed, axis=0, keepdims=True)
+    )
+    out_ref[...] = result.T.astype(jnp.bfloat16)
+
+
+def token_back(back, slope, normed, inv_std, weights):
+    count = back.shape[-1]
+    return pl.pallas_call(
+        back_kernel,
+        out_shape=jax.ShapeDtypeStruct((count, D), jnp.bfloat16),
+        compiler_params=params(56),
+        cost_estimate=pl.CostEstimate(
+            flops=20 * count * D * D, bytes_accessed=8_000_000, transcendentals=0
+        ),
+        name="token_back",
+    )(back, slope, normed, inv_std, *weights)
+
+
+def pair_back_kernel(factor, pair_ref, grads_ref, weight_ref, out_ref, part_ref, flat_ref):
+    _, count, length, width = pair_ref.shape
+    whole = flat_ref.shape[0] // H
+    weight = weight_ref[...].astype(jnp.float32)
+    weight = halves(weight - jnp.mean(weight, axis=1, keepdims=True))
+    weight = jnp.concatenate([weight[0], weight[0], weight[1], weight[1]], axis=0).T
+    many = 4
+    base = pl.program_id(0) * count
+
+    @pl.when(pl.program_id(0) == 0)
+    def _():
+        part_ref[...] = jnp.zeros_like(part_ref)
+        for h in range(H):
+            grads = grads_ref[h]
+            both = jnp.concatenate([grads[:, :whole], grads[:, whole:]], axis=0)
+            flat_ref[h * whole : (h + 1) * whole, :] = both.T
+
+    def step(n, carry):
+        k = n * many
+        centred, inv_std = pair_columns(pair_ref, k, many)
+        normed = centred * inv_std
+        grads = jnp.concatenate(
+            [flat_ref[pl.ds(base + k + m, H, stride=whole), :] for m in range(many)], axis=1
+        )
+        grads = jnp.concatenate(halves(grads), axis=0)
+        grad_in = matmul(weight, jnp.concatenate([grads, grads], axis=0))
+        overlap = jnp.mean(grad_in * normed, axis=0, keepdims=True)
+        result = (grad_in - normed * overlap) * (inv_std * factor)
+        result = result.astype(jnp.bfloat16).T.reshape(many, 2 * length, width)
+        for p in range(2):
+            out_ref[p, pl.ds(k, many)] = result[:, p * length : (p + 1) * length]
+        return carry + matmul_nt(jnp.concatenate(halves(normed), axis=0), grads)
+
+    parts = jnp.zeros((2 * width, 2 * H), jnp.float32)
+    parts = lax.fori_loop(0, count // many, step, parts, unroll=2)
+    parts = parts[:, :H] + parts[:, H:]
+    part_ref[...] += (parts[:width] + parts[width:]).T
+
+
+def pair_backward(pair, grads, weight_t, factor):
+    row_count, tok_col, width = pair.shape
+    steps = 4
+    whole = row_count // 2
+    pair_spec = pl.BlockSpec((2, whole // steps, tok_col, width), lambda i: (0, i, 0, 0))
+    pair_grad, part = pl.pallas_call(
+        lambda *refs: pair_back_kernel(factor, *refs),
+        out_shape=[
+            jax.ShapeDtypeStruct((2, whole, tok_col, width), jnp.bfloat16),
+            jax.ShapeDtypeStruct((H, width), jnp.float32),
+        ],
+        grid=(steps,),
+        in_specs=[
+            pair_spec,
+            pl.BlockSpec(grads.shape, lambda i: (0, 0, 0)),
+            pl.BlockSpec(weight_t.shape, lambda i: (0, 0)),
+        ],
+        out_specs=[pair_spec, pl.BlockSpec((H, width), lambda i: (0, 0))],
+        scratch_shapes=[pltpu.VMEM((H * whole, 2 * tok_col), jnp.float32)],
+        compiler_params=params(24),
+        cost_estimate=pl.CostEstimate(
+            flops=row_count * tok_col * width * 5000, bytes_accessed=11_000_000, transcendentals=0
+        ),
+        name="pair_backward",
+    )(pair.reshape(2, whole, tok_col, width), grads, weight_t)
+    return pair_grad.reshape(pair.shape), part
+
+
+def unscaled(block, rows):
+    block = block.astype(jnp.float32)
+    return block[:, :rows] * jnp.exp2(-block[:, rows : rows + 1])
+
+
+def swap(block, axis):
+    return lax.ppermute(block, axis, [(0, 1), (1, 0)])
+
+
+def body_heads(
+    tokens, restype, type_table, key_mask, pair, w_bias, w_query, w_key, w_value, w_gate, cotangent
+):
+    n_row = lax.axis_size("row")
+    n_col = lax.axis_size("col")
+    n_samp = lax.axis_size("samp")
+    samp_dev = tokens.shape[0]
+    tok_col = tokens.shape[1]
+    row_count = pair.shape[0]
+    total_tokens = tok_col * n_col
+    half = samp_dev // n_row
+    row_index = lax.axis_index("row")
+    row = row_index.astype(jnp.int32).reshape(1)
+    types = restype.reshape(1, tok_col)
+    weight_t = w_bias.T
+    weights = (w_query, w_key, w_value, w_gate)
+
+    message = token_messages(
+        row, tokens, types, type_table, weights, cotangent, n_row, n_col
+    )
+    message, bias_weight = lax.optimization_barrier((message, weight_t))
+    arrived = lax.all_to_all(message, "col", 0, 0, tiled=True)
+    bias = pair_bias(pair, bias_weight, key_mask.reshape(1, tok_col))
+    arrived, bias = lax.optimization_barrier((arrived, bias.astype(jnp.float16)))
+    bias = lax.all_to_all(bias, ("row", "col"), 0, 0, tiled=True).astype(jnp.float32)
+    slope, normed, inv_std = own_rows(row, tokens, types, type_table, w_gate, cotangent, half)
+
+    back, grad_bias = attention(arrived, bias, n_row)
+    grad_bias = lax.all_to_all(
+        grad_bias.astype(jnp.float16), ("row", "col"), 0, 0, tiled=True
+    )
+    other_bias = swap(grad_bias, "samp")
+    back = lax.all_to_all(back.astype(jnp.float16), ("row", "col"), 0, 0, tiled=True)
+    grads = unscaled(grad_bias, tok_col) + unscaled(other_bias, tok_col)
+
+    samples = samp_dev * n_samp
+    pair_grad, part = pair_backward(pair, grads, weight_t, total_tokens / samples)
+    parts = lax.all_to_all(
+        jnp.broadcast_to(part[None], (H,) + part.shape), ("row", "col"), 0, 0, tiled=True
+    )
+    bias_weight_grad = jnp.sum(parts, axis=0).T / samples
+
+    back, part = lax.optimization_barrier((back, part))
+    back = back.astype(jnp.float32)
+    token_half = token_back(back, slope, normed, inv_std, weights)
+    token_half = token_half.reshape(half, tok_col, D)
+    other = swap(token_half, "row")
+    first = row_index == 0
+    token_grad = jnp.concatenate(
+        [jnp.where(first, token_half, other), jnp.where(first, other, token_half)], axis=0
+    )
+    return (token_grad, pair_grad, bias_weight_grad)
+
+
+def body(*args):
+    n_row = lax.axis_size("row")
+    n_col = lax.axis_size("col")
+    tokens = args[0]
+    pair = args[4]
+    fits = n_row == 2 and n_row * n_col == H and lax.axis_size("samp") == 2
+    square = pair.shape[0] * n_row == pair.shape[1] * n_col
+    if fits and square and tokens.shape[0] == 4 and tokens.shape[1] == 64:
+        return body_heads(*args)
+    return body_any(*args)
+
+
 def solution(mesh):
     placed = (
         P("samp", "col", None),

time: 502 us -> 130 us (0.26); the launches traced: 493 us -> 129 us
  waiting for transfers between devices: 288 us -> 24.2 us
  matrix products: 68.4 us -> 0 us
  local copies, waits for them, and re-layouts: 55.1 us -> 4.74 us
  Pallas kernels: 0 us -> 38.8 us
  other arithmetic: 31.5 us -> 5.35 us
  starting transfers between devices: 0.63 us -> 16.4 us
  between operations: 15 us -> 0.78 us
    psum x4 -> x0, waiting for transfers between devices: 196 us -> none  [the longest x1 69.1 us: body(): lax.psum((jnp.sum(expo, axis=-1), partial_out.reshape(samp_dev, row_count...]
    dot_general x18 -> x0, matrix products: 68.4 us -> none  [the longest x4 10.6 us: project(): jnp.einsum('std,de->ste', rows_in, weight, preferred_element_type=jnp.flo...]
    pmax x1 -> x0, waiting for transfers between devices: 50.6 us -> none  [body(): top = lax.pmax(jnp.max(scores, axis=-1), 'col')]
    reduce_scatter x1 -> x0, waiting for transfers between devices: 41.8 us -> none  [body(): lax.psum_scatter(lax.dynamic_update_slice_in_dim(blank, grad_query, row_i...]
    pallas_call x0 -> x6, Pallas kernels: none -> 38.8 us  [the longest x1 12.4 us: pair_backward(): pl.pallas_call(lambda *refs: pair_back_kernel(factor, *refs), out_shape=[...]
    all_to_all x0 -> x2, blocking collectives: none -> 38.7 us  [the longest x1 21.1 us: body_heads(): lax.all_to_all(grad_bias.astype(jnp.float16), ('row', 'col'), 0, 0, tiled...]
    psum x1 -> x0, blocking collectives: 34.2 us -> none  [body(): weight_sum = lax.psum(weight_part, ('row', 'col'))]
    unnamed x54 -> x10, local copies, waits for them, and re-layouts: 22.1 us -> 4.08 us
  transfers between devices with their start and end apart: 6 -> 5, of which waited for: 6 -> 4; matrix products, arithmetic and copies ran while one was open for 18% -> 3% of each run, Pallas kernels for 0% -> 17%
where the time goes in v1:
time: 130 us; the launch traced here: 129 us
  Pallas kernels  38.8 us (30%)
  blocking collectives  38.7 us (30%)
  waiting for transfers between devices  24.2 us (19%)
  starting transfers between devices  16.4 us (13%)
  other arithmetic  5.35 us (4%)
  local copies, waits for them, and re-layouts  4.74 us (4%)
    all_to_all x1, blocking collectives, body_heads(): lax.all_to_all(grad_bias.astype(jnp.float16), ('row', 'col'), 0, 0, tiled...  21.1 us
    all_to_all x1, blocking collectives, body_heads(): lax.all_to_all(bias, ('row', 'col'), 0, 0, tiled=True).astype(jnp.float32)  17.6 us
    pallas_call x1, Pallas kernels, pair_backward(): pl.pallas_call(lambda *refs: pair_back_kernel(factor, *refs), out_shape=[...  12.4 us
    all_to_all x1, waiting for transfers between devices, body_heads(): arrived = lax.all_to_all(message, 'col', 0, 0, tiled=True)  12 us
    ppermute x2, waiting for transfers between devices, swap(): return lax.ppermute(block, axis, [(0, 1), (1, 0)])  7.47 us
    pallas_call x1, Pallas kernels, attention(): pl.pallas_call(attention_kernel, out_shape=[jax.ShapeDtypeStruct(back_sha...  7.33 us
    pallas_call x1, Pallas kernels, pair_bias(): pl.pallas_call(bias_kernel, out_shape=jax.ShapeDtypeStruct((H, tok_col, r...  6.63 us
    all_to_all x1, starting transfers between devices, body_heads(): arrived = lax.all_to_all(message, 'col', 0, 0, tiled=True)  6.46 us
  transfers between devices with their start and end apart: 5, of which 4 were waited for; matrix products, arithmetic and copies ran while one was open for 3% of the time, Pallas kernels for 17%

profile of v1, /device:TPU:0, one launch (start us, length us, event | category | flops | bytes accessed | tf_op | source)
XLA Modules:
  0.0 129.0 jit_solution(13125762285896430119)
XLA Ops:
  0.6 4.1 %token_messages.1 = bf16[8,4,48,256]{3,2,1,0:T(8,128)(2,1)} custom-call(s32[1]{0:T(128)} %bitcast.row_ref, bf16[4,64,768]{2,1,0:T(8,128)(2,1)} %tokens_ref.3, s32[1,64]{1,0:T(1,128)} %bitcast.24, bf16[32,768]{1,0:T(8,128)(2,1)} %table_ref.3, bf16[768,768]{1,0:T(8,128)(2,1)} %wq_ref.3, bf16[768,768]{1,0:T(8,128)(2,1)} %wk_ref.3, bf16[768,768]{1,0:T(8,128)(2,1)} %wv_ref.3, ...), custom_call_target="tpu_custom_call" | custom-call | flops 603979776 | bytes 4000000 | tf_op jit(solution)/shard_map/token_messages/pallas_call | solution.py:244
  4.8 0.0 copy-start.2
  4.8 0.0 copy-start.3
  4.8 6.5 %all-to-all-start = ((bf16[8,4,48,256]{3,2,1,0:T(8,128)(2,1)}), bf16[8,4,48,256]{3,2,1,0:T(8,128)(2,1)S(1)}, u32[]{:S(2)}, u32[]{:S(2)}) async-start(bf16[8,4,48,256]{3,2,1,0:T(8,128)(2,1)} %token_messages.1), calls=%async_computation | async-start | bytes 1572864 | tf_op jit(solution)/shard_map/all_to_all | solution.py:629
  11.2 0.0 copy-done.2
  11.2 0.0 copy-done.3
  11.3 0.0 copy-start
  11.3 2.2 %copy-done = bf16[256,64,128]{2,1,0:T(8,128)(2,1)S(1)} copy-done((bf16[256,64,128]{2,1,0:T(8,128)(2,1)S(1)}, bf16[256,64,128]{2,1,0:T(8,128)(2,1)}, u32[]{:S(2)}) %copy-start) | copy-done | bytes 4194328
  13.4 6.6 %pair_bias.1 = f32[16,64,256]{2,1,0:T(8,128)S(1)} custom-call(bf16[2,128,64,128]{3,2,1,0:T(8,128)(2,1)S(1)} %bitcast.15, bf16[16,128]{1,0:T(8,128)(2,1)S(1)} %bitcast.17, s32[1,64]{1,0:T(1,128)S(1)} %bitcast.19), custom_call_target="tpu_custom_call" | custom-call | flops 6291456000 | bytes 5000000 | tf_op jit(solution)/shard_map/pair_bias/pallas_call | solution.py:361
  20.1 0.1 convert_element_type.21
  20.2 12.0 %all-to-all-done.tokens_ref = bf16[8,4,48,256]{3,2,1,0:T(8,128)(2,1)S(1)} async-done(((bf16[8,4,48,256]{3,2,1,0:T(8,128)(2,1)}), bf16[8,4,48,256]{3,2,1,0:T(8,128)(2,1)S(1)}, u32[]{:S(2)}, u32[]{:S(2)}) %all-to-all-start) | async-done | bytes 786464 | tf_op jit(solution)/shard_map/all_to_all | solution.py:629
  32.2 17.6 %all_to_all.25 = f16[16,64,256]{2,1,0:T(8,128)(2,1)S(1)} all-to-all(f16[16,64,256]{2,1,0:T(8,128)(2,1)S(1)} %convert_element_type.21), channel_id=1, replica_groups=mesh['samp'=2,'row'=2,'col'=8] {'row','col'}, dimensions={0} | all-to-all | bytes 1048576 | tf_op jit(solution)/shard_map/all_to_all | solution.py:632
  49.8 0.1 convert_element_type.22.bias_ref
  49.9 7.3 %attention.1 = (f32[16,200,128]{2,1,0:T(8,128)S(1)}, f32[16,72,256]{2,1,0:T(8,128)S(1)}) custom-call(bf16[8,4,48,256]{3,2,1,0:T(8,128)(2,1)S(1)} %all-to-all-done.tokens_ref, f32[16,64,256]{2,1,0:T(8,128)S(1)} %convert_element_type.22.bias_ref), custom_call_target="tpu_custom_call" | custom-call | flops 8000000000 | bytes 6000000 | tf_op jit(solution)/shard_map/attention/pallas_call | solution.py:472
  57.3 0.1 convert_element_type.24
  57.4 21.1 %all_to_all.26 = f16[16,72,256]{2,1,0:T(8,128)(2,1)S(1)} all-to-all(f16[16,72,256]{2,1,0:T(8,128)(2,1)S(1)} %convert_element_type.24), channel_id=1, replica_groups=mesh['samp'=2,'row'=2,'col'=8] {'row','col'}, dimensions={0} | all-to-all | bytes 1179648 | tf_op jit(solution)/shard_map/all_to_all | solution.py:636
  78.4 1.5 %collective-permute-start = (f16[16,72,256]{2,1,0:T(8,128)(2,1)S(1)}, f16[16,72,256]{2,1,0:T(8,128)(2,1)S(1)}, u32[]{:S(2)}, u32[]{:S(2)}) collective-permute-start(f16[16,72,256]{2,1,0:T(8,128)(2,1)S(1)} %all_to_all.26), channel_id=1, source_target_pairs={{0,16},{16,0},{1,17},{17,1},{2,18},{18,2},{3,19},{19,3},{4,20},{20... | collective-permute-start | bytes 1769480 | tf_op jit(solution)/shard_map/ppermute | solution.py:605
  79.9 3.0 %own_rows.1 = (f32[768,128]{1,0:T(8,128)}, f32[768,128]{1,0:T(8,128)}, f32[8,128]{1,0:T(8,128)}) custom-call(s32[1]{0:T(128)} %bitcast.row_ref, bf16[4,64,768]{2,1,0:T(8,128)(2,1)} %tokens_ref.3, s32[1,64]{1,0:T(1,128)} %bitcast.25, bf16[32,768]{1,0:T(8,128)(2,1)} %table_ref.3, bf16[768,768]{1,0:T(8,128)(2,1)} %wg_ref.5, bf16[4,64,768]{2,1,0:T(8,128)(2,1)} %cot_ref.3), custom_call_target="tpu_custom_call" | custom-call | flops 150994944 | bytes 3000000 | tf_op jit(solution)/shard_map/own_rows/pallas_call | solution.py:287
  83.0 1.0 convert_element_type.23
  84.0 3.6 %all-to-all-start.2 = ((f16[16,200,128]{2,1,0:T(8,128)(2,1)}), f16[16,200,128]{2,1,0:T(8,128)(2,1)S(1)}, u32[]{:S(2)}, u32[]{:S(2)}) async-start(f16[16,200,128]{2,1,0:T(8,128)(2,1)} %convert_element_type.23), calls=%async_computation.2 | async-start | bytes 1638400 | tf_op jit(solution)/shard_map/all_to_all | solution.py:640
  87.6 0.1 convert_element_type.25
  87.8 6.0 %collective-permute-done = f16[16,72,256]{2,1,0:T(8,128)(2,1)S(1)} collective-permute-done((f16[16,72,256]{2,1,0:T(8,128)(2,1)S(1)}, f16[16,72,256]{2,1,0:T(8,128)(2,1)S(1)}, u32[]{:S(2)}, u32[]{:S(2)}) %collective-permute-start) | collective-permute-done | bytes 589856 | tf_op jit(solution)/shard_map/ppermute | solution.py:605
  93.8 0.0 copy-start.1
  93.8 0.1 convert_element_type.26
  93.9 0.2 fusion.refs_1_
  94.1 1.9 %copy-done.1 = bf16[256,64,128]{2,1,0:T(8,128)(2,1)S(1)} copy-done((bf16[256,64,128]{2,1,0:T(8,128)(2,1)S(1)}, bf16[256,64,128]{2,1,0:T(8,128)(2,1)}, u32[]{:S(2)}) %copy-start.1) | copy-done | bytes 4194328
  96.0 12.4 %pair_backward.1 = (bf16[2,128,64,128]{3,2,1,0:T(8,128)(2,1)}, f32[16,128]{1,0:T(8,128)S(1)}) custom-call(bf16[2,128,64,128]{3,2,1,0:T(8,128)(2,1)S(1)} %bitcast.16, f32[16,64,256]{2,1,0:T(8,128)S(1)} %fusion.refs_1_, bf16[16,128]{1,0:T(8,128)(2,1)S(1)} %bitcast.18), custom_call_target="tpu_custom_call" | custom-call | flops 10485760000 | bytes 11000000 | tf_op jit(solution)/shard_map/pair_backward/pallas_call | solution.py:576
  108.3 0.0 all-to-all-done.2
  108.3 1.3 %convert_element_type.27.back_ref = f32[16,200,128]{2,1,0:T(8,128)} convert(f16[16,200,128]{2,1,0:T(8,128)(2,1)S(1)} %all-to-all-done.2) | non-fusion elementwise | flops 409600 | bytes 2457600 | tf_op jit(solution)/shard_map/convert_element_type | solution.py:651
  109.6 5.3 %token_back.1 = bf16[128,768]{1,0:T(8,128)(2,1)} custom-call(f32[16,200,128]{2,1,0:T(8,128)} %convert_element_type.27.back_ref, f32[768,128]{1,0:T(8,128)} %get-tuple-element.23.slope_ref, f32[768,128]{1,0:T(8,128)} %get-tuple-element.24.normed_ref, f32[8,128]{1,0:T(8,128)} %get-tuple-element.25.inv_ref, bf16[768,768]{1,0:T(8,128)(2,1)} %wq_ref.3, ...), custom_call_target="tpu_custom_call" | custom-call | flops 1509949440 | bytes 8000000 | tf_op jit(solution)/shard_map/token_back/pallas_call | solution.py:521
  115.0 0.7 collective-permute-start.1
  115.7 0.7 broadcast_in_dim.2
  116.3 4.1 %all-to-all-start.4 = ((f32[16,16,128]{2,1,0:T(8,128)}), f32[16,16,128]{2,1,0:T(8,128)S(1)}, u32[]{:S(2)}, u32[]{:S(2)}) async-start(f32[16,16,128]{2,1,0:T(8,128)} %broadcast_in_dim.2), calls=%async_computation.4 | async-start | bytes 262144 | tf_op jit(solution)/shard_map/all_to_all | solution.py:645
  120.5 1.5 %collective-permute-done.1 = bf16[2,64,768]{2,1,0:T(8,128)(2,1)S(1)} collective-permute-done((bf16[2,64,768]{2,1,0:T(8,128)(2,1)}, bf16[2,64,768]{2,1,0:T(8,128)(2,1)S(1)}, u32[]{:S(2)}, u32[]{:S(2)}) %collective-permute-start.1) | collective-permute-done | bytes 196640 | tf_op jit(solution)/shard_map/ppermute | solution.py:605
  121.9 1.0 broadcast_select_fusion.1
  122.9 0.8 pad_maximum_fusion
  123.7 4.7 %all-to-all-done.4 = f32[16,16,128]{2,1,0:T(8,128)S(1)} async-done(((f32[16,16,128]{2,1,0:T(8,128)}), f32[16,16,128]{2,1,0:T(8,128)S(1)}, u32[]{:S(2)}, u32[]{:S(2)}) %all-to-all-start.4) | async-done | bytes 131104 | tf_op jit(solution)/shard_map/all_to_all | solution.py:645
  128.4 0.6 multiply_bitcast_fusion
  (5 shorter events, 0.1 us)
Async XLA Ops:
  4.8 6.5 %copy-start.2 = (bf16[128,16]{0,1:T(8,128)(2,1)S(1)}, bf16[128,16]{0,1:T(8,128)(2,1)}, u32[]{:S(2)}) copy-start(bf16[128,16]{0,1:T(8,128)(2,1)} %param.16) | copy-start | bytes 12292
  4.8 6.5 %copy-start.3 = (s32[64]{0:T(128)S(1)}, s32[64]{0:T(128)}, u32[]{:S(2)}) copy-start(s32[64]{0:T(128)} %param.14) | copy-start | bytes 772
  4.8 27.4 %all-to-all-start = ((bf16[8,4,48,256]{3,2,1,0:T(8,128)(2,1)}), bf16[8,4,48,256]{3,2,1,0:T(8,128)(2,1)S(1)}, u32[]{:S(2)}, u32[]{:S(2)}) async-start(bf16[8,4,48,256]{3,2,1,0:T(8,128)(2,1)} %token_messages.1), calls=%async_computation | async-start | bytes 1572864 | tf_op jit(solution)/shard_map/all_to_all | solution.py:629
  11.3 2.2 %copy-start = (bf16[256,64,128]{2,1,0:T(8,128)(2,1)S(1)}, bf16[256,64,128]{2,1,0:T(8,128)(2,1)}, u32[]{:S(2)}) copy-start(bf16[256,64,128]{2,1,0:T(8,128)(2,1)} %param.15) | copy-start | bytes 12582916
  78.4 15.3 %collective-permute-start = (f16[16,72,256]{2,1,0:T(8,128)(2,1)S(1)}, f16[16,72,256]{2,1,0:T(8,128)(2,1)S(1)}, u32[]{:S(2)}, u32[]{:S(2)}) collective-permute-start(f16[16,72,256]{2,1,0:T(8,128)(2,1)S(1)} %all_to_all.26), channel_id=1, source_target_pairs={{0,16},{16,0},{1,17},{17,1},{2,18},{18,2},{3,19},{19,3},{4,20},{20... | collective-permute-start | bytes 1769480 | tf_op jit(solution)/shard_map/ppermute | solution.py:605
  84.0 24.3 %all-to-all-start.2 = ((f16[16,200,128]{2,1,0:T(8,128)(2,1)}), f16[16,200,128]{2,1,0:T(8,128)(2,1)S(1)}, u32[]{:S(2)}, u32[]{:S(2)}) async-start(f16[16,200,128]{2,1,0:T(8,128)(2,1)} %convert_element_type.23), calls=%async_computation.2 | async-start | bytes 1638400 | tf_op jit(solution)/shard_map/all_to_all | solution.py:640
  93.8 2.2 %copy-start.1 = (bf16[256,64,128]{2,1,0:T(8,128)(2,1)S(1)}, bf16[256,64,128]{2,1,0:T(8,128)(2,1)}, u32[]{:S(2)}) copy-start(bf16[256,64,128]{2,1,0:T(8,128)(2,1)} %param.15) | copy-start | bytes 12582916
  115.0 7.0 %collective-permute-start.1 = (bf16[2,64,768]{2,1,0:T(8,128)(2,1)}, bf16[2,64,768]{2,1,0:T(8,128)(2,1)S(1)}, u32[]{:S(2)}, u32[]{:S(2)}) collective-permute-start(bf16[2,64,768]{2,1,0:T(8,128)(2,1)} %bitcast.20), channel_id=1, source_target_pairs={{0,8},{8,0},{1,9},{9,1},{2,10},{10,2},{3,11},{11,3},{4,12},{12,4},... | collective-permute-start | bytes 589832 | tf_op jit(solution)/shard_map/ppermute | solution.py:605
  116.3 12.1 %all-to-all-start.4 = ((f32[16,16,128]{2,1,0:T(8,128)}), f32[16,16,128]{2,1,0:T(8,128)S(1)}, u32[]{:S(2)}, u32[]{:S(2)}) async-start(f32[16,16,128]{2,1,0:T(8,128)} %broadcast_in_dim.2), calls=%async_computation.4 | async-start | bytes 262144 | tf_op jit(solution)/shard_map/all_to_all | solution.py:645

commit v2 on v1

--- a/solution.py
+++ b/solution.py
@@ -217,35 +217,36 @@
     return unit_rows(embedded.reshape(count * length, width))
 
 
-def token_kernel(
-    row_ref, tokens_ref, types_ref, table_ref, wq_ref, wk_ref, wv_ref, wg_ref, cot_ref, out_ref
-):
+def token_kernel(row_ref, col_ref, tokens_ref, types_ref, table_ref, *refs):
+    wq_ref, wk_ref, wv_ref, wg_ref, cot_ref = refs[:5]
+    out_refs, side_ref = refs[5:-1], refs[-1]
     normed, _ = embed_rows(tokens_ref, types_ref, table_ref)
     act = normed.astype(jnp.bfloat16)
-    heads, _, _, count = out_ref.shape
-
-    def store(slot, rounded):
-        out_ref[:, slot] = rounded.T.reshape(heads, CH, count)
-
     for slot, ref in enumerate((wq_ref, wk_ref, wv_ref)):
-        store(slot, matmul(act, ref[...]).astype(jnp.bfloat16))
+        side_ref[slot] = matmul(act, ref[...]).astype(jnp.bfloat16).T
     gate = matmul(act, wg_ref[...]).astype(jnp.bfloat16).astype(jnp.float32)
     cot = cot_ref[...].reshape(gate.shape).astype(jnp.float32)
-    store(3, (cot * jax.nn.sigmoid(gate)).astype(jnp.bfloat16))
-
-
-def token_messages(row, tokens, types, table, weights, cotangent, n_row, n_col):
+    side_ref[3] = (cot * jax.nn.sigmoid(gate)).astype(jnp.bfloat16).T
+    for offset, out_ref in enumerate(out_refs):
+        for core in range(2):
+            start = pl.multiple_of((col_ref[0] ^ (2 * offset + core)) * CH, 16)
+            out_ref[core] = side_ref[:, pl.ds(start, CH), :]
+
+
+def token_messages(row, col, tokens, types, table, weights, cotangent, n_row, n_col):
     samp_dev, tok_col, _ = tokens.shape
     width = D // n_row
-    whole3 = lambda i, r: (0, 0, 0)
-    whole2 = lambda i, r: (0, 0)
-    weight_spec = pl.BlockSpec((D, width), lambda i, r: (0, r[0]))
-    shape = (n_col, 4, CH, samp_dev * tok_col)
+    held = samp_dev * tok_col
+    whole3 = lambda i, r, c: (0, 0, 0)
+    whole2 = lambda i, r, c: (0, 0)
+    weight_spec = pl.BlockSpec((D, width), lambda i, r, c: (0, r[0]))
+    shape = (2, 4, CH, held)
+    count = n_col // 2
     return pl.pallas_call(
         token_kernel,
-        out_shape=jax.ShapeDtypeStruct(shape, jnp.bfloat16),
+        out_shape=[jax.ShapeDtypeStruct(shape, jnp.bfloat16)] * count,
         grid_spec=pltpu.PrefetchScalarGridSpec(
-            num_scalar_prefetch=1,
+            num_scalar_prefetch=2,
             grid=(1,),
             in_specs=[
                 pl.BlockSpec(tokens.shape, whole3),
@@ -255,16 +256,17 @@
                 weight_spec,
                 weight_spec,
                 weight_spec,
-                pl.BlockSpec((samp_dev, tok_col, width), lambda i, r: (0, 0, r[0])),
+                pl.BlockSpec((samp_dev, tok_col, width), lambda i, r, c: (0, 0, r[0])),
             ],
-            out_specs=pl.BlockSpec(shape, lambda i, r: (0, 0, 0, 0)),
+            out_specs=[pl.BlockSpec(shape, lambda i, r, c: (0, 0, 0, 0))] * count,
+            scratch_shapes=[pltpu.VMEM((4, width, held), jnp.bfloat16)],
         ),
         compiler_params=params(56),
         cost_estimate=pl.CostEstimate(
-            flops=2 * samp_dev * tok_col * D * width * 4, bytes_accessed=4_000_000, transcendentals=0
+            flops=4_000_000_000, bytes_accessed=4_000_000, transcendentals=0
         ),
         name="token_messages",
-    )(row, tokens, types, table, *weights, cotangent)
+    )(row, col, tokens, types, table, *weights, cotangent)
 
 
 def own_kernel(
@@ -309,39 +311,43 @@
         ),
         compiler_params=params(56),
         cost_estimate=pl.CostEstimate(
-            flops=2 * count * D * D, bytes_accessed=3_000_000, transcendentals=0
+            flops=3_000_000_000, bytes_accessed=3_000_000, transcendentals=0
         ),
         name="own_rows",
     )(row, tokens, types, table, w_gate, cotangent)
+
+
+MANY = 4
 
 
 def pair_columns(pair_ref, k, many):
     _, _, length, width = pair_ref.shape
     blocks = [pair_ref[p, pl.ds(k, many)] for p in range(2)]
     rows = jnp.concatenate(blocks, axis=1).reshape(many * 2 * length, width)
-    values = rows.T.astype(jnp.float32)
-    centred = values - jnp.mean(values, axis=0, keepdims=True)
-    inv_std = lax.rsqrt(jnp.mean(centred * centred, axis=0, keepdims=True) + EPS)
-    return centred, inv_std
+    same = lax.broadcasted_iota(jnp.int32, (width, width), 0) == lax.broadcasted_iota(
+        jnp.int32, (width, width), 1
+    )
+    centring = (jnp.where(same, 1.0, 0.0) - 1.0 / width).astype(jnp.bfloat16)
+    centred = matmul_nt(centring, rows)
+    return centred, lax.rsqrt(jnp.mean(centred * centred, axis=0, keepdims=True) + EPS)
 
 
 def bias_kernel(pair_ref, weight_ref, mask_ref, out_ref, flat_ref):
     _, count, length, width = pair_ref.shape
     whole = flat_ref.shape[0] // H
     weight = jnp.concatenate([weight_ref[...]] * 2, axis=1)
-    many = 4
     base = pl.program_id(0) * count
 
     def step(n, carry):
-        k = n * many
-        centred, inv_std = pair_columns(pair_ref, k, many)
+        k = n * MANY
+        centred, inv_std = pair_columns(pair_ref, k, MANY)
         bias = matmul(weight, jnp.concatenate(halves(centred), axis=0)) * inv_std
-        for m in range(many):
+        for m in range(MANY):
             lanes = slice(m * 2 * length, (m + 1) * 2 * length)
             flat_ref[pl.ds(base + k + m, H, stride=whole), :] = bias[:, lanes]
         return carry
 
-    lax.fori_loop(0, count // many, step, 0, unroll=2)
+    lax.fori_loop(0, count // MANY, step, 0, unroll=2)
 
     @pl.when(pl.program_id(0) == pl.num_programs(0) - 1)
     def _():
@@ -353,35 +359,84 @@
             out_ref[h] = jnp.where(keep, bias, MASKED)
 
 
+STEPS = 4
+
+
+def split_spec(shape):
+    block = (shape[0] // STEPS,) + tuple(shape[1:])
+    return pl.BlockSpec(block, lambda i: (i,) + (0,) * (len(shape) - 1))
+
+
+def whole_spec(shape):
+    return pl.BlockSpec(tuple(shape), lambda i: (0,) * len(shape))
+
+
+def pair_spec(pair):
+    row_count, tok_col, width = pair.shape
+    block = (2, row_count // 2 // STEPS, tok_col, width)
+    return pl.BlockSpec(block, lambda i: (0, i, 0, 0))
+
+
 def pair_bias(pair, weight_t, mask):
     row_count, tok_col, width = pair.shape
-    steps = 4
     whole = row_count // 2
-    count = whole // steps
     return pl.pallas_call(
         bias_kernel,
         out_shape=jax.ShapeDtypeStruct((H, tok_col, row_count), jnp.float32),
-        grid=(steps,),
-        in_specs=[
-            pl.BlockSpec((2, count, tok_col, width), lambda i: (0, i, 0, 0)),
-            pl.BlockSpec(weight_t.shape, lambda i: (0, 0)),
-            pl.BlockSpec(mask.shape, lambda i: (0, 0)),
-        ],
-        out_specs=pl.BlockSpec((H, tok_col, row_count), lambda i: (0, 0, 0)),
+        grid=(STEPS,),
+        in_specs=[pair_spec(pair), whole_spec(weight_t.shape), whole_spec(mask.shape)],
+        out_specs=whole_spec((H, tok_col, row_count)),
         scratch_shapes=[pltpu.VMEM((H * whole, 2 * tok_col), jnp.float32)],
         compiler_params=params(24),
         cost_estimate=pl.CostEstimate(
-            flops=row_count * tok_col * width * 3000, bytes_accessed=5_000_000, transcendentals=0
+            flops=6_000_000_000, bytes_accessed=5_000_000, transcendentals=0
         ),
         name="pair_bias",
     )(pair.reshape(2, whole, tok_col, width), weight_t, mask)
 
 
+def norm_kernel(pair_ref, normed_ref, inv_ref):
+    def step(n, carry):
+        centred, inv_std = pair_columns(pair_ref, n * MANY, MANY)
+        normed_ref[n] = jnp.concatenate(halves(centred * inv_std), axis=0)
+        inv_ref[n] = jnp.broadcast_to(inv_std, inv_ref.shape[1:])
+        return carry
+
+    lax.fori_loop(0, normed_ref.shape[0], step, 0, unroll=2)
+
+
+def pair_units(pair):
+    row_count, tok_col, width = pair.shape
+    whole = row_count // 2
+    chunks, lanes = whole // MANY, MANY * 2 * tok_col
+    shapes = [(chunks, 2 * width, lanes), (chunks, 8, lanes)]
+    return pl.pallas_call(
+        norm_kernel,
+        out_shape=[
+            jax.ShapeDtypeStruct(shapes[0], jnp.bfloat16),
+            jax.ShapeDtypeStruct(shapes[1], jnp.float32),
+        ],
+        grid=(STEPS,),
+        in_specs=[pair_spec(pair)],
+        out_specs=[split_spec(shape) for shape in shapes],
+        compiler_params=params(56),
+        cost_estimate=pl.CostEstimate(
+            flops=6_000_000_000, bytes_accessed=12_000_000, transcendentals=0
+        ),
+        name="pair_units",
+    )(pair.reshape(2, whole, tok_col, width))
+
+
 def shift_of(top):
     return jnp.floor(jnp.clip(14.0 - jnp.log2(top), -100.0, 100.0))
 
 
-def attention_kernel(tokens_ref, bias_ref, back_ref, grad_bias_ref, sum_ref):
+def attention_kernel(col_ref, *refs):
+    other_ref, bias_ref, back_ref, grad_bias_ref, sum_ref, tokens_ref = refs[-6:]
+    col = col_ref[0]
+    for offset, ref in enumerate(refs[:-6]):
+        tokens_ref[col ^ (2 * offset)] = ref[0]
+        tokens_ref[col ^ (2 * offset + 1)] = other_ref[offset]
     n_col = tokens_ref.shape[0]
     tok_col, row_count = bias_ref.shape[1:]
     half = back_ref.shape[2] // tok_col
@@ -462,10 +517,11 @@
             grad_bias_ref[head, tok_col:, :] = jnp.broadcast_to(shift, (8, row_count))
 
 
-def attention(arrived, bias, n_row):
-    n_col, _, _, held = arrived.shape
+def attention(col, arrived, other, bias, n_row):
+    count = len(arrived)
+    n_col = 2 * count
     _, tok_col, row_count = bias.shape
-    half = held // tok_col // n_row
+    half = arrived[0].shape[-1] // tok_col // n_row
     width = half * tok_col
     back_shape = (n_row * n_col, 4 * CH + 8, width)
     bias_shape = (n_row * n_col, tok_col + 8, row_count)
@@ -475,125 +531,191 @@
             jax.ShapeDtypeStruct(back_shape, jnp.float32),
             jax.ShapeDtypeStruct(bias_shape, jnp.float32),
         ],
-        grid=(n_row,),
-        in_specs=[
-            pl.BlockSpec((n_col, 4, CH, width), lambda i: (0, 0, 0, i)),
-            pl.BlockSpec(bias.shape, lambda i: (0, 0, 0)),
-        ],
-        out_specs=[
-            pl.BlockSpec((n_col, 4 * CH + 8, width), lambda i: (i, 0, 0)),
-            pl.BlockSpec(bias_shape, lambda i: (0, 0, 0)),
-        ],
-        scratch_shapes=[pltpu.VMEM(bias.shape, jnp.float32)],
+        grid_spec=pltpu.PrefetchScalarGridSpec(
+            num_scalar_prefetch=1,
+            grid=(n_row,),
+            in_specs=[pl.BlockSpec((1, 4, CH, width), lambda i, r: (0, 0, 0, i))] * count
+            + [
+                pl.BlockSpec((count, 4, CH, width), lambda i, r: (0, 0, 0, i)),
+                pl.BlockSpec(bias.shape, lambda i, r: (0, 0, 0)),
+            ],
+            out_specs=[
+                pl.BlockSpec((n_col, 4 * CH + 8, width), lambda i, r: (i, 0, 0)),
+                pl.BlockSpec(bias_shape, lambda i, r: (0, 0, 0)),
+            ],
+            scratch_shapes=[
+                pltpu.VMEM(bias.shape, jnp.float32),
+                pltpu.VMEM((n_col, 4, CH, width), jnp.bfloat16),
+            ],
+        ),
         compiler_params=params(24),
         cost_estimate=pl.CostEstimate(
             flops=8_000_000_000, bytes_accessed=6_000_000, transcendentals=1_000_000
         ),
         name="attention",
-    )(arrived, bias)
-
-
-def back_kernel(
-    back_ref, slope_ref, normed_ref, inv_ref, wq_ref, wk_ref, wv_ref, wg_ref, out_ref
-):
-    count = back_ref.shape[-1]
-
-    def side(slot):
-        scale = jnp.exp2(-back_ref[:, 4 * CH + slot : 4 * CH + slot + 1, :])
-        return (back_ref[:, slot * CH : (slot + 1) * CH, :] * scale).reshape(D, count)
-
-    total = jnp.zeros((D, count), jnp.float32)
+    )(col, *arrived, other, bias)
+
+
+def back_kernel(*refs):
+    slope_ref, normed_ref, inv_ref, wq_ref, wk_ref, wv_ref, wg_ref = refs[-11:-4]
+    out_ref, parts_ref, gate_ref, total_ref = refs[-4:]
+    back_ref = refs[0]
+    count = normed_ref.shape[-1]
+    step = pl.program_id(0)
+    rows = wq_ref.shape[0]
+
+    @pl.when(step == 0)
+    def _():
+        for slot in range(4):
+            scale = jnp.exp2(-back_ref[:, 4 * CH + slot : 4 * CH + slot + 1, :])
+            values = back_ref[:, slot * CH : (slot + 1) * CH, :] * scale
+            values = values.reshape(gate_ref.shape)
+            if slot < 3:
+                parts_ref[slot] = jnp.concatenate(halves(values), axis=1)
+            else:
+                gate_ref[...] = (values * slope_ref[...]).astype(jnp.bfloat16)
+
+    total = matmul(wg_ref[...], gate_ref[...])
     for slot, ref in enumerate((wq_ref, wk_ref, wv_ref)):
-        parts = matmul(ref[...], jnp.concatenate(halves(side(slot)), axis=1))
+        parts = matmul(ref[...], parts_ref[slot])
         total = total + (parts[:, :count] + parts[:, count:])
-    total = total + matmul(wg_ref[...], (side(3) * slope_ref[...]).astype(jnp.bfloat16))
-    normed = normed_ref[...]
-    result = inv_ref[:1] * (
-        total
-        - jnp.mean(total, axis=0, keepdims=True)
-        - normed * jnp.mean(total * normed, axis=0, keepdims=True)
-    )
-    out_ref[...] = result.T.astype(jnp.bfloat16)
+    total_ref[pl.ds(pl.multiple_of(step * rows, 8), rows), :] = total
+
+    @pl.when(step == pl.num_programs(0) - 1)
+    def _():
+        whole = total_ref[...]
+        normed = normed_ref[...]
+        result = inv_ref[:1] * (
+            whole
+            - jnp.mean(whole, axis=0, keepdims=True)
+            - normed * jnp.mean(whole * normed, axis=0, keepdims=True)
+        )
+        out_ref[...] = result.T.astype(jnp.bfloat16)
 
 
 def token_back(back, slope, normed, inv_std, weights):
-    count = back.shape[-1]
+    count = normed.shape[-1]
+    steps = 2
+    whole = lambda shape: pl.BlockSpec(shape, lambda i: (0,) * len(shape))
+    weight_spec = pl.BlockSpec((D // steps, D), lambda i: (i, 0))
     return pl.pallas_call(
         back_kernel,
         out_shape=jax.ShapeDtypeStruct((count, D), jnp.bfloat16),
-        compiler_params=params(56),
+        grid=(steps,),
+        in_specs=[whole(array.shape) for array in (back, slope, normed, inv_std)]
+        + [weight_spec] * 4,
+        out_specs=whole((count, D)),
+        scratch_shapes=[
+            pltpu.VMEM((3, D, 2 * count), jnp.bfloat16),
+            pltpu.VMEM((D, count), jnp.bfloat16),
+            pltpu.VMEM((D, count), jnp.float32),
+        ],
+        compiler_params=params(40),
         cost_estimate=pl.CostEstimate(
-            flops=20 * count * D * D, bytes_accessed=8_000_000, transcendentals=0
+            flops=4_000_000_000, bytes_accessed=8_000_000, transcendentals=0
         ),
         name="token_back",
     )(back, slope, normed, inv_std, *weights)
 
 
-def pair_back_kernel(factor, pair_ref, grads_ref, weight_ref, out_ref, part_ref, flat_ref):
-    _, count, length, width = pair_ref.shape
+def flatten(grads_ref, flat_ref):
     whole = flat_ref.shape[0] // H
+    for h in range(H):
+        grads = grads_ref[h]
+        both = jnp.concatenate([grads[:, :whole], grads[:, whole:]], axis=0)
+        flat_ref[h * whole : (h + 1) * whole, :] = both.T
+
+
+def flat_columns(flat_ref, k, many):
+    whole = flat_ref.shape[0] // H
+    grads = [flat_ref[pl.ds(k + m, H, stride=whole), :] for m in range(many)]
+    return jnp.concatenate(halves(jnp.concatenate(grads, axis=1)), axis=0)
+
+
+def pair_weight_kernel(normed_ref, grads_ref, part_ref, flat_ref):
+    chunks, width, _ = normed_ref.shape
+    base = pl.program_id(0) * chunks
+
+    @pl.when(pl.program_id(0) == 0)
+    def _():
+        part_ref[...] = jnp.zeros_like(part_ref)
+        flatten(grads_ref, flat_ref)
+
+    def step(n, carry):
+        return carry + matmul_nt(normed_ref[n], flat_columns(flat_ref, (base + n) * MANY, MANY))
+
+    parts = lax.fori_loop(0, chunks, step, jnp.zeros((width, 2 * H), jnp.float32), unroll=2)
+    parts = parts[:, :H] + parts[:, H:]
+    part_ref[...] += (parts[: width // 2] + parts[width // 2 :]).T
+
+
+def pair_back_kernel(factor, normed_ref, inv_ref, grads_ref, weight_ref, out_ref, flat_ref):
+    _, count, length, width = out_ref.shape
     weight = weight_ref[...].astype(jnp.float32)
     weight = halves(weight - jnp.mean(weight, axis=1, keepdims=True))
     weight = jnp.concatenate([weight[0], weight[0], weight[1], weight[1]], axis=0).T
-    many = 4
     base = pl.program_id(0) * count
 
     @pl.when(pl.program_id(0) == 0)
     def _():
-        part_ref[...] = jnp.zeros_like(part_ref)
-        for h in range(H):
-            grads = grads_ref[h]
-            both = jnp.concatenate([grads[:, :whole], grads[:, whole:]], axis=0)
-            flat_ref[h * whole : (h + 1) * whole, :] = both.T
+        flatten(grads_ref, flat_ref)
 
     def step(n, carry):
-        k = n * many
-        centred, inv_std = pair_columns(pair_ref, k, many)
-        normed = centred * inv_std
-        grads = jnp.concatenate(
-            [flat_ref[pl.ds(base + k + m, H, stride=whole), :] for m in range(many)], axis=1
-        )
-        grads = jnp.concatenate(halves(grads), axis=0)
+        k = n * MANY
+        normed = normed_ref[n].astype(jnp.float32)
+        normed = normed[:width] + normed[width:]
+        grads = flat_columns(flat_ref, base + k, MANY)
         grad_in = matmul(weight, jnp.concatenate([grads, grads], axis=0))
         overlap = jnp.mean(grad_in * normed, axis=0, keepdims=True)
-        result = (grad_in - normed * overlap) * (inv_std * factor)
-        result = result.astype(jnp.bfloat16).T.reshape(many, 2 * length, width)
+        result = (grad_in - normed * overlap) * (inv_ref[n, :1] * factor)
+        result = result.astype(jnp.bfloat16).T.reshape(MANY, 2 * length, width)
         for p in range(2):
-            out_ref[p, pl.ds(k, many)] = result[:, p * length : (p + 1) * length]
-        return carry + matmul_nt(jnp.concatenate(halves(normed), axis=0), grads)
-
-    parts = jnp.zeros((2 * width, 2 * H), jnp.float32)
-    parts = lax.fori_loop(0, count // many, step, parts, unroll=2)
-    parts = parts[:, :H] + parts[:, H:]
-    part_ref[...] += (parts[:width] + parts[width:]).T
-
-
-def pair_backward(pair, grads, weight_t, factor):
-    row_count, tok_col, width = pair.shape
-    steps = 4
+            out_ref[p, pl.ds(k, MANY)] = result[:, p * length : (p + 1) * length]
+        return carry
+
+    lax.fori_loop(0, count // MANY, step, 0, unroll=2)
+
+
+def pair_weight(normed, grads):
+    heads, length, rows = grads.shape
+    part_shape = (H, normed.shape[1] // 2)
+    return pl.pallas_call(
+        pair_weight_kernel,
+        out_shape=jax.ShapeDtypeStruct(part_shape, jnp.float32),
+        grid=(STEPS,),
+        in_specs=[split_spec(normed.shape), whole_spec(grads.shape)],
+        out_specs=whole_spec(part_shape),
+        scratch_shapes=[pltpu.VMEM((H * rows // 2, 2 * length), jnp.float32)],
+        compiler_params=params(24),
+        cost_estimate=pl.CostEstimate(
+            flops=5_000_000_000, bytes_accessed=100_000, transcendentals=0
+        ),
+        name="pair_weight",
+    )(normed, grads)
+
+
+def pair_backward(shape, normed, inv_std, grads, weight_t, factor):
+    row_count, tok_col, width = shape
     whole = row_count // 2
-    pair_spec = pl.BlockSpec((2, whole // steps, tok_col, width), lambda i: (0, i, 0, 0))
-    pair_grad, part = pl.pallas_call(
+    pair_grad = pl.pallas_call(
         lambda *refs: pair_back_kernel(factor, *refs),
-        out_shape=[
-            jax.ShapeDtypeStruct((2, whole, tok_col, width), jnp.bfloat16),
-            jax.ShapeDtypeStruct((H, width), jnp.float32),
+        out_shape=jax.ShapeDtypeStruct((2, whole, tok_col, width), jnp.bfloat16),
+        grid=(STEPS,),
+        in_specs=[
+            split_spec(normed.shape),
+            split_spec(inv_std.shape),
+            whole_spec(grads.shape),
+            whole_spec(weight_t.shape),
         ],
-        grid=(steps,),
-        in_specs=[
-            pair_spec,
-            pl.BlockSpec(grads.shape, lambda i: (0, 0, 0)),
-            pl.BlockSpec(weight_t.shape, lambda i: (0, 0)),
-        ],
-        out_specs=[pair_spec, pl.BlockSpec((H, width), lambda i: (0, 0))],
+        out_specs=pl.BlockSpec((2, whole // STEPS, tok_col, width), lambda i: (0, i, 0, 0)),
         scratch_shapes=[pltpu.VMEM((H * whole, 2 * tok_col), jnp.float32)],
         compiler_params=params(24),
         cost_estimate=pl.CostEstimate(
-            flops=row_count * tok_col * width * 5000, bytes_accessed=11_000_000, transcendentals=0
+            flops=8_000_000_000, bytes_accessed=100_000, transcendentals=0
         ),
         name="pair_backward",
-    )(pair.reshape(2, whole, tok_col, width), grads, weight_t)
-    return pair_grad.reshape(pair.shape), part
+    )(normed, inv_std, grads, weight_t)
+    return pair_grad.reshape(shape)
 
 
 def unscaled(block, rows):
@@ -618,45 +740,72 @@
     half = samp_dev // n_row
     row_index = lax.axis_index("row")
     row = row_index.astype(jnp.int32).reshape(1)
+    col = lax.axis_index("col").astype(jnp.int32).reshape(1)
     types = restype.reshape(1, tok_col)
     weight_t = w_bias.T
     weights = (w_query, w_key, w_value, w_gate)
-
-    message = token_messages(
-        row, tokens, types, type_table, weights, cotangent, n_row, n_col
-    )
-    message, bias_weight = lax.optimization_barrier((message, weight_t))
-    arrived = lax.all_to_all(message, "col", 0, 0, tiled=True)
-    bias = pair_bias(pair, bias_weight, key_mask.reshape(1, tok_col))
-    arrived, bias = lax.optimization_barrier((arrived, bias.astype(jnp.float16)))
-    bias = lax.all_to_all(bias, ("row", "col"), 0, 0, tiled=True).astype(jnp.float32)
-    slope, normed, inv_std = own_rows(row, tokens, types, type_table, w_gate, cotangent, half)
-
-    back, grad_bias = attention(arrived, bias, n_row)
+    samples = samp_dev * n_samp
+
+    def send(block, offset):
+        return lax.ppermute(block, "col", [(c, c ^ offset) for c in range(n_col)])
+
+    def by_chip(blocks):
+        return [blocks[0]] + [send(blocks[n], 2 * n) for n in range(1, n_col // 2)]
+
+    def across(blocks):
+        return send(jnp.stack([block[1] for block in blocks]), 1)
+
+    messages = token_messages(
+        row, col, tokens, types, type_table, weights, cotangent, n_row, n_col
+    )
+    arrived = by_chip(messages)
+    bias = pair_bias(pair, weight_t, key_mask.reshape(1, tok_col))
+    bias, arrived, types = lax.optimization_barrier(
+        (bias.astype(jnp.float16), arrived, types)
+    )
+    own = own_rows(row, tokens, types, type_table, w_gate, cotangent, half)
+    bias = lax.all_to_all(bias, ("row", "col"), 0, 0, tiled=True)
+    other = across(arrived)
+    bias, other, own = lax.optimization_barrier((bias, other, own))
+
+    back, grad_bias = attention(col, arrived, other, bias.astype(jnp.float32), n_row)
     grad_bias = lax.all_to_all(
         grad_bias.astype(jnp.float16), ("row", "col"), 0, 0, tiled=True
     )
+    back, late_pair = lax.optimization_barrier((back.astype(jnp.float16), pair))
+    pair_normed, pair_inv = pair_units(late_pair)
+    back, _, pair_normed = lax.optimization_barrier((back, grad_bias, pair_normed))
+    back = lax.all_to_all(back, ("row", "col"), 0, 0, tiled=True)
+
     other_bias = swap(grad_bias, "samp")
-    back = lax.all_to_all(back.astype(jnp.float16), ("row", "col"), 0, 0, tiled=True)
-    grads = unscaled(grad_bias, tok_col) + unscaled(other_bias, tok_col)
-
-    samples = samp_dev * n_samp
-    pair_grad, part = pair_backward(pair, grads, weight_t, total_tokens / samples)
-    parts = lax.all_to_all(
-        jnp.broadcast_to(part[None], (H,) + part.shape), ("row", "col"), 0, 0, tiled=True
-    )
-    bias_weight_grad = jnp.sum(parts, axis=0).T / samples
-
-    back, part = lax.optimization_barrier((back, part))
-    back = back.astype(jnp.float32)
-    token_half = token_back(back, slope, normed, inv_std, weights)
+    own_bias = unscaled(grad_bias, tok_col)
+    part = pair_weight(pair_normed, own_bias)
+    samp_part = swap(part, "samp")
+    row_part = swap(part, "row")
+    both_part = lax.ppermute(part, ("samp", "row"), [(n, 3 - n) for n in range(4)])
+    other_bias, part = lax.optimization_barrier((other_bias, part))
+    grads = own_bias + unscaled(other_bias, tok_col)
+    part = (part + samp_part) + (row_part + both_part)
+    grads, part = lax.optimization_barrier((grads, part))
+    sums = (send(part, 1), send(part, 2), send(part, 3))
+    pair_grad = pair_backward(
+        pair.shape, pair_normed, pair_inv, grads, weight_t, total_tokens / samples
+    )
+
+    pair_grad, back, sums = lax.optimization_barrier((pair_grad, back, sums))
+    part = (part + sums[0]) + (sums[1] + sums[2])
+    last = send(part, 4)
+    token_half = token_back(back.astype(jnp.float32), *own, weights)
+    token_half, last = lax.optimization_barrier((token_half, last))
+    part = part + last
     token_half = token_half.reshape(half, tok_col, D)
-    other = swap(token_half, "row")
+    other_half = swap(token_half, "row")
     first = row_index == 0
     token_grad = jnp.concatenate(
-        [jnp.where(first, token_half, other), jnp.where(first, other, token_half)], axis=0
-    )
-    return (token_grad, pair_grad, bias_weight_grad)
+        [jnp.where(first, token_half, other_half), jnp.where(first, other_half, token_half)],
+        axis=0,
+    )
+    return (token_grad, pair_grad, part.T / samples)
 
 
 def body(*args):
@@ -664,7 +813,7 @@
     n_col = lax.axis_size("col")
     tokens = args[0]
     pair = args[4]
-    fits = n_row == 2 and n_row * n_col == H and lax.axis_size("samp") == 2
+    fits = n_row == 2 and n_col == 8 and n_row * n_col == H and lax.axis_size("samp") == 2
     square = pair.shape[0] * n_row == pair.shape[1] * n_col
     if fits and square and tokens.shape[0] == 4 and tokens.shape[1] == 64:
         return body_heads(*args)

time: 130 us -> 119 us (0.915)
  blocking collectives: 38.7 us -> 0 us
  starting transfers between devices: 16.4 us -> 32.4 us
  Pallas kernels: 38.8 us -> 48.7 us
  other arithmetic: 5.35 us -> 7.25 us
  waiting for transfers between devices: 24.2 us -> 25.7 us
    all_to_all x2 -> x0, blocking collectives: 38.7 us -> none  [the longest x1 21.1 us: body_heads(): lax.all_to_all(grad_bias.astype(jnp.float16), ('row', 'col'), 0, 0, tiled...]
    ppermute x0 -> x9, starting transfers between devices: none -> 12.6 us  [the longest x8 10.8 us: send(): return lax.ppermute(block, 'col', [(c, c ^ offset) for c in range(n_col)])]
    pallas_call x2 -> x4, Pallas kernels: 16.5 us -> 26.3 us  [the longest x1 8.82 us: pair_units(): pl.pallas_call(norm_kernel, out_shape=[jax.ShapeDtypeStruct(shapes[0], jn...]
    ppermute x0 -> x9, waiting for transfers between devices: none -> 4.07 us  [the longest x8 4.07 us: send(): return lax.ppermute(block, 'col', [(c, c ^ offset) for c in range(n_col)])]
    pallas_call x1, Pallas kernels: 5.33 us -> 2.14 us  [token_back(): pl.pallas_call(back_kernel, out_shape=jax.ShapeDtypeStruct((count, D), jn...]
    pallas_call x1, Pallas kernels: 6.63 us -> 9.78 us  [pair_bias(): pl.pallas_call(bias_kernel, out_shape=jax.ShapeDtypeStruct((H, tok_col, r...]
    ppermute x2 -> x4, starting transfers between devices: 2.22 us -> 4.91 us  [swap(): return lax.ppermute(block, axis, [(0, 1), (1, 0)])]
    ppermute x2 -> x4, waiting for transfers between devices: 7.47 us -> 5.53 us  [swap(): return lax.ppermute(block, axis, [(0, 1), (1, 0)])]
  transfers between devices with their start and end apart: 5 -> 16, of which waited for: 4 -> 6; matrix products, arithmetic and copies ran while one was open for 3% -> 5% of each run, Pallas kernels for 17% -> 31%
where the time goes in v2:
time: 119 us
  Pallas kernels  48.7 us (41%)
  starting transfers between devices  32.4 us (27%)
  waiting for transfers between devices  25.7 us (22%)
  other arithmetic  7.25 us (6%)
  local copies, waits for them, and re-layouts  3.47 us (3%)
    ppermute x8, starting transfers between devices, send(): return lax.ppermute(block, 'col', [(c, c ^ offset) for c in range(n_col)])  10.8 us
    all_to_all x1, waiting for transfers between devices, body_heads(): bias = lax.all_to_all(bias, ('row', 'col'), 0, 0, tiled=True)  10.6 us
    pallas_call x1, Pallas kernels, pair_bias(): pl.pallas_call(bias_kernel, out_shape=jax.ShapeDtypeStruct((H, tok_col, r...  9.78 us
    pallas_call x1, Pallas kernels, pair_units(): pl.pallas_call(norm_kernel, out_shape=[jax.ShapeDtypeStruct(shapes[0], jn...  8.82 us
    pallas_call x1, Pallas kernels, pair_backward(): pl.pallas_call(lambda *refs: pair_back_kernel(factor, *refs), out_shape=j...  7.68 us
    pallas_call x1, Pallas kernels, attention(): pl.pallas_call(attention_kernel, out_shape=[jax.ShapeDtypeStruct(back_sha...  7.42 us
    all_to_all x1, starting transfers between devices, body_heads(): bias = lax.all_to_all(bias, ('row', 'col'), 0, 0, tiled=True)  6.67 us
    ppermute x4, waiting for transfers between devices, swap(): return lax.ppermute(block, axis, [(0, 1), (1, 0)])  5.53 us
  transfers between devices with their start and end apart: 16, of which 6 were waited for; matrix products, arithmetic and copies ran while one was open for 5% of the time, Pallas kernels for 31%

profile of v2, /device:TPU:0, one launch (start us, length us, event | category | flops | bytes accessed | tf_op | source)
XLA Modules:
  0.0 118.6 jit_solution(11282291690408735951)
XLA Ops:
  0.6 0.0 copy-start.1
  0.6 0.0 copy-start.6
  0.7 0.0 copy-start.7
  0.7 4.3 %token_messages.1 = (bf16[2,4,48,256]{3,2,1,0:T(8,128)(2,1)}, bf16[2,4,48,256]{3,2,1,0:T(8,128)(2,1)}, bf16[2,4,48,256]{3,2,1,0:T(8,128)(2,1)}, bf16[2,4,48,256]{3,2,1,0:T(8,128)(2,1)}) custom-call(s32[1]{0:T(128)} %bitcast.4.row_ref, s32[1]{0:T(128)} %bitcast.col_ref, bf16[4,64,768]{2,1,0:T(8,128)(2,1)} %tokens_ref.3, s32[1,64]{1,0:T(1,128)} %bitcast.27, ...), custom_call_target="tpu_custom_call" | custom-call | flops 4000000000 | bytes 4000000 | tf_op jit(solution)/shard_map/token_messages/pallas_call | solution.py:245
  5.0 3.0 %collective-permute-start = (bf16[2,4,48,256]{3,2,1,0:T(8,128)(2,1)}, bf16[2,4,48,256]{3,2,1,0:T(8,128)(2,1)S(1)}, u32[]{:S(2)}, u32[]{:S(2)}) collective-permute-start(bf16[2,4,48,256]{3,2,1,0:T(8,128)(2,1)} %get-tuple-element.41), channel_id=1, source_target_pairs={{0,2},{1,3},{2,0},{3,1},{4,6},{5,7},{6,4},{7,5},{8,10},{9,11},{10,... | collective-permute-start | bytes 589832 | tf_op jit(solution)/shard_map/ppermute | solution.py:750
  8.0 2.6 %collective-permute-start.1 = (bf16[2,4,48,256]{3,2,1,0:T(8,128)(2,1)}, bf16[2,4,48,256]{3,2,1,0:T(8,128)(2,1)S(1)}, u32[]{:S(2)}, u32[]{:S(2)}) collective-permute-start(bf16[2,4,48,256]{3,2,1,0:T(8,128)(2,1)} %get-tuple-element.42), channel_id=1, source_target_pairs={{0,4},{1,5},{2,6},{3,7},{4,0},{5,1},{6,2},{7,3},{8,12},{9,13},{10,... | collective-permute-start | bytes 589832 | tf_op jit(solution)/shard_map/ppermute | solution.py:750
  10.6 0.0 collective-permute-start.2
  10.6 0.0 copy-done.1
  10.6 0.0 copy-done.6
  10.6 0.0 copy-done.7
  10.6 9.8 %pair_bias.1 = f32[16,64,256]{2,1,0:T(8,128)S(1)} custom-call(bf16[2,128,64,128]{3,2,1,0:T(8,128)(2,1)S(1)} %bitcast.20, bf16[16,128]{1,0:T(8,128)(2,1)S(1)} %bitcast.21, s32[1,64]{1,0:T(1,128)S(1)} %bitcast.23), custom_call_target="tpu_custom_call" | custom-call | flops 6000000000 | bytes 5000000 | tf_op jit(solution)/shard_map/pair_bias/pallas_call | solution.py:383
  20.4 0.0 copy-start
  20.4 0.9 convert_element_type.21
  21.3 0.0 collective-permute-done.refs_1_
  21.3 4.0 %collective-permute-done.1.refs_2_ = bf16[2,4,48,256]{3,2,1,0:T(8,128)(2,1)S(1)} collective-permute-done((bf16[2,4,48,256]{3,2,1,0:T(8,128)(2,1)}, bf16[2,4,48,256]{3,2,1,0:T(8,128)(2,1)S(1)}, u32[]{:S(2)}, u32[]{:S(2)}) %collective-permute-start.1) | collective-permute-done | bytes 196640 | tf_op jit(solution)/shard_map/ppermute | solution.py:750
  25.4 0.0 collective-permute-done.2.refs_3_
  25.4 6.7 %all-to-all-start = ((f16[16,64,256]{2,1,0:T(8,128)(2,1)}), f16[16,64,256]{2,1,0:T(8,128)(2,1)S(1)}, u32[]{:S(2)}, u32[]{:S(2)}) async-start(f16[16,64,256]{2,1,0:T(8,128)(2,1)} %convert_element_type.21), calls=%async_computation | async-start | bytes 1048576 | tf_op jit(solution)/shard_map/all_to_all | solution.py:767
  32.0 0.0 copy-done
  32.1 0.1 pad_maximum_fusion
  32.2 0.5 collective-permute-start.3
  32.6 3.0 %own_rows.1 = (f32[768,128]{1,0:T(8,128)}, f32[768,128]{1,0:T(8,128)}, f32[8,128]{1,0:T(8,128)}) custom-call(s32[1]{0:T(128)} %bitcast.4.row_ref, bf16[4,64,768]{2,1,0:T(8,128)(2,1)} %tokens_ref.3, s32[1,64]{1,0:T(1,128)} %bitcast.28, bf16[32,768]{1,0:T(8,128)(2,1)} %table_ref.3, bf16[768,768]{1,0:T(8,128)(2,1)} %refs_7_.1, bf16[4,64,768]{2,1,0:T(8,128)(2,1)} %cot_ref.1), custom_call_target="tpu_custom_call" | custom-call | flops 3000000000 | bytes 3000000 | tf_op jit(solution)/shard_map/own_rows/pallas_call | solution.py:289
  35.7 0.0 collective-permute-done.3.refs_4_
  35.7 10.6 %all-to-all-done = f16[16,64,256]{2,1,0:T(8,128)(2,1)S(1)} async-done(((f16[16,64,256]{2,1,0:T(8,128)(2,1)}), f16[16,64,256]{2,1,0:T(8,128)(2,1)S(1)}, u32[]{:S(2)}, u32[]{:S(2)}) %all-to-all-start) | async-done | bytes 524320 | tf_op jit(solution)/shard_map/all_to_all | solution.py:767
  46.3 0.1 convert_element_type.22.refs_5_
  46.4 7.4 %attention.1 = (f32[16,200,128]{2,1,0:T(8,128)S(1)}, f32[16,72,256]{2,1,0:T(8,128)S(1)}) custom-call(s32[1]{0:T(128)} %bitcast.col_ref, bf16[2,4,48,256]{3,2,1,0:T(8,128)(2,1)S(1)} %copy-done, bf16[2,4,48,256]{3,2,1,0:T(8,128)(2,1)S(1)} %collective-permute-done.refs_1_, bf16[2,4,48,256]{3,2,1,0:T(8,128)(2,1)S(1)} %collective-permute-done.1.refs_2_, ...), custom_call_target="tpu_custom_call" | custom-call | flops 8000000000 | bytes 6000000 | tf_op jit(solution)/shard_map/attention/pallas_call | solution.py:528
  53.8 0.9 convert_element_type.24
  54.7 4.0 %all-to-all-start.1 = ((f16[16,72,256]{2,1,0:T(8,128)(2,1)}), f16[16,72,256]{2,1,0:T(8,128)(2,1)S(1)}, u32[]{:S(2)}, u32[]{:S(2)}) async-start(f16[16,72,256]{2,1,0:T(8,128)(2,1)} %convert_element_type.24), calls=%async_computation.1 | async-start | bytes 1179648 | tf_op jit(solution)/shard_map/all_to_all | solution.py:772
  58.7 1.1 convert_element_type.23
  59.8 8.8 %pair_units.1 = (bf16[32,256,512]{2,1,0:T(8,128)(2,1)}, f32[32,8,512]{2,1,0:T(8,128)}) custom-call(bf16[2,128,64,128]{3,2,1,0:T(8,128)(2,1)} %bitcast.19), custom_call_target="tpu_custom_call" | custom-call | flops 6000000000 | bytes 12000000 | tf_op jit(solution)/shard_map/pair_units/pallas_call | solution.py:413
  68.6 5.5 %all-to-all-done.1 = f16[16,72,256]{2,1,0:T(8,128)(2,1)S(1)} async-done(((f16[16,72,256]{2,1,0:T(8,128)(2,1)}), f16[16,72,256]{2,1,0:T(8,128)(2,1)S(1)}, u32[]{:S(2)}, u32[]{:S(2)}) %all-to-all-start.1) | async-done | bytes 589856 | tf_op jit(solution)/shard_map/all_to_all | solution.py:772
  74.1 0.1 convert_element_type.25
  74.3 1.6 %collective-permute-start.4 = (f16[16,72,256]{2,1,0:T(8,128)(2,1)S(1)}, f16[16,72,256]{2,1,0:T(8,128)(2,1)}, u32[]{:S(2)}, u32[]{:S(2)}) collective-permute-start(f16[16,72,256]{2,1,0:T(8,128)(2,1)S(1)} %all-to-all-done.1), channel_id=1, source_target_pairs={{0,16},{16,0},{1,17},{17,1},{2,18},{18,2},{3,19},{19,3},{4,20},{20... | collective-permute-start | bytes 1769480 | tf_op jit(solution)/shard_map/ppermute | solution.py:727
  75.9 0.1 slice_multiply_fusion.1.grads_ref
  76.0 4.3 %all-to-all-start.2 = ((f16[16,200,128]{2,1,0:T(8,128)(2,1)}), f16[16,200,128]{2,1,0:T(8,128)(2,1)}, u32[]{:S(2)}, u32[]{:S(2)}) async-start(f16[16,200,128]{2,1,0:T(8,128)(2,1)} %convert_element_type.23), calls=%async_computation.2 | async-start | bytes 1638400 | tf_op jit(solution)/shard_map/all_to_all | solution.py:778
  80.3 3.4 %copy-done.8 = bf16[32,256,512]{2,1,0:T(8,128)(2,1)S(1)} copy-done((bf16[32,256,512]{2,1,0:T(8,128)(2,1)S(1)}, bf16[32,256,512]{2,1,0:T(8,128)(2,1)}, u32[]{:S(2)}) %copy-start.8) | copy-done | bytes 8388632
  83.7 5.5 %pair_weight.1 = f32[16,128]{1,0:T(8,128)S(1)} custom-call(bf16[32,256,512]{2,1,0:T(8,128)(2,1)S(1)} %copy-done.8, f32[16,64,256]{2,1,0:T(8,128)S(1)} %slice_multiply_fusion.1.grads_ref), custom_call_target="tpu_custom_call" | custom-call | flops 5000000000 | bytes 100000 | tf_op jit(solution)/shard_map/pair_weight/pallas_call | solution.py:682
  89.2 1.8 %collective-permute-start.7 = (f32[16,128]{1,0:T(8,128)S(1)}, f32[16,128]{1,0:T(8,128)S(1)}, u32[]{:S(2)}, u32[]{:S(2)}) collective-permute-start(f32[16,128]{1,0:T(8,128)S(1)} %pair_weight.1), channel_id=1, source_target_pairs={{0,24},{8,16},{16,8},{24,0},{1,25},{9,17},{17,9},{25,1},{2,26},{10... | collective-permute-start | bytes 24584 | tf_op jit(solution)/shard_map/ppermute | solution.py:785
  91.0 0.2 collective-permute-start.6
  91.2 1.5 %collective-permute-start.5 = (f32[16,128]{1,0:T(8,128)S(1)}, f32[16,128]{1,0:T(8,128)S(1)}, u32[]{:S(2)}, u32[]{:S(2)}) collective-permute-start(f32[16,128]{1,0:T(8,128)S(1)} %pair_weight.1), channel_id=1, source_target_pairs={{0,16},{16,0},{1,17},{17,1},{2,18},{18,2},{3,19},{19,3},{4,20},{20... | collective-permute-start | bytes 24584 | tf_op jit(solution)/shard_map/ppermute | solution.py:727
  92.7 0.0 collective-permute-done.4
  92.7 1.1 convert_element_type.26
  94.0 0.0 collective-permute-done.7
  94.0 0.7 collective-permute-done.6
  94.6 0.2 collective-permute-done.5
  94.9 0.2 fusion.refs_2_
  95.0 0.4 collective-permute-start.10
  95.4 1.5 %collective-permute-start.9 = (f32[16,128]{1,0:T(8,128)S(1)}, f32[16,128]{1,0:T(8,128)S(1)}, u32[]{:S(2)}, u32[]{:S(2)}) collective-permute-start(f32[16,128]{1,0:T(8,128)S(1)} %add_add_fusion.1), channel_id=1, source_target_pairs={{0,2},{1,3},{2,0},{3,1},{4,6},{5,7},{6,4},{7,5},{8,10},{9,11},{10,... | collective-permute-start | bytes 24584 | tf_op jit(solution)/shard_map/ppermute | solution.py:750
  97.0 0.0 collective-permute-start.8
  97.0 7.7 %pair_backward.1 = bf16[2,128,64,128]{3,2,1,0:T(8,128)(2,1)} custom-call(bf16[32,256,512]{2,1,0:T(8,128)(2,1)S(1)} %copy-done.8, f32[32,8,512]{2,1,0:T(8,128)S(1)} %copy-done.11, f32[16,64,256]{2,1,0:T(8,128)S(1)} %fusion.refs_2_, bf16[16,128]{1,0:T(8,128)(2,1)S(1)} %bitcast.22), custom_call_target="tpu_custom_call" | custom-call | flops 8000000000 | bytes 100000 | tf_op jit(solution)/shard_map/pair_backward/pallas_call | solution.py:700
  104.7 0.0 collective-permute-done.10
  104.7 0.0 collective-permute-done.9
  104.7 0.0 collective-permute-done.8
  104.7 0.0 all-to-all-done.2
  104.8 0.0 copy-start.2
  104.8 0.0 copy-start.3
  104.8 0.0 copy-start.12
  104.8 2.7 %collective-permute-start.11 = (f32[16,128]{1,0:T(8,128)S(1)}, f32[16,128]{1,0:T(8,128)S(1)}, u32[]{:S(2)}, u32[]{:S(2)}) collective-permute-start(f32[16,128]{1,0:T(8,128)S(1)} %add_add_fusion), channel_id=1, source_target_pairs={{0,4},{1,5},{2,6},{3,7},{4,0},{5,1},{6,2},{7,3},{8,12},{9,13},{10,... | collective-permute-start | bytes 24584 | tf_op jit(solution)/shard_map/ppermute | solution.py:750
  107.5 1.3 %convert_element_type.27.refs_0_ = f32[16,200,128]{2,1,0:T(8,128)S(1)} convert(f16[16,200,128]{2,1,0:T(8,128)(2,1)} %all-to-all-done.2) | non-fusion elementwise | flops 409600 | bytes 2457600 | tf_op jit(solution)/shard_map/convert_element_type | solution.py:798
  108.8 2.1 %token_back.1 = bf16[128,768]{1,0:T(8,128)(2,1)S(1)} custom-call(f32[16,200,128]{2,1,0:T(8,128)S(1)} %convert_element_type.27.refs_0_, f32[768,128]{1,0:T(8,128)S(1)} %copy-done.9, f32[768,128]{1,0:T(8,128)S(1)} %copy-done.10, f32[8,128]{1,0:T(8,128)S(1)} %copy-done.12, bf16[768,768]{1,0:T(8,128)(2,1)S(1)} %copy-done.2, bf16[768,768]{1,0:T(8,128)(2,1)S(1)} %copy-done.3, ...), custom_call_target="tpu_custom_call" | custom-call | flops 4000000000 | bytes 8000000 | tf_op jit(solution)/shard_map/token_back/pallas_call | solution.py:601
  111.0 0.0 collective-permute-done.11
  111.0 1.6 %collective-permute-start.12 = (bf16[2,64,768]{2,1,0:T(8,128)(2,1)S(1)}, bf16[2,64,768]{2,1,0:T(8,128)(2,1)S(1)}, u32[]{:S(2)}, u32[]{:S(2)}) collective-permute-start(bf16[2,64,768]{2,1,0:T(8,128)(2,1)S(1)} %bitcast.17), channel_id=1, source_target_pairs={{0,8},{8,0},{1,9},{9,1},{2,10},{10,2},{3,11},{11,3},{4,12},{12,4},... | collective-permute-start | bytes 589832 | tf_op jit(solution)/shard_map/ppermute | solution.py:727
  112.6 0.6 multiply_bitcast_fusion
  113.2 4.6 %collective-permute-done.12 = bf16[2,64,768]{2,1,0:T(8,128)(2,1)S(1)} collective-permute-done((bf16[2,64,768]{2,1,0:T(8,128)(2,1)S(1)}, bf16[2,64,768]{2,1,0:T(8,128)(2,1)S(1)}, u32[]{:S(2)}, u32[]{:S(2)}) %collective-permute-start.12) | collective-permute-done | bytes 196640 | tf_op jit(solution)/shard_map/ppermute | solution.py:727
  117.8 0.8 pad_maximum_fusion.1
  (25 shorter events, 0.2 us)
Async XLA Ops:
  0.6 10.0 %copy-start.1 = (bf16[256,64,128]{2,1,0:T(8,128)(2,1)S(1)}, bf16[256,64,128]{2,1,0:T(8,128)(2,1)}, u32[]{:S(2)}) copy-start(bf16[256,64,128]{2,1,0:T(8,128)(2,1)} %param.15) | copy-start | bytes 12582916
  0.6 9.9 %copy-start.6 = (bf16[128,16]{0,1:T(8,128)(2,1)S(1)}, bf16[128,16]{0,1:T(8,128)(2,1)}, u32[]{:S(2)}) copy-start(bf16[128,16]{0,1:T(8,128)(2,1)} %param.16) | copy-start | bytes 12292
  0.7 9.9 %copy-start.7 = (s32[64]{0:T(128)S(1)}, s32[64]{0:T(128)}, u32[]{:S(2)}) copy-start(s32[64]{0:T(128)} %param.14) | copy-start | bytes 772
  5.0 16.3 %collective-permute-start = (bf16[2,4,48,256]{3,2,1,0:T(8,128)(2,1)}, bf16[2,4,48,256]{3,2,1,0:T(8,128)(2,1)S(1)}, u32[]{:S(2)}, u32[]{:S(2)}) collective-permute-start(bf16[2,4,48,256]{3,2,1,0:T(8,128)(2,1)} %get-tuple-element.41), channel_id=1, source_target_pairs={{0,2},{1,3},{2,0},{3,1},{4,6},{5,7},{6,4},{7,5},{8,10},{9,11},{10,... | collective-permute-start | bytes 589832 | tf_op jit(solution)/shard_map/ppermute | solution.py:750
  8.0 17.4 %collective-permute-start.1 = (bf16[2,4,48,256]{3,2,1,0:T(8,128)(2,1)}, bf16[2,4,48,256]{3,2,1,0:T(8,128)(2,1)S(1)}, u32[]{:S(2)}, u32[]{:S(2)}) collective-permute-start(bf16[2,4,48,256]{3,2,1,0:T(8,128)(2,1)} %get-tuple-element.42), channel_id=1, source_target_pairs={{0,4},{1,5},{2,6},{3,7},{4,0},{5,1},{6,2},{7,3},{8,12},{9,13},{10,... | collective-permute-start | bytes 589832 | tf_op jit(solution)/shard_map/ppermute | solution.py:750
  10.6 14.8 %collective-permute-start.2 = (bf16[2,4,48,256]{3,2,1,0:T(8,128)(2,1)}, bf16[2,4,48,256]{3,2,1,0:T(8,128)(2,1)S(1)}, u32[]{:S(2)}, u32[]{:S(2)}) collective-permute-start(bf16[2,4,48,256]{3,2,1,0:T(8,128)(2,1)} %get-tuple-element.43), channel_id=1, source_target_pairs={{0,6},{1,7},{2,4},{3,5},{4,2},{5,3},{6,0},{7,1},{8,14},{9,15},{10,... | collective-permute-start | bytes 589832 | tf_op jit(solution)/shard_map/ppermute | solution.py:750
  20.4 11.7 %copy-start = (bf16[2,4,48,256]{3,2,1,0:T(8,128)(2,1)S(1)}, bf16[2,4,48,256]{3,2,1,0:T(8,128)(2,1)}, u32[]{:S(2)}) copy-start(bf16[2,4,48,256]{3,2,1,0:T(8,128)(2,1)} %get-tuple-element.44.refs_0_) | copy-start | bytes 589828
  25.4 20.9 %all-to-all-start = ((f16[16,64,256]{2,1,0:T(8,128)(2,1)}), f16[16,64,256]{2,1,0:T(8,128)(2,1)S(1)}, u32[]{:S(2)}, u32[]{:S(2)}) async-start(f16[16,64,256]{2,1,0:T(8,128)(2,1)} %convert_element_type.21), calls=%async_computation | async-start | bytes 1048576 | tf_op jit(solution)/shard_map/all_to_all | solution.py:767
  32.2 3.5 %collective-permute-start.3 = (bf16[4,4,48,256]{3,2,1,0:T(8,128)(2,1)S(1)}, bf16[4,4,48,256]{3,2,1,0:T(8,128)(2,1)S(1)}, u32[]{:S(2)}, u32[]{:S(2)}) collective-permute-start(bf16[4,4,48,256]{3,2,1,0:T(8,128)(2,1)S(1)} %pad_maximum_fusion), channel_id=1, source_target_pairs={{0,1},{1,0},{2,3},{3,2},{4,5},{5,4},{6,7},{7,6},{8,9},{9,8},{10,11... | collective-permute-start | bytes 1179656 | tf_op jit(solution)/shard_map/ppermute | solution.py:750
  54.7 19.4 %all-to-all-start.1 = ((f16[16,72,256]{2,1,0:T(8,128)(2,1)}), f16[16,72,256]{2,1,0:T(8,128)(2,1)S(1)}, u32[]{:S(2)}, u32[]{:S(2)}) async-start(f16[16,72,256]{2,1,0:T(8,128)(2,1)} %convert_element_type.24), calls=%async_computation.1 | async-start | bytes 1179648 | tf_op jit(solution)/shard_map/all_to_all | solution.py:772
  74.3 18.5 %collective-permute-start.4 = (f16[16,72,256]{2,1,0:T(8,128)(2,1)S(1)}, f16[16,72,256]{2,1,0:T(8,128)(2,1)}, u32[]{:S(2)}, u32[]{:S(2)}) collective-permute-start(f16[16,72,256]{2,1,0:T(8,128)(2,1)S(1)} %all-to-all-done.1), channel_id=1, source_target_pairs={{0,16},{16,0},{1,17},{17,1},{2,18},{18,2},{3,19},{19,3},{4,20},{20... | collective-permute-start | bytes 1769480 | tf_op jit(solution)/shard_map/ppermute | solution.py:727
  76.0 28.8 %all-to-all-start.2 = ((f16[16,200,128]{2,1,0:T(8,128)(2,1)}), f16[16,200,128]{2,1,0:T(8,128)(2,1)}, u32[]{:S(2)}, u32[]{:S(2)}) async-start(f16[16,200,128]{2,1,0:T(8,128)(2,1)} %convert_element_type.23), calls=%async_computation.2 | async-start | bytes 1638400 | tf_op jit(solution)/shard_map/all_to_all | solution.py:778
  80.3 3.4 %copy-start.8 = (bf16[32,256,512]{2,1,0:T(8,128)(2,1)S(1)}, bf16[32,256,512]{2,1,0:T(8,128)(2,1)}, u32[]{:S(2)}) copy-start(bf16[32,256,512]{2,1,0:T(8,128)(2,1)} %get-tuple-element.60.normed_ref.refs_0_) | copy-start | bytes 25165828
  89.2 4.8 %collective-permute-start.7 = (f32[16,128]{1,0:T(8,128)S(1)}, f32[16,128]{1,0:T(8,128)S(1)}, u32[]{:S(2)}, u32[]{:S(2)}) collective-permute-start(f32[16,128]{1,0:T(8,128)S(1)} %pair_weight.1), channel_id=1, source_target_pairs={{0,24},{8,16},{16,8},{24,0},{1,25},{9,17},{17,9},{25,1},{2,26},{10... | collective-permute-start | bytes 24584 | tf_op jit(solution)/shard_map/ppermute | solution.py:785
  91.0 3.7 %collective-permute-start.6 = (f32[16,128]{1,0:T(8,128)S(1)}, f32[16,128]{1,0:T(8,128)S(1)}, u32[]{:S(2)}, u32[]{:S(2)}) collective-permute-start(f32[16,128]{1,0:T(8,128)S(1)} %pair_weight.1), channel_id=1, source_target_pairs={{0,8},{8,0},{1,9},{9,1},{2,10},{10,2},{3,11},{11,3},{4,12},{12,4},... | collective-permute-start | bytes 24584 | tf_op jit(solution)/shard_map/ppermute | solution.py:727
  91.2 3.7 %collective-permute-start.5 = (f32[16,128]{1,0:T(8,128)S(1)}, f32[16,128]{1,0:T(8,128)S(1)}, u32[]{:S(2)}, u32[]{:S(2)}) collective-permute-start(f32[16,128]{1,0:T(8,128)S(1)} %pair_weight.1), channel_id=1, source_target_pairs={{0,16},{16,0},{1,17},{17,1},{2,18},{18,2},{3,19},{19,3},{4,20},{20... | collective-permute-start | bytes 24584 | tf_op jit(solution)/shard_map/ppermute | solution.py:727
  94.9 2.2 %copy-start.11 = (f32[32,8,512]{2,1,0:T(8,128)S(1)}, f32[32,8,512]{2,1,0:T(8,128)}, u32[]{:S(2)}) copy-start(f32[32,8,512]{2,1,0:T(8,128)} %get-tuple-element.61.refs_1_) | copy-start | bytes 1572868
  95.0 9.7 %collective-permute-start.10 = (f32[16,128]{1,0:T(8,128)S(1)}, f32[16,128]{1,0:T(8,128)S(1)}, u32[]{:S(2)}, u32[]{:S(2)}) collective-permute-start(f32[16,128]{1,0:T(8,128)S(1)} %add_add_fusion.1), channel_id=1, source_target_pairs={{0,3},{1,2},{2,1},{3,0},{4,7},{5,6},{6,5},{7,4},{8,11},{9,10},{10,... | collective-permute-start | bytes 24584 | tf_op jit(solution)/shard_map/ppermute | solution.py:750
  95.4 9.3 %collective-permute-start.9 = (f32[16,128]{1,0:T(8,128)S(1)}, f32[16,128]{1,0:T(8,128)S(1)}, u32[]{:S(2)}, u32[]{:S(2)}) collective-permute-start(f32[16,128]{1,0:T(8,128)S(1)} %add_add_fusion.1), channel_id=1, source_target_pairs={{0,2},{1,3},{2,0},{3,1},{4,6},{5,7},{6,4},{7,5},{8,10},{9,11},{10,... | collective-permute-start | bytes 24584 | tf_op jit(solution)/shard_map/ppermute | solution.py:750
  97.0 7.8 %collective-permute-start.8 = (f32[16,128]{1,0:T(8,128)S(1)}, f32[16,128]{1,0:T(8,128)S(1)}, u32[]{:S(2)}, u32[]{:S(2)}) collective-permute-start(f32[16,128]{1,0:T(8,128)S(1)} %add_add_fusion.1), channel_id=1, source_target_pairs={{0,1},{1,0},{2,3},{3,2},{4,5},{5,4},{6,7},{7,6},{8,9},{9,8},{10,11... | collective-permute-start | bytes 24584 | tf_op jit(solution)/shard_map/ppermute | solution.py:750
  97.0 11.7 %copy-start.4 = (bf16[768,768]{1,0:T(8,128)(2,1)S(1)}, bf16[768,768]{1,0:T(8,128)(2,1)}, u32[]{:S(2)}) copy-start(bf16[768,768]{1,0:T(8,128)(2,1)} %refs_6_.1) | copy-start | bytes 3538948
  97.0 11.7 %copy-start.5 = (bf16[768,768]{1,0:T(8,128)(2,1)S(1)}, bf16[768,768]{1,0:T(8,128)(2,1)}, u32[]{:S(2)}) copy-start(bf16[768,768]{1,0:T(8,128)(2,1)} %refs_7_.1) | copy-start | bytes 3538948
  97.0 11.8 %copy-start.9 = (f32[768,128]{1,0:T(8,128)S(1)}, f32[768,128]{1,0:T(8,128)}, u32[]{:S(2)}) copy-start(f32[768,128]{1,0:T(8,128)} %get-tuple-element.68.refs_1_) | copy-start | bytes 1179652
  97.0 11.8 %copy-start.10 = (f32[768,128]{1,0:T(8,128)S(1)}, f32[768,128]{1,0:T(8,128)}, u32[]{:S(2)}) copy-start(f32[768,128]{1,0:T(8,128)} %get-tuple-element.69.refs_2_) | copy-start | bytes 1179652
  104.8 4.0 %copy-start.2 = (bf16[768,768]{1,0:T(8,128)(2,1)S(1)}, bf16[768,768]{1,0:T(8,128)(2,1)}, u32[]{:S(2)}) copy-start(bf16[768,768]{1,0:T(8,128)(2,1)} %refs_4_.3) | copy-start | bytes 3538948
  104.8 4.0 %copy-start.3 = (bf16[768,768]{1,0:T(8,128)(2,1)S(1)}, bf16[768,768]{1,0:T(8,128)(2,1)}, u32[]{:S(2)}) copy-start(bf16[768,768]{1,0:T(8,128)(2,1)} %refs_5_.1) | copy-start | bytes 3538948
  104.8 4.0 %copy-start.12 = (f32[8,128]{1,0:T(8,128)S(1)}, f32[8,128]{1,0:T(8,128)}, u32[]{:S(2)}) copy-start(f32[8,128]{1,0:T(8,128)} %get-tuple-element.70.refs_3_) | copy-start | bytes 12292
  104.8 6.2 %collective-permute-start.11 = (f32[16,128]{1,0:T(8,128)S(1)}, f32[16,128]{1,0:T(8,128)S(1)}, u32[]{:S(2)}, u32[]{:S(2)}) collective-permute-start(f32[16,128]{1,0:T(8,128)S(1)} %add_add_fusion), channel_id=1, source_target_pairs={{0,4},{1,5},{2,6},{3,7},{4,0},{5,1},{6,2},{7,3},{8,12},{9,13},{10,... | collective-permute-start | bytes 24584 | tf_op jit(solution)/shard_map/ppermute | solution.py:750
  111.0 6.8 %collective-permute-start.12 = (bf16[2,64,768]{2,1,0:T(8,128)(2,1)S(1)}, bf16[2,64,768]{2,1,0:T(8,128)(2,1)S(1)}, u32[]{:S(2)}, u32[]{:S(2)}) collective-permute-start(bf16[2,64,768]{2,1,0:T(8,128)(2,1)S(1)} %bitcast.17), channel_id=1, source_target_pairs={{0,8},{8,0},{1,9},{9,1},{2,10},{10,2},{3,11},{11,3},{4,12},{12,4},... | collective-permute-start | bytes 589832 | tf_op jit(solution)/shard_map/ppermute | solution.py:727

commit v3 on v2

--- a/solution.py
+++ b/solution.py
@@ -318,6 +318,7 @@
 
 
 MANY = 4
+PARTS = 2
 
 
 def pair_columns(pair_ref, k, many):
@@ -510,8 +511,17 @@
 
     @pl.when(step == pl.num_programs(0) - 1)
     def _():
+        piece = row_count // 2 // PARTS
         for head in range(n_row * n_col):
             sums = sum_ref[head]
+            sums = jnp.concatenate(
+                [
+                    sums[:, (p * PARTS + n) * piece : (p * PARTS + n + 1) * piece]
+                    for n in range(PARTS)
+                    for p in range(2)
+                ],
+                axis=1,
+            )
             shift = shift_of(jnp.max(jnp.abs(sums), axis=0, keepdims=True))
             grad_bias_ref[head, :tok_col, :] = sums * jnp.exp2(shift)
             grad_bias_ref[head, tok_col:, :] = jnp.broadcast_to(shift, (8, row_count))
@@ -632,24 +642,8 @@
     return jnp.concatenate(halves(jnp.concatenate(grads, axis=1)), axis=0)
 
 
-def pair_weight_kernel(normed_ref, grads_ref, part_ref, flat_ref):
-    chunks, width, _ = normed_ref.shape
-    base = pl.program_id(0) * chunks
-
-    @pl.when(pl.program_id(0) == 0)
-    def _():
-        part_ref[...] = jnp.zeros_like(part_ref)
-        flatten(grads_ref, flat_ref)
-
-    def step(n, carry):
-        return carry + matmul_nt(normed_ref[n], flat_columns(flat_ref, (base + n) * MANY, MANY))
-
-    parts = lax.fori_loop(0, chunks, step, jnp.zeros((width, 2 * H), jnp.float32), unroll=2)
-    parts = parts[:, :H] + parts[:, H:]
-    part_ref[...] += (parts[: width // 2] + parts[width // 2 :]).T
-
-
-def pair_back_kernel(factor, normed_ref, inv_ref, grads_ref, weight_ref, out_ref, flat_ref):
+def pair_back_kernel(factor, normed_ref, inv_ref, grads_ref, weight_ref, *refs):
+    out_ref, part_ref, flat_ref = refs[-3:]
     _, count, length, width = out_ref.shape
     weight = weight_ref[...].astype(jnp.float32)
     weight = halves(weight - jnp.mean(weight, axis=1, keepdims=True))
@@ -658,12 +652,13 @@
 
     @pl.when(pl.program_id(0) == 0)
     def _():
+        part_ref[...] = jnp.zeros_like(part_ref)
         flatten(grads_ref, flat_ref)
 
     def step(n, carry):
         k = n * MANY
-        normed = normed_ref[n].astype(jnp.float32)
-        normed = normed[:width] + normed[width:]
+        both = normed_ref[n]
+        normed = both[:width].astype(jnp.float32) + both[width:].astype(jnp.float32)
         grads = flat_columns(flat_ref, base + k, MANY)
         grad_in = matmul(weight, jnp.concatenate([grads, grads], axis=0))
         overlap = jnp.mean(grad_in * normed, axis=0, keepdims=True)
@@ -671,51 +666,51 @@
         result = result.astype(jnp.bfloat16).T.reshape(MANY, 2 * length, width)
         for p in range(2):
             out_ref[p, pl.ds(k, MANY)] = result[:, p * length : (p + 1) * length]
-        return carry
-
-    lax.fori_loop(0, count // MANY, step, 0, unroll=2)
-
-
-def pair_weight(normed, grads):
-    heads, length, rows = grads.shape
-    part_shape = (H, normed.shape[1] // 2)
+        return carry + matmul_nt(both, grads)
+
+    parts = jnp.zeros((2 * width, 2 * H), jnp.float32)
+    parts = lax.fori_loop(0, count // MANY, step, parts, unroll=2)
+    parts = parts[:, :H] + parts[:, H:]
+    part_ref[...] += (parts[:width] + parts[width:]).T
+
+
+def pair_backward(number, so_far, shape, normed, inv_std, grads, weight_t, factor):
+    row_count, tok_col, width = shape
+    whole = row_count // 2
+    steps = STEPS // PARTS
+    first = number * steps
+
+    def split(shape):
+        block = (shape[0] // STEPS,) + tuple(shape[1:])
+        return pl.BlockSpec(block, lambda i: (i + first,) + (0,) * (len(shape) - 1))
+
+    previous = [] if so_far is None else [so_far]
     return pl.pallas_call(
-        pair_weight_kernel,
-        out_shape=jax.ShapeDtypeStruct(part_shape, jnp.float32),
-        grid=(STEPS,),
-        in_specs=[split_spec(normed.shape), whole_spec(grads.shape)],
-        out_specs=whole_spec(part_shape),
-        scratch_shapes=[pltpu.VMEM((H * rows // 2, 2 * length), jnp.float32)],
+        lambda *refs: pair_back_kernel(factor, *refs),
+        out_shape=[
+            jax.ShapeDtypeStruct((2, whole, tok_col, width), jnp.bfloat16),
+            jax.ShapeDtypeStruct((H, width), jnp.float32),
+        ],
+        grid=(steps,),
+        in_specs=[
+            split(normed.shape),
+            split(inv_std.shape),
+            whole_spec(grads.shape),
+            whole_spec(weight_t.shape),
+        ]
+        + [pl.BlockSpec(memory_space=pl.ANY)] * len(previous),
+        out_specs=[
+            pl.BlockSpec((2, whole // STEPS, tok_col, width), lambda i: (0, i + first, 0, 0)),
+            whole_spec((H, width)),
+        ],
+        scratch_shapes=[pltpu.VMEM((H * whole // PARTS, 2 * tok_col), jnp.float32)],
+        input_output_aliases={4: 0} if previous else {},
         compiler_params=params(24),
         cost_estimate=pl.CostEstimate(
-            flops=5_000_000_000, bytes_accessed=100_000, transcendentals=0
-        ),
-        name="pair_weight",
-    )(normed, grads)
-
-
-def pair_backward(shape, normed, inv_std, grads, weight_t, factor):
-    row_count, tok_col, width = shape
-    whole = row_count // 2
-    pair_grad = pl.pallas_call(
-        lambda *refs: pair_back_kernel(factor, *refs),
-        out_shape=jax.ShapeDtypeStruct((2, whole, tok_col, width), jnp.bfloat16),
-        grid=(STEPS,),
-        in_specs=[
-            split_spec(normed.shape),
-            split_spec(inv_std.shape),
-            whole_spec(grads.shape),
-            whole_spec(weight_t.shape),
-        ],
-        out_specs=pl.BlockSpec((2, whole // STEPS, tok_col, width), lambda i: (0, i, 0, 0)),
-        scratch_shapes=[pltpu.VMEM((H * whole, 2 * tok_col), jnp.float32)],
-        compiler_params=params(24),
-        cost_estimate=pl.CostEstimate(
-            flops=8_000_000_000, bytes_accessed=100_000, transcendentals=0
+            flops=6_000_000_000, bytes_accessed=100_000, transcendentals=0
         ),
         name="pair_backward",
-    )(normed, inv_std, grads, weight_t)
-    return pair_grad.reshape(shape)
+    )(normed, inv_std, grads, weight_t, *previous)
 
 
 def unscaled(block, rows):
@@ -777,29 +772,27 @@
     back, _, pair_normed = lax.optimization_barrier((back, grad_bias, pair_normed))
     back = lax.all_to_all(back, ("row", "col"), 0, 0, tiled=True)
 
-    other_bias = swap(grad_bias, "samp")
-    own_bias = unscaled(grad_bias, tok_col)
-    part = pair_weight(pair_normed, own_bias)
-    samp_part = swap(part, "samp")
-    row_part = swap(part, "row")
-    both_part = lax.ppermute(part, ("samp", "row"), [(n, 3 - n) for n in range(4)])
-    other_bias, part = lax.optimization_barrier((other_bias, part))
-    grads = own_bias + unscaled(other_bias, tok_col)
-    part = (part + samp_part) + (row_part + both_part)
-    grads, part = lax.optimization_barrier((grads, part))
-    sums = (send(part, 1), send(part, 2), send(part, 3))
-    pair_grad = pair_backward(
-        pair.shape, pair_normed, pair_inv, grads, weight_t, total_tokens / samples
-    )
-
-    pair_grad, back, sums = lax.optimization_barrier((pair_grad, back, sums))
-    part = (part + sums[0]) + (sums[1] + sums[2])
-    last = send(part, 4)
+    pair_grad, part = None, 0.0
+    pieces = jnp.split(grad_bias, PARTS, axis=2)
+    others = [swap(piece, "samp") for piece in pieces]
+    for n, (piece, other) in enumerate(zip(pieces, others)):
+        grads = unscaled(piece, tok_col) + unscaled(other, tok_col)
+        pair_grad, more = pair_backward(
+            n, pair_grad, pair.shape, pair_normed, pair_inv, grads, weight_t,
+            total_tokens / samples,
+        )
+        part = part + more
+    pair_grad = pair_grad.reshape(pair.shape)
+
+    pair_grad, back, part = lax.optimization_barrier((pair_grad, back, part))
+    flip = [(n, n ^ (n_col + 1)) for n in range(n_row * n_col)]
+    sums = (swap(part, "row"), send(part, 1), lax.ppermute(part, ("row", "col"), flip))
     token_half = token_back(back.astype(jnp.float32), *own, weights)
-    token_half, last = lax.optimization_barrier((token_half, last))
-    part = part + last
+    token_half, sums = lax.optimization_barrier((token_half, sums))
     token_half = token_half.reshape(half, tok_col, D)
     other_half = swap(token_half, "row")
+    part = (part + sums[0]) + (sums[1] + sums[2])
+    part = (part + send(part, 2)) + (send(part, 4) + send(part, 6))
     first = row_index == 0
     token_grad = jnp.concatenate(
         [jnp.where(first, token_half, other_half), jnp.where(first, other_half, token_half)],

time: 119 us -> 131 us (1.10)
  waiting for transfers between devices: 25.7 us -> 37.8 us
  local copies, waits for them, and re-layouts: 3.47 us -> 6.98 us
  Pallas kernels: 48.7 us -> 47.1 us
    all_to_all x1, waiting for transfers between devices: 5.53 us -> 14.3 us  [body_heads(): lax.all_to_all(grad_bias.astype(jnp.float16), ('row', 'col'), 0, 0, tiled...]
    unnamed x28 -> x26, local copies, waits for them, and re-layouts: 3.44 us -> 6.95 us
    pallas_call x2, Pallas kernels: 13.2 us -> 11.5 us  [pair_backward(): pl.pallas_call(lambda *refs: pair_back_kernel(factor, *refs), out_shape=[...]
    ppermute x4, waiting for transfers between devices: 5.53 us -> 7.21 us  [swap(): return lax.ppermute(block, axis, [(0, 1), (1, 0)])]
  transfers between devices with their start and end apart: 16 -> 16, of which waited for: 6 -> 7; matrix products, arithmetic and copies ran while one was open for 5% -> 3% of each run, Pallas kernels for 31% -> 27%
where the time goes in v3:
time: 131 us
  Pallas kernels  47.1 us (36%)
  waiting for transfers between devices  37.8 us (29%)
  starting transfers between devices  31.5 us (24%)
  local copies, waits for them, and re-layouts  6.98 us (5%)
  other arithmetic  6.17 us (5%)
    all_to_all x1, waiting for transfers between devices, body_heads(): lax.all_to_all(grad_bias.astype(jnp.float16), ('row', 'col'), 0, 0, tiled...  14.3 us
    pallas_call x2, Pallas kernels, pair_backward(): pl.pallas_call(lambda *refs: pair_back_kernel(factor, *refs), out_shape=[...  11.5 us
    all_to_all x1, waiting for transfers between devices, body_heads(): bias = lax.all_to_all(bias, ('row', 'col'), 0, 0, tiled=True)  10.6 us
    ppermute x8, starting transfers between devices, send(): return lax.ppermute(block, 'col', [(c, c ^ offset) for c in range(n_col)])  10.5 us
    pallas_call x1, Pallas kernels, pair_bias(): pl.pallas_call(bias_kernel, out_shape=jax.ShapeDtypeStruct((H, tok_col, r...  9.77 us
    pallas_call x1, Pallas kernels, pair_units(): pl.pallas_call(norm_kernel, out_shape=[jax.ShapeDtypeStruct(shapes[0], jn...  8.75 us
    pallas_call x1, Pallas kernels, attention(): pl.pallas_call(attention_kernel, out_shape=[jax.ShapeDtypeStruct(back_sha...  7.66 us
    ppermute x4, waiting for transfers between devices, swap(): return lax.ppermute(block, axis, [(0, 1), (1, 0)])  7.21 us
  transfers between devices with their start and end apart: 16, of which 7 were waited for; matrix products, arithmetic and copies ran while one was open for 3% of the time, Pallas kernels for 27%

profile of v3, /device:TPU:0, one launch (start us, length us, event | category | flops | bytes accessed | tf_op | source)
XLA Modules:
  0.0 130.6 jit_solution(1492683345696137467)
XLA Ops:
  0.6 0.0 copy-start.1
  0.6 0.0 copy-start.6
  0.7 0.0 copy-start.7
  0.7 4.3 %token_messages.1 = (bf16[2,4,48,256]{3,2,1,0:T(8,128)(2,1)}, bf16[2,4,48,256]{3,2,1,0:T(8,128)(2,1)}, bf16[2,4,48,256]{3,2,1,0:T(8,128)(2,1)}, bf16[2,4,48,256]{3,2,1,0:T(8,128)(2,1)}) custom-call(s32[1]{0:T(128)} %bitcast.4.row_ref, s32[1]{0:T(128)} %bitcast.col_ref, bf16[4,64,768]{2,1,0:T(8,128)(2,1)} %tokens_ref.3, s32[1,64]{1,0:T(1,128)} %bitcast.27, ...), custom_call_target="tpu_custom_call" | custom-call | flops 4000000000 | bytes 4000000 | tf_op jit(solution)/shard_map/token_messages/pallas_call | solution.py:245
  5.0 3.0 %collective-permute-start = (bf16[2,4,48,256]{3,2,1,0:T(8,128)(2,1)}, bf16[2,4,48,256]{3,2,1,0:T(8,128)(2,1)S(1)}, u32[]{:S(2)}, u32[]{:S(2)}) collective-permute-start(bf16[2,4,48,256]{3,2,1,0:T(8,128)(2,1)} %get-tuple-element.41), channel_id=1, source_target_pairs={{0,2},{1,3},{2,0},{3,1},{4,6},{5,7},{6,4},{7,5},{8,10},{9,11},{10,... | collective-permute-start | bytes 589832 | tf_op jit(solution)/shard_map/ppermute | solution.py:745
  8.0 2.6 %collective-permute-start.1 = (bf16[2,4,48,256]{3,2,1,0:T(8,128)(2,1)}, bf16[2,4,48,256]{3,2,1,0:T(8,128)(2,1)S(1)}, u32[]{:S(2)}, u32[]{:S(2)}) collective-permute-start(bf16[2,4,48,256]{3,2,1,0:T(8,128)(2,1)} %get-tuple-element.42), channel_id=1, source_target_pairs={{0,4},{1,5},{2,6},{3,7},{4,0},{5,1},{6,2},{7,3},{8,12},{9,13},{10,... | collective-permute-start | bytes 589832 | tf_op jit(solution)/shard_map/ppermute | solution.py:745
  10.6 0.0 collective-permute-start.2
  10.6 0.0 copy-done.1
  10.6 0.0 copy-done.6
  10.6 0.0 copy-done.7
  10.6 9.8 %pair_bias.1 = f32[16,64,256]{2,1,0:T(8,128)S(1)} custom-call(bf16[2,128,64,128]{3,2,1,0:T(8,128)(2,1)S(1)} %bitcast.18, bf16[16,128]{1,0:T(8,128)(2,1)S(1)} %bitcast.19, s32[1,64]{1,0:T(1,128)S(1)} %bitcast.22), custom_call_target="tpu_custom_call" | custom-call | flops 6000000000 | bytes 5000000 | tf_op jit(solution)/shard_map/pair_bias/pallas_call | solution.py:384
  20.4 0.0 copy-start
  20.4 0.9 convert_element_type.27
  21.3 0.0 collective-permute-done.refs_1_
  21.3 4.1 %collective-permute-done.1.refs_2_ = bf16[2,4,48,256]{3,2,1,0:T(8,128)(2,1)S(1)} collective-permute-done((bf16[2,4,48,256]{3,2,1,0:T(8,128)(2,1)}, bf16[2,4,48,256]{3,2,1,0:T(8,128)(2,1)S(1)}, u32[]{:S(2)}, u32[]{:S(2)}) %collective-permute-start.1) | collective-permute-done | bytes 196640 | tf_op jit(solution)/shard_map/ppermute | solution.py:745
  25.4 0.0 collective-permute-done.2.refs_3_
  25.4 6.7 %all-to-all-start = ((f16[16,64,256]{2,1,0:T(8,128)(2,1)}), f16[16,64,256]{2,1,0:T(8,128)(2,1)S(1)}, u32[]{:S(2)}, u32[]{:S(2)}) async-start(f16[16,64,256]{2,1,0:T(8,128)(2,1)} %convert_element_type.27), calls=%async_computation | async-start | bytes 1048576 | tf_op jit(solution)/shard_map/all_to_all | solution.py:762
  32.1 0.1 pad_maximum_fusion
  32.2 0.5 collective-permute-start.3
  32.7 3.0 %own_rows.1 = (f32[768,128]{1,0:T(8,128)}, f32[768,128]{1,0:T(8,128)}, f32[8,128]{1,0:T(8,128)}) custom-call(s32[1]{0:T(128)} %bitcast.4.row_ref, bf16[4,64,768]{2,1,0:T(8,128)(2,1)} %tokens_ref.3, s32[1,64]{1,0:T(1,128)} %bitcast.28, bf16[32,768]{1,0:T(8,128)(2,1)} %table_ref.3, bf16[768,768]{1,0:T(8,128)(2,1)} %refs_7_.1, bf16[4,64,768]{2,1,0:T(8,128)(2,1)} %cot_ref.1), custom_call_target="tpu_custom_call" | custom-call | flops 3000000000 | bytes 3000000 | tf_op jit(solution)/shard_map/own_rows/pallas_call | solution.py:289
  35.7 0.0 collective-permute-done.3.refs_4_
  35.7 10.6 %all-to-all-done = f16[16,64,256]{2,1,0:T(8,128)(2,1)S(1)} async-done(((f16[16,64,256]{2,1,0:T(8,128)(2,1)}), f16[16,64,256]{2,1,0:T(8,128)(2,1)S(1)}, u32[]{:S(2)}, u32[]{:S(2)}) %all-to-all-start) | async-done | bytes 524320 | tf_op jit(solution)/shard_map/all_to_all | solution.py:762
  46.3 0.1 convert_element_type.28.refs_5_
  46.4 7.7 %attention.1 = (f32[16,200,128]{2,1,0:T(8,128)S(1)}, f32[16,72,256]{2,1,0:T(8,128)S(1)}) custom-call(s32[1]{0:T(128)} %bitcast.col_ref, bf16[2,4,48,256]{3,2,1,0:T(8,128)(2,1)S(1)} %copy-done, bf16[2,4,48,256]{3,2,1,0:T(8,128)(2,1)S(1)} %collective-permute-done.refs_1_, bf16[2,4,48,256]{3,2,1,0:T(8,128)(2,1)S(1)} %collective-permute-done.1.refs_2_, ...), custom_call_target="tpu_custom_call" | custom-call | flops 8000000000 | bytes 6000000 | tf_op jit(solution)/shard_map/attention/pallas_call | solution.py:538
  54.1 0.9 convert_element_type.30
  55.0 4.0 %all-to-all-start.1 = ((f16[16,72,256]{2,1,0:T(8,128)(2,1)}), f16[16,72,256]{2,1,0:T(8,128)(2,1)S(1)}, u32[]{:S(2)}, u32[]{:S(2)}) async-start(f16[16,72,256]{2,1,0:T(8,128)(2,1)} %convert_element_type.30), calls=%async_computation.1 | async-start | bytes 1179648 | tf_op jit(solution)/shard_map/all_to_all | solution.py:767
  59.0 1.1 convert_element_type.29
  60.1 14.3 %all-to-all-done.1 = f16[16,72,256]{2,1,0:T(8,128)(2,1)S(1)} async-done(((f16[16,72,256]{2,1,0:T(8,128)(2,1)}), f16[16,72,256]{2,1,0:T(8,128)(2,1)S(1)}, u32[]{:S(2)}, u32[]{:S(2)}) %all-to-all-start.1) | async-done | bytes 589856 | tf_op jit(solution)/shard_map/all_to_all | solution.py:767
  74.4 0.2 slice_convert_fusion
  74.5 1.6 %collective-permute-start.5 = (f16[16,72,128]{2,1,0:T(8,128)(2,1)S(1)}, f16[16,72,128]{2,1,0:T(8,128)(2,1)S(1)}, u32[]{:S(2)}, u32[]{:S(2)}) collective-permute-start(f16[16,72,128]{2,1,0:T(8,128)(2,1)S(1)} %get-tuple-element.79), channel_id=1, source_target_pairs={{0,16},{16,0},{1,17},{17,1},{2,18},{18,2},{3,19},{19,3},{4,20},{20... | collective-permute-start | bytes 884744 | tf_op jit(solution)/shard_map/ppermute | solution.py:722
  76.1 8.7 %pair_units.1 = (bf16[32,256,512]{2,1,0:T(8,128)(2,1)}, f32[32,8,512]{2,1,0:T(8,128)}) custom-call(bf16[2,128,64,128]{3,2,1,0:T(8,128)(2,1)} %bitcast.17), custom_call_target="tpu_custom_call" | custom-call | flops 6000000000 | bytes 12000000 | tf_op jit(solution)/shard_map/pair_units/pallas_call | solution.py:414
  84.9 0.5 collective-permute-start.4
  85.4 4.3 %all-to-all-start.2 = ((f16[16,200,128]{2,1,0:T(8,128)(2,1)}), f16[16,200,128]{2,1,0:T(8,128)(2,1)}, u32[]{:S(2)}, u32[]{:S(2)}) async-start(f16[16,200,128]{2,1,0:T(8,128)(2,1)} %convert_element_type.29), calls=%async_computation.2 | async-start | bytes 1638400 | tf_op jit(solution)/shard_map/all_to_all | solution.py:773
  89.7 0.0 collective-permute-done.5
  89.8 0.1 fusion.refs_2_
  89.9 0.0 copy-start.9
  89.9 4.3 %collective-permute-done.4 = f16[16,72,128]{2,1,0:T(8,128)(2,1)S(1)} collective-permute-done((f16[16,72,128]{2,1,0:T(8,128)(2,1)S(1)}, f16[16,72,128]{2,1,0:T(8,128)(2,1)S(1)}, u32[]{:S(2)}, u32[]{:S(2)}) %collective-permute-start.4) | collective-permute-done | bytes 294944 | tf_op jit(solution)/shard_map/ppermute | solution.py:722
  94.3 0.1 fusion.1.refs_2_
  94.4 3.4 %copy-done.8 = bf16[32,256,512]{2,1,0:T(8,128)(2,1)S(1)} copy-done((bf16[32,256,512]{2,1,0:T(8,128)(2,1)S(1)}, bf16[32,256,512]{2,1,0:T(8,128)(2,1)}, u32[]{:S(2)}) %copy-start.8) | copy-done | bytes 8388632
  97.8 5.7 %pair_backward.2 = (bf16[2,128,64,128]{3,2,1,0:T(8,128)(2,1)}, f32[16,128]{1,0:T(8,128)S(1)}) custom-call(bf16[32,256,512]{2,1,0:T(8,128)(2,1)S(1)} %copy-done.8, f32[32,8,512]{2,1,0:T(8,128)S(1)} %copy-done.9, f32[16,64,128]{2,1,0:T(8,128)S(1)} %fusion.refs_2_, bf16[16,128]{1,0:T(8,128)(2,1)S(1)} %bitcast.20), custom_call_target="tpu_custom_call" | custom-call | flops 6000000000 | bytes 100000 | tf_op jit(solution)/shard_map/pair_backward/pallas_call | solution.py:688
  103.5 5.7 %pair_backward.3 = (bf16[2,128,64,128]{3,2,1,0:T(8,128)(2,1)}, f32[16,128]{1,0:T(8,128)S(1)}) custom-call(bf16[32,256,512]{2,1,0:T(8,128)(2,1)S(1)} %copy-done.8, f32[32,8,512]{2,1,0:T(8,128)S(1)} %copy-done.9, f32[16,64,128]{2,1,0:T(8,128)S(1)} %fusion.1.refs_2_, bf16[16,128]{1,0:T(8,128)(2,1)S(1)} %bitcast.21, ...), custom_call_target="tpu_custom_call", output_to_operand_aliasing={{0}: (4, {})} | custom-call | flops 6000000000 | bytes 100000 | tf_op jit(solution)/shard_map/pair_backward/pallas_call | solution.py:688
  109.3 0.4 all-to-all-done.2
  109.7 1.9 %collective-permute-start.8 = (f32[16,128]{1,0:T(8,128)S(1)}, f32[16,128]{1,0:T(8,128)S(1)}, u32[]{:S(2)}, u32[]{:S(2)}) collective-permute-start(f32[16,128]{1,0:T(8,128)S(1)} %add.29), channel_id=1, source_target_pairs={{0,9},{1,8},{2,11},{3,10},{4,13},{5,12},{6,15},{7,14},{8,1},{9,0},... | collective-permute-start | bytes 24584 | tf_op jit(solution)/shard_map/ppermute | solution.py:789
  111.6 0.0 collective-permute-start.7
  111.6 0.5 collective-permute-start.6
  112.1 1.3 convert_element_type.35.refs_0_
  113.4 0.0 copy-start.4
  113.4 1.3 copy-done.4
  114.7 1.3 copy-done.5
  115.9 1.0 copy-done.11
  116.9 2.1 %token_back.1 = bf16[128,768]{1,0:T(8,128)(2,1)S(1)} custom-call(f32[16,200,128]{2,1,0:T(8,128)S(1)} %convert_element_type.35.refs_0_, f32[768,128]{1,0:T(8,128)S(1)} %copy-done.10, f32[768,128]{1,0:T(8,128)S(1)} %copy-done.11, f32[8,128]{1,0:T(8,128)S(1)} %copy-done.12, bf16[768,768]{1,0:T(8,128)(2,1)S(1)} %copy-done.2, bf16[768,768]{1,0:T(8,128)(2,1)S(1)} %copy-done.3, ...), custom_call_target="tpu_custom_call" | custom-call | flops 4000000000 | bytes 8000000 | tf_op jit(solution)/shard_map/token_back/pallas_call | solution.py:611
  119.0 0.0 collective-permute-done.8
  119.0 0.0 collective-permute-done.7
  119.1 0.0 collective-permute-done.6
  119.1 2.6 %collective-permute-start.12 = (f32[16,128]{1,0:T(8,128)S(1)}, f32[16,128]{1,0:T(8,128)S(1)}, u32[]{:S(2)}, u32[]{:S(2)}) collective-permute-start(f32[16,128]{1,0:T(8,128)S(1)} %add_add_fusion), channel_id=1, source_target_pairs={{0,6},{1,7},{2,4},{3,5},{4,2},{5,3},{6,0},{7,1},{8,14},{9,15},{10,... | collective-permute-start | bytes 24584 | tf_op jit(solution)/shard_map/ppermute | solution.py:745
  121.7 0.3 collective-permute-start.11
  122.0 1.5 %collective-permute-start.10 = (f32[16,128]{1,0:T(8,128)S(1)}, f32[16,128]{1,0:T(8,128)S(1)}, u32[]{:S(2)}, u32[]{:S(2)}) collective-permute-start(f32[16,128]{1,0:T(8,128)S(1)} %add_add_fusion), channel_id=1, source_target_pairs={{0,2},{1,3},{2,0},{3,1},{4,6},{5,7},{6,4},{7,5},{8,10},{9,11},{10,... | collective-permute-start | bytes 24584 | tf_op jit(solution)/shard_map/ppermute | solution.py:745
  123.5 1.5 %collective-permute-start.9 = (bf16[2,64,768]{2,1,0:T(8,128)(2,1)S(1)}, bf16[2,64,768]{2,1,0:T(8,128)(2,1)S(1)}, u32[]{:S(2)}, u32[]{:S(2)}) collective-permute-start(bf16[2,64,768]{2,1,0:T(8,128)(2,1)S(1)} %bitcast.15), channel_id=1, source_target_pairs={{0,8},{8,0},{1,9},{9,1},{2,10},{10,2},{3,11},{11,3},{4,12},{12,4},... | collective-permute-start | bytes 589832 | tf_op jit(solution)/shard_map/ppermute | solution.py:722
  125.0 0.0 collective-permute-done.12
  125.0 1.2 collective-permute-done.11
  126.2 0.0 collective-permute-done.10
  126.2 0.6 multiply_bitcast_fusion
  126.8 2.9 %collective-permute-done.9 = bf16[2,64,768]{2,1,0:T(8,128)(2,1)S(1)} collective-permute-done((bf16[2,64,768]{2,1,0:T(8,128)(2,1)S(1)}, bf16[2,64,768]{2,1,0:T(8,128)(2,1)S(1)}, u32[]{:S(2)}, u32[]{:S(2)}) %collective-permute-start.9) | collective-permute-done | bytes 196640 | tf_op jit(solution)/shard_map/ppermute | solution.py:722
  129.8 0.8 pad_maximum_fusion.1
  (25 shorter events, 0.3 us)
Async XLA Ops:
  0.6 10.0 %copy-start.1 = (bf16[256,64,128]{2,1,0:T(8,128)(2,1)S(1)}, bf16[256,64,128]{2,1,0:T(8,128)(2,1)}, u32[]{:S(2)}) copy-start(bf16[256,64,128]{2,1,0:T(8,128)(2,1)} %param.15) | copy-start | bytes 12582916
  0.6 10.0 %copy-start.6 = (bf16[128,16]{0,1:T(8,128)(2,1)S(1)}, bf16[128,16]{0,1:T(8,128)(2,1)}, u32[]{:S(2)}) copy-start(bf16[128,16]{0,1:T(8,128)(2,1)} %param.16) | copy-start | bytes 12292
  0.7 9.9 %copy-start.7 = (s32[64]{0:T(128)S(1)}, s32[64]{0:T(128)}, u32[]{:S(2)}) copy-start(s32[64]{0:T(128)} %param.14) | copy-start | bytes 772
  5.0 16.3 %collective-permute-start = (bf16[2,4,48,256]{3,2,1,0:T(8,128)(2,1)}, bf16[2,4,48,256]{3,2,1,0:T(8,128)(2,1)S(1)}, u32[]{:S(2)}, u32[]{:S(2)}) collective-permute-start(bf16[2,4,48,256]{3,2,1,0:T(8,128)(2,1)} %get-tuple-element.41), channel_id=1, source_target_pairs={{0,2},{1,3},{2,0},{3,1},{4,6},{5,7},{6,4},{7,5},{8,10},{9,11},{10,... | collective-permute-start | bytes 589832 | tf_op jit(solution)/shard_map/ppermute | solution.py:745
  8.0 17.4 %collective-permute-start.1 = (bf16[2,4,48,256]{3,2,1,0:T(8,128)(2,1)}, bf16[2,4,48,256]{3,2,1,0:T(8,128)(2,1)S(1)}, u32[]{:S(2)}, u32[]{:S(2)}) collective-permute-start(bf16[2,4,48,256]{3,2,1,0:T(8,128)(2,1)} %get-tuple-element.42), channel_id=1, source_target_pairs={{0,4},{1,5},{2,6},{3,7},{4,0},{5,1},{6,2},{7,3},{8,12},{9,13},{10,... | collective-permute-start | bytes 589832 | tf_op jit(solution)/shard_map/ppermute | solution.py:745
  10.6 14.8 %collective-permute-start.2 = (bf16[2,4,48,256]{3,2,1,0:T(8,128)(2,1)}, bf16[2,4,48,256]{3,2,1,0:T(8,128)(2,1)S(1)}, u32[]{:S(2)}, u32[]{:S(2)}) collective-permute-start(bf16[2,4,48,256]{3,2,1,0:T(8,128)(2,1)} %get-tuple-element.43), channel_id=1, source_target_pairs={{0,6},{1,7},{2,4},{3,5},{4,2},{5,3},{6,0},{7,1},{8,14},{9,15},{10,... | collective-permute-start | bytes 589832 | tf_op jit(solution)/shard_map/ppermute | solution.py:745
  20.4 11.7 %copy-start = (bf16[2,4,48,256]{3,2,1,0:T(8,128)(2,1)S(1)}, bf16[2,4,48,256]{3,2,1,0:T(8,128)(2,1)}, u32[]{:S(2)}) copy-start(bf16[2,4,48,256]{3,2,1,0:T(8,128)(2,1)} %get-tuple-element.44.refs_0_) | copy-start | bytes 589828
  25.4 20.9 %all-to-all-start = ((f16[16,64,256]{2,1,0:T(8,128)(2,1)}), f16[16,64,256]{2,1,0:T(8,128)(2,1)S(1)}, u32[]{:S(2)}, u32[]{:S(2)}) async-start(f16[16,64,256]{2,1,0:T(8,128)(2,1)} %convert_element_type.27), calls=%async_computation | async-start | bytes 1048576 | tf_op jit(solution)/shard_map/all_to_all | solution.py:762
  32.2 3.5 %collective-permute-start.3 = (bf16[4,4,48,256]{3,2,1,0:T(8,128)(2,1)S(1)}, bf16[4,4,48,256]{3,2,1,0:T(8,128)(2,1)S(1)}, u32[]{:S(2)}, u32[]{:S(2)}) collective-permute-start(bf16[4,4,48,256]{3,2,1,0:T(8,128)(2,1)S(1)} %pad_maximum_fusion), channel_id=1, source_target_pairs={{0,1},{1,0},{2,3},{3,2},{4,5},{5,4},{6,7},{7,6},{8,9},{9,8},{10,11... | collective-permute-start | bytes 1179656 | tf_op jit(solution)/shard_map/ppermute | solution.py:745
  55.0 19.4 %all-to-all-start.1 = ((f16[16,72,256]{2,1,0:T(8,128)(2,1)}), f16[16,72,256]{2,1,0:T(8,128)(2,1)S(1)}, u32[]{:S(2)}, u32[]{:S(2)}) async-start(f16[16,72,256]{2,1,0:T(8,128)(2,1)} %convert_element_type.30), calls=%async_computation.1 | async-start | bytes 1179648 | tf_op jit(solution)/shard_map/all_to_all | solution.py:767
  74.5 15.2 %collective-permute-start.5 = (f16[16,72,128]{2,1,0:T(8,128)(2,1)S(1)}, f16[16,72,128]{2,1,0:T(8,128)(2,1)S(1)}, u32[]{:S(2)}, u32[]{:S(2)}) collective-permute-start(f16[16,72,128]{2,1,0:T(8,128)(2,1)S(1)} %get-tuple-element.79), channel_id=1, source_target_pairs={{0,16},{16,0},{1,17},{17,1},{2,18},{18,2},{3,19},{19,3},{4,20},{20... | collective-permute-start | bytes 884744 | tf_op jit(solution)/shard_map/ppermute | solution.py:722
  84.9 9.3 %collective-permute-start.4 = (f16[16,72,128]{2,1,0:T(8,128)(2,1)S(1)}, f16[16,72,128]{2,1,0:T(8,128)(2,1)S(1)}, u32[]{:S(2)}, u32[]{:S(2)}) collective-permute-start(f16[16,72,128]{2,1,0:T(8,128)(2,1)S(1)} %get-tuple-element.80), channel_id=1, source_target_pairs={{0,16},{16,0},{1,17},{17,1},{2,18},{18,2},{3,19},{19,3},{4,20},{20... | collective-permute-start | bytes 884744 | tf_op jit(solution)/shard_map/ppermute | solution.py:722
  85.4 24.3 %all-to-all-start.2 = ((f16[16,200,128]{2,1,0:T(8,128)(2,1)}), f16[16,200,128]{2,1,0:T(8,128)(2,1)}, u32[]{:S(2)}, u32[]{:S(2)}) async-start(f16[16,200,128]{2,1,0:T(8,128)(2,1)} %convert_element_type.29), calls=%async_computation.2 | async-start | bytes 1638400 | tf_op jit(solution)/shard_map/all_to_all | solution.py:773
  89.9 4.5 %copy-start.9 = (f32[32,8,512]{2,1,0:T(8,128)S(1)}, f32[32,8,512]{2,1,0:T(8,128)}, u32[]{:S(2)}) copy-start(f32[32,8,512]{2,1,0:T(8,128)} %get-tuple-element.61.refs_1_) | copy-start | bytes 1572868
  94.4 3.4 %copy-start.8 = (bf16[32,256,512]{2,1,0:T(8,128)(2,1)S(1)}, bf16[32,256,512]{2,1,0:T(8,128)(2,1)}, u32[]{:S(2)}) copy-start(bf16[32,256,512]{2,1,0:T(8,128)(2,1)} %get-tuple-element.60.refs_0_) | copy-start | bytes 25165828
  103.5 9.8 %copy-start.10 = (f32[768,128]{1,0:T(8,128)S(1)}, f32[768,128]{1,0:T(8,128)}, u32[]{:S(2)}) copy-start(f32[768,128]{1,0:T(8,128)} %get-tuple-element.68.refs_1_) | copy-start | bytes 1179652
  109.3 4.1 %copy-start.2 = (bf16[768,768]{1,0:T(8,128)(2,1)S(1)}, bf16[768,768]{1,0:T(8,128)(2,1)}, u32[]{:S(2)}) copy-start(bf16[768,768]{1,0:T(8,128)(2,1)} %refs_4_.3) | copy-start | bytes 3538948
  109.3 4.1 %copy-start.3 = (bf16[768,768]{1,0:T(8,128)(2,1)S(1)}, bf16[768,768]{1,0:T(8,128)(2,1)}, u32[]{:S(2)}) copy-start(bf16[768,768]{1,0:T(8,128)(2,1)} %refs_5_.1) | copy-start | bytes 3538948
  109.3 4.1 %copy-start.12 = (f32[8,128]{1,0:T(8,128)S(1)}, f32[8,128]{1,0:T(8,128)}, u32[]{:S(2)}) copy-start(f32[8,128]{1,0:T(8,128)} %get-tuple-element.70.refs_3_) | copy-start | bytes 12292
  109.7 9.3 %collective-permute-start.8 = (f32[16,128]{1,0:T(8,128)S(1)}, f32[16,128]{1,0:T(8,128)S(1)}, u32[]{:S(2)}, u32[]{:S(2)}) collective-permute-start(f32[16,128]{1,0:T(8,128)S(1)} %add.29), channel_id=1, source_target_pairs={{0,9},{1,8},{2,11},{3,10},{4,13},{5,12},{6,15},{7,14},{8,1},{9,0},... | collective-permute-start | bytes 24584 | tf_op jit(solution)/shard_map/ppermute | solution.py:789
  111.6 7.5 %collective-permute-start.7 = (f32[16,128]{1,0:T(8,128)S(1)}, f32[16,128]{1,0:T(8,128)S(1)}, u32[]{:S(2)}, u32[]{:S(2)}) collective-permute-start(f32[16,128]{1,0:T(8,128)S(1)} %add.29), channel_id=1, source_target_pairs={{0,1},{1,0},{2,3},{3,2},{4,5},{5,4},{6,7},{7,6},{8,9},{9,8},{10,11... | collective-permute-start | bytes 24584 | tf_op jit(solution)/shard_map/ppermute | solution.py:745
  111.6 7.5 %collective-permute-start.6 = (f32[16,128]{1,0:T(8,128)S(1)}, f32[16,128]{1,0:T(8,128)S(1)}, u32[]{:S(2)}, u32[]{:S(2)}) collective-permute-start(f32[16,128]{1,0:T(8,128)S(1)} %add.29), channel_id=1, source_target_pairs={{0,8},{8,0},{1,9},{9,1},{2,10},{10,2},{3,11},{11,3},{4,12},{12,4},... | collective-permute-start | bytes 24584 | tf_op jit(solution)/shard_map/ppermute | solution.py:722
  113.4 1.3 copy-start.4
  114.7 1.3 copy-start.5
  115.9 1.0 copy-start.11
  119.1 5.9 %collective-permute-start.12 = (f32[16,128]{1,0:T(8,128)S(1)}, f32[16,128]{1,0:T(8,128)S(1)}, u32[]{:S(2)}, u32[]{:S(2)}) collective-permute-start(f32[16,128]{1,0:T(8,128)S(1)} %add_add_fusion), channel_id=1, source_target_pairs={{0,6},{1,7},{2,4},{3,5},{4,2},{5,3},{6,0},{7,1},{8,14},{9,15},{10,... | collective-permute-start | bytes 24584 | tf_op jit(solution)/shard_map/ppermute | solution.py:745
  121.7 4.5 %collective-permute-start.11 = (f32[16,128]{1,0:T(8,128)S(1)}, f32[16,128]{1,0:T(8,128)S(1)}, u32[]{:S(2)}, u32[]{:S(2)}) collective-permute-start(f32[16,128]{1,0:T(8,128)S(1)} %add_add_fusion), channel_id=1, source_target_pairs={{0,4},{1,5},{2,6},{3,7},{4,0},{5,1},{6,2},{7,3},{8,12},{9,13},{10,... | collective-permute-start | bytes 24584 | tf_op jit(solution)/shard_map/ppermute | solution.py:745
  122.0 4.2 %collective-permute-start.10 = (f32[16,128]{1,0:T(8,128)S(1)}, f32[16,128]{1,0:T(8,128)S(1)}, u32[]{:S(2)}, u32[]{:S(2)}) collective-permute-start(f32[16,128]{1,0:T(8,128)S(1)} %add_add_fusion), channel_id=1, source_target_pairs={{0,2},{1,3},{2,0},{3,1},{4,6},{5,7},{6,4},{7,5},{8,10},{9,11},{10,... | collective-permute-start | bytes 24584 | tf_op jit(solution)/shard_map/ppermute | solution.py:745
  123.5 6.2 %collective-permute-start.9 = (bf16[2,64,768]{2,1,0:T(8,128)(2,1)S(1)}, bf16[2,64,768]{2,1,0:T(8,128)(2,1)S(1)}, u32[]{:S(2)}, u32[]{:S(2)}) collective-permute-start(bf16[2,64,768]{2,1,0:T(8,128)(2,1)S(1)} %bitcast.15), channel_id=1, source_target_pairs={{0,8},{8,0},{1,9},{9,1},{2,10},{10,2},{3,11},{11,3},{4,12},{12,4},... | collective-permute-start | bytes 589832 | tf_op jit(solution)/shard_map/ppermute | solution.py:722

commit v4 on v3

--- a/solution.py
+++ b/solution.py
@@ -769,7 +769,7 @@
     )
     back, late_pair = lax.optimization_barrier((back.astype(jnp.float16), pair))
     pair_normed, pair_inv = pair_units(late_pair)
-    back, _, pair_normed = lax.optimization_barrier((back, grad_bias, pair_normed))
+    back, grad_bias, pair_normed = lax.optimization_barrier((back, grad_bias, pair_normed))
     back = lax.all_to_all(back, ("row", "col"), 0, 0, tiled=True)
 
     pair_grad, part = None, 0.0

time: 131 us -> 126 us (0.962)
  waiting for transfers between devices: 37.8 us -> 33.2 us
    all_to_all x1, waiting for transfers between devices: 14.3 us -> 5.56 us  [body_heads(): lax.all_to_all(grad_bias.astype(jnp.float16), ('row', 'col'), 0, 0, tiled...]
    ppermute x4, waiting for transfers between devices: 7.21 us -> 11.7 us  [swap(): return lax.ppermute(block, axis, [(0, 1), (1, 0)])]
  transfers between devices with their start and end apart: 16 -> 16, of which waited for: 7 -> 7; matrix products, arithmetic and copies ran while one was open for 3% -> 3% of each run, Pallas kernels for 27% -> 28%
where the time goes in v4:
time: 126 us
  Pallas kernels  47.1 us (37%)
  waiting for transfers between devices  33.2 us (26%)
  starting transfers between devices  31.3 us (25%)
  local copies, waits for them, and re-layouts  6.98 us (6%)
  other arithmetic  6.17 us (5%)
    ppermute x4, waiting for transfers between devices, swap(): return lax.ppermute(block, axis, [(0, 1), (1, 0)])  11.7 us
    pallas_call x2, Pallas kernels, pair_backward(): pl.pallas_call(lambda *refs: pair_back_kernel(factor, *refs), out_shape=[...  11.5 us
    ppermute x8, starting transfers between devices, send(): return lax.ppermute(block, 'col', [(c, c ^ offset) for c in range(n_col)])  11.1 us
    all_to_all x1, waiting for transfers between devices, body_heads(): bias = lax.all_to_all(bias, ('row', 'col'), 0, 0, tiled=True)  10.6 us
    pallas_call x1, Pallas kernels, pair_bias(): pl.pallas_call(bias_kernel, out_shape=jax.ShapeDtypeStruct((H, tok_col, r...  9.77 us
    pallas_call x1, Pallas kernels, pair_units(): pl.pallas_call(norm_kernel, out_shape=[jax.ShapeDtypeStruct(shapes[0], jn...  8.77 us
    pallas_call x1, Pallas kernels, attention(): pl.pallas_call(attention_kernel, out_shape=[jax.ShapeDtypeStruct(back_sha...  7.66 us
    unnamed x26, local copies, waits for them, and re-layouts  6.95 us
  transfers between devices with their start and end apart: 16, of which 7 were waited for; matrix products, arithmetic and copies ran while one was open for 3% of the time, Pallas kernels for 28%

profile of v4, /device:TPU:0, one launch (start us, length us, event | category | flops | bytes accessed | tf_op | source)
XLA Modules:
  0.0 125.7 jit_solution(9903321020976928375)
XLA Ops:
  0.6 0.0 copy-start.1
  0.6 0.0 copy-start.6
  0.7 0.0 copy-start.7
  0.7 4.3 %token_messages.1 = (bf16[2,4,48,256]{3,2,1,0:T(8,128)(2,1)}, bf16[2,4,48,256]{3,2,1,0:T(8,128)(2,1)}, bf16[2,4,48,256]{3,2,1,0:T(8,128)(2,1)}, bf16[2,4,48,256]{3,2,1,0:T(8,128)(2,1)}) custom-call(s32[1]{0:T(128)} %bitcast.4.row_ref, s32[1]{0:T(128)} %bitcast.col_ref, bf16[4,64,768]{2,1,0:T(8,128)(2,1)} %tokens_ref.3, s32[1,64]{1,0:T(1,128)} %bitcast.27, ...), custom_call_target="tpu_custom_call" | custom-call | flops 4000000000 | bytes 4000000 | tf_op jit(solution)/shard_map/token_messages/pallas_call | solution.py:245
  5.0 3.0 %collective-permute-start = (bf16[2,4,48,256]{3,2,1,0:T(8,128)(2,1)}, bf16[2,4,48,256]{3,2,1,0:T(8,128)(2,1)S(1)}, u32[]{:S(2)}, u32[]{:S(2)}) collective-permute-start(bf16[2,4,48,256]{3,2,1,0:T(8,128)(2,1)} %get-tuple-element.42), channel_id=1, source_target_pairs={{0,2},{1,3},{2,0},{3,1},{4,6},{5,7},{6,4},{7,5},{8,10},{9,11},{10,... | collective-permute-start | bytes 589832 | tf_op jit(solution)/shard_map/ppermute | solution.py:745
  8.0 2.6 %collective-permute-start.1 = (bf16[2,4,48,256]{3,2,1,0:T(8,128)(2,1)}, bf16[2,4,48,256]{3,2,1,0:T(8,128)(2,1)S(1)}, u32[]{:S(2)}, u32[]{:S(2)}) collective-permute-start(bf16[2,4,48,256]{3,2,1,0:T(8,128)(2,1)} %get-tuple-element.43), channel_id=1, source_target_pairs={{0,4},{1,5},{2,6},{3,7},{4,0},{5,1},{6,2},{7,3},{8,12},{9,13},{10,... | collective-permute-start | bytes 589832 | tf_op jit(solution)/shard_map/ppermute | solution.py:745
  10.6 0.0 collective-permute-start.2
  10.6 0.0 copy-done.1
  10.6 0.0 copy-done.6
  10.6 0.0 copy-done.7
  10.6 9.8 %pair_bias.1 = f32[16,64,256]{2,1,0:T(8,128)S(1)} custom-call(bf16[2,128,64,128]{3,2,1,0:T(8,128)(2,1)S(1)} %bitcast.18, bf16[16,128]{1,0:T(8,128)(2,1)S(1)} %bitcast.19, s32[1,64]{1,0:T(1,128)S(1)} %bitcast.22), custom_call_target="tpu_custom_call" | custom-call | flops 6000000000 | bytes 5000000 | tf_op jit(solution)/shard_map/pair_bias/pallas_call | solution.py:384
  20.4 0.0 copy-start
  20.4 0.9 convert_element_type.27
  21.3 0.0 collective-permute-done.refs_1_
  21.3 4.1 %collective-permute-done.1.refs_2_ = bf16[2,4,48,256]{3,2,1,0:T(8,128)(2,1)S(1)} collective-permute-done((bf16[2,4,48,256]{3,2,1,0:T(8,128)(2,1)}, bf16[2,4,48,256]{3,2,1,0:T(8,128)(2,1)S(1)}, u32[]{:S(2)}, u32[]{:S(2)}) %collective-permute-start.1) | collective-permute-done | bytes 196640 | tf_op jit(solution)/shard_map/ppermute | solution.py:745
  25.4 0.0 collective-permute-done.2.refs_3_
  25.4 6.7 %all-to-all-start = ((f16[16,64,256]{2,1,0:T(8,128)(2,1)}), f16[16,64,256]{2,1,0:T(8,128)(2,1)S(1)}, u32[]{:S(2)}, u32[]{:S(2)}) async-start(f16[16,64,256]{2,1,0:T(8,128)(2,1)} %convert_element_type.27), calls=%async_computation | async-start | bytes 1048576 | tf_op jit(solution)/shard_map/all_to_all | solution.py:762
  32.0 0.0 copy-done
  32.1 0.1 pad_maximum_fusion
  32.2 0.5 collective-permute-start.3
  32.7 3.0 %own_rows.1 = (f32[768,128]{1,0:T(8,128)}, f32[768,128]{1,0:T(8,128)}, f32[8,128]{1,0:T(8,128)}) custom-call(s32[1]{0:T(128)} %bitcast.4.row_ref, bf16[4,64,768]{2,1,0:T(8,128)(2,1)} %tokens_ref.3, s32[1,64]{1,0:T(1,128)} %bitcast.28, bf16[32,768]{1,0:T(8,128)(2,1)} %table_ref.3, bf16[768,768]{1,0:T(8,128)(2,1)} %refs_7_.1, bf16[4,64,768]{2,1,0:T(8,128)(2,1)} %cot_ref.1), custom_call_target="tpu_custom_call" | custom-call | flops 3000000000 | bytes 3000000 | tf_op jit(solution)/shard_map/own_rows/pallas_call | solution.py:289
  35.7 0.0 collective-permute-done.3.refs_4_
  35.7 10.6 %all-to-all-done = f16[16,64,256]{2,1,0:T(8,128)(2,1)S(1)} async-done(((f16[16,64,256]{2,1,0:T(8,128)(2,1)}), f16[16,64,256]{2,1,0:T(8,128)(2,1)S(1)}, u32[]{:S(2)}, u32[]{:S(2)}) %all-to-all-start) | async-done | bytes 524320 | tf_op jit(solution)/shard_map/all_to_all | solution.py:762
  46.3 0.1 convert_element_type.28.refs_5_
  46.4 7.7 %attention.1 = (f32[16,200,128]{2,1,0:T(8,128)S(1)}, f32[16,72,256]{2,1,0:T(8,128)S(1)}) custom-call(s32[1]{0:T(128)} %bitcast.col_ref, bf16[2,4,48,256]{3,2,1,0:T(8,128)(2,1)S(1)} %copy-done, bf16[2,4,48,256]{3,2,1,0:T(8,128)(2,1)S(1)} %collective-permute-done.refs_1_, bf16[2,4,48,256]{3,2,1,0:T(8,128)(2,1)S(1)} %collective-permute-done.1.refs_2_, ...), custom_call_target="tpu_custom_call" | custom-call | flops 8000000000 | bytes 6000000 | tf_op jit(solution)/shard_map/attention/pallas_call | solution.py:538
  54.1 0.9 convert_element_type.30
  55.0 4.0 %all-to-all-start.1 = ((f16[16,72,256]{2,1,0:T(8,128)(2,1)}), f16[16,72,256]{2,1,0:T(8,128)(2,1)S(1)}, u32[]{:S(2)}, u32[]{:S(2)}) async-start(f16[16,72,256]{2,1,0:T(8,128)(2,1)} %convert_element_type.30), calls=%async_computation.1 | async-start | bytes 1179648 | tf_op jit(solution)/shard_map/all_to_all | solution.py:767
  59.0 1.1 convert_element_type.29
  60.1 8.8 %pair_units.1 = (bf16[32,256,512]{2,1,0:T(8,128)(2,1)}, f32[32,8,512]{2,1,0:T(8,128)}) custom-call(bf16[2,128,64,128]{3,2,1,0:T(8,128)(2,1)} %bitcast.17), custom_call_target="tpu_custom_call" | custom-call | flops 6000000000 | bytes 12000000 | tf_op jit(solution)/shard_map/pair_units/pallas_call | solution.py:414
  68.8 5.6 %all-to-all-done.1 = f16[16,72,256]{2,1,0:T(8,128)(2,1)S(1)} async-done(((f16[16,72,256]{2,1,0:T(8,128)(2,1)}), f16[16,72,256]{2,1,0:T(8,128)(2,1)S(1)}, u32[]{:S(2)}, u32[]{:S(2)}) %all-to-all-start.1) | async-done | bytes 589856 | tf_op jit(solution)/shard_map/all_to_all | solution.py:767
  74.4 0.2 slice_convert_fusion
  74.5 1.6 %collective-permute-start.5 = (f16[16,72,128]{2,1,0:T(8,128)(2,1)S(1)}, f16[16,72,128]{2,1,0:T(8,128)(2,1)S(1)}, u32[]{:S(2)}, u32[]{:S(2)}) collective-permute-start(f16[16,72,128]{2,1,0:T(8,128)(2,1)S(1)} %get-tuple-element.81), channel_id=1, source_target_pairs={{0,16},{16,0},{1,17},{17,1},{2,18},{18,2},{3,19},{19,3},{4,20},{20... | collective-permute-start | bytes 884744 | tf_op jit(solution)/shard_map/ppermute | solution.py:722
  76.1 4.3 %all-to-all-start.2 = ((f16[16,200,128]{2,1,0:T(8,128)(2,1)}), f16[16,200,128]{2,1,0:T(8,128)(2,1)}, u32[]{:S(2)}, u32[]{:S(2)}) async-start(f16[16,200,128]{2,1,0:T(8,128)(2,1)} %convert_element_type.29), calls=%async_computation.2 | async-start | bytes 1638400 | tf_op jit(solution)/shard_map/all_to_all | solution.py:773
  80.5 0.6 collective-permute-start.4
  81.0 3.4 %collective-permute-done.5 = f16[16,72,128]{2,1,0:T(8,128)(2,1)S(1)} collective-permute-done((f16[16,72,128]{2,1,0:T(8,128)(2,1)S(1)}, f16[16,72,128]{2,1,0:T(8,128)(2,1)S(1)}, u32[]{:S(2)}, u32[]{:S(2)}) %collective-permute-start.5) | collective-permute-done | bytes 294944 | tf_op jit(solution)/shard_map/ppermute | solution.py:722
  84.6 0.1 fusion.refs_2_
  84.7 5.9 %collective-permute-done.4 = f16[16,72,128]{2,1,0:T(8,128)(2,1)S(1)} collective-permute-done((f16[16,72,128]{2,1,0:T(8,128)(2,1)S(1)}, f16[16,72,128]{2,1,0:T(8,128)(2,1)S(1)}, u32[]{:S(2)}, u32[]{:S(2)}) %collective-permute-start.4) | collective-permute-done | bytes 294944 | tf_op jit(solution)/shard_map/ppermute | solution.py:722
  90.6 0.1 fusion.1.refs_2_
  90.7 3.4 %copy-done.8 = bf16[32,256,512]{2,1,0:T(8,128)(2,1)S(1)} copy-done((bf16[32,256,512]{2,1,0:T(8,128)(2,1)S(1)}, bf16[32,256,512]{2,1,0:T(8,128)(2,1)}, u32[]{:S(2)}) %copy-start.8) | copy-done | bytes 8388632
  94.1 5.7 %pair_backward.2 = (bf16[2,128,64,128]{3,2,1,0:T(8,128)(2,1)}, f32[16,128]{1,0:T(8,128)S(1)}) custom-call(bf16[32,256,512]{2,1,0:T(8,128)(2,1)S(1)} %copy-done.8, f32[32,8,512]{2,1,0:T(8,128)S(1)} %copy-done.9, f32[16,64,128]{2,1,0:T(8,128)S(1)} %fusion.refs_2_, bf16[16,128]{1,0:T(8,128)(2,1)S(1)} %bitcast.20), custom_call_target="tpu_custom_call" | custom-call | flops 6000000000 | bytes 100000 | tf_op jit(solution)/shard_map/pair_backward/pallas_call | solution.py:688
  99.8 5.7 %pair_backward.3 = (bf16[2,128,64,128]{3,2,1,0:T(8,128)(2,1)}, f32[16,128]{1,0:T(8,128)S(1)}) custom-call(bf16[32,256,512]{2,1,0:T(8,128)(2,1)S(1)} %copy-done.8, f32[32,8,512]{2,1,0:T(8,128)S(1)} %copy-done.9, f32[16,64,128]{2,1,0:T(8,128)S(1)} %fusion.1.refs_2_, bf16[16,128]{1,0:T(8,128)(2,1)S(1)} %bitcast.21, ...), custom_call_target="tpu_custom_call", output_to_operand_aliasing={{0}: (4, {})} | custom-call | flops 6000000000 | bytes 100000 | tf_op jit(solution)/shard_map/pair_backward/pallas_call | solution.py:688
  105.6 0.0 all-to-all-done.2
  105.6 1.1 collective-permute-start.8
  106.7 0.6 collective-permute-start.7
  107.2 0.5 collective-permute-start.6
  107.8 1.3 convert_element_type.35.refs_0_
  109.1 0.0 copy-start.4
  109.1 1.3 %copy-done.4 = bf16[768,768]{1,0:T(8,128)(2,1)S(1)} copy-done((bf16[768,768]{1,0:T(8,128)(2,1)S(1)}, bf16[768,768]{1,0:T(8,128)(2,1)}, u32[]{:S(2)}) %copy-start.4) | copy-done | bytes 1179672
  110.4 1.3 %copy-done.5 = bf16[768,768]{1,0:T(8,128)(2,1)S(1)} copy-done((bf16[768,768]{1,0:T(8,128)(2,1)S(1)}, bf16[768,768]{1,0:T(8,128)(2,1)}, u32[]{:S(2)}) %copy-start.5) | copy-done | bytes 1179672
  111.6 1.0 copy-done.11
  112.6 2.1 %token_back.1 = bf16[128,768]{1,0:T(8,128)(2,1)S(1)} custom-call(f32[16,200,128]{2,1,0:T(8,128)S(1)} %convert_element_type.35.refs_0_, f32[768,128]{1,0:T(8,128)S(1)} %copy-done.10, f32[768,128]{1,0:T(8,128)S(1)} %copy-done.11, f32[8,128]{1,0:T(8,128)S(1)} %copy-done.12, bf16[768,768]{1,0:T(8,128)(2,1)S(1)} %copy-done.2, bf16[768,768]{1,0:T(8,128)(2,1)S(1)} %copy-done.3, ...), custom_call_target="tpu_custom_call" | custom-call | flops 4000000000 | bytes 8000000 | tf_op jit(solution)/shard_map/token_back/pallas_call | solution.py:611
  114.7 0.0 collective-permute-done.8
  114.7 0.0 collective-permute-done.7
  114.7 0.0 collective-permute-done.6
  114.8 2.6 %collective-permute-start.12 = (f32[16,128]{1,0:T(8,128)S(1)}, f32[16,128]{1,0:T(8,128)S(1)}, u32[]{:S(2)}, u32[]{:S(2)}) collective-permute-start(f32[16,128]{1,0:T(8,128)S(1)} %add_add_fusion), channel_id=1, source_target_pairs={{0,6},{1,7},{2,4},{3,5},{4,2},{5,3},{6,0},{7,1},{8,14},{9,15},{10,... | collective-permute-start | bytes 24584 | tf_op jit(solution)/shard_map/ppermute | solution.py:745
  117.4 0.0 collective-permute-start.11
  117.4 1.8 %collective-permute-start.10 = (f32[16,128]{1,0:T(8,128)S(1)}, f32[16,128]{1,0:T(8,128)S(1)}, u32[]{:S(2)}, u32[]{:S(2)}) collective-permute-start(f32[16,128]{1,0:T(8,128)S(1)} %add_add_fusion), channel_id=1, source_target_pairs={{0,2},{1,3},{2,0},{3,1},{4,6},{5,7},{6,4},{7,5},{8,10},{9,11},{10,... | collective-permute-start | bytes 24584 | tf_op jit(solution)/shard_map/ppermute | solution.py:745
  119.2 1.5 %collective-permute-start.9 = (bf16[2,64,768]{2,1,0:T(8,128)(2,1)S(1)}, bf16[2,64,768]{2,1,0:T(8,128)(2,1)S(1)}, u32[]{:S(2)}, u32[]{:S(2)}) collective-permute-start(bf16[2,64,768]{2,1,0:T(8,128)(2,1)S(1)} %bitcast.15), channel_id=1, source_target_pairs={{0,8},{8,0},{1,9},{9,1},{2,10},{10,2},{3,11},{11,3},{4,12},{12,4},... | collective-permute-start | bytes 589832 | tf_op jit(solution)/shard_map/ppermute | solution.py:722
  120.7 0.0 collective-permute-done.12
  120.7 1.2 collective-permute-done.11
  122.0 0.0 collective-permute-done.10
  122.0 0.6 multiply_bitcast_fusion
  122.6 2.3 %collective-permute-done.9 = bf16[2,64,768]{2,1,0:T(8,128)(2,1)S(1)} collective-permute-done((bf16[2,64,768]{2,1,0:T(8,128)(2,1)S(1)}, bf16[2,64,768]{2,1,0:T(8,128)(2,1)S(1)}, u32[]{:S(2)}, u32[]{:S(2)}) %collective-permute-start.9) | collective-permute-done | bytes 196640 | tf_op jit(solution)/shard_map/ppermute | solution.py:722
  125.0 0.8 pad_maximum_fusion.1
  (25 shorter events, 0.3 us)
Async XLA Ops:
  0.6 10.0 %copy-start.1 = (bf16[256,64,128]{2,1,0:T(8,128)(2,1)S(1)}, bf16[256,64,128]{2,1,0:T(8,128)(2,1)}, u32[]{:S(2)}) copy-start(bf16[256,64,128]{2,1,0:T(8,128)(2,1)} %param.15) | copy-start | bytes 12582916
  0.6 10.0 %copy-start.6 = (bf16[128,16]{0,1:T(8,128)(2,1)S(1)}, bf16[128,16]{0,1:T(8,128)(2,1)}, u32[]{:S(2)}) copy-start(bf16[128,16]{0,1:T(8,128)(2,1)} %param.16) | copy-start | bytes 12292
  0.7 9.9 %copy-start.7 = (s32[64]{0:T(128)S(1)}, s32[64]{0:T(128)}, u32[]{:S(2)}) copy-start(s32[64]{0:T(128)} %param.14) | copy-start | bytes 772
  5.0 16.3 %collective-permute-start = (bf16[2,4,48,256]{3,2,1,0:T(8,128)(2,1)}, bf16[2,4,48,256]{3,2,1,0:T(8,128)(2,1)S(1)}, u32[]{:S(2)}, u32[]{:S(2)}) collective-permute-start(bf16[2,4,48,256]{3,2,1,0:T(8,128)(2,1)} %get-tuple-element.42), channel_id=1, source_target_pairs={{0,2},{1,3},{2,0},{3,1},{4,6},{5,7},{6,4},{7,5},{8,10},{9,11},{10,... | collective-permute-start | bytes 589832 | tf_op jit(solution)/shard_map/ppermute | solution.py:745
  8.0 17.4 %collective-permute-start.1 = (bf16[2,4,48,256]{3,2,1,0:T(8,128)(2,1)}, bf16[2,4,48,256]{3,2,1,0:T(8,128)(2,1)S(1)}, u32[]{:S(2)}, u32[]{:S(2)}) collective-permute-start(bf16[2,4,48,256]{3,2,1,0:T(8,128)(2,1)} %get-tuple-element.43), channel_id=1, source_target_pairs={{0,4},{1,5},{2,6},{3,7},{4,0},{5,1},{6,2},{7,3},{8,12},{9,13},{10,... | collective-permute-start | bytes 589832 | tf_op jit(solution)/shard_map/ppermute | solution.py:745
  10.6 14.8 %collective-permute-start.2 = (bf16[2,4,48,256]{3,2,1,0:T(8,128)(2,1)}, bf16[2,4,48,256]{3,2,1,0:T(8,128)(2,1)S(1)}, u32[]{:S(2)}, u32[]{:S(2)}) collective-permute-start(bf16[2,4,48,256]{3,2,1,0:T(8,128)(2,1)} %get-tuple-element.44), channel_id=1, source_target_pairs={{0,6},{1,7},{2,4},{3,5},{4,2},{5,3},{6,0},{7,1},{8,14},{9,15},{10,... | collective-permute-start | bytes 589832 | tf_op jit(solution)/shard_map/ppermute | solution.py:745
  20.4 11.7 %copy-start = (bf16[2,4,48,256]{3,2,1,0:T(8,128)(2,1)S(1)}, bf16[2,4,48,256]{3,2,1,0:T(8,128)(2,1)}, u32[]{:S(2)}) copy-start(bf16[2,4,48,256]{3,2,1,0:T(8,128)(2,1)} %get-tuple-element.45.refs_0_) | copy-start | bytes 589828
  25.4 20.9 %all-to-all-start = ((f16[16,64,256]{2,1,0:T(8,128)(2,1)}), f16[16,64,256]{2,1,0:T(8,128)(2,1)S(1)}, u32[]{:S(2)}, u32[]{:S(2)}) async-start(f16[16,64,256]{2,1,0:T(8,128)(2,1)} %convert_element_type.27), calls=%async_computation | async-start | bytes 1048576 | tf_op jit(solution)/shard_map/all_to_all | solution.py:762
  32.2 3.5 %collective-permute-start.3 = (bf16[4,4,48,256]{3,2,1,0:T(8,128)(2,1)S(1)}, bf16[4,4,48,256]{3,2,1,0:T(8,128)(2,1)S(1)}, u32[]{:S(2)}, u32[]{:S(2)}) collective-permute-start(bf16[4,4,48,256]{3,2,1,0:T(8,128)(2,1)S(1)} %pad_maximum_fusion), channel_id=1, source_target_pairs={{0,1},{1,0},{2,3},{3,2},{4,5},{5,4},{6,7},{7,6},{8,9},{9,8},{10,11... | collective-permute-start | bytes 1179656 | tf_op jit(solution)/shard_map/ppermute | solution.py:745
  55.0 19.4 %all-to-all-start.1 = ((f16[16,72,256]{2,1,0:T(8,128)(2,1)}), f16[16,72,256]{2,1,0:T(8,128)(2,1)S(1)}, u32[]{:S(2)}, u32[]{:S(2)}) async-start(f16[16,72,256]{2,1,0:T(8,128)(2,1)} %convert_element_type.30), calls=%async_computation.1 | async-start | bytes 1179648 | tf_op jit(solution)/shard_map/all_to_all | solution.py:767
  74.5 9.9 %collective-permute-start.5 = (f16[16,72,128]{2,1,0:T(8,128)(2,1)S(1)}, f16[16,72,128]{2,1,0:T(8,128)(2,1)S(1)}, u32[]{:S(2)}, u32[]{:S(2)}) collective-permute-start(f16[16,72,128]{2,1,0:T(8,128)(2,1)S(1)} %get-tuple-element.81), channel_id=1, source_target_pairs={{0,16},{16,0},{1,17},{17,1},{2,18},{18,2},{3,19},{19,3},{4,20},{20... | collective-permute-start | bytes 884744 | tf_op jit(solution)/shard_map/ppermute | solution.py:722
  76.1 29.4 %all-to-all-start.2 = ((f16[16,200,128]{2,1,0:T(8,128)(2,1)}), f16[16,200,128]{2,1,0:T(8,128)(2,1)}, u32[]{:S(2)}, u32[]{:S(2)}) async-start(f16[16,200,128]{2,1,0:T(8,128)(2,1)} %convert_element_type.29), calls=%async_computation.2 | async-start | bytes 1638400 | tf_op jit(solution)/shard_map/all_to_all | solution.py:773
  80.5 10.1 %collective-permute-start.4 = (f16[16,72,128]{2,1,0:T(8,128)(2,1)S(1)}, f16[16,72,128]{2,1,0:T(8,128)(2,1)S(1)}, u32[]{:S(2)}, u32[]{:S(2)}) collective-permute-start(f16[16,72,128]{2,1,0:T(8,128)(2,1)S(1)} %get-tuple-element.82), channel_id=1, source_target_pairs={{0,16},{16,0},{1,17},{17,1},{2,18},{18,2},{3,19},{19,3},{4,20},{20... | collective-permute-start | bytes 884744 | tf_op jit(solution)/shard_map/ppermute | solution.py:722
  84.6 6.1 %copy-start.9 = (f32[32,8,512]{2,1,0:T(8,128)S(1)}, f32[32,8,512]{2,1,0:T(8,128)}, u32[]{:S(2)}) copy-start(f32[32,8,512]{2,1,0:T(8,128)} %get-tuple-element.62.refs_1_) | copy-start | bytes 1572868
  90.7 3.4 %copy-start.8 = (bf16[32,256,512]{2,1,0:T(8,128)(2,1)S(1)}, bf16[32,256,512]{2,1,0:T(8,128)(2,1)}, u32[]{:S(2)}) copy-start(bf16[32,256,512]{2,1,0:T(8,128)(2,1)} %get-tuple-element.61.refs_0_) | copy-start | bytes 25165828
  99.8 9.2 %copy-start.10 = (f32[768,128]{1,0:T(8,128)S(1)}, f32[768,128]{1,0:T(8,128)}, u32[]{:S(2)}) copy-start(f32[768,128]{1,0:T(8,128)} %get-tuple-element.70.refs_1_) | copy-start | bytes 1179652
  105.6 3.5 %copy-start.2 = (bf16[768,768]{1,0:T(8,128)(2,1)S(1)}, bf16[768,768]{1,0:T(8,128)(2,1)}, u32[]{:S(2)}) copy-start(bf16[768,768]{1,0:T(8,128)(2,1)} %refs_4_.3) | copy-start | bytes 3538948
  105.6 3.5 %copy-start.3 = (bf16[768,768]{1,0:T(8,128)(2,1)S(1)}, bf16[768,768]{1,0:T(8,128)(2,1)}, u32[]{:S(2)}) copy-start(bf16[768,768]{1,0:T(8,128)(2,1)} %refs_5_.1) | copy-start | bytes 3538948
  105.6 3.5 %copy-start.12 = (f32[8,128]{1,0:T(8,128)S(1)}, f32[8,128]{1,0:T(8,128)}, u32[]{:S(2)}) copy-start(f32[8,128]{1,0:T(8,128)} %get-tuple-element.72.refs_3_) | copy-start | bytes 12292
  105.6 9.1 %collective-permute-start.8 = (f32[16,128]{1,0:T(8,128)S(1)}, f32[16,128]{1,0:T(8,128)S(1)}, u32[]{:S(2)}, u32[]{:S(2)}) collective-permute-start(f32[16,128]{1,0:T(8,128)S(1)} %add.29), channel_id=1, source_target_pairs={{0,9},{1,8},{2,11},{3,10},{4,13},{5,12},{6,15},{7,14},{8,1},{9,0},... | collective-permute-start | bytes 24584 | tf_op jit(solution)/shard_map/ppermute | solution.py:789
  106.7 8.1 %collective-permute-start.7 = (f32[16,128]{1,0:T(8,128)S(1)}, f32[16,128]{1,0:T(8,128)S(1)}, u32[]{:S(2)}, u32[]{:S(2)}) collective-permute-start(f32[16,128]{1,0:T(8,128)S(1)} %add.29), channel_id=1, source_target_pairs={{0,1},{1,0},{2,3},{3,2},{4,5},{5,4},{6,7},{7,6},{8,9},{9,8},{10,11... | collective-permute-start | bytes 24584 | tf_op jit(solution)/shard_map/ppermute | solution.py:745
  107.2 7.5 %collective-permute-start.6 = (f32[16,128]{1,0:T(8,128)S(1)}, f32[16,128]{1,0:T(8,128)S(1)}, u32[]{:S(2)}, u32[]{:S(2)}) collective-permute-start(f32[16,128]{1,0:T(8,128)S(1)} %add.29), channel_id=1, source_target_pairs={{0,8},{8,0},{1,9},{9,1},{2,10},{10,2},{3,11},{11,3},{4,12},{12,4},... | collective-permute-start | bytes 24584 | tf_op jit(solution)/shard_map/ppermute | solution.py:722
  109.1 1.3 %copy-start.4 = (bf16[768,768]{1,0:T(8,128)(2,1)S(1)}, bf16[768,768]{1,0:T(8,128)(2,1)}, u32[]{:S(2)}) copy-start(bf16[768,768]{1,0:T(8,128)(2,1)} %refs_6_.1) | copy-start | bytes 3538948
  110.4 1.3 %copy-start.5 = (bf16[768,768]{1,0:T(8,128)(2,1)S(1)}, bf16[768,768]{1,0:T(8,128)(2,1)}, u32[]{:S(2)}) copy-start(bf16[768,768]{1,0:T(8,128)(2,1)} %refs_7_.1) | copy-start | bytes 3538948
  111.6 1.0 copy-start.11
  114.8 5.9 %collective-permute-start.12 = (f32[16,128]{1,0:T(8,128)S(1)}, f32[16,128]{1,0:T(8,128)S(1)}, u32[]{:S(2)}, u32[]{:S(2)}) collective-permute-start(f32[16,128]{1,0:T(8,128)S(1)} %add_add_fusion), channel_id=1, source_target_pairs={{0,6},{1,7},{2,4},{3,5},{4,2},{5,3},{6,0},{7,1},{8,14},{9,15},{10,... | collective-permute-start | bytes 24584 | tf_op jit(solution)/shard_map/ppermute | solution.py:745
  117.4 4.5 %collective-permute-start.11 = (f32[16,128]{1,0:T(8,128)S(1)}, f32[16,128]{1,0:T(8,128)S(1)}, u32[]{:S(2)}, u32[]{:S(2)}) collective-permute-start(f32[16,128]{1,0:T(8,128)S(1)} %add_add_fusion), channel_id=1, source_target_pairs={{0,4},{1,5},{2,6},{3,7},{4,0},{5,1},{6,2},{7,3},{8,12},{9,13},{10,... | collective-permute-start | bytes 24584 | tf_op jit(solution)/shard_map/ppermute | solution.py:745
  117.4 4.5 %collective-permute-start.10 = (f32[16,128]{1,0:T(8,128)S(1)}, f32[16,128]{1,0:T(8,128)S(1)}, u32[]{:S(2)}, u32[]{:S(2)}) collective-permute-start(f32[16,128]{1,0:T(8,128)S(1)} %add_add_fusion), channel_id=1, source_target_pairs={{0,2},{1,3},{2,0},{3,1},{4,6},{5,7},{6,4},{7,5},{8,10},{9,11},{10,... | collective-permute-start | bytes 24584 | tf_op jit(solution)/shard_map/ppermute | solution.py:745
  119.2 5.7 %collective-permute-start.9 = (bf16[2,64,768]{2,1,0:T(8,128)(2,1)S(1)}, bf16[2,64,768]{2,1,0:T(8,128)(2,1)S(1)}, u32[]{:S(2)}, u32[]{:S(2)}) collective-permute-start(bf16[2,64,768]{2,1,0:T(8,128)(2,1)S(1)} %bitcast.15), channel_id=1, source_target_pairs={{0,8},{8,0},{1,9},{9,1},{2,10},{10,2},{3,11},{11,3},{4,12},{12,4},... | collective-permute-start | bytes 589832 | tf_op jit(solution)/shard_map/ppermute | solution.py:722

commit v5 on v2

--- a/solution.py
+++ b/solution.py
@@ -413,13 +413,13 @@
     return pl.pallas_call(
         norm_kernel,
         out_shape=[
-            jax.ShapeDtypeStruct(shapes[0], jnp.bfloat16),
-            jax.ShapeDtypeStruct(shapes[1], jnp.float32),
+            pltpu.VMEM(shapes[0], jnp.bfloat16),
+            pltpu.VMEM(shapes[1], jnp.float32),
         ],
         grid=(STEPS,),
         in_specs=[pair_spec(pair)],
         out_specs=[split_spec(shape) for shape in shapes],
-        compiler_params=params(56),
+        compiler_params=params(24),
         cost_estimate=pl.CostEstimate(
             flops=6_000_000_000, bytes_accessed=12_000_000, transcendentals=0
         ),
@@ -528,8 +528,8 @@
     return pl.pallas_call(
         attention_kernel,
         out_shape=[
-            jax.ShapeDtypeStruct(back_shape, jnp.float32),
-            jax.ShapeDtypeStruct(bias_shape, jnp.float32),
+            pltpu.VMEM(back_shape, jnp.float32),
+            pltpu.VMEM(bias_shape, jnp.float32),
         ],
         grid_spec=pltpu.PrefetchScalarGridSpec(
             num_scalar_prefetch=1,

time: 119 us -> 119 us (level)
  local copies, waits for them, and re-layouts: 3.47 us -> 9.74 us
  Pallas kernels: 48.7 us -> 45.6 us
  waiting for transfers between devices: 25.7 us -> 22.6 us
    unnamed x28 -> x34, local copies, waits for them, and re-layouts: 3.44 us -> 9.7 us
    all_to_all x1, waiting for transfers between devices: 5.53 us -> 2.36 us  [body_heads(): lax.all_to_all(grad_bias.astype(jnp.float16), ('row', 'col'), 0, 0, tiled...]
    pallas_call x2, Pallas kernels: 16.2 us -> 13.1 us  [the longest x1 7.42 us: attention(): pl.pallas_call(attention_kernel, out_shape=[pltpu.VMEM(back_shape, jnp.fl...]
  transfers between devices with their start and end apart: 16 -> 16, of which waited for: 6 -> 6; matrix products, arithmetic and copies ran while one was open for 5% -> 5% of each run, Pallas kernels for 31% -> 29%
where the time goes in v5:
time: 119 us
  Pallas kernels  45.6 us (38%)
  starting transfers between devices  32.4 us (27%)
  waiting for transfers between devices  22.6 us (19%)
  local copies, waits for them, and re-layouts  9.74 us (8%)
  other arithmetic  7.27 us (6%)
    ppermute x8, starting transfers between devices, send(): return lax.ppermute(block, 'col', [(c, c ^ offset) for c in range(n_col)])  10.8 us
    all_to_all x1, waiting for transfers between devices, body_heads(): bias = lax.all_to_all(bias, ('row', 'col'), 0, 0, tiled=True)  10.6 us
    pallas_call x1, Pallas kernels, pair_bias(): pl.pallas_call(bias_kernel, out_shape=jax.ShapeDtypeStruct((H, tok_col, r...  9.78 us
    unnamed x34, local copies, waits for them, and re-layouts  9.7 us
    pallas_call x1, Pallas kernels, pair_backward(): pl.pallas_call(lambda *refs: pair_back_kernel(factor, *refs), out_shape=j...  7.68 us
    pallas_call x1, Pallas kernels, attention(): pl.pallas_call(attention_kernel, out_shape=[pltpu.VMEM(back_shape, jnp.fl...  7.42 us
    all_to_all x1, starting transfers between devices, body_heads(): bias = lax.all_to_all(bias, ('row', 'col'), 0, 0, tiled=True)  6.67 us
    pallas_call x1, Pallas kernels, pair_units(): pl.pallas_call(norm_kernel, out_shape=[pltpu.VMEM(shapes[0], jnp.bfloat16...  5.68 us
  transfers between devices with their start and end apart: 16, of which 6 were waited for; matrix products, arithmetic and copies ran while one was open for 5% of the time, Pallas kernels for 29%

profile of v5, /device:TPU:0, one launch (start us, length us, event | category | flops | bytes accessed | tf_op | source)
XLA Modules:
  0.0 118.6 jit_solution(1780673999403472804)
XLA Ops:
  0.6 0.0 copy-start.1
  0.7 4.3 %token_messages.1 = (bf16[2,4,48,256]{3,2,1,0:T(8,128)(2,1)}, bf16[2,4,48,256]{3,2,1,0:T(8,128)(2,1)}, bf16[2,4,48,256]{3,2,1,0:T(8,128)(2,1)}, bf16[2,4,48,256]{3,2,1,0:T(8,128)(2,1)}) custom-call(s32[1]{0:T(128)} %bitcast.4.row_ref, s32[1]{0:T(128)} %bitcast.col_ref, bf16[4,64,768]{2,1,0:T(8,128)(2,1)} %tokens_ref.3, s32[1,64]{1,0:T(1,128)} %bitcast.27, ...), custom_call_target="tpu_custom_call" | custom-call | flops 4000000000 | bytes 4000000 | tf_op jit(solution)/shard_map/token_messages/pallas_call | solution.py:245
  5.0 3.0 %collective-permute-start = (bf16[2,4,48,256]{3,2,1,0:T(8,128)(2,1)}, bf16[2,4,48,256]{3,2,1,0:T(8,128)(2,1)S(1)}, u32[]{:S(2)}, u32[]{:S(2)}) collective-permute-start(bf16[2,4,48,256]{3,2,1,0:T(8,128)(2,1)} %get-tuple-element.41), channel_id=1, source_target_pairs={{0,2},{1,3},{2,0},{3,1},{4,6},{5,7},{6,4},{7,5},{8,10},{9,11},{10,... | collective-permute-start | bytes 589832 | tf_op jit(solution)/shard_map/ppermute | solution.py:750
  8.0 2.6 %collective-permute-start.1 = (bf16[2,4,48,256]{3,2,1,0:T(8,128)(2,1)}, bf16[2,4,48,256]{3,2,1,0:T(8,128)(2,1)S(1)}, u32[]{:S(2)}, u32[]{:S(2)}) collective-permute-start(bf16[2,4,48,256]{3,2,1,0:T(8,128)(2,1)} %get-tuple-element.42), channel_id=1, source_target_pairs={{0,4},{1,5},{2,6},{3,7},{4,0},{5,1},{6,2},{7,3},{8,12},{9,13},{10,... | collective-permute-start | bytes 589832 | tf_op jit(solution)/shard_map/ppermute | solution.py:750
  10.6 0.0 collective-permute-start.2
  10.6 0.0 copy-done.7
  10.6 0.0 copy-done.8
  10.6 9.8 %pair_bias.1 = f32[16,64,256]{2,1,0:T(8,128)S(1)} custom-call(bf16[2,128,64,128]{3,2,1,0:T(8,128)(2,1)S(1)} %bitcast.19, bf16[16,128]{1,0:T(8,128)(2,1)S(1)} %bitcast.21, s32[1,64]{1,0:T(1,128)S(1)} %bitcast.23), custom_call_target="tpu_custom_call" | custom-call | flops 6000000000 | bytes 5000000 | tf_op jit(solution)/shard_map/pair_bias/pallas_call | solution.py:383
  20.4 0.0 copy-start
  20.4 0.9 convert_element_type.21
  21.3 0.0 collective-permute-done.refs_1_
  21.3 4.0 %collective-permute-done.1.refs_2_ = bf16[2,4,48,256]{3,2,1,0:T(8,128)(2,1)S(1)} collective-permute-done((bf16[2,4,48,256]{3,2,1,0:T(8,128)(2,1)}, bf16[2,4,48,256]{3,2,1,0:T(8,128)(2,1)S(1)}, u32[]{:S(2)}, u32[]{:S(2)}) %collective-permute-start.1) | collective-permute-done | bytes 196640 | tf_op jit(solution)/shard_map/ppermute | solution.py:750
  25.4 0.0 collective-permute-done.2.refs_3_
  25.4 6.7 %all-to-all-start = ((f16[16,64,256]{2,1,0:T(8,128)(2,1)}), f16[16,64,256]{2,1,0:T(8,128)(2,1)S(1)}, u32[]{:S(2)}, u32[]{:S(2)}) async-start(f16[16,64,256]{2,1,0:T(8,128)(2,1)} %convert_element_type.21), calls=%async_computation | async-start | bytes 1048576 | tf_op jit(solution)/shard_map/all_to_all | solution.py:767
  32.1 0.1 pad_maximum_fusion
  32.2 0.5 collective-permute-start.3
  32.7 3.0 %own_rows.1 = (f32[768,128]{1,0:T(8,128)}, f32[768,128]{1,0:T(8,128)}, f32[8,128]{1,0:T(8,128)}) custom-call(s32[1]{0:T(128)} %bitcast.4.row_ref, bf16[4,64,768]{2,1,0:T(8,128)(2,1)} %tokens_ref.3, s32[1,64]{1,0:T(1,128)} %bitcast.28, bf16[32,768]{1,0:T(8,128)(2,1)} %table_ref.3, bf16[768,768]{1,0:T(8,128)(2,1)} %refs_7_.1, bf16[4,64,768]{2,1,0:T(8,128)(2,1)} %cot_ref.1), custom_call_target="tpu_custom_call" | custom-call | flops 3000000000 | bytes 3000000 | tf_op jit(solution)/shard_map/own_rows/pallas_call | solution.py:289
  35.7 0.0 collective-permute-done.3.refs_4_
  35.7 10.6 %all-to-all-done = f16[16,64,256]{2,1,0:T(8,128)(2,1)S(1)} async-done(((f16[16,64,256]{2,1,0:T(8,128)(2,1)}), f16[16,64,256]{2,1,0:T(8,128)(2,1)S(1)}, u32[]{:S(2)}, u32[]{:S(2)}) %all-to-all-start) | async-done | bytes 524320 | tf_op jit(solution)/shard_map/all_to_all | solution.py:767
  46.3 0.1 convert_element_type.22.refs_5_
  46.4 7.4 %attention.1 = (f32[16,200,128]{2,1,0:T(8,128)S(1)}, f32[16,72,256]{2,1,0:T(8,128)S(1)}) custom-call(s32[1]{0:T(128)} %bitcast.col_ref, bf16[2,4,48,256]{3,2,1,0:T(8,128)(2,1)S(1)} %copy-done, bf16[2,4,48,256]{3,2,1,0:T(8,128)(2,1)S(1)} %collective-permute-done.refs_1_, bf16[2,4,48,256]{3,2,1,0:T(8,128)(2,1)S(1)} %collective-permute-done.1.refs_2_, ...), custom_call_target="tpu_custom_call" | custom-call | flops 8000000000 | bytes 6000000 | tf_op jit(solution)/shard_map/attention/pallas_call | solution.py:528
  53.8 0.9 convert_element_type.24
  54.7 4.0 %all-to-all-start.1 = ((f16[16,72,256]{2,1,0:T(8,128)(2,1)}), f16[16,72,256]{2,1,0:T(8,128)(2,1)S(1)}, u32[]{:S(2)}, u32[]{:S(2)}) async-start(f16[16,72,256]{2,1,0:T(8,128)(2,1)} %convert_element_type.24), calls=%async_computation.1 | async-start | bytes 1179648 | tf_op jit(solution)/shard_map/all_to_all | solution.py:772
  58.7 1.1 convert_element_type.23
  59.8 2.2 %copy-done.2 = bf16[256,64,128]{2,1,0:T(8,128)(2,1)S(1)} copy-done((bf16[256,64,128]{2,1,0:T(8,128)(2,1)S(1)}, bf16[256,64,128]{2,1,0:T(8,128)(2,1)}, u32[]{:S(2)}) %copy-start.2) | copy-done | bytes 4194328
  62.0 5.7 %pair_units.1 = (bf16[32,256,512]{2,1,0:T(8,128)(2,1)S(1)}, f32[32,8,512]{2,1,0:T(8,128)S(1)}) custom-call(bf16[2,128,64,128]{3,2,1,0:T(8,128)(2,1)S(1)} %bitcast.20), custom_call_target="tpu_custom_call" | custom-call | flops 6000000000 | bytes 12000000 | tf_op jit(solution)/shard_map/pair_units/pallas_call | solution.py:413
  67.7 0.0 copy-start.9
  67.7 3.3 %copy-done.9 = bf16[32,256,512]{2,1,0:T(8,128)(2,1)} copy-done((bf16[32,256,512]{2,1,0:T(8,128)(2,1)}, bf16[32,256,512]{2,1,0:T(8,128)(2,1)S(1)}, u32[]{:S(2)}) %copy-start.9) | copy-done | bytes 8388632
  71.0 0.8 copy-done.13
  71.8 2.4 %all-to-all-done.1 = f16[16,72,256]{2,1,0:T(8,128)(2,1)S(1)} async-done(((f16[16,72,256]{2,1,0:T(8,128)(2,1)}), f16[16,72,256]{2,1,0:T(8,128)(2,1)S(1)}, u32[]{:S(2)}, u32[]{:S(2)}) %all-to-all-start.1) | async-done | bytes 589856 | tf_op jit(solution)/shard_map/all_to_all | solution.py:772
  74.1 0.1 convert_element_type.25
  74.3 1.6 %collective-permute-start.4 = (f16[16,72,256]{2,1,0:T(8,128)(2,1)S(1)}, f16[16,72,256]{2,1,0:T(8,128)(2,1)}, u32[]{:S(2)}, u32[]{:S(2)}) collective-permute-start(f16[16,72,256]{2,1,0:T(8,128)(2,1)S(1)} %all-to-all-done.1), channel_id=1, source_target_pairs={{0,16},{16,0},{1,17},{17,1},{2,18},{18,2},{3,19},{19,3},{4,20},{20... | collective-permute-start | bytes 1769480 | tf_op jit(solution)/shard_map/ppermute | solution.py:727
  75.9 0.1 slice_multiply_fusion.1.grads_ref
  76.0 4.3 %all-to-all-start.2 = ((f16[16,200,128]{2,1,0:T(8,128)(2,1)}), f16[16,200,128]{2,1,0:T(8,128)(2,1)}, u32[]{:S(2)}, u32[]{:S(2)}) async-start(f16[16,200,128]{2,1,0:T(8,128)(2,1)} %convert_element_type.23), calls=%async_computation.2 | async-start | bytes 1638400 | tf_op jit(solution)/shard_map/all_to_all | solution.py:778
  80.3 3.4 %copy-done.10 = bf16[32,256,512]{2,1,0:T(8,128)(2,1)S(1)} copy-done((bf16[32,256,512]{2,1,0:T(8,128)(2,1)S(1)}, bf16[32,256,512]{2,1,0:T(8,128)(2,1)}, u32[]{:S(2)}) %copy-start.10) | copy-done | bytes 8388632
  83.7 5.5 %pair_weight.1 = f32[16,128]{1,0:T(8,128)S(1)} custom-call(bf16[32,256,512]{2,1,0:T(8,128)(2,1)S(1)} %copy-done.10, f32[16,64,256]{2,1,0:T(8,128)S(1)} %slice_multiply_fusion.1.grads_ref), custom_call_target="tpu_custom_call" | custom-call | flops 5000000000 | bytes 100000 | tf_op jit(solution)/shard_map/pair_weight/pallas_call | solution.py:682
  89.2 1.8 %collective-permute-start.7 = (f32[16,128]{1,0:T(8,128)S(1)}, f32[16,128]{1,0:T(8,128)S(1)}, u32[]{:S(2)}, u32[]{:S(2)}) collective-permute-start(f32[16,128]{1,0:T(8,128)S(1)} %pair_weight.1), channel_id=1, source_target_pairs={{0,24},{8,16},{16,8},{24,0},{1,25},{9,17},{17,9},{25,1},{2,26},{10... | collective-permute-start | bytes 24584 | tf_op jit(solution)/shard_map/ppermute | solution.py:785
  91.0 0.2 collective-permute-start.6
  91.2 1.5 %collective-permute-start.5 = (f32[16,128]{1,0:T(8,128)S(1)}, f32[16,128]{1,0:T(8,128)S(1)}, u32[]{:S(2)}, u32[]{:S(2)}) collective-permute-start(f32[16,128]{1,0:T(8,128)S(1)} %pair_weight.1), channel_id=1, source_target_pairs={{0,16},{16,0},{1,17},{17,1},{2,18},{18,2},{3,19},{19,3},{4,20},{20... | collective-permute-start | bytes 24584 | tf_op jit(solution)/shard_map/ppermute | solution.py:727
  92.7 0.0 collective-permute-done.4
  92.7 1.1 convert_element_type.26
  94.0 0.0 collective-permute-done.7
  94.0 0.7 collective-permute-done.6
  94.7 0.2 collective-permute-done.5
  94.9 0.2 fusion.refs_2_
  95.0 0.4 collective-permute-start.10
  95.4 1.5 %collective-permute-start.9 = (f32[16,128]{1,0:T(8,128)S(1)}, f32[16,128]{1,0:T(8,128)S(1)}, u32[]{:S(2)}, u32[]{:S(2)}) collective-permute-start(f32[16,128]{1,0:T(8,128)S(1)} %add_add_fusion.1), channel_id=1, source_target_pairs={{0,2},{1,3},{2,0},{3,1},{4,6},{5,7},{6,4},{7,5},{8,10},{9,11},{10,... | collective-permute-start | bytes 24584 | tf_op jit(solution)/shard_map/ppermute | solution.py:750
  97.0 0.0 collective-permute-start.8
  97.1 7.7 %pair_backward.1 = bf16[2,128,64,128]{3,2,1,0:T(8,128)(2,1)} custom-call(bf16[32,256,512]{2,1,0:T(8,128)(2,1)S(1)} %copy-done.10, f32[32,8,512]{2,1,0:T(8,128)S(1)} %copy-done.14, f32[16,64,256]{2,1,0:T(8,128)S(1)} %fusion.refs_2_, bf16[16,128]{1,0:T(8,128)(2,1)S(1)} %bitcast.22), custom_call_target="tpu_custom_call" | custom-call | flops 8000000000 | bytes 100000 | tf_op jit(solution)/shard_map/pair_backward/pallas_call | solution.py:700
  104.7 0.0 collective-permute-done.10
  104.7 0.0 collective-permute-done.9
  104.7 0.0 collective-permute-done.8
  104.8 0.0 all-to-all-done.2
  104.8 0.0 copy-start.3
  104.8 0.0 copy-start.4
  104.8 0.0 copy-start.15
  104.8 2.7 %collective-permute-start.11 = (f32[16,128]{1,0:T(8,128)S(1)}, f32[16,128]{1,0:T(8,128)S(1)}, u32[]{:S(2)}, u32[]{:S(2)}) collective-permute-start(f32[16,128]{1,0:T(8,128)S(1)} %add_add_fusion), channel_id=1, source_target_pairs={{0,4},{1,5},{2,6},{3,7},{4,0},{5,1},{6,2},{7,3},{8,12},{9,13},{10,... | collective-permute-start | bytes 24584 | tf_op jit(solution)/shard_map/ppermute | solution.py:750
  107.5 1.3 %convert_element_type.27.refs_0_ = f32[16,200,128]{2,1,0:T(8,128)S(1)} convert(f16[16,200,128]{2,1,0:T(8,128)(2,1)} %all-to-all-done.2) | non-fusion elementwise | flops 409600 | bytes 2457600 | tf_op jit(solution)/shard_map/convert_element_type | solution.py:798
  108.8 2.1 %token_back.1 = bf16[128,768]{1,0:T(8,128)(2,1)S(1)} custom-call(f32[16,200,128]{2,1,0:T(8,128)S(1)} %convert_element_type.27.refs_0_, f32[768,128]{1,0:T(8,128)S(1)} %copy-done.11, f32[768,128]{1,0:T(8,128)S(1)} %copy-done.12, f32[8,128]{1,0:T(8,128)S(1)} %copy-done.15, bf16[768,768]{1,0:T(8,128)(2,1)S(1)} %copy-done.3, bf16[768,768]{1,0:T(8,128)(2,1)S(1)} %copy-done.4, ...), custom_call_target="tpu_custom_call" | custom-call | flops 4000000000 | bytes 8000000 | tf_op jit(solution)/shard_map/token_back/pallas_call | solution.py:601
  111.0 0.0 collective-permute-done.11
  111.0 1.6 %collective-permute-start.12 = (bf16[2,64,768]{2,1,0:T(8,128)(2,1)S(1)}, bf16[2,64,768]{2,1,0:T(8,128)(2,1)S(1)}, u32[]{:S(2)}, u32[]{:S(2)}) collective-permute-start(bf16[2,64,768]{2,1,0:T(8,128)(2,1)S(1)} %bitcast.17), channel_id=1, source_target_pairs={{0,8},{8,0},{1,9},{9,1},{2,10},{10,2},{3,11},{11,3},{4,12},{12,4},... | collective-permute-start | bytes 589832 | tf_op jit(solution)/shard_map/ppermute | solution.py:727
  112.6 0.6 multiply_bitcast_fusion
  113.2 4.6 %collective-permute-done.12 = bf16[2,64,768]{2,1,0:T(8,128)(2,1)S(1)} collective-permute-done((bf16[2,64,768]{2,1,0:T(8,128)(2,1)S(1)}, bf16[2,64,768]{2,1,0:T(8,128)(2,1)S(1)}, u32[]{:S(2)}, u32[]{:S(2)}) %collective-permute-start.12) | collective-permute-done | bytes 196640 | tf_op jit(solution)/shard_map/ppermute | solution.py:727
  117.8 0.8 pad_maximum_fusion.1
  (31 shorter events, 0.2 us)
Async XLA Ops:
  0.6 10.0 %copy-start.1 = (bf16[256,64,128]{2,1,0:T(8,128)(2,1)S(1)}, bf16[256,64,128]{2,1,0:T(8,128)(2,1)}, u32[]{:S(2)}) copy-start(bf16[256,64,128]{2,1,0:T(8,128)(2,1)} %param.15) | copy-start | bytes 12582916
  0.6 10.0 %copy-start.7 = (bf16[128,16]{0,1:T(8,128)(2,1)S(1)}, bf16[128,16]{0,1:T(8,128)(2,1)}, u32[]{:S(2)}) copy-start(bf16[128,16]{0,1:T(8,128)(2,1)} %param.16) | copy-start | bytes 12292
  0.7 9.9 %copy-start.8 = (s32[64]{0:T(128)S(1)}, s32[64]{0:T(128)}, u32[]{:S(2)}) copy-start(s32[64]{0:T(128)} %param.14) | copy-start | bytes 772
  5.0 16.3 %collective-permute-start = (bf16[2,4,48,256]{3,2,1,0:T(8,128)(2,1)}, bf16[2,4,48,256]{3,2,1,0:T(8,128)(2,1)S(1)}, u32[]{:S(2)}, u32[]{:S(2)}) collective-permute-start(bf16[2,4,48,256]{3,2,1,0:T(8,128)(2,1)} %get-tuple-element.41), channel_id=1, source_target_pairs={{0,2},{1,3},{2,0},{3,1},{4,6},{5,7},{6,4},{7,5},{8,10},{9,11},{10,... | collective-permute-start | bytes 589832 | tf_op jit(solution)/shard_map/ppermute | solution.py:750
  8.0 17.4 %collective-permute-start.1 = (bf16[2,4,48,256]{3,2,1,0:T(8,128)(2,1)}, bf16[2,4,48,256]{3,2,1,0:T(8,128)(2,1)S(1)}, u32[]{:S(2)}, u32[]{:S(2)}) collective-permute-start(bf16[2,4,48,256]{3,2,1,0:T(8,128)(2,1)} %get-tuple-element.42), channel_id=1, source_target_pairs={{0,4},{1,5},{2,6},{3,7},{4,0},{5,1},{6,2},{7,3},{8,12},{9,13},{10,... | collective-permute-start | bytes 589832 | tf_op jit(solution)/shard_map/ppermute | solution.py:750
  10.6 14.8 %collective-permute-start.2 = (bf16[2,4,48,256]{3,2,1,0:T(8,128)(2,1)}, bf16[2,4,48,256]{3,2,1,0:T(8,128)(2,1)S(1)}, u32[]{:S(2)}, u32[]{:S(2)}) collective-permute-start(bf16[2,4,48,256]{3,2,1,0:T(8,128)(2,1)} %get-tuple-element.43), channel_id=1, source_target_pairs={{0,6},{1,7},{2,4},{3,5},{4,2},{5,3},{6,0},{7,1},{8,14},{9,15},{10,... | collective-permute-start | bytes 589832 | tf_op jit(solution)/shard_map/ppermute | solution.py:750
  20.4 11.6 %copy-start = (bf16[2,4,48,256]{3,2,1,0:T(8,128)(2,1)S(1)}, bf16[2,4,48,256]{3,2,1,0:T(8,128)(2,1)}, u32[]{:S(2)}) copy-start(bf16[2,4,48,256]{3,2,1,0:T(8,128)(2,1)} %get-tuple-element.44.refs_0_) | copy-start | bytes 589828
  25.4 20.9 %all-to-all-start = ((f16[16,64,256]{2,1,0:T(8,128)(2,1)}), f16[16,64,256]{2,1,0:T(8,128)(2,1)S(1)}, u32[]{:S(2)}, u32[]{:S(2)}) async-start(f16[16,64,256]{2,1,0:T(8,128)(2,1)} %convert_element_type.21), calls=%async_computation | async-start | bytes 1048576 | tf_op jit(solution)/shard_map/all_to_all | solution.py:767
  32.2 3.5 %collective-permute-start.3 = (bf16[4,4,48,256]{3,2,1,0:T(8,128)(2,1)S(1)}, bf16[4,4,48,256]{3,2,1,0:T(8,128)(2,1)S(1)}, u32[]{:S(2)}, u32[]{:S(2)}) collective-permute-start(bf16[4,4,48,256]{3,2,1,0:T(8,128)(2,1)S(1)} %pad_maximum_fusion), channel_id=1, source_target_pairs={{0,1},{1,0},{2,3},{3,2},{4,5},{5,4},{6,7},{7,6},{8,9},{9,8},{10,11... | collective-permute-start | bytes 1179656 | tf_op jit(solution)/shard_map/ppermute | solution.py:750
  54.7 19.4 %all-to-all-start.1 = ((f16[16,72,256]{2,1,0:T(8,128)(2,1)}), f16[16,72,256]{2,1,0:T(8,128)(2,1)S(1)}, u32[]{:S(2)}, u32[]{:S(2)}) async-start(f16[16,72,256]{2,1,0:T(8,128)(2,1)} %convert_element_type.24), calls=%async_computation.1 | async-start | bytes 1179648 | tf_op jit(solution)/shard_map/all_to_all | solution.py:772
  59.8 2.2 %copy-start.2 = (bf16[256,64,128]{2,1,0:T(8,128)(2,1)S(1)}, bf16[256,64,128]{2,1,0:T(8,128)(2,1)}, u32[]{:S(2)}) copy-start(bf16[256,64,128]{2,1,0:T(8,128)(2,1)} %param.15) | copy-start | bytes 12582916
  67.7 3.3 %copy-start.9 = (bf16[32,256,512]{2,1,0:T(8,128)(2,1)}, bf16[32,256,512]{2,1,0:T(8,128)(2,1)S(1)}, u32[]{:S(2)}) copy-start(bf16[32,256,512]{2,1,0:T(8,128)(2,1)S(1)} %get-tuple-element.60.normed_ref.refs_0_) | copy-start | bytes 25165828
  71.0 0.8 copy-start.13
  74.3 18.5 %collective-permute-start.4 = (f16[16,72,256]{2,1,0:T(8,128)(2,1)S(1)}, f16[16,72,256]{2,1,0:T(8,128)(2,1)}, u32[]{:S(2)}, u32[]{:S(2)}) collective-permute-start(f16[16,72,256]{2,1,0:T(8,128)(2,1)S(1)} %all-to-all-done.1), channel_id=1, source_target_pairs={{0,16},{16,0},{1,17},{17,1},{2,18},{18,2},{3,19},{19,3},{4,20},{20... | collective-permute-start | bytes 1769480 | tf_op jit(solution)/shard_map/ppermute | solution.py:727
  76.0 28.8 %all-to-all-start.2 = ((f16[16,200,128]{2,1,0:T(8,128)(2,1)}), f16[16,200,128]{2,1,0:T(8,128)(2,1)}, u32[]{:S(2)}, u32[]{:S(2)}) async-start(f16[16,200,128]{2,1,0:T(8,128)(2,1)} %convert_element_type.23), calls=%async_computation.2 | async-start | bytes 1638400 | tf_op jit(solution)/shard_map/all_to_all | solution.py:778
  80.3 3.4 %copy-start.10 = (bf16[32,256,512]{2,1,0:T(8,128)(2,1)S(1)}, bf16[32,256,512]{2,1,0:T(8,128)(2,1)}, u32[]{:S(2)}) copy-start(bf16[32,256,512]{2,1,0:T(8,128)(2,1)} %copy-done.9) | copy-start | bytes 25165828
  89.2 4.8 %collective-permute-start.7 = (f32[16,128]{1,0:T(8,128)S(1)}, f32[16,128]{1,0:T(8,128)S(1)}, u32[]{:S(2)}, u32[]{:S(2)}) collective-permute-start(f32[16,128]{1,0:T(8,128)S(1)} %pair_weight.1), channel_id=1, source_target_pairs={{0,24},{8,16},{16,8},{24,0},{1,25},{9,17},{17,9},{25,1},{2,26},{10... | collective-permute-start | bytes 24584 | tf_op jit(solution)/shard_map/ppermute | solution.py:785
  91.0 3.7 %collective-permute-start.6 = (f32[16,128]{1,0:T(8,128)S(1)}, f32[16,128]{1,0:T(8,128)S(1)}, u32[]{:S(2)}, u32[]{:S(2)}) collective-permute-start(f32[16,128]{1,0:T(8,128)S(1)} %pair_weight.1), channel_id=1, source_target_pairs={{0,8},{8,0},{1,9},{9,1},{2,10},{10,2},{3,11},{11,3},{4,12},{12,4},... | collective-permute-start | bytes 24584 | tf_op jit(solution)/shard_map/ppermute | solution.py:727
  91.2 3.7 %collective-permute-start.5 = (f32[16,128]{1,0:T(8,128)S(1)}, f32[16,128]{1,0:T(8,128)S(1)}, u32[]{:S(2)}, u32[]{:S(2)}) collective-permute-start(f32[16,128]{1,0:T(8,128)S(1)} %pair_weight.1), channel_id=1, source_target_pairs={{0,16},{16,0},{1,17},{17,1},{2,18},{18,2},{3,19},{19,3},{4,20},{20... | collective-permute-start | bytes 24584 | tf_op jit(solution)/shard_map/ppermute | solution.py:727
  94.9 2.2 %copy-start.14 = (f32[32,8,512]{2,1,0:T(8,128)S(1)}, f32[32,8,512]{2,1,0:T(8,128)}, u32[]{:S(2)}) copy-start(f32[32,8,512]{2,1,0:T(8,128)} %copy-done.13) | copy-start | bytes 1572868
  95.0 9.7 %collective-permute-start.10 = (f32[16,128]{1,0:T(8,128)S(1)}, f32[16,128]{1,0:T(8,128)S(1)}, u32[]{:S(2)}, u32[]{:S(2)}) collective-permute-start(f32[16,128]{1,0:T(8,128)S(1)} %add_add_fusion.1), channel_id=1, source_target_pairs={{0,3},{1,2},{2,1},{3,0},{4,7},{5,6},{6,5},{7,4},{8,11},{9,10},{10,... | collective-permute-start | bytes 24584 | tf_op jit(solution)/shard_map/ppermute | solution.py:750
  95.4 9.3 %collective-permute-start.9 = (f32[16,128]{1,0:T(8,128)S(1)}, f32[16,128]{1,0:T(8,128)S(1)}, u32[]{:S(2)}, u32[]{:S(2)}) collective-permute-start(f32[16,128]{1,0:T(8,128)S(1)} %add_add_fusion.1), channel_id=1, source_target_pairs={{0,2},{1,3},{2,0},{3,1},{4,6},{5,7},{6,4},{7,5},{8,10},{9,11},{10,... | collective-permute-start | bytes 24584 | tf_op jit(solution)/shard_map/ppermute | solution.py:750
  97.0 7.8 %collective-permute-start.8 = (f32[16,128]{1,0:T(8,128)S(1)}, f32[16,128]{1,0:T(8,128)S(1)}, u32[]{:S(2)}, u32[]{:S(2)}) collective-permute-start(f32[16,128]{1,0:T(8,128)S(1)} %add_add_fusion.1), channel_id=1, source_target_pairs={{0,1},{1,0},{2,3},{3,2},{4,5},{5,4},{6,7},{7,6},{8,9},{9,8},{10,11... | collective-permute-start | bytes 24584 | tf_op jit(solution)/shard_map/ppermute | solution.py:750
  97.0 11.7 %copy-start.5 = (bf16[768,768]{1,0:T(8,128)(2,1)S(1)}, bf16[768,768]{1,0:T(8,128)(2,1)}, u32[]{:S(2)}) copy-start(bf16[768,768]{1,0:T(8,128)(2,1)} %refs_6_.1) | copy-start | bytes 3538948
  97.0 11.7 %copy-start.6 = (bf16[768,768]{1,0:T(8,128)(2,1)S(1)}, bf16[768,768]{1,0:T(8,128)(2,1)}, u32[]{:S(2)}) copy-start(bf16[768,768]{1,0:T(8,128)(2,1)} %refs_7_.1) | copy-start | bytes 3538948
  97.0 11.8 %copy-start.11 = (f32[768,128]{1,0:T(8,128)S(1)}, f32[768,128]{1,0:T(8,128)}, u32[]{:S(2)}) copy-start(f32[768,128]{1,0:T(8,128)} %get-tuple-element.68.refs_1_) | copy-start | bytes 1179652
  97.0 11.8 %copy-start.12 = (f32[768,128]{1,0:T(8,128)S(1)}, f32[768,128]{1,0:T(8,128)}, u32[]{:S(2)}) copy-start(f32[768,128]{1,0:T(8,128)} %get-tuple-element.69.refs_2_) | copy-start | bytes 1179652
  104.8 4.0 %copy-start.3 = (bf16[768,768]{1,0:T(8,128)(2,1)S(1)}, bf16[768,768]{1,0:T(8,128)(2,1)}, u32[]{:S(2)}) copy-start(bf16[768,768]{1,0:T(8,128)(2,1)} %refs_4_.3) | copy-start | bytes 3538948
  104.8 4.0 %copy-start.4 = (bf16[768,768]{1,0:T(8,128)(2,1)S(1)}, bf16[768,768]{1,0:T(8,128)(2,1)}, u32[]{:S(2)}) copy-start(bf16[768,768]{1,0:T(8,128)(2,1)} %refs_5_.1) | copy-start | bytes 3538948
  104.8 4.0 %copy-start.15 = (f32[8,128]{1,0:T(8,128)S(1)}, f32[8,128]{1,0:T(8,128)}, u32[]{:S(2)}) copy-start(f32[8,128]{1,0:T(8,128)} %get-tuple-element.70.refs_3_) | copy-start | bytes 12292
  104.8 6.2 %collective-permute-start.11 = (f32[16,128]{1,0:T(8,128)S(1)}, f32[16,128]{1,0:T(8,128)S(1)}, u32[]{:S(2)}, u32[]{:S(2)}) collective-permute-start(f32[16,128]{1,0:T(8,128)S(1)} %add_add_fusion), channel_id=1, source_target_pairs={{0,4},{1,5},{2,6},{3,7},{4,0},{5,1},{6,2},{7,3},{8,12},{9,13},{10,... | collective-permute-start | bytes 24584 | tf_op jit(solution)/shard_map/ppermute | solution.py:750
  111.0 6.8 %collective-permute-start.12 = (bf16[2,64,768]{2,1,0:T(8,128)(2,1)S(1)}, bf16[2,64,768]{2,1,0:T(8,128)(2,1)S(1)}, u32[]{:S(2)}, u32[]{:S(2)}) collective-permute-start(bf16[2,64,768]{2,1,0:T(8,128)(2,1)S(1)} %bitcast.17), channel_id=1, source_target_pairs={{0,8},{8,0},{1,9},{9,1},{2,10},{10,2},{3,11},{11,3},{4,12},{12,4},... | collective-permute-start | bytes 589832 | tf_op jit(solution)/shard_map/ppermute | solution.py:727

commit v6 on v2

--- a/solution.py
+++ b/solution.py
@@ -318,6 +318,7 @@
 
 
 MANY = 4
+PARTS = 2
 
 
 def pair_columns(pair_ref, k, many):
@@ -510,8 +511,17 @@
 
     @pl.when(step == pl.num_programs(0) - 1)
     def _():
+        piece = row_count // 2 // PARTS
         for head in range(n_row * n_col):
             sums = sum_ref[head]
+            sums = jnp.concatenate(
+                [
+                    sums[:, (p * PARTS + n) * piece : (p * PARTS + n + 1) * piece]
+                    for n in range(PARTS)
+                    for p in range(2)
+                ],
+                axis=1,
+            )
             shift = shift_of(jnp.max(jnp.abs(sums), axis=0, keepdims=True))
             grad_bias_ref[head, :tok_col, :] = sums * jnp.exp2(shift)
             grad_bias_ref[head, tok_col:, :] = jnp.broadcast_to(shift, (8, row_count))
@@ -610,7 +620,7 @@
             pltpu.VMEM((D, count), jnp.bfloat16),
             pltpu.VMEM((D, count), jnp.float32),
         ],
-        compiler_params=params(40),
+        compiler_params=params(24),
         cost_estimate=pl.CostEstimate(
             flops=4_000_000_000, bytes_accessed=8_000_000, transcendentals=0
         ),
@@ -632,14 +642,22 @@
     return jnp.concatenate(halves(jnp.concatenate(grads, axis=1)), axis=0)
 
 
-def pair_weight_kernel(normed_ref, grads_ref, part_ref, flat_ref):
+def pair_weight_kernel(normed_ref, *refs):
+    pieces, (part_ref, flat_ref) = refs[:-2], refs[-2:]
     chunks, width, _ = normed_ref.shape
-    base = pl.program_id(0) * chunks
-
-    @pl.when(pl.program_id(0) == 0)
+    number = pl.program_id(0)
+    steps = STEPS // len(pieces)
+    base = lax.rem(number, steps) * chunks
+
+    @pl.when(number == 0)
     def _():
         part_ref[...] = jnp.zeros_like(part_ref)
-        flatten(grads_ref, flat_ref)
+
+    for n, piece in enumerate(pieces):
+
+        @pl.when(number == n * steps)
+        def _():
+            flatten(piece, flat_ref)
 
     def step(n, carry):
         return carry + matmul_nt(normed_ref[n], flat_columns(flat_ref, (base + n) * MANY, MANY))
@@ -649,7 +667,8 @@
     part_ref[...] += (parts[: width // 2] + parts[width // 2 :]).T
 
 
-def pair_back_kernel(factor, normed_ref, inv_ref, grads_ref, weight_ref, out_ref, flat_ref):
+def pair_back_kernel(factor, normed_ref, inv_ref, grads_ref, weight_ref, *refs):
+    out_ref, flat_ref = refs[-2:]
     _, count, length, width = out_ref.shape
     weight = weight_ref[...].astype(jnp.float32)
     weight = halves(weight - jnp.mean(weight, axis=1, keepdims=True))
@@ -676,46 +695,57 @@
     lax.fori_loop(0, count // MANY, step, 0, unroll=2)
 
 
-def pair_weight(normed, grads):
-    heads, length, rows = grads.shape
+def pair_weight(normed, pieces):
+    _, length, rows = pieces[0].shape
     part_shape = (H, normed.shape[1] // 2)
     return pl.pallas_call(
         pair_weight_kernel,
         out_shape=jax.ShapeDtypeStruct(part_shape, jnp.float32),
         grid=(STEPS,),
-        in_specs=[split_spec(normed.shape), whole_spec(grads.shape)],
+        in_specs=[split_spec(normed.shape)] + [whole_spec(piece.shape) for piece in pieces],
         out_specs=whole_spec(part_shape),
         scratch_shapes=[pltpu.VMEM((H * rows // 2, 2 * length), jnp.float32)],
         compiler_params=params(24),
         cost_estimate=pl.CostEstimate(
-            flops=5_000_000_000, bytes_accessed=100_000, transcendentals=0
+            flops=1_000_000, bytes_accessed=100_000, transcendentals=0
         ),
         name="pair_weight",
-    )(normed, grads)
-
-
-def pair_backward(shape, normed, inv_std, grads, weight_t, factor):
+    )(normed, *pieces)
+
+
+def pair_backward(number, so_far, shape, normed, inv_std, grads, weight_t, factor):
     row_count, tok_col, width = shape
     whole = row_count // 2
-    pair_grad = pl.pallas_call(
+    steps = STEPS // PARTS
+    first = number * steps
+
+    def split(shape):
+        block = (shape[0] // STEPS,) + tuple(shape[1:])
+        return pl.BlockSpec(block, lambda i: (i + first,) + (0,) * (len(shape) - 1))
+
+    previous = [] if so_far is None else [so_far]
+    return pl.pallas_call(
         lambda *refs: pair_back_kernel(factor, *refs),
         out_shape=jax.ShapeDtypeStruct((2, whole, tok_col, width), jnp.bfloat16),
-        grid=(STEPS,),
+        grid=(steps,),
         in_specs=[
-            split_spec(normed.shape),
-            split_spec(inv_std.shape),
+            split(normed.shape),
+            split(inv_std.shape),
             whole_spec(grads.shape),
             whole_spec(weight_t.shape),
-        ],
-        out_specs=pl.BlockSpec((2, whole // STEPS, tok_col, width), lambda i: (0, i, 0, 0)),
-        scratch_shapes=[pltpu.VMEM((H * whole, 2 * tok_col), jnp.float32)],
+        ]
+        + [pl.BlockSpec(memory_space=pl.ANY)] * len(previous),
+        out_specs=pl.BlockSpec(
+            (2, whole // STEPS, tok_col, width), lambda i: (0, i + first, 0, 0)
+        ),
+        scratch_shapes=[pltpu.VMEM((H * whole // PARTS, 2 * tok_col), jnp.float32)],
+        input_output_aliases={4: 0} if previous else {},
         compiler_params=params(24),
         cost_estimate=pl.CostEstimate(
-            flops=8_000_000_000, bytes_accessed=100_000, transcendentals=0
+            flops=1_000_000, bytes_accessed=100_000, transcendentals=0
         ),
         name="pair_backward",
-    )(normed, inv_std, grads, weight_t)
-    return pair_grad.reshape(shape)
+    )(normed, inv_std, grads, weight_t, *previous)
 
 
 def unscaled(block, rows):
@@ -778,28 +808,36 @@
     back = lax.all_to_all(back, ("row", "col"), 0, 0, tiled=True)
 
     other_bias = swap(grad_bias, "samp")
-    own_bias = unscaled(grad_bias, tok_col)
-    part = pair_weight(pair_normed, own_bias)
+    own_pieces = [unscaled(piece, tok_col) for piece in jnp.split(grad_bias, PARTS, axis=2)]
+    part = pair_weight(pair_normed, own_pieces)
     samp_part = swap(part, "samp")
     row_part = swap(part, "row")
     both_part = lax.ppermute(part, ("samp", "row"), [(n, 3 - n) for n in range(4)])
     other_bias, part = lax.optimization_barrier((other_bias, part))
-    grads = own_bias + unscaled(other_bias, tok_col)
+    pieces = [
+        mine + unscaled(piece, tok_col)
+        for mine, piece in zip(own_pieces, jnp.split(other_bias, PARTS, axis=2))
+    ]
     part = (part + samp_part) + (row_part + both_part)
-    grads, part = lax.optimization_barrier((grads, part))
+    pieces, part = lax.optimization_barrier((pieces, part))
     sums = (send(part, 1), send(part, 2), send(part, 3))
-    pair_grad = pair_backward(
-        pair.shape, pair_normed, pair_inv, grads, weight_t, total_tokens / samples
-    )
-
-    pair_grad, back, sums = lax.optimization_barrier((pair_grad, back, sums))
-    part = (part + sums[0]) + (sums[1] + sums[2])
-    last = send(part, 4)
-    token_half = token_back(back.astype(jnp.float32), *own, weights)
-    token_half, last = lax.optimization_barrier((token_half, last))
+    pair_grad = None
+    for n, piece in enumerate(pieces):
+        pair_grad = pair_backward(
+            n, pair_grad, pair.shape, pair_normed, pair_inv, piece, weight_t,
+            total_tokens / samples,
+        )
+        if n == 0:
+            pair_grad, back, sums = lax.optimization_barrier((pair_grad, back, sums))
+            part = (part + sums[0]) + (sums[1] + sums[2])
+            last = send(part, 4)
+            token_half = token_back(back.astype(jnp.float32), *own, weights)
+            token_half = token_half.reshape(half, tok_col, D)
+            pair_grad, token_half = lax.optimization_barrier((pair_grad, token_half))
+            other_half = swap(token_half, "row")
+    pair_grad, other_half, last = lax.optimization_barrier((pair_grad, other_half, last))
+    pair_grad = pair_grad.reshape(pair.shape)
     part = part + last
-    token_half = token_half.reshape(half, tok_col, D)
-    other_half = swap(token_half, "row")
     first = row_index == 0
     token_grad = jnp.concatenate(
         [jnp.where(first, token_half, other_half), jnp.where(first, other_half, token_half)],

time: 119 us -> 125 us (1.050)
  local copies, waits for them, and re-layouts: 3.47 us -> 10.9 us
  waiting for transfers between devices: 25.7 us -> 22.4 us
  Pallas kernels: 48.7 us -> 51.1 us
    unnamed x28 -> x30, local copies, waits for them, and re-layouts: 3.44 us -> 10.9 us
    ppermute x4, waiting for transfers between devices: 5.53 us -> 1.05 us  [swap(): return lax.ppermute(block, axis, [(0, 1), (1, 0)])]
    pallas_call x1 -> x2, Pallas kernels: 7.68 us -> 9.29 us  [pair_backward(): pl.pallas_call(lambda *refs: pair_back_kernel(factor, *refs), out_shape=j...]
  transfers between devices with their start and end apart: 16 -> 16, of which waited for: 6 -> 6; matrix products, arithmetic and copies ran while one was open for 5% -> 2% of each run, Pallas kernels for 31% -> 30%
where the time goes in v6:
time: 125 us; the launch traced here: 124 us
  Pallas kernels  51.1 us (41%)
  starting transfers between devices  32.3 us (26%)
  waiting for transfers between devices  22.4 us (18%)
  local copies, waits for them, and re-layouts  10.9 us (9%)
  other arithmetic  6.31 us (5%)
    unnamed x30, local copies, waits for them, and re-layouts  10.9 us
    all_to_all x1, waiting for transfers between devices, body_heads(): bias = lax.all_to_all(bias, ('row', 'col'), 0, 0, tiled=True)  10.6 us
    ppermute x8, starting transfers between devices, send(): return lax.ppermute(block, 'col', [(c, c ^ offset) for c in range(n_col)])  10.4 us
    pallas_call x1, Pallas kernels, pair_bias(): pl.pallas_call(bias_kernel, out_shape=jax.ShapeDtypeStruct((H, tok_col, r...  9.77 us
    pallas_call x2, Pallas kernels, pair_backward(): pl.pallas_call(lambda *refs: pair_back_kernel(factor, *refs), out_shape=j...  9.29 us
    pallas_call x1, Pallas kernels, pair_units(): pl.pallas_call(norm_kernel, out_shape=[jax.ShapeDtypeStruct(shapes[0], jn...  8.81 us
    pallas_call x1, Pallas kernels, attention(): pl.pallas_call(attention_kernel, out_shape=[jax.ShapeDtypeStruct(back_sha...  7.67 us
    all_to_all x1, starting transfers between devices, body_heads(): bias = lax.all_to_all(bias, ('row', 'col'), 0, 0, tiled=True)  6.67 us
  transfers between devices with their start and end apart: 16, of which 6 were waited for; matrix products, arithmetic and copies ran while one was open for 2% of the time, Pallas kernels for 30%

profile of v6, /device:TPU:0, one launch (start us, length us, event | category | flops | bytes accessed | tf_op | source)
XLA Modules:
  0.0 123.9 jit_solution(15924640193788549445)
XLA Ops:
  0.6 0.0 copy-start.6
  0.7 4.3 %token_messages.1 = (bf16[2,4,48,256]{3,2,1,0:T(8,128)(2,1)}, bf16[2,4,48,256]{3,2,1,0:T(8,128)(2,1)}, bf16[2,4,48,256]{3,2,1,0:T(8,128)(2,1)}, bf16[2,4,48,256]{3,2,1,0:T(8,128)(2,1)}) custom-call(s32[1]{0:T(128)} %bitcast.4.row_ref, s32[1]{0:T(128)} %bitcast.col_ref, bf16[4,64,768]{2,1,0:T(8,128)(2,1)} %tokens_ref.3, s32[1,64]{1,0:T(1,128)} %bitcast.28, ...), custom_call_target="tpu_custom_call" | custom-call | flops 4000000000 | bytes 4000000 | tf_op jit(solution)/shard_map/token_messages/pallas_call | solution.py:245
  5.0 3.0 %collective-permute-start = (bf16[2,4,48,256]{3,2,1,0:T(8,128)(2,1)}, bf16[2,4,48,256]{3,2,1,0:T(8,128)(2,1)S(1)}, u32[]{:S(2)}, u32[]{:S(2)}) collective-permute-start(bf16[2,4,48,256]{3,2,1,0:T(8,128)(2,1)} %get-tuple-element.45), channel_id=1, source_target_pairs={{0,2},{1,3},{2,0},{3,1},{4,6},{5,7},{6,4},{7,5},{8,10},{9,11},{10,... | collective-permute-start | bytes 589832 | tf_op jit(solution)/shard_map/ppermute | solution.py:780
  8.0 2.6 %collective-permute-start.1 = (bf16[2,4,48,256]{3,2,1,0:T(8,128)(2,1)}, bf16[2,4,48,256]{3,2,1,0:T(8,128)(2,1)S(1)}, u32[]{:S(2)}, u32[]{:S(2)}) collective-permute-start(bf16[2,4,48,256]{3,2,1,0:T(8,128)(2,1)} %get-tuple-element.46), channel_id=1, source_target_pairs={{0,4},{1,5},{2,6},{3,7},{4,0},{5,1},{6,2},{7,3},{8,12},{9,13},{10,... | collective-permute-start | bytes 589832 | tf_op jit(solution)/shard_map/ppermute | solution.py:780
  10.6 0.0 collective-permute-start.2
  10.6 9.8 %pair_bias.1 = f32[16,64,256]{2,1,0:T(8,128)S(1)} custom-call(bf16[2,128,64,128]{3,2,1,0:T(8,128)(2,1)S(1)} %bitcast.21, bf16[16,128]{1,0:T(8,128)(2,1)S(1)} %bitcast.17, s32[1,64]{1,0:T(1,128)S(1)} %bitcast.22), custom_call_target="tpu_custom_call" | custom-call | flops 6000000000 | bytes 5000000 | tf_op jit(solution)/shard_map/pair_bias/pallas_call | solution.py:384
  20.4 0.0 copy-start.4
  20.4 0.9 convert_element_type.27
  21.3 0.0 collective-permute-done.refs_1_
  21.3 4.1 %collective-permute-done.1.refs_2_ = bf16[2,4,48,256]{3,2,1,0:T(8,128)(2,1)S(1)} collective-permute-done((bf16[2,4,48,256]{3,2,1,0:T(8,128)(2,1)}, bf16[2,4,48,256]{3,2,1,0:T(8,128)(2,1)S(1)}, u32[]{:S(2)}, u32[]{:S(2)}) %collective-permute-start.1) | collective-permute-done | bytes 196640 | tf_op jit(solution)/shard_map/ppermute | solution.py:780
  25.4 0.0 collective-permute-done.2.refs_3_
  25.4 6.7 %all-to-all-start = ((f16[16,64,256]{2,1,0:T(8,128)(2,1)}), f16[16,64,256]{2,1,0:T(8,128)(2,1)S(1)}, u32[]{:S(2)}, u32[]{:S(2)}) async-start(f16[16,64,256]{2,1,0:T(8,128)(2,1)} %convert_element_type.27), calls=%async_computation | async-start | bytes 1048576 | tf_op jit(solution)/shard_map/all_to_all | solution.py:797
  32.1 0.1 pad_maximum_fusion
  32.2 0.5 collective-permute-start.3
  32.7 3.0 %own_rows.1 = (f32[768,128]{1,0:T(8,128)}, f32[768,128]{1,0:T(8,128)}, f32[8,128]{1,0:T(8,128)}) custom-call(s32[1]{0:T(128)} %bitcast.4.row_ref, bf16[4,64,768]{2,1,0:T(8,128)(2,1)} %tokens_ref.3, s32[1,64]{1,0:T(1,128)} %bitcast.29, bf16[32,768]{1,0:T(8,128)(2,1)} %table_ref.3, bf16[768,768]{1,0:T(8,128)(2,1)} %refs_7_.1, bf16[4,64,768]{2,1,0:T(8,128)(2,1)} %cot_ref.1), custom_call_target="tpu_custom_call" | custom-call | flops 3000000000 | bytes 3000000 | tf_op jit(solution)/shard_map/own_rows/pallas_call | solution.py:289
  35.7 0.0 collective-permute-done.3.refs_4_
  35.7 10.6 %all-to-all-done = f16[16,64,256]{2,1,0:T(8,128)(2,1)S(1)} async-done(((f16[16,64,256]{2,1,0:T(8,128)(2,1)}), f16[16,64,256]{2,1,0:T(8,128)(2,1)S(1)}, u32[]{:S(2)}, u32[]{:S(2)}) %all-to-all-start) | async-done | bytes 524320 | tf_op jit(solution)/shard_map/all_to_all | solution.py:797
  46.3 0.1 convert_element_type.28.refs_5_
  46.4 7.7 %attention.1 = (f32[16,200,128]{2,1,0:T(8,128)S(1)}, f32[16,72,256]{2,1,0:T(8,128)S(1)}) custom-call(s32[1]{0:T(128)} %bitcast.col_ref, bf16[2,4,48,256]{3,2,1,0:T(8,128)(2,1)S(1)} %copy-done.4, bf16[2,4,48,256]{3,2,1,0:T(8,128)(2,1)S(1)} %collective-permute-done.refs_1_, bf16[2,4,48,256]{3,2,1,0:T(8,128)(2,1)S(1)} %collective-permute-done.1.refs_2_, ...), custom_call_target="tpu_custom_call" | custom-call | flops 8000000000 | bytes 6000000 | tf_op jit(solution)/shard_map/attention/pallas_call | solution.py:538
  54.1 0.9 convert_element_type.30
  55.0 4.0 %all-to-all-start.1 = ((f16[16,72,256]{2,1,0:T(8,128)(2,1)}), f16[16,72,256]{2,1,0:T(8,128)(2,1)S(1)}, u32[]{:S(2)}, u32[]{:S(2)}) async-start(f16[16,72,256]{2,1,0:T(8,128)(2,1)} %convert_element_type.30), calls=%async_computation.1 | async-start | bytes 1179648 | tf_op jit(solution)/shard_map/all_to_all | solution.py:802
  59.0 1.1 convert_element_type.29
  60.0 8.8 %pair_units.1 = (bf16[32,256,512]{2,1,0:T(8,128)(2,1)}, f32[32,8,512]{2,1,0:T(8,128)}) custom-call(bf16[2,128,64,128]{3,2,1,0:T(8,128)(2,1)} %bitcast.20), custom_call_target="tpu_custom_call" | custom-call | flops 6000000000 | bytes 12000000 | tf_op jit(solution)/shard_map/pair_units/pallas_call | solution.py:414
  68.9 5.5 %all-to-all-done.1 = f16[16,72,256]{2,1,0:T(8,128)(2,1)S(1)} async-done(((f16[16,72,256]{2,1,0:T(8,128)(2,1)}), f16[16,72,256]{2,1,0:T(8,128)(2,1)S(1)}, u32[]{:S(2)}, u32[]{:S(2)}) %all-to-all-start.1) | async-done | bytes 589856 | tf_op jit(solution)/shard_map/all_to_all | solution.py:802
  74.4 1.5 %collective-permute-start.4 = (f16[16,72,256]{2,1,0:T(8,128)(2,1)S(1)}, f16[16,72,256]{2,1,0:T(8,128)(2,1)S(1)}, u32[]{:S(2)}, u32[]{:S(2)}) collective-permute-start(f16[16,72,256]{2,1,0:T(8,128)(2,1)S(1)} %all-to-all-done.1), channel_id=1, source_target_pairs={{0,16},{16,0},{1,17},{17,1},{2,18},{18,2},{3,19},{19,3},{4,20},{20... | collective-permute-start | bytes 1769480 | tf_op jit(solution)/shard_map/ppermute | solution.py:757
  75.9 0.1 slice_convert_fusion
  76.0 4.5 %all-to-all-start.2 = ((f16[16,200,128]{2,1,0:T(8,128)(2,1)}), f16[16,200,128]{2,1,0:T(8,128)(2,1)}, u32[]{:S(2)}, u32[]{:S(2)}) async-start(f16[16,200,128]{2,1,0:T(8,128)(2,1)} %convert_element_type.29), calls=%async_computation.2 | async-start | bytes 1638400 | tf_op jit(solution)/shard_map/all_to_all | solution.py:808
  80.5 0.1 slice_multiply_fusion.2
  80.7 3.4 %copy-done = bf16[32,256,512]{2,1,0:T(8,128)(2,1)S(1)} copy-done((bf16[32,256,512]{2,1,0:T(8,128)(2,1)S(1)}, bf16[32,256,512]{2,1,0:T(8,128)(2,1)}, u32[]{:S(2)}) %copy-start) | copy-done | bytes 8388632
  84.1 6.2 %pair_weight.1 = f32[16,128]{1,0:T(8,128)S(1)} custom-call(bf16[32,256,512]{2,1,0:T(8,128)(2,1)S(1)} %copy-done, f32[16,64,128]{2,1,0:T(8,128)S(1)} %get-tuple-element.92.refs_0_, f32[16,64,128]{2,1,0:T(8,128)S(1)} %get-tuple-element.91.refs_1_), custom_call_target="tpu_custom_call" | custom-call | flops 1000000 | bytes 100000 | tf_op jit(solution)/shard_map/pair_weight/pallas_call | solution.py:701
  90.2 1.6 %collective-permute-start.7 = (f32[16,128]{1,0:T(8,128)S(1)}, f32[16,128]{1,0:T(8,128)S(1)}, u32[]{:S(2)}, u32[]{:S(2)}) collective-permute-start(f32[16,128]{1,0:T(8,128)S(1)} %pair_weight.1), channel_id=1, source_target_pairs={{0,24},{8,16},{16,8},{24,0},{1,25},{9,17},{17,9},{25,1},{2,26},{10... | collective-permute-start | bytes 24584 | tf_op jit(solution)/shard_map/ppermute | solution.py:815
  91.8 0.4 collective-permute-start.6
  92.2 1.5 %collective-permute-start.5 = (f32[16,128]{1,0:T(8,128)S(1)}, f32[16,128]{1,0:T(8,128)S(1)}, u32[]{:S(2)}, u32[]{:S(2)}) collective-permute-start(f32[16,128]{1,0:T(8,128)S(1)} %pair_weight.1), channel_id=1, source_target_pairs={{0,16},{16,0},{1,17},{17,1},{2,18},{18,2},{3,19},{19,3},{4,20},{20... | collective-permute-start | bytes 24584 | tf_op jit(solution)/shard_map/ppermute | solution.py:757
  93.8 0.0 collective-permute-done.4
  93.8 1.1 collective-permute-done.7
  94.8 0.7 collective-permute-done.6
  95.5 0.4 collective-permute-done.5
  95.9 0.1 slice_convert_fusion.2
  96.0 0.1 fusion.refs_2_
  96.1 0.1 fusion.1.refs_2_
  96.2 0.1 collective-permute-start.10
  96.3 1.6 %collective-permute-start.9 = (f32[16,128]{1,0:T(8,128)S(1)}, f32[16,128]{1,0:T(8,128)S(1)}, u32[]{:S(2)}, u32[]{:S(2)}) collective-permute-start(f32[16,128]{1,0:T(8,128)S(1)} %add_add_fusion.1), channel_id=1, source_target_pairs={{0,2},{1,3},{2,0},{3,1},{4,6},{5,7},{6,4},{7,5},{8,10},{9,11},{10,... | collective-permute-start | bytes 24584 | tf_op jit(solution)/shard_map/ppermute | solution.py:780
  98.0 0.2 collective-permute-start.8
  98.1 4.6 %pair_backward.2.refs_4_ = bf16[2,128,64,128]{3,2,1,0:T(8,128)(2,1)} custom-call(bf16[32,256,512]{2,1,0:T(8,128)(2,1)S(1)} %copy-done.1, f32[32,8,512]{2,1,0:T(8,128)S(1)} %copy-done.3, f32[16,64,128]{2,1,0:T(8,128)S(1)} %fusion.1.refs_2_, bf16[16,128]{1,0:T(8,128)(2,1)S(1)} %bitcast.18), custom_call_target="tpu_custom_call" | custom-call | flops 1000000 | bytes 100000 | tf_op jit(solution)/shard_map/pair_backward/pallas_call | solution.py:727
  102.8 0.0 collective-permute-done.10
  102.8 0.0 collective-permute-done.9
  102.8 0.0 collective-permute-done.8
  102.8 0.0 all-to-all-done.2
  102.8 1.4 %convert_element_type.35.refs_0_ = f32[16,200,128]{2,1,0:T(8,128)S(1)} convert(f16[16,200,128]{2,1,0:T(8,128)(2,1)} %all-to-all-done.2) | non-fusion elementwise | flops 409600 | bytes 2457600 | tf_op jit(solution)/shard_map/convert_element_type | solution.py:834
  104.2 0.1 copy-done.7
  104.3 0.1 copy-done.12
  104.4 0.1 copy-done.13
  104.5 1.3 %copy-done.8 = bf16[768,768]{1,0:T(8,128)(2,1)S(1)} copy-done((bf16[768,768]{1,0:T(8,128)(2,1)S(1)}, bf16[768,768]{1,0:T(8,128)(2,1)}, u32[]{:S(2)}) %copy-start.8) | copy-done | bytes 1179672
  105.8 1.3 %copy-done.9 = bf16[768,768]{1,0:T(8,128)(2,1)S(1)} copy-done((bf16[768,768]{1,0:T(8,128)(2,1)S(1)}, bf16[768,768]{1,0:T(8,128)(2,1)}, u32[]{:S(2)}) %copy-start.9) | copy-done | bytes 1179672
  107.0 1.3 %copy-done.10 = bf16[768,768]{1,0:T(8,128)(2,1)S(1)} copy-done((bf16[768,768]{1,0:T(8,128)(2,1)S(1)}, bf16[768,768]{1,0:T(8,128)(2,1)}, u32[]{:S(2)}) %copy-start.10) | copy-done | bytes 1179672
  108.3 2.1 %token_back.1 = bf16[128,768]{1,0:T(8,128)(2,1)S(1)} custom-call(f32[16,200,128]{2,1,0:T(8,128)S(1)} %convert_element_type.35.refs_0_, f32[768,128]{1,0:T(8,128)S(1)} %copy-done.12, f32[768,128]{1,0:T(8,128)S(1)} %copy-done.13, f32[8,128]{1,0:T(8,128)S(1)} %copy-done.14, bf16[768,768]{1,0:T(8,128)(2,1)S(1)} %copy-done.7, bf16[768,768]{1,0:T(8,128)(2,1)S(1)} %copy-done.8, ...), custom_call_target="tpu_custom_call" | custom-call | flops 4000000000 | bytes 8000000 | tf_op jit(solution)/shard_map/token_back/pallas_call | solution.py:611
  110.4 1.7 %collective-permute-start.11 = (bf16[2,64,768]{2,1,0:T(8,128)(2,1)S(1)}, bf16[2,64,768]{2,1,0:T(8,128)(2,1)S(1)}, u32[]{:S(2)}, u32[]{:S(2)}) collective-permute-start(bf16[2,64,768]{2,1,0:T(8,128)(2,1)S(1)} %bitcast.15), channel_id=1, source_target_pairs={{0,8},{8,0},{1,9},{9,1},{2,10},{10,2},{3,11},{11,3},{4,12},{12,4},... | collective-permute-start | bytes 589832 | tf_op jit(solution)/shard_map/ppermute | solution.py:757
  112.1 2.4 %collective-permute-start.12 = (f32[16,128]{1,0:T(8,128)S(1)}, f32[16,128]{1,0:T(8,128)S(1)}, u32[]{:S(2)}, u32[]{:S(2)}) collective-permute-start(f32[16,128]{1,0:T(8,128)S(1)} %add_add_fusion), channel_id=1, source_target_pairs={{0,4},{1,5},{2,6},{3,7},{4,0},{5,1},{6,2},{7,3},{8,12},{9,13},{10,... | collective-permute-start | bytes 24584 | tf_op jit(solution)/shard_map/ppermute | solution.py:780
  114.5 3.4 %copy-done.2 = bf16[32,256,512]{2,1,0:T(8,128)(2,1)S(1)} copy-done((bf16[32,256,512]{2,1,0:T(8,128)(2,1)S(1)}, bf16[32,256,512]{2,1,0:T(8,128)(2,1)}, u32[]{:S(2)}) %copy-start.2) | copy-done | bytes 8388632
  117.9 4.6 %pair_backward.3 = bf16[2,128,64,128]{3,2,1,0:T(8,128)(2,1)} custom-call(bf16[32,256,512]{2,1,0:T(8,128)(2,1)S(1)} %copy-done.2, f32[32,8,512]{2,1,0:T(8,128)S(1)} %copy-done.3, f32[16,64,128]{2,1,0:T(8,128)S(1)} %fusion.refs_2_, bf16[16,128]{1,0:T(8,128)(2,1)S(1)} %bitcast.19, ...), custom_call_target="tpu_custom_call", output_to_operand_aliasing={{}: (4, {})} | custom-call | flops 1000000 | bytes 100000 | tf_op jit(solution)/shard_map/pair_backward/pallas_call | solution.py:727
  122.5 0.0 collective-permute-done.12
  122.5 0.0 collective-permute-done.11
  122.5 0.6 multiply_bitcast_fusion
  123.2 0.8 pad_maximum_fusion.1
  (31 shorter events, 0.2 us)
Async XLA Ops:
  0.6 10.0 %copy-start.5 = (bf16[128,16]{0,1:T(8,128)(2,1)S(1)}, bf16[128,16]{0,1:T(8,128)(2,1)}, u32[]{:S(2)}) copy-start(bf16[128,16]{0,1:T(8,128)(2,1)} %param.16) | copy-start | bytes 12292
  0.6 10.0 %copy-start.6 = (bf16[256,64,128]{2,1,0:T(8,128)(2,1)S(1)}, bf16[256,64,128]{2,1,0:T(8,128)(2,1)}, u32[]{:S(2)}) copy-start(bf16[256,64,128]{2,1,0:T(8,128)(2,1)} %param.15) | copy-start | bytes 12582916
  0.7 9.9 %copy-start.11 = (s32[64]{0:T(128)S(1)}, s32[64]{0:T(128)}, u32[]{:S(2)}) copy-start(s32[64]{0:T(128)} %param.14) | copy-start | bytes 772
  5.0 16.3 %collective-permute-start = (bf16[2,4,48,256]{3,2,1,0:T(8,128)(2,1)}, bf16[2,4,48,256]{3,2,1,0:T(8,128)(2,1)S(1)}, u32[]{:S(2)}, u32[]{:S(2)}) collective-permute-start(bf16[2,4,48,256]{3,2,1,0:T(8,128)(2,1)} %get-tuple-element.45), channel_id=1, source_target_pairs={{0,2},{1,3},{2,0},{3,1},{4,6},{5,7},{6,4},{7,5},{8,10},{9,11},{10,... | collective-permute-start | bytes 589832 | tf_op jit(solution)/shard_map/ppermute | solution.py:780
  8.0 17.4 %collective-permute-start.1 = (bf16[2,4,48,256]{3,2,1,0:T(8,128)(2,1)}, bf16[2,4,48,256]{3,2,1,0:T(8,128)(2,1)S(1)}, u32[]{:S(2)}, u32[]{:S(2)}) collective-permute-start(bf16[2,4,48,256]{3,2,1,0:T(8,128)(2,1)} %get-tuple-element.46), channel_id=1, source_target_pairs={{0,4},{1,5},{2,6},{3,7},{4,0},{5,1},{6,2},{7,3},{8,12},{9,13},{10,... | collective-permute-start | bytes 589832 | tf_op jit(solution)/shard_map/ppermute | solution.py:780
  10.6 14.8 %collective-permute-start.2 = (bf16[2,4,48,256]{3,2,1,0:T(8,128)(2,1)}, bf16[2,4,48,256]{3,2,1,0:T(8,128)(2,1)S(1)}, u32[]{:S(2)}, u32[]{:S(2)}) collective-permute-start(bf16[2,4,48,256]{3,2,1,0:T(8,128)(2,1)} %get-tuple-element.47), channel_id=1, source_target_pairs={{0,6},{1,7},{2,4},{3,5},{4,2},{5,3},{6,0},{7,1},{8,14},{9,15},{10,... | collective-permute-start | bytes 589832 | tf_op jit(solution)/shard_map/ppermute | solution.py:780
  20.4 11.7 %copy-start.4 = (bf16[2,4,48,256]{3,2,1,0:T(8,128)(2,1)S(1)}, bf16[2,4,48,256]{3,2,1,0:T(8,128)(2,1)}, u32[]{:S(2)}) copy-start(bf16[2,4,48,256]{3,2,1,0:T(8,128)(2,1)} %get-tuple-element.48.refs_0_) | copy-start | bytes 589828
  25.4 20.9 %all-to-all-start = ((f16[16,64,256]{2,1,0:T(8,128)(2,1)}), f16[16,64,256]{2,1,0:T(8,128)(2,1)S(1)}, u32[]{:S(2)}, u32[]{:S(2)}) async-start(f16[16,64,256]{2,1,0:T(8,128)(2,1)} %convert_element_type.27), calls=%async_computation | async-start | bytes 1048576 | tf_op jit(solution)/shard_map/all_to_all | solution.py:797
  32.2 3.5 %collective-permute-start.3 = (bf16[4,4,48,256]{3,2,1,0:T(8,128)(2,1)S(1)}, bf16[4,4,48,256]{3,2,1,0:T(8,128)(2,1)S(1)}, u32[]{:S(2)}, u32[]{:S(2)}) collective-permute-start(bf16[4,4,48,256]{3,2,1,0:T(8,128)(2,1)S(1)} %pad_maximum_fusion), channel_id=1, source_target_pairs={{0,1},{1,0},{2,3},{3,2},{4,5},{5,4},{6,7},{7,6},{8,9},{9,8},{10,11... | collective-permute-start | bytes 1179656 | tf_op jit(solution)/shard_map/ppermute | solution.py:780
  55.0 19.4 %all-to-all-start.1 = ((f16[16,72,256]{2,1,0:T(8,128)(2,1)}), f16[16,72,256]{2,1,0:T(8,128)(2,1)S(1)}, u32[]{:S(2)}, u32[]{:S(2)}) async-start(f16[16,72,256]{2,1,0:T(8,128)(2,1)} %convert_element_type.30), calls=%async_computation.1 | async-start | bytes 1179648 | tf_op jit(solution)/shard_map/all_to_all | solution.py:802
  74.4 19.4 %collective-permute-start.4 = (f16[16,72,256]{2,1,0:T(8,128)(2,1)S(1)}, f16[16,72,256]{2,1,0:T(8,128)(2,1)S(1)}, u32[]{:S(2)}, u32[]{:S(2)}) collective-permute-start(f16[16,72,256]{2,1,0:T(8,128)(2,1)S(1)} %all-to-all-done.1), channel_id=1, source_target_pairs={{0,16},{16,0},{1,17},{17,1},{2,18},{18,2},{3,19},{19,3},{4,20},{20... | collective-permute-start | bytes 1769480 | tf_op jit(solution)/shard_map/ppermute | solution.py:757
  76.0 26.8 %all-to-all-start.2 = ((f16[16,200,128]{2,1,0:T(8,128)(2,1)}), f16[16,200,128]{2,1,0:T(8,128)(2,1)}, u32[]{:S(2)}, u32[]{:S(2)}) async-start(f16[16,200,128]{2,1,0:T(8,128)(2,1)} %convert_element_type.29), calls=%async_computation.2 | async-start | bytes 1638400 | tf_op jit(solution)/shard_map/all_to_all | solution.py:808
  80.7 3.4 %copy-start = (bf16[32,256,512]{2,1,0:T(8,128)(2,1)S(1)}, bf16[32,256,512]{2,1,0:T(8,128)(2,1)}, u32[]{:S(2)}) copy-start(bf16[32,256,512]{2,1,0:T(8,128)(2,1)} %get-tuple-element.64.normed_ref.refs_0_) | copy-start | bytes 25165828
  84.1 14.1 %copy-start.1 = (bf16[32,256,512]{2,1,0:T(8,128)(2,1)S(1)}, bf16[32,256,512]{2,1,0:T(8,128)(2,1)}, u32[]{:S(2)}) copy-start(bf16[32,256,512]{2,1,0:T(8,128)(2,1)} %get-tuple-element.64.normed_ref.refs_0_) | copy-start | bytes 25165828
  90.2 4.6 %collective-permute-start.7 = (f32[16,128]{1,0:T(8,128)S(1)}, f32[16,128]{1,0:T(8,128)S(1)}, u32[]{:S(2)}, u32[]{:S(2)}) collective-permute-start(f32[16,128]{1,0:T(8,128)S(1)} %pair_weight.1), channel_id=1, source_target_pairs={{0,24},{8,16},{16,8},{24,0},{1,25},{9,17},{17,9},{25,1},{2,26},{10... | collective-permute-start | bytes 24584 | tf_op jit(solution)/shard_map/ppermute | solution.py:815
  91.8 3.7 %collective-permute-start.6 = (f32[16,128]{1,0:T(8,128)S(1)}, f32[16,128]{1,0:T(8,128)S(1)}, u32[]{:S(2)}, u32[]{:S(2)}) collective-permute-start(f32[16,128]{1,0:T(8,128)S(1)} %pair_weight.1), channel_id=1, source_target_pairs={{0,8},{8,0},{1,9},{9,1},{2,10},{10,2},{3,11},{11,3},{4,12},{12,4},... | collective-permute-start | bytes 24584 | tf_op jit(solution)/shard_map/ppermute | solution.py:757
  92.2 3.7 %collective-permute-start.5 = (f32[16,128]{1,0:T(8,128)S(1)}, f32[16,128]{1,0:T(8,128)S(1)}, u32[]{:S(2)}, u32[]{:S(2)}) collective-permute-start(f32[16,128]{1,0:T(8,128)S(1)} %pair_weight.1), channel_id=1, source_target_pairs={{0,16},{16,0},{1,17},{17,1},{2,18},{18,2},{3,19},{19,3},{4,20},{20... | collective-permute-start | bytes 24584 | tf_op jit(solution)/shard_map/ppermute | solution.py:757
  96.0 2.1 %copy-start.3 = (f32[32,8,512]{2,1,0:T(8,128)S(1)}, f32[32,8,512]{2,1,0:T(8,128)}, u32[]{:S(2)}) copy-start(f32[32,8,512]{2,1,0:T(8,128)} %get-tuple-element.65.refs_1_) | copy-start | bytes 1572868
  96.2 6.6 %collective-permute-start.10 = (f32[16,128]{1,0:T(8,128)S(1)}, f32[16,128]{1,0:T(8,128)S(1)}, u32[]{:S(2)}, u32[]{:S(2)}) collective-permute-start(f32[16,128]{1,0:T(8,128)S(1)} %add_add_fusion.1), channel_id=1, source_target_pairs={{0,3},{1,2},{2,1},{3,0},{4,7},{5,6},{6,5},{7,4},{8,11},{9,10},{10,... | collective-permute-start | bytes 24584 | tf_op jit(solution)/shard_map/ppermute | solution.py:780
  96.3 6.5 %collective-permute-start.9 = (f32[16,128]{1,0:T(8,128)S(1)}, f32[16,128]{1,0:T(8,128)S(1)}, u32[]{:S(2)}, u32[]{:S(2)}) collective-permute-start(f32[16,128]{1,0:T(8,128)S(1)} %add_add_fusion.1), channel_id=1, source_target_pairs={{0,2},{1,3},{2,0},{3,1},{4,6},{5,7},{6,4},{7,5},{8,10},{9,11},{10,... | collective-permute-start | bytes 24584 | tf_op jit(solution)/shard_map/ppermute | solution.py:780
  98.0 4.8 %collective-permute-start.8 = (f32[16,128]{1,0:T(8,128)S(1)}, f32[16,128]{1,0:T(8,128)S(1)}, u32[]{:S(2)}, u32[]{:S(2)}) collective-permute-start(f32[16,128]{1,0:T(8,128)S(1)} %add_add_fusion.1), channel_id=1, source_target_pairs={{0,1},{1,0},{2,3},{3,2},{4,5},{5,4},{6,7},{7,6},{8,9},{9,8},{10,11... | collective-permute-start | bytes 24584 | tf_op jit(solution)/shard_map/ppermute | solution.py:780
  102.8 1.5 %copy-start.7 = (bf16[768,768]{1,0:T(8,128)(2,1)S(1)}, bf16[768,768]{1,0:T(8,128)(2,1)}, u32[]{:S(2)}) copy-start(bf16[768,768]{1,0:T(8,128)(2,1)} %refs_4_.3) | copy-start | bytes 3538948
  102.8 1.6 %copy-start.12 = (f32[768,128]{1,0:T(8,128)S(1)}, f32[768,128]{1,0:T(8,128)}, u32[]{:S(2)}) copy-start(f32[768,128]{1,0:T(8,128)} %get-tuple-element.73.refs_1_) | copy-start | bytes 1179652
  102.8 1.7 %copy-start.13 = (f32[768,128]{1,0:T(8,128)S(1)}, f32[768,128]{1,0:T(8,128)}, u32[]{:S(2)}) copy-start(f32[768,128]{1,0:T(8,128)} %get-tuple-element.74.refs_2_) | copy-start | bytes 1179652
  102.8 1.7 %copy-start.14 = (f32[8,128]{1,0:T(8,128)S(1)}, f32[8,128]{1,0:T(8,128)}, u32[]{:S(2)}) copy-start(f32[8,128]{1,0:T(8,128)} %get-tuple-element.75.refs_3_) | copy-start | bytes 12292
  104.5 1.3 %copy-start.8 = (bf16[768,768]{1,0:T(8,128)(2,1)S(1)}, bf16[768,768]{1,0:T(8,128)(2,1)}, u32[]{:S(2)}) copy-start(bf16[768,768]{1,0:T(8,128)(2,1)} %refs_5_.1) | copy-start | bytes 3538948
  105.8 1.3 %copy-start.9 = (bf16[768,768]{1,0:T(8,128)(2,1)S(1)}, bf16[768,768]{1,0:T(8,128)(2,1)}, u32[]{:S(2)}) copy-start(bf16[768,768]{1,0:T(8,128)(2,1)} %refs_6_.1) | copy-start | bytes 3538948
  107.0 1.3 %copy-start.10 = (bf16[768,768]{1,0:T(8,128)(2,1)S(1)}, bf16[768,768]{1,0:T(8,128)(2,1)}, u32[]{:S(2)}) copy-start(bf16[768,768]{1,0:T(8,128)(2,1)} %refs_7_.1) | copy-start | bytes 3538948
  110.4 12.1 %collective-permute-start.11 = (bf16[2,64,768]{2,1,0:T(8,128)(2,1)S(1)}, bf16[2,64,768]{2,1,0:T(8,128)(2,1)S(1)}, u32[]{:S(2)}, u32[]{:S(2)}) collective-permute-start(bf16[2,64,768]{2,1,0:T(8,128)(2,1)S(1)} %bitcast.15), channel_id=1, source_target_pairs={{0,8},{8,0},{1,9},{9,1},{2,10},{10,2},{3,11},{11,3},{4,12},{12,4},... | collective-permute-start | bytes 589832 | tf_op jit(solution)/shard_map/ppermute | solution.py:757
  112.1 10.4 %collective-permute-start.12 = (f32[16,128]{1,0:T(8,128)S(1)}, f32[16,128]{1,0:T(8,128)S(1)}, u32[]{:S(2)}, u32[]{:S(2)}) collective-permute-start(f32[16,128]{1,0:T(8,128)S(1)} %add_add_fusion), channel_id=1, source_target_pairs={{0,4},{1,5},{2,6},{3,7},{4,0},{5,1},{6,2},{7,3},{8,12},{9,13},{10,... | collective-permute-start | bytes 24584 | tf_op jit(solution)/shard_map/ppermute | solution.py:780
  114.5 3.4 %copy-start.2 = (bf16[32,256,512]{2,1,0:T(8,128)(2,1)S(1)}, bf16[32,256,512]{2,1,0:T(8,128)(2,1)}, u32[]{:S(2)}) copy-start(bf16[32,256,512]{2,1,0:T(8,128)(2,1)} %get-tuple-element.64.normed_ref.refs_0_) | copy-start | bytes 25165828

commit v7 on v2

--- a/solution.py
+++ b/solution.py
@@ -218,13 +218,23 @@
 
 
 def token_kernel(row_ref, col_ref, tokens_ref, types_ref, table_ref, *refs):
-    wq_ref, wk_ref, wv_ref, wg_ref, cot_ref = refs[:5]
-    out_refs, side_ref = refs[5:-1], refs[-1]
+    weight_refs, cot_ref, out_refs = refs[:4], refs[4], refs[5:-3]
+    side_ref, held_ref, sems = refs[-3:]
+    width = held_ref.shape[-1]
+    mine = pl.ds(pl.multiple_of(row_ref[0] * width, 128), width)
+    copies = [
+        pltpu.make_async_copy(ref.at[:, mine], held_ref.at[slot], sems.at[slot])
+        for slot, ref in enumerate(weight_refs)
+    ]
+    for copy in copies:
+        copy.start()
     normed, _ = embed_rows(tokens_ref, types_ref, table_ref)
     act = normed.astype(jnp.bfloat16)
-    for slot, ref in enumerate((wq_ref, wk_ref, wv_ref)):
-        side_ref[slot] = matmul(act, ref[...]).astype(jnp.bfloat16).T
-    gate = matmul(act, wg_ref[...]).astype(jnp.bfloat16).astype(jnp.float32)
+    for slot in range(3):
+        copies[slot].wait()
+        side_ref[slot] = matmul(act, held_ref[slot]).astype(jnp.bfloat16).T
+    copies[3].wait()
+    gate = matmul(act, held_ref[3]).astype(jnp.bfloat16).astype(jnp.float32)
     cot = cot_ref[...].reshape(gate.shape).astype(jnp.float32)
     side_ref[3] = (cot * jax.nn.sigmoid(gate)).astype(jnp.bfloat16).T
     for offset, out_ref in enumerate(out_refs):
@@ -239,7 +249,7 @@
     held = samp_dev * tok_col
     whole3 = lambda i, r, c: (0, 0, 0)
     whole2 = lambda i, r, c: (0, 0)
-    weight_spec = pl.BlockSpec((D, width), lambda i, r, c: (0, r[0]))
+    weight_spec = pl.BlockSpec(memory_space=pl.ANY)
     shape = (2, 4, CH, held)
     count = n_col // 2
     return pl.pallas_call(
@@ -259,7 +269,11 @@
                 pl.BlockSpec((samp_dev, tok_col, width), lambda i, r, c: (0, 0, r[0])),
             ],
             out_specs=[pl.BlockSpec(shape, lambda i, r, c: (0, 0, 0, 0))] * count,
-            scratch_shapes=[pltpu.VMEM((4, width, held), jnp.bfloat16)],
+            scratch_shapes=[
+                pltpu.VMEM((4, width, held), jnp.bfloat16),
+                pltpu.VMEM((4, D, width), jnp.bfloat16),
+                pltpu.SemaphoreType.DMA((4,)),
+            ],
         ),
         compiler_params=params(56),
         cost_estimate=pl.CostEstimate(
@@ -347,7 +361,7 @@
             flat_ref[pl.ds(base + k + m, H, stride=whole), :] = bias[:, lanes]
         return carry
 
-    lax.fori_loop(0, count // MANY, step, 0, unroll=2)
+    lax.fori_loop(0, count // MANY, step, 0, unroll=4)
 
     @pl.when(pl.program_id(0) == pl.num_programs(0) - 1)
     def _():
@@ -402,7 +416,7 @@
         inv_ref[n] = jnp.broadcast_to(inv_std, inv_ref.shape[1:])
         return carry
 
-    lax.fori_loop(0, normed_ref.shape[0], step, 0, unroll=2)
+    lax.fori_loop(0, normed_ref.shape[0], step, 0, unroll=4)
 
 
 def pair_units(pair):
@@ -644,7 +658,7 @@
     def step(n, carry):
         return carry + matmul_nt(normed_ref[n], flat_columns(flat_ref, (base + n) * MANY, MANY))
 
-    parts = lax.fori_loop(0, chunks, step, jnp.zeros((width, 2 * H), jnp.float32), unroll=2)
+    parts = lax.fori_loop(0, chunks, step, jnp.zeros((width, 2 * H), jnp.float32), unroll=4)
     parts = parts[:, :H] + parts[:, H:]
     part_ref[...] += (parts[: width // 2] + parts[width // 2 :]).T
 
@@ -673,7 +687,7 @@
             out_ref[p, pl.ds(k, MANY)] = result[:, p * length : (p + 1) * length]
         return carry
 
-    lax.fori_loop(0, count // MANY, step, 0, unroll=2)
+    lax.fori_loop(0, count // MANY, step, 0, unroll=4)
 
 
 def pair_weight(normed, grads):
@@ -793,11 +807,10 @@
     )
 
     pair_grad, back, sums = lax.optimization_barrier((pair_grad, back, sums))
-    part = (part + sums[0]) + (sums[1] + sums[2])
+    part = ((part + sums[0]) + (sums[1] + sums[2])) / samples
+    token_half = token_back(back.astype(jnp.float32), *own, weights)
+    token_half, part = lax.optimization_barrier((token_half, part))
     last = send(part, 4)
-    token_half = token_back(back.astype(jnp.float32), *own, weights)
-    token_half, last = lax.optimization_barrier((token_half, last))
-    part = part + last
     token_half = token_half.reshape(half, tok_col, D)
     other_half = swap(token_half, "row")
     first = row_index == 0
@@ -805,7 +818,8 @@
         [jnp.where(first, token_half, other_half), jnp.where(first, other_half, token_half)],
         axis=0,
     )
-    return (token_grad, pair_grad, part.T / samples)
+    token_grad, last = lax.optimization_barrier((token_grad, last))
+    return (token_grad, pair_grad, (part + last).T)
 
 
 def body(*args):

time: 119 us -> 118 us (level)
  Pallas kernels: 48.7 us -> 45.1 us
  waiting for transfers between devices: 25.7 us -> 27.3 us
  local copies, waits for them, and re-layouts: 3.47 us -> 4.85 us
    ppermute x4, waiting for transfers between devices: 5.53 us -> 4.13 us  [swap(): return lax.ppermute(block, axis, [(0, 1), (1, 0)])]
    unnamed x28, local copies, waits for them, and re-layouts: 3.44 us -> 4.82 us
    pallas_call x1, Pallas kernels: 7.68 us -> 6.39 us  [pair_backward(): pl.pallas_call(lambda *refs: pair_back_kernel(factor, *refs), out_shape=j...]
    pallas_call x1, Pallas kernels: 5.52 us -> 4.29 us  [pair_weight(): pl.pallas_call(pair_weight_kernel, out_shape=jax.ShapeDtypeStruct(part_sh...]
  transfers between devices with their start and end apart: 16 -> 16, of which waited for: 6 -> 7; matrix products, arithmetic and copies ran while one was open for 5% -> 3% of each run, Pallas kernels for 31% -> 26%
where the time goes in v7:
time: 118 us; the launch traced here: 117 us
  Pallas kernels  45.1 us (38%)
  starting transfers between devices  32.4 us (27%)
  waiting for transfers between devices  27.3 us (23%)
  other arithmetic  6.32 us (5%)
  local copies, waits for them, and re-layouts  4.85 us (4%)
    all_to_all x1, waiting for transfers between devices, body_heads(): bias = lax.all_to_all(bias, ('row', 'col'), 0, 0, tiled=True)  10.6 us
    ppermute x8, starting transfers between devices, send(): return lax.ppermute(block, 'col', [(c, c ^ offset) for c in range(n_col)])  10.5 us
    pallas_call x1, Pallas kernels, pair_bias(): pl.pallas_call(bias_kernel, out_shape=jax.ShapeDtypeStruct((H, tok_col, r...  8.79 us
    pallas_call x1, Pallas kernels, pair_units(): pl.pallas_call(norm_kernel, out_shape=[jax.ShapeDtypeStruct(shapes[0], jn...  7.8 us
    pallas_call x1, Pallas kernels, attention(): pl.pallas_call(attention_kernel, out_shape=[jax.ShapeDtypeStruct(back_sha...  7.42 us
    all_to_all x1, starting transfers between devices, body_heads(): bias = lax.all_to_all(bias, ('row', 'col'), 0, 0, tiled=True)  6.68 us
    all_to_all x1, waiting for transfers between devices, body_heads(): lax.all_to_all(grad_bias.astype(jnp.float16), ('row', 'col'), 0, 0, tiled...  6.55 us
    pallas_call x1, Pallas kernels, pair_backward(): pl.pallas_call(lambda *refs: pair_back_kernel(factor, *refs), out_shape=j...  6.39 us
  transfers between devices with their start and end apart: 16, of which 7 were waited for; matrix products, arithmetic and copies ran while one was open for 3% of the time, Pallas kernels for 26%

profile of v7, /device:TPU:0, one launch (start us, length us, event | category | flops | bytes accessed | tf_op | source)
XLA Modules:
  0.0 117.0 jit_solution(15235206392180677334)
XLA Ops:
  0.6 0.0 copy-start.1
  0.7 5.3 %token_messages.1 = (bf16[2,4,48,256]{3,2,1,0:T(8,128)(2,1)}, bf16[2,4,48,256]{3,2,1,0:T(8,128)(2,1)}, bf16[2,4,48,256]{3,2,1,0:T(8,128)(2,1)}, bf16[2,4,48,256]{3,2,1,0:T(8,128)(2,1)}) custom-call(s32[1]{0:T(128)} %bitcast.4.row_ref, s32[1]{0:T(128)} %bitcast.col_ref, bf16[4,64,768]{2,1,0:T(8,128)(2,1)} %tokens_ref.3, s32[1,64]{1,0:T(1,128)} %bitcast.27, ...), custom_call_target="tpu_custom_call" | custom-call | flops 4000000000 | bytes 4000000 | tf_op jit(solution)/shard_map/token_messages/pallas_call | solution.py:255
  5.9 3.1 %collective-permute-start = (bf16[2,4,48,256]{3,2,1,0:T(8,128)(2,1)}, bf16[2,4,48,256]{3,2,1,0:T(8,128)(2,1)S(1)}, u32[]{:S(2)}, u32[]{:S(2)}) collective-permute-start(bf16[2,4,48,256]{3,2,1,0:T(8,128)(2,1)} %get-tuple-element.43), channel_id=1, source_target_pairs={{0,2},{1,3},{2,0},{3,1},{4,6},{5,7},{6,4},{7,5},{8,10},{9,11},{10,... | collective-permute-start | bytes 589832 | tf_op jit(solution)/shard_map/ppermute | solution.py:764
  9.0 2.6 %collective-permute-start.1 = (bf16[2,4,48,256]{3,2,1,0:T(8,128)(2,1)}, bf16[2,4,48,256]{3,2,1,0:T(8,128)(2,1)S(1)}, u32[]{:S(2)}, u32[]{:S(2)}) collective-permute-start(bf16[2,4,48,256]{3,2,1,0:T(8,128)(2,1)} %get-tuple-element.44), channel_id=1, source_target_pairs={{0,4},{1,5},{2,6},{3,7},{4,0},{5,1},{6,2},{7,3},{8,12},{9,13},{10,... | collective-permute-start | bytes 589832 | tf_op jit(solution)/shard_map/ppermute | solution.py:764
  11.6 0.0 collective-permute-start.2
  11.6 0.0 copy-done.7
  11.6 8.8 %pair_bias.1 = f32[16,64,256]{2,1,0:T(8,128)S(1)} custom-call(bf16[2,128,64,128]{3,2,1,0:T(8,128)(2,1)S(1)} %bitcast.20, bf16[16,128]{1,0:T(8,128)(2,1)S(1)} %bitcast.21, s32[1,64]{1,0:T(1,128)S(1)} %bitcast.23), custom_call_target="tpu_custom_call" | custom-call | flops 6000000000 | bytes 5000000 | tf_op jit(solution)/shard_map/pair_bias/pallas_call | solution.py:397
  20.4 0.0 copy-start
  20.5 0.9 convert_element_type.21
  21.4 0.0 collective-permute-done.refs_1_
  21.4 5.0 %collective-permute-done.1.refs_2_ = bf16[2,4,48,256]{3,2,1,0:T(8,128)(2,1)S(1)} collective-permute-done((bf16[2,4,48,256]{3,2,1,0:T(8,128)(2,1)}, bf16[2,4,48,256]{3,2,1,0:T(8,128)(2,1)S(1)}, u32[]{:S(2)}, u32[]{:S(2)}) %collective-permute-start.1) | collective-permute-done | bytes 196640 | tf_op jit(solution)/shard_map/ppermute | solution.py:764
  26.4 0.0 collective-permute-done.2.refs_3_
  26.4 6.7 %all-to-all-start = ((f16[16,64,256]{2,1,0:T(8,128)(2,1)}), f16[16,64,256]{2,1,0:T(8,128)(2,1)S(1)}, u32[]{:S(2)}, u32[]{:S(2)}) async-start(f16[16,64,256]{2,1,0:T(8,128)(2,1)} %convert_element_type.21), calls=%async_computation | async-start | bytes 1048576 | tf_op jit(solution)/shard_map/all_to_all | solution.py:781
  33.1 0.0 copy-done
  33.2 0.1 pad_maximum_fusion
  33.2 0.5 collective-permute-start.3
  33.7 3.1 %own_rows.1 = (f32[768,128]{1,0:T(8,128)}, f32[768,128]{1,0:T(8,128)}, f32[8,128]{1,0:T(8,128)}) custom-call(s32[1]{0:T(128)} %bitcast.4.row_ref, bf16[4,64,768]{2,1,0:T(8,128)(2,1)} %tokens_ref.3, s32[1,64]{1,0:T(1,128)} %bitcast.28, bf16[32,768]{1,0:T(8,128)(2,1)} %table_ref.3, bf16[768,768]{1,0:T(8,128)(2,1)} %refs_7_.1, bf16[4,64,768]{2,1,0:T(8,128)(2,1)} %cot_ref.1), custom_call_target="tpu_custom_call" | custom-call | flops 3000000000 | bytes 3000000 | tf_op jit(solution)/shard_map/own_rows/pallas_call | solution.py:303
  36.7 0.0 collective-permute-done.3.refs_4_
  36.7 10.6 %all-to-all-done = f16[16,64,256]{2,1,0:T(8,128)(2,1)S(1)} async-done(((f16[16,64,256]{2,1,0:T(8,128)(2,1)}), f16[16,64,256]{2,1,0:T(8,128)(2,1)S(1)}, u32[]{:S(2)}, u32[]{:S(2)}) %all-to-all-start) | async-done | bytes 524320 | tf_op jit(solution)/shard_map/all_to_all | solution.py:781
  47.3 0.1 convert_element_type.22.refs_5_
  47.4 7.4 %attention.1 = (f32[16,200,128]{2,1,0:T(8,128)S(1)}, f32[16,72,256]{2,1,0:T(8,128)S(1)}) custom-call(s32[1]{0:T(128)} %bitcast.col_ref, bf16[2,4,48,256]{3,2,1,0:T(8,128)(2,1)S(1)} %copy-done, bf16[2,4,48,256]{3,2,1,0:T(8,128)(2,1)S(1)} %collective-permute-done.refs_1_, bf16[2,4,48,256]{3,2,1,0:T(8,128)(2,1)S(1)} %collective-permute-done.1.refs_2_, ...), custom_call_target="tpu_custom_call" | custom-call | flops 8000000000 | bytes 6000000 | tf_op jit(solution)/shard_map/attention/pallas_call | solution.py:542
  54.9 0.9 convert_element_type.24
  55.8 4.0 %all-to-all-start.1 = ((f16[16,72,256]{2,1,0:T(8,128)(2,1)}), f16[16,72,256]{2,1,0:T(8,128)(2,1)S(1)}, u32[]{:S(2)}, u32[]{:S(2)}) async-start(f16[16,72,256]{2,1,0:T(8,128)(2,1)} %convert_element_type.24), calls=%async_computation.1 | async-start | bytes 1179648 | tf_op jit(solution)/shard_map/all_to_all | solution.py:786
  59.8 1.1 convert_element_type.23
  60.8 7.8 %pair_units.1 = (bf16[32,256,512]{2,1,0:T(8,128)(2,1)}, f32[32,8,512]{2,1,0:T(8,128)}) custom-call(bf16[2,128,64,128]{3,2,1,0:T(8,128)(2,1)} %bitcast.19), custom_call_target="tpu_custom_call" | custom-call | flops 6000000000 | bytes 12000000 | tf_op jit(solution)/shard_map/pair_units/pallas_call | solution.py:427
  68.6 6.6 %all-to-all-done.1 = f16[16,72,256]{2,1,0:T(8,128)(2,1)S(1)} async-done(((f16[16,72,256]{2,1,0:T(8,128)(2,1)}), f16[16,72,256]{2,1,0:T(8,128)(2,1)S(1)}, u32[]{:S(2)}, u32[]{:S(2)}) %all-to-all-start.1) | async-done | bytes 589856 | tf_op jit(solution)/shard_map/all_to_all | solution.py:786
  75.2 0.1 convert_element_type.25
  75.3 1.6 %collective-permute-start.4 = (f16[16,72,256]{2,1,0:T(8,128)(2,1)S(1)}, f16[16,72,256]{2,1,0:T(8,128)(2,1)S(1)}, u32[]{:S(2)}, u32[]{:S(2)}) collective-permute-start(f16[16,72,256]{2,1,0:T(8,128)(2,1)S(1)} %all-to-all-done.1), channel_id=1, source_target_pairs={{0,16},{16,0},{1,17},{17,1},{2,18},{18,2},{3,19},{19,3},{4,20},{20... | collective-permute-start | bytes 1769480 | tf_op jit(solution)/shard_map/ppermute | solution.py:741
  76.9 0.1 slice_multiply_fusion.1.grads_ref
  77.0 4.5 %all-to-all-start.2 = ((f16[16,200,128]{2,1,0:T(8,128)(2,1)}), f16[16,200,128]{2,1,0:T(8,128)(2,1)}, u32[]{:S(2)}, u32[]{:S(2)}) async-start(f16[16,200,128]{2,1,0:T(8,128)(2,1)} %convert_element_type.23), calls=%async_computation.2 | async-start | bytes 1638400 | tf_op jit(solution)/shard_map/all_to_all | solution.py:792
  81.5 3.4 %copy-done.8 = bf16[32,256,512]{2,1,0:T(8,128)(2,1)S(1)} copy-done((bf16[32,256,512]{2,1,0:T(8,128)(2,1)S(1)}, bf16[32,256,512]{2,1,0:T(8,128)(2,1)}, u32[]{:S(2)}) %copy-start.8) | copy-done | bytes 8388632
  84.9 4.3 %pair_weight.1 = f32[16,128]{1,0:T(8,128)S(1)} custom-call(bf16[32,256,512]{2,1,0:T(8,128)(2,1)S(1)} %copy-done.8, f32[16,64,256]{2,1,0:T(8,128)S(1)} %slice_multiply_fusion.1.grads_ref), custom_call_target="tpu_custom_call" | custom-call | flops 5000000000 | bytes 100000 | tf_op jit(solution)/shard_map/pair_weight/pallas_call | solution.py:696
  89.2 1.6 %collective-permute-start.7 = (f32[16,128]{1,0:T(8,128)S(1)}, f32[16,128]{1,0:T(8,128)S(1)}, u32[]{:S(2)}, u32[]{:S(2)}) collective-permute-start(f32[16,128]{1,0:T(8,128)S(1)} %pair_weight.1), channel_id=1, source_target_pairs={{0,24},{8,16},{16,8},{24,0},{1,25},{9,17},{17,9},{25,1},{2,26},{10... | collective-permute-start | bytes 24584 | tf_op jit(solution)/shard_map/ppermute | solution.py:799
  90.8 0.4 collective-permute-start.6
  91.2 1.5 %collective-permute-start.5 = (f32[16,128]{1,0:T(8,128)S(1)}, f32[16,128]{1,0:T(8,128)S(1)}, u32[]{:S(2)}, u32[]{:S(2)}) collective-permute-start(f32[16,128]{1,0:T(8,128)S(1)} %pair_weight.1), channel_id=1, source_target_pairs={{0,16},{16,0},{1,17},{17,1},{2,18},{18,2},{3,19},{19,3},{4,20},{20... | collective-permute-start | bytes 24584 | tf_op jit(solution)/shard_map/ppermute | solution.py:741
  92.7 0.0 collective-permute-done.4
  92.7 0.1 convert_element_type.26
  92.9 1.0 collective-permute-done.7
  93.9 0.6 collective-permute-done.6
  94.5 0.4 collective-permute-done.5
  94.9 0.2 fusion.refs_2_
  95.0 1.4 %collective-permute-start.10 = (f32[16,128]{1,0:T(8,128)S(1)}, f32[16,128]{1,0:T(8,128)S(1)}, u32[]{:S(2)}, u32[]{:S(2)}) collective-permute-start(f32[16,128]{1,0:T(8,128)S(1)} %add_add_fusion), channel_id=1, source_target_pairs={{0,3},{1,2},{2,1},{3,0},{4,7},{5,6},{6,5},{7,4},{8,11},{9,10},{10,... | collective-permute-start | bytes 24584 | tf_op jit(solution)/shard_map/ppermute | solution.py:764
  96.4 0.4 collective-permute-start.9
  96.8 0.2 collective-permute-start.8
  97.0 6.4 %pair_backward.1 = bf16[2,128,64,128]{3,2,1,0:T(8,128)(2,1)} custom-call(bf16[32,256,512]{2,1,0:T(8,128)(2,1)S(1)} %copy-done.8, f32[32,8,512]{2,1,0:T(8,128)S(1)} %copy-done.11, f32[16,64,256]{2,1,0:T(8,128)S(1)} %fusion.refs_2_, bf16[16,128]{1,0:T(8,128)(2,1)S(1)} %bitcast.22), custom_call_target="tpu_custom_call" | custom-call | flops 8000000000 | bytes 100000 | tf_op jit(solution)/shard_map/pair_backward/pallas_call | solution.py:714
  103.4 0.0 collective-permute-done.10
  103.4 0.0 collective-permute-done.9
  103.4 0.0 collective-permute-done.8
  103.4 0.0 all-to-all-done.2
  103.4 0.0 copy-start.2
  103.4 0.0 copy-start.3
  103.4 0.0 copy-start.12
  103.4 1.4 %convert_element_type.27.refs_0_ = f32[16,200,128]{2,1,0:T(8,128)S(1)} convert(f16[16,200,128]{2,1,0:T(8,128)(2,1)} %all-to-all-done.2) | non-fusion elementwise | flops 409600 | bytes 2457600 | tf_op jit(solution)/shard_map/convert_element_type | solution.py:811
  104.8 0.0 copy-done.4
  104.9 0.0 copy-done.2
  104.9 0.4 copy-done.3
  105.3 1.0 copy-done.10
  106.3 2.1 %token_back.1 = bf16[128,768]{1,0:T(8,128)(2,1)S(1)} custom-call(f32[16,200,128]{2,1,0:T(8,128)S(1)} %convert_element_type.27.refs_0_, f32[768,128]{1,0:T(8,128)S(1)} %copy-done.9, f32[768,128]{1,0:T(8,128)S(1)} %copy-done.10, f32[8,128]{1,0:T(8,128)S(1)} %copy-done.12, bf16[768,768]{1,0:T(8,128)(2,1)S(1)} %copy-done.2, bf16[768,768]{1,0:T(8,128)(2,1)S(1)} %copy-done.3, ...), custom_call_target="tpu_custom_call" | custom-call | flops 4000000000 | bytes 8000000 | tf_op jit(solution)/shard_map/token_back/pallas_call | solution.py:615
  108.4 1.7 %collective-permute-start.11 = (bf16[2,64,768]{2,1,0:T(8,128)(2,1)S(1)}, bf16[2,64,768]{2,1,0:T(8,128)(2,1)S(1)}, u32[]{:S(2)}, u32[]{:S(2)}) collective-permute-start(bf16[2,64,768]{2,1,0:T(8,128)(2,1)S(1)} %bitcast.17), channel_id=1, source_target_pairs={{0,8},{8,0},{1,9},{9,1},{2,10},{10,2},{3,11},{11,3},{4,12},{12,4},... | collective-permute-start | bytes 589832 | tf_op jit(solution)/shard_map/ppermute | solution.py:741
  110.1 2.4 %collective-permute-start.12 = (f32[16,128]{1,0:T(8,128)S(1)}, f32[16,128]{1,0:T(8,128)S(1)}, u32[]{:S(2)}, u32[]{:S(2)}) collective-permute-start(f32[16,128]{1,0:T(8,128)S(1)} %add_multiply_fusion), channel_id=1, source_target_pairs={{0,4},{1,5},{2,6},{3,7},{4,0},{5,1},{6,2},{7,3},{8,12},{9,13},{10,... | collective-permute-start | bytes 24584 | tf_op jit(solution)/shard_map/ppermute | solution.py:764
  112.5 3.1 %collective-permute-done.11 = bf16[2,64,768]{2,1,0:T(8,128)(2,1)S(1)} collective-permute-done((bf16[2,64,768]{2,1,0:T(8,128)(2,1)S(1)}, bf16[2,64,768]{2,1,0:T(8,128)(2,1)S(1)}, u32[]{:S(2)}, u32[]{:S(2)}) %collective-permute-start.11) | collective-permute-done | bytes 196640 | tf_op jit(solution)/shard_map/ppermute | solution.py:741
  115.6 0.8 pad_maximum_fusion.1
  116.4 0.0 collective-permute-done.12
  116.4 0.6 add_bitcast_fusion
  (25 shorter events, 0.2 us)
Async XLA Ops:
  0.6 11.0 %copy-start.1 = (bf16[256,64,128]{2,1,0:T(8,128)(2,1)S(1)}, bf16[256,64,128]{2,1,0:T(8,128)(2,1)}, u32[]{:S(2)}) copy-start(bf16[256,64,128]{2,1,0:T(8,128)(2,1)} %param.15) | copy-start | bytes 12582916
  0.6 11.0 %copy-start.6 = (bf16[128,16]{0,1:T(8,128)(2,1)S(1)}, bf16[128,16]{0,1:T(8,128)(2,1)}, u32[]{:S(2)}) copy-start(bf16[128,16]{0,1:T(8,128)(2,1)} %param.16) | copy-start | bytes 12292
  0.7 11.0 %copy-start.7 = (s32[64]{0:T(128)S(1)}, s32[64]{0:T(128)}, u32[]{:S(2)}) copy-start(s32[64]{0:T(128)} %param.14) | copy-start | bytes 772
  5.9 15.4 %collective-permute-start = (bf16[2,4,48,256]{3,2,1,0:T(8,128)(2,1)}, bf16[2,4,48,256]{3,2,1,0:T(8,128)(2,1)S(1)}, u32[]{:S(2)}, u32[]{:S(2)}) collective-permute-start(bf16[2,4,48,256]{3,2,1,0:T(8,128)(2,1)} %get-tuple-element.43), channel_id=1, source_target_pairs={{0,2},{1,3},{2,0},{3,1},{4,6},{5,7},{6,4},{7,5},{8,10},{9,11},{10,... | collective-permute-start | bytes 589832 | tf_op jit(solution)/shard_map/ppermute | solution.py:764
  9.0 17.4 %collective-permute-start.1 = (bf16[2,4,48,256]{3,2,1,0:T(8,128)(2,1)}, bf16[2,4,48,256]{3,2,1,0:T(8,128)(2,1)S(1)}, u32[]{:S(2)}, u32[]{:S(2)}) collective-permute-start(bf16[2,4,48,256]{3,2,1,0:T(8,128)(2,1)} %get-tuple-element.44), channel_id=1, source_target_pairs={{0,4},{1,5},{2,6},{3,7},{4,0},{5,1},{6,2},{7,3},{8,12},{9,13},{10,... | collective-permute-start | bytes 589832 | tf_op jit(solution)/shard_map/ppermute | solution.py:764
  11.6 14.8 %collective-permute-start.2 = (bf16[2,4,48,256]{3,2,1,0:T(8,128)(2,1)}, bf16[2,4,48,256]{3,2,1,0:T(8,128)(2,1)S(1)}, u32[]{:S(2)}, u32[]{:S(2)}) collective-permute-start(bf16[2,4,48,256]{3,2,1,0:T(8,128)(2,1)} %get-tuple-element.45), channel_id=1, source_target_pairs={{0,6},{1,7},{2,4},{3,5},{4,2},{5,3},{6,0},{7,1},{8,14},{9,15},{10,... | collective-permute-start | bytes 589832 | tf_op jit(solution)/shard_map/ppermute | solution.py:764
  20.4 12.6 %copy-start = (bf16[2,4,48,256]{3,2,1,0:T(8,128)(2,1)S(1)}, bf16[2,4,48,256]{3,2,1,0:T(8,128)(2,1)}, u32[]{:S(2)}) copy-start(bf16[2,4,48,256]{3,2,1,0:T(8,128)(2,1)} %get-tuple-element.46.refs_0_) | copy-start | bytes 589828
  26.4 20.9 %all-to-all-start = ((f16[16,64,256]{2,1,0:T(8,128)(2,1)}), f16[16,64,256]{2,1,0:T(8,128)(2,1)S(1)}, u32[]{:S(2)}, u32[]{:S(2)}) async-start(f16[16,64,256]{2,1,0:T(8,128)(2,1)} %convert_element_type.21), calls=%async_computation | async-start | bytes 1048576 | tf_op jit(solution)/shard_map/all_to_all | solution.py:781
  33.2 3.5 %collective-permute-start.3 = (bf16[4,4,48,256]{3,2,1,0:T(8,128)(2,1)S(1)}, bf16[4,4,48,256]{3,2,1,0:T(8,128)(2,1)S(1)}, u32[]{:S(2)}, u32[]{:S(2)}) collective-permute-start(bf16[4,4,48,256]{3,2,1,0:T(8,128)(2,1)S(1)} %pad_maximum_fusion), channel_id=1, source_target_pairs={{0,1},{1,0},{2,3},{3,2},{4,5},{5,4},{6,7},{7,6},{8,9},{9,8},{10,11... | collective-permute-start | bytes 1179656 | tf_op jit(solution)/shard_map/ppermute | solution.py:764
  55.8 19.4 %all-to-all-start.1 = ((f16[16,72,256]{2,1,0:T(8,128)(2,1)}), f16[16,72,256]{2,1,0:T(8,128)(2,1)S(1)}, u32[]{:S(2)}, u32[]{:S(2)}) async-start(f16[16,72,256]{2,1,0:T(8,128)(2,1)} %convert_element_type.24), calls=%async_computation.1 | async-start | bytes 1179648 | tf_op jit(solution)/shard_map/all_to_all | solution.py:786
  75.3 17.4 %collective-permute-start.4 = (f16[16,72,256]{2,1,0:T(8,128)(2,1)S(1)}, f16[16,72,256]{2,1,0:T(8,128)(2,1)S(1)}, u32[]{:S(2)}, u32[]{:S(2)}) collective-permute-start(f16[16,72,256]{2,1,0:T(8,128)(2,1)S(1)} %all-to-all-done.1), channel_id=1, source_target_pairs={{0,16},{16,0},{1,17},{17,1},{2,18},{18,2},{3,19},{19,3},{4,20},{20... | collective-permute-start | bytes 1769480 | tf_op jit(solution)/shard_map/ppermute | solution.py:741
  77.0 26.4 %all-to-all-start.2 = ((f16[16,200,128]{2,1,0:T(8,128)(2,1)}), f16[16,200,128]{2,1,0:T(8,128)(2,1)}, u32[]{:S(2)}, u32[]{:S(2)}) async-start(f16[16,200,128]{2,1,0:T(8,128)(2,1)} %convert_element_type.23), calls=%async_computation.2 | async-start | bytes 1638400 | tf_op jit(solution)/shard_map/all_to_all | solution.py:792
  81.5 3.4 %copy-start.8 = (bf16[32,256,512]{2,1,0:T(8,128)(2,1)S(1)}, bf16[32,256,512]{2,1,0:T(8,128)(2,1)}, u32[]{:S(2)}) copy-start(bf16[32,256,512]{2,1,0:T(8,128)(2,1)} %get-tuple-element.62.normed_ref.refs_0_) | copy-start | bytes 25165828
  89.2 4.7 %collective-permute-start.7 = (f32[16,128]{1,0:T(8,128)S(1)}, f32[16,128]{1,0:T(8,128)S(1)}, u32[]{:S(2)}, u32[]{:S(2)}) collective-permute-start(f32[16,128]{1,0:T(8,128)S(1)} %pair_weight.1), channel_id=1, source_target_pairs={{0,24},{8,16},{16,8},{24,0},{1,25},{9,17},{17,9},{25,1},{2,26},{10... | collective-permute-start | bytes 24584 | tf_op jit(solution)/shard_map/ppermute | solution.py:799
  90.8 3.7 %collective-permute-start.6 = (f32[16,128]{1,0:T(8,128)S(1)}, f32[16,128]{1,0:T(8,128)S(1)}, u32[]{:S(2)}, u32[]{:S(2)}) collective-permute-start(f32[16,128]{1,0:T(8,128)S(1)} %pair_weight.1), channel_id=1, source_target_pairs={{0,8},{8,0},{1,9},{9,1},{2,10},{10,2},{3,11},{11,3},{4,12},{12,4},... | collective-permute-start | bytes 24584 | tf_op jit(solution)/shard_map/ppermute | solution.py:741
  91.2 3.7 %collective-permute-start.5 = (f32[16,128]{1,0:T(8,128)S(1)}, f32[16,128]{1,0:T(8,128)S(1)}, u32[]{:S(2)}, u32[]{:S(2)}) collective-permute-start(f32[16,128]{1,0:T(8,128)S(1)} %pair_weight.1), channel_id=1, source_target_pairs={{0,16},{16,0},{1,17},{17,1},{2,18},{18,2},{3,19},{19,3},{4,20},{20... | collective-permute-start | bytes 24584 | tf_op jit(solution)/shard_map/ppermute | solution.py:741
  94.9 2.1 %copy-start.11 = (f32[32,8,512]{2,1,0:T(8,128)S(1)}, f32[32,8,512]{2,1,0:T(8,128)}, u32[]{:S(2)}) copy-start(f32[32,8,512]{2,1,0:T(8,128)} %get-tuple-element.63.refs_1_) | copy-start | bytes 1572868
  95.0 8.3 %collective-permute-start.10 = (f32[16,128]{1,0:T(8,128)S(1)}, f32[16,128]{1,0:T(8,128)S(1)}, u32[]{:S(2)}, u32[]{:S(2)}) collective-permute-start(f32[16,128]{1,0:T(8,128)S(1)} %add_add_fusion), channel_id=1, source_target_pairs={{0,3},{1,2},{2,1},{3,0},{4,7},{5,6},{6,5},{7,4},{8,11},{9,10},{10,... | collective-permute-start | bytes 24584 | tf_op jit(solution)/shard_map/ppermute | solution.py:764
  96.4 7.0 %collective-permute-start.9 = (f32[16,128]{1,0:T(8,128)S(1)}, f32[16,128]{1,0:T(8,128)S(1)}, u32[]{:S(2)}, u32[]{:S(2)}) collective-permute-start(f32[16,128]{1,0:T(8,128)S(1)} %add_add_fusion), channel_id=1, source_target_pairs={{0,2},{1,3},{2,0},{3,1},{4,6},{5,7},{6,4},{7,5},{8,10},{9,11},{10,... | collective-permute-start | bytes 24584 | tf_op jit(solution)/shard_map/ppermute | solution.py:764
  96.8 6.6 %collective-permute-start.8 = (f32[16,128]{1,0:T(8,128)S(1)}, f32[16,128]{1,0:T(8,128)S(1)}, u32[]{:S(2)}, u32[]{:S(2)}) collective-permute-start(f32[16,128]{1,0:T(8,128)S(1)} %add_add_fusion), channel_id=1, source_target_pairs={{0,1},{1,0},{2,3},{3,2},{4,5},{5,4},{6,7},{7,6},{8,9},{9,8},{10,11... | collective-permute-start | bytes 24584 | tf_op jit(solution)/shard_map/ppermute | solution.py:764
  97.0 7.9 %copy-start.4 = (bf16[768,768]{1,0:T(8,128)(2,1)S(1)}, bf16[768,768]{1,0:T(8,128)(2,1)}, u32[]{:S(2)}) copy-start(bf16[768,768]{1,0:T(8,128)(2,1)} %refs_6_.1) | copy-start | bytes 3538948
  97.0 7.9 %copy-start.5 = (bf16[768,768]{1,0:T(8,128)(2,1)S(1)}, bf16[768,768]{1,0:T(8,128)(2,1)}, u32[]{:S(2)}) copy-start(bf16[768,768]{1,0:T(8,128)(2,1)} %refs_7_.1) | copy-start | bytes 3538948
  97.0 7.9 %copy-start.9 = (f32[768,128]{1,0:T(8,128)S(1)}, f32[768,128]{1,0:T(8,128)}, u32[]{:S(2)}) copy-start(f32[768,128]{1,0:T(8,128)} %get-tuple-element.70.refs_1_) | copy-start | bytes 1179652
  103.4 1.5 %copy-start.2 = (bf16[768,768]{1,0:T(8,128)(2,1)S(1)}, bf16[768,768]{1,0:T(8,128)(2,1)}, u32[]{:S(2)}) copy-start(bf16[768,768]{1,0:T(8,128)(2,1)} %refs_4_.3) | copy-start | bytes 3538948
  103.4 1.9 %copy-start.3 = (bf16[768,768]{1,0:T(8,128)(2,1)S(1)}, bf16[768,768]{1,0:T(8,128)(2,1)}, u32[]{:S(2)}) copy-start(bf16[768,768]{1,0:T(8,128)(2,1)} %refs_5_.1) | copy-start | bytes 3538948
  103.4 1.9 %copy-start.12 = (f32[8,128]{1,0:T(8,128)S(1)}, f32[8,128]{1,0:T(8,128)}, u32[]{:S(2)}) copy-start(f32[8,128]{1,0:T(8,128)} %get-tuple-element.72.refs_3_) | copy-start | bytes 12292
  105.3 1.0 copy-start.10
  108.4 7.2 %collective-permute-start.11 = (bf16[2,64,768]{2,1,0:T(8,128)(2,1)S(1)}, bf16[2,64,768]{2,1,0:T(8,128)(2,1)S(1)}, u32[]{:S(2)}, u32[]{:S(2)}) collective-permute-start(bf16[2,64,768]{2,1,0:T(8,128)(2,1)S(1)} %bitcast.17), channel_id=1, source_target_pairs={{0,8},{8,0},{1,9},{9,1},{2,10},{10,2},{3,11},{11,3},{4,12},{12,4},... | collective-permute-start | bytes 589832 | tf_op jit(solution)/shard_map/ppermute | solution.py:741
  110.1 6.3 %collective-permute-start.12 = (f32[16,128]{1,0:T(8,128)S(1)}, f32[16,128]{1,0:T(8,128)S(1)}, u32[]{:S(2)}, u32[]{:S(2)}) collective-permute-start(f32[16,128]{1,0:T(8,128)S(1)} %add_multiply_fusion), channel_id=1, source_target_pairs={{0,4},{1,5},{2,6},{3,7},{4,0},{5,1},{6,2},{7,3},{8,12},{9,13},{10,... | collective-permute-start | bytes 24584 | tf_op jit(solution)/shard_map/ppermute | solution.py:764

commit v8 on v2

--- a/solution.py
+++ b/solution.py
@@ -347,7 +347,7 @@
             flat_ref[pl.ds(base + k + m, H, stride=whole), :] = bias[:, lanes]
         return carry
 
-    lax.fori_loop(0, count // MANY, step, 0, unroll=2)
+    lax.fori_loop(0, count // MANY, step, 0, unroll=8)
 
     @pl.when(pl.program_id(0) == pl.num_programs(0) - 1)
     def _():
@@ -402,7 +402,7 @@
         inv_ref[n] = jnp.broadcast_to(inv_std, inv_ref.shape[1:])
         return carry
 
-    lax.fori_loop(0, normed_ref.shape[0], step, 0, unroll=2)
+    lax.fori_loop(0, normed_ref.shape[0], step, 0, unroll=8)
 
 
 def pair_units(pair):
@@ -510,11 +510,13 @@
 
     @pl.when(step == pl.num_programs(0) - 1)
     def _():
+        whole = row_count // 2
         for head in range(n_row * n_col):
             sums = sum_ref[head]
+            sums = jnp.concatenate([sums[:, :whole], sums[:, whole:]], axis=0).T
             shift = shift_of(jnp.max(jnp.abs(sums), axis=0, keepdims=True))
-            grad_bias_ref[head, :tok_col, :] = sums * jnp.exp2(shift)
-            grad_bias_ref[head, tok_col:, :] = jnp.broadcast_to(shift, (8, row_count))
+            grad_bias_ref[head, :whole, :] = sums * jnp.exp2(shift)
+            grad_bias_ref[head, whole:, :] = jnp.broadcast_to(shift, (8, 2 * tok_col))
 
 
 def attention(col, arrived, other, bias, n_row):
@@ -524,7 +526,7 @@
     half = arrived[0].shape[-1] // tok_col // n_row
     width = half * tok_col
     back_shape = (n_row * n_col, 4 * CH + 8, width)
-    bias_shape = (n_row * n_col, tok_col + 8, row_count)
+    bias_shape = (n_row * n_col, row_count // 2 + 8, 2 * tok_col)
     return pl.pallas_call(
         attention_kernel,
         out_shape=[
@@ -618,53 +620,40 @@
     )(back, slope, normed, inv_std, *weights)
 
 
-def flatten(grads_ref, flat_ref):
-    whole = flat_ref.shape[0] // H
-    for h in range(H):
-        grads = grads_ref[h]
-        both = jnp.concatenate([grads[:, :whole], grads[:, whole:]], axis=0)
-        flat_ref[h * whole : (h + 1) * whole, :] = both.T
-
-
 def flat_columns(flat_ref, k, many):
     whole = flat_ref.shape[0] // H
     grads = [flat_ref[pl.ds(k + m, H, stride=whole), :] for m in range(many)]
     return jnp.concatenate(halves(jnp.concatenate(grads, axis=1)), axis=0)
 
 
-def pair_weight_kernel(normed_ref, grads_ref, part_ref, flat_ref):
+def pair_weight_kernel(normed_ref, grads_ref, part_ref):
     chunks, width, _ = normed_ref.shape
     base = pl.program_id(0) * chunks
 
     @pl.when(pl.program_id(0) == 0)
     def _():
         part_ref[...] = jnp.zeros_like(part_ref)
-        flatten(grads_ref, flat_ref)
 
     def step(n, carry):
-        return carry + matmul_nt(normed_ref[n], flat_columns(flat_ref, (base + n) * MANY, MANY))
-
-    parts = lax.fori_loop(0, chunks, step, jnp.zeros((width, 2 * H), jnp.float32), unroll=2)
+        return carry + matmul_nt(normed_ref[n], flat_columns(grads_ref, (base + n) * MANY, MANY))
+
+    parts = lax.fori_loop(0, chunks, step, jnp.zeros((width, 2 * H), jnp.float32), unroll=8)
     parts = parts[:, :H] + parts[:, H:]
     part_ref[...] += (parts[: width // 2] + parts[width // 2 :]).T
 
 
-def pair_back_kernel(factor, normed_ref, inv_ref, grads_ref, weight_ref, out_ref, flat_ref):
+def pair_back_kernel(factor, normed_ref, inv_ref, grads_ref, weight_ref, out_ref):
     _, count, length, width = out_ref.shape
     weight = weight_ref[...].astype(jnp.float32)
     weight = halves(weight - jnp.mean(weight, axis=1, keepdims=True))
     weight = jnp.concatenate([weight[0], weight[0], weight[1], weight[1]], axis=0).T
     base = pl.program_id(0) * count
 
-    @pl.when(pl.program_id(0) == 0)
-    def _():
-        flatten(grads_ref, flat_ref)
-
     def step(n, carry):
         k = n * MANY
         normed = normed_ref[n].astype(jnp.float32)
         normed = normed[:width] + normed[width:]
-        grads = flat_columns(flat_ref, base + k, MANY)
+        grads = flat_columns(grads_ref, base + k, MANY)
         grad_in = matmul(weight, jnp.concatenate([grads, grads], axis=0))
         overlap = jnp.mean(grad_in * normed, axis=0, keepdims=True)
         result = (grad_in - normed * overlap) * (inv_ref[n, :1] * factor)
@@ -673,11 +662,10 @@
             out_ref[p, pl.ds(k, MANY)] = result[:, p * length : (p + 1) * length]
         return carry
 
-    lax.fori_loop(0, count // MANY, step, 0, unroll=2)
+    lax.fori_loop(0, count // MANY, step, 0, unroll=8)
 
 
 def pair_weight(normed, grads):
-    heads, length, rows = grads.shape
     part_shape = (H, normed.shape[1] // 2)
     return pl.pallas_call(
         pair_weight_kernel,
@@ -685,7 +673,6 @@
         grid=(STEPS,),
         in_specs=[split_spec(normed.shape), whole_spec(grads.shape)],
         out_specs=whole_spec(part_shape),
-        scratch_shapes=[pltpu.VMEM((H * rows // 2, 2 * length), jnp.float32)],
         compiler_params=params(24),
         cost_estimate=pl.CostEstimate(
             flops=5_000_000_000, bytes_accessed=100_000, transcendentals=0
@@ -708,7 +695,6 @@
             whole_spec(weight_t.shape),
         ],
         out_specs=pl.BlockSpec((2, whole // STEPS, tok_col, width), lambda i: (0, i, 0, 0)),
-        scratch_shapes=[pltpu.VMEM((H * whole, 2 * tok_col), jnp.float32)],
         compiler_params=params(24),
         cost_estimate=pl.CostEstimate(
             flops=8_000_000_000, bytes_accessed=100_000, transcendentals=0
@@ -720,7 +706,8 @@
 
 def unscaled(block, rows):
     block = block.astype(jnp.float32)
-    return block[:, :rows] * jnp.exp2(-block[:, rows : rows + 1])
+    block = block[:, :rows] * jnp.exp2(-block[:, rows : rows + 1])
+    return block.reshape(-1, block.shape[2])
 
 
 def swap(block, axis):
@@ -778,26 +765,26 @@
     back = lax.all_to_all(back, ("row", "col"), 0, 0, tiled=True)
 
     other_bias = swap(grad_bias, "samp")
-    own_bias = unscaled(grad_bias, tok_col)
+    own_bias = unscaled(grad_bias, row_count // 2)
     part = pair_weight(pair_normed, own_bias)
     samp_part = swap(part, "samp")
     row_part = swap(part, "row")
     both_part = lax.ppermute(part, ("samp", "row"), [(n, 3 - n) for n in range(4)])
     other_bias, part = lax.optimization_barrier((other_bias, part))
-    grads = own_bias + unscaled(other_bias, tok_col)
-    part = (part + samp_part) + (row_part + both_part)
-    grads, part = lax.optimization_barrier((grads, part))
-    sums = (send(part, 1), send(part, 2), send(part, 3))
+    grads = own_bias + unscaled(other_bias, row_count // 2)
     pair_grad = pair_backward(
         pair.shape, pair_normed, pair_inv, grads, weight_t, total_tokens / samples
     )
 
-    pair_grad, back, sums = lax.optimization_barrier((pair_grad, back, sums))
-    part = (part + sums[0]) + (sums[1] + sums[2])
+    pair_grad, back, sums = lax.optimization_barrier(
+        (pair_grad, back, (part, samp_part, row_part, both_part))
+    )
+    part = (sums[0] + sums[1]) + (sums[2] + sums[3])
+    sums = (send(part, 1), send(part, 2), send(part, 3))
+    token_half = token_back(back.astype(jnp.float32), *own, weights)
+    token_half, sums = lax.optimization_barrier((token_half, sums))
+    part = ((part + sums[0]) + (sums[1] + sums[2])) / samples
     last = send(part, 4)
-    token_half = token_back(back.astype(jnp.float32), *own, weights)
-    token_half, last = lax.optimization_barrier((token_half, last))
-    part = part + last
     token_half = token_half.reshape(half, tok_col, D)
     other_half = swap(token_half, "row")
     first = row_index == 0
@@ -805,7 +792,8 @@
         [jnp.where(first, token_half, other_half), jnp.where(first, other_half, token_half)],
         axis=0,
     )
-    return (token_grad, pair_grad, part.T / samples)
+    token_grad, last = lax.optimization_barrier((token_grad, last))
+    return (token_grad, pair_grad, (part + last).T)
 
 
 def body(*args):

time: 119 us -> 125 us (1.050)
  waiting for transfers between devices: 25.7 us -> 36 us
  Pallas kernels: 48.7 us -> 41.4 us
  local copies, waits for them, and re-layouts: 3.47 us -> 7.74 us
    all_to_all x1, waiting for transfers between devices: 0.01 us -> 9.72 us  [body_heads(): back = lax.all_to_all(back, ('row', 'col'), 0, 0, tiled=True)]
    unnamed x28, local copies, waits for them, and re-layouts: 3.44 us -> 7.71 us
    pallas_call x1, Pallas kernels: 7.68 us -> 5.38 us  [pair_backward(): pl.pallas_call(lambda *refs: pair_back_kernel(factor, *refs), out_shape=j...]
    pallas_call x1, Pallas kernels: 5.52 us -> 3.26 us  [pair_weight(): pl.pallas_call(pair_weight_kernel, out_shape=jax.ShapeDtypeStruct(part_sh...]
    ppermute x4, waiting for transfers between devices: 5.53 us -> 3.68 us  [swap(): return lax.ppermute(block, axis, [(0, 1), (1, 0)])]
    ppermute x8, waiting for transfers between devices: 4.07 us -> 5.72 us  [send(): return lax.ppermute(block, 'col', [(c, c ^ offset) for c in range(n_col)])]
    pallas_call x1, Pallas kernels: 9.78 us -> 8.13 us  [pair_bias(): pl.pallas_call(bias_kernel, out_shape=jax.ShapeDtypeStruct((H, tok_col, r...]
    pallas_call x1, Pallas kernels: 8.82 us -> 7.45 us  [pair_units(): pl.pallas_call(norm_kernel, out_shape=[jax.ShapeDtypeStruct(shapes[0], jn...]
  transfers between devices with their start and end apart: 16 -> 16, of which waited for: 6 -> 5; matrix products, arithmetic and copies ran while one was open for 5% -> 4% of each run, Pallas kernels for 31% -> 24%
where the time goes in v8:
time: 125 us
  Pallas kernels  41.4 us (33%)
  waiting for transfers between devices  36 us (29%)
  starting transfers between devices  32.2 us (26%)
  local copies, waits for them, and re-layouts  7.74 us (6%)
  other arithmetic  6.16 us (5%)
    all_to_all x1, waiting for transfers between devices, body_heads(): bias = lax.all_to_all(bias, ('row', 'col'), 0, 0, tiled=True)  10.6 us
    ppermute x8, starting transfers between devices, send(): return lax.ppermute(block, 'col', [(c, c ^ offset) for c in range(n_col)])  10.4 us
    all_to_all x1, waiting for transfers between devices, body_heads(): back = lax.all_to_all(back, ('row', 'col'), 0, 0, tiled=True)  9.72 us
    pallas_call x1, Pallas kernels, pair_bias(): pl.pallas_call(bias_kernel, out_shape=jax.ShapeDtypeStruct((H, tok_col, r...  8.13 us
    unnamed x28, local copies, waits for them, and re-layouts  7.71 us
    pallas_call x1, Pallas kernels, attention(): pl.pallas_call(attention_kernel, out_shape=[jax.ShapeDtypeStruct(back_sha...  7.67 us
    pallas_call x1, Pallas kernels, pair_units(): pl.pallas_call(norm_kernel, out_shape=[jax.ShapeDtypeStruct(shapes[0], jn...  7.45 us
    all_to_all x1, starting transfers between devices, body_heads(): bias = lax.all_to_all(bias, ('row', 'col'), 0, 0, tiled=True)  6.67 us
  transfers between devices with their start and end apart: 16, of which 5 were waited for; matrix products, arithmetic and copies ran while one was open for 4% of the time, Pallas kernels for 24%

profile of v8, /device:TPU:0, one launch (start us, length us, event | category | flops | bytes accessed | tf_op | source)
XLA Modules:
  0.0 124.5 jit_solution(17998667655610827304)
XLA Ops:
  0.6 0.0 copy-start.1
  0.6 0.0 copy-start.6
  0.7 0.0 copy-start.7
  0.7 4.3 %token_messages.1 = (bf16[2,4,48,256]{3,2,1,0:T(8,128)(2,1)}, bf16[2,4,48,256]{3,2,1,0:T(8,128)(2,1)}, bf16[2,4,48,256]{3,2,1,0:T(8,128)(2,1)}, bf16[2,4,48,256]{3,2,1,0:T(8,128)(2,1)}) custom-call(s32[1]{0:T(128)} %bitcast.4.row_ref, s32[1]{0:T(128)} %bitcast.col_ref, bf16[4,64,768]{2,1,0:T(8,128)(2,1)} %tokens_ref.3, s32[1,64]{1,0:T(1,128)} %bitcast.27, ...), custom_call_target="tpu_custom_call" | custom-call | flops 4000000000 | bytes 4000000 | tf_op jit(solution)/shard_map/token_messages/pallas_call | solution.py:245
  5.0 3.0 %collective-permute-start = (bf16[2,4,48,256]{3,2,1,0:T(8,128)(2,1)}, bf16[2,4,48,256]{3,2,1,0:T(8,128)(2,1)S(1)}, u32[]{:S(2)}, u32[]{:S(2)}) collective-permute-start(bf16[2,4,48,256]{3,2,1,0:T(8,128)(2,1)} %get-tuple-element.44), channel_id=1, source_target_pairs={{0,2},{1,3},{2,0},{3,1},{4,6},{5,7},{6,4},{7,5},{8,10},{9,11},{10,... | collective-permute-start | bytes 589832 | tf_op jit(solution)/shard_map/ppermute | solution.py:737
  8.0 2.6 %collective-permute-start.1 = (bf16[2,4,48,256]{3,2,1,0:T(8,128)(2,1)}, bf16[2,4,48,256]{3,2,1,0:T(8,128)(2,1)S(1)}, u32[]{:S(2)}, u32[]{:S(2)}) collective-permute-start(bf16[2,4,48,256]{3,2,1,0:T(8,128)(2,1)} %get-tuple-element.45), channel_id=1, source_target_pairs={{0,4},{1,5},{2,6},{3,7},{4,0},{5,1},{6,2},{7,3},{8,12},{9,13},{10,... | collective-permute-start | bytes 589832 | tf_op jit(solution)/shard_map/ppermute | solution.py:737
  10.6 0.0 collective-permute-start.2
  10.6 0.0 copy-done.1
  10.6 0.0 copy-done.6
  10.6 0.0 copy-done.7
  10.6 8.1 %pair_bias.1 = f32[16,64,256]{2,1,0:T(8,128)S(1)} custom-call(bf16[2,128,64,128]{3,2,1,0:T(8,128)(2,1)S(1)} %bitcast.21, bf16[16,128]{1,0:T(8,128)(2,1)S(1)} %bitcast.22, s32[1,64]{1,0:T(1,128)S(1)} %bitcast.24), custom_call_target="tpu_custom_call" | custom-call | flops 6000000000 | bytes 5000000 | tf_op jit(solution)/shard_map/pair_bias/pallas_call | solution.py:383
  18.7 0.0 copy-start
  18.8 0.9 convert_element_type.21
  19.7 0.0 collective-permute-done.refs_1_
  19.7 5.7 %collective-permute-done.1.refs_2_ = bf16[2,4,48,256]{3,2,1,0:T(8,128)(2,1)S(1)} collective-permute-done((bf16[2,4,48,256]{3,2,1,0:T(8,128)(2,1)}, bf16[2,4,48,256]{3,2,1,0:T(8,128)(2,1)S(1)}, u32[]{:S(2)}, u32[]{:S(2)}) %collective-permute-start.1) | collective-permute-done | bytes 196640 | tf_op jit(solution)/shard_map/ppermute | solution.py:737
  25.4 0.0 collective-permute-done.2.refs_3_
  25.4 6.7 %all-to-all-start = ((f16[16,64,256]{2,1,0:T(8,128)(2,1)}), f16[16,64,256]{2,1,0:T(8,128)(2,1)S(1)}, u32[]{:S(2)}, u32[]{:S(2)}) async-start(f16[16,64,256]{2,1,0:T(8,128)(2,1)} %convert_element_type.21), calls=%async_computation | async-start | bytes 1048576 | tf_op jit(solution)/shard_map/all_to_all | solution.py:754
  32.1 0.1 pad_maximum_fusion
  32.2 0.5 collective-permute-start.3
  32.7 3.0 %own_rows.1 = (f32[768,128]{1,0:T(8,128)}, f32[768,128]{1,0:T(8,128)}, f32[8,128]{1,0:T(8,128)}) custom-call(s32[1]{0:T(128)} %bitcast.4.row_ref, bf16[4,64,768]{2,1,0:T(8,128)(2,1)} %tokens_ref.3, s32[1,64]{1,0:T(1,128)} %bitcast.28, bf16[32,768]{1,0:T(8,128)(2,1)} %table_ref.3, bf16[768,768]{1,0:T(8,128)(2,1)} %refs_7_.1, bf16[4,64,768]{2,1,0:T(8,128)(2,1)} %cot_ref.1), custom_call_target="tpu_custom_call" | custom-call | flops 3000000000 | bytes 3000000 | tf_op jit(solution)/shard_map/own_rows/pallas_call | solution.py:289
  35.7 0.0 collective-permute-done.3.refs_4_
  35.7 10.6 %all-to-all-done = f16[16,64,256]{2,1,0:T(8,128)(2,1)S(1)} async-done(((f16[16,64,256]{2,1,0:T(8,128)(2,1)}), f16[16,64,256]{2,1,0:T(8,128)(2,1)S(1)}, u32[]{:S(2)}, u32[]{:S(2)}) %all-to-all-start) | async-done | bytes 524320 | tf_op jit(solution)/shard_map/all_to_all | solution.py:754
  46.3 0.1 convert_element_type.22.refs_5_
  46.4 7.7 %attention.1 = (f32[16,200,128]{2,1,0:T(8,128)S(1)}, f32[16,136,128]{2,1,0:T(8,128)S(1)}) custom-call(s32[1]{0:T(128)} %bitcast.col_ref, bf16[2,4,48,256]{3,2,1,0:T(8,128)(2,1)S(1)} %copy-done, bf16[2,4,48,256]{3,2,1,0:T(8,128)(2,1)S(1)} %collective-permute-done.refs_1_, bf16[2,4,48,256]{3,2,1,0:T(8,128)(2,1)S(1)} %collective-permute-done.1.refs_2_, ...), custom_call_target="tpu_custom_call" | custom-call | flops 8000000000 | bytes 6000000 | tf_op jit(solution)/shard_map/attention/pallas_call | solution.py:530
  54.1 0.9 convert_element_type.24
  55.0 4.0 %all-to-all-start.1 = ((f16[16,136,128]{2,1,0:T(8,128)(2,1)}), f16[16,136,128]{2,1,0:T(8,128)(2,1)S(1)}, u32[]{:S(2)}, u32[]{:S(2)}) async-start(f16[16,136,128]{2,1,0:T(8,128)(2,1)} %convert_element_type.24), calls=%async_computation.1 | async-start | bytes 1114112 | tf_op jit(solution)/shard_map/all_to_all | solution.py:759
  59.0 1.0 convert_element_type.23
  60.0 7.4 %pair_units.1 = (bf16[32,256,512]{2,1,0:T(8,128)(2,1)}, f32[32,8,512]{2,1,0:T(8,128)}) custom-call(bf16[2,128,64,128]{3,2,1,0:T(8,128)(2,1)} %bitcast.20), custom_call_target="tpu_custom_call" | custom-call | flops 6000000000 | bytes 12000000 | tf_op jit(solution)/shard_map/pair_units/pallas_call | solution.py:413
  67.5 6.3 %all-to-all-done.1 = f16[16,136,128]{2,1,0:T(8,128)(2,1)S(1)} async-done(((f16[16,136,128]{2,1,0:T(8,128)(2,1)}), f16[16,136,128]{2,1,0:T(8,128)(2,1)S(1)}, u32[]{:S(2)}, u32[]{:S(2)}) %all-to-all-start.1) | async-done | bytes 557088 | tf_op jit(solution)/shard_map/all_to_all | solution.py:759
  73.7 0.1 convert_element_type.25
  73.8 1.6 %collective-permute-start.4 = (f16[16,136,128]{2,1,0:T(8,128)(2,1)S(1)}, f16[16,136,128]{2,1,0:T(8,128)(2,1)S(1)}, u32[]{:S(2)}, u32[]{:S(2)}) collective-permute-start(f16[16,136,128]{2,1,0:T(8,128)(2,1)S(1)} %all-to-all-done.1), channel_id=1, source_target_pairs={{0,16},{16,0},{1,17},{17,1},{2,18},{18,2},{3,19},{19,3},{4,20},{20... | collective-permute-start | bytes 1671176 | tf_op jit(solution)/shard_map/ppermute | solution.py:714
  75.4 0.1 slice_multiply_fusion.1
  75.5 3.4 %copy-done.8 = bf16[32,256,512]{2,1,0:T(8,128)(2,1)S(1)} copy-done((bf16[32,256,512]{2,1,0:T(8,128)(2,1)S(1)}, bf16[32,256,512]{2,1,0:T(8,128)(2,1)}, u32[]{:S(2)}) %copy-start.8) | copy-done | bytes 8388632
  78.9 3.3 %pair_weight.1 = f32[16,128]{1,0:T(8,128)S(1)} custom-call(bf16[32,256,512]{2,1,0:T(8,128)(2,1)S(1)} %copy-done.8, f32[2048,128]{1,0:T(8,128)S(1)} %bitcast.17), custom_call_target="tpu_custom_call" | custom-call | flops 5000000000 | bytes 100000 | tf_op jit(solution)/shard_map/pair_weight/pallas_call | solution.py:670
  82.2 0.6 collective-permute-start.5
  82.7 1.4 %collective-permute-start.6 = (f32[16,128]{1,0:T(8,128)S(1)}, f32[16,128]{1,0:T(8,128)S(1)}, u32[]{:S(2)}, u32[]{:S(2)}) collective-permute-start(f32[16,128]{1,0:T(8,128)S(1)} %pair_weight.1), channel_id=1, source_target_pairs={{0,8},{8,0},{1,9},{9,1},{2,10},{10,2},{3,11},{11,3},{4,12},{12,4},... | collective-permute-start | bytes 24584 | tf_op jit(solution)/shard_map/ppermute | solution.py:714
  84.2 1.5 %collective-permute-start.7 = (f32[16,128]{1,0:T(8,128)S(1)}, f32[16,128]{1,0:T(8,128)S(1)}, u32[]{:S(2)}, u32[]{:S(2)}) collective-permute-start(f32[16,128]{1,0:T(8,128)S(1)} %pair_weight.1), channel_id=1, source_target_pairs={{0,24},{8,16},{16,8},{24,0},{1,25},{9,17},{17,9},{25,1},{2,26},{10... | collective-permute-start | bytes 24584 | tf_op jit(solution)/shard_map/ppermute | solution.py:772
  85.7 4.5 %all-to-all-start.2 = ((f16[16,200,128]{2,1,0:T(8,128)(2,1)}), f16[16,200,128]{2,1,0:T(8,128)(2,1)}, u32[]{:S(2)}, u32[]{:S(2)}) async-start(f16[16,200,128]{2,1,0:T(8,128)(2,1)} %convert_element_type.23), calls=%async_computation.2 | async-start | bytes 1638400 | tf_op jit(solution)/shard_map/all_to_all | solution.py:765
  90.2 0.0 collective-permute-done.4
  90.2 0.1 convert_element_type.26
  90.3 0.1 slice_multiply_fusion
  90.4 0.1 bitcast_add_fusion.refs_2_
  90.6 0.9 copy-done.12
  91.5 3.4 %copy-done.9 = bf16[32,256,512]{2,1,0:T(8,128)(2,1)S(1)} copy-done((bf16[32,256,512]{2,1,0:T(8,128)(2,1)S(1)}, bf16[32,256,512]{2,1,0:T(8,128)(2,1)}, u32[]{:S(2)}) %copy-start.9) | copy-done | bytes 8388632
  94.9 5.4 %pair_backward.1 = bf16[2,128,64,128]{3,2,1,0:T(8,128)(2,1)} custom-call(bf16[32,256,512]{2,1,0:T(8,128)(2,1)S(1)} %copy-done.9, f32[32,8,512]{2,1,0:T(8,128)S(1)} %copy-done.12, f32[2048,128]{1,0:T(8,128)S(1)} %bitcast_add_fusion.refs_2_, bf16[16,128]{1,0:T(8,128)(2,1)S(1)} %bitcast.23), custom_call_target="tpu_custom_call" | custom-call | flops 8000000000 | bytes 100000 | tf_op jit(solution)/shard_map/pair_backward/pallas_call | solution.py:687
  100.3 0.0 collective-permute-done.5
  100.3 0.0 collective-permute-done.6
  100.3 0.0 collective-permute-done.7
  100.3 9.7 %all-to-all-done.2 = f16[16,200,128]{2,1,0:T(8,128)(2,1)} async-done(((f16[16,200,128]{2,1,0:T(8,128)(2,1)}), f16[16,200,128]{2,1,0:T(8,128)(2,1)}, u32[]{:S(2)}, u32[]{:S(2)}) %all-to-all-start.2) | async-done | bytes 819232 | tf_op jit(solution)/shard_map/all_to_all | solution.py:765
  110.0 0.0 copy-start.13
  110.0 1.6 %collective-permute-start.10 = (f32[16,128]{1,0:T(8,128)S(1)}, f32[16,128]{1,0:T(8,128)S(1)}, u32[]{:S(2)}, u32[]{:S(2)}) collective-permute-start(f32[16,128]{1,0:T(8,128)S(1)} %add_add_fusion), channel_id=1, source_target_pairs={{0,3},{1,2},{2,1},{3,0},{4,7},{5,6},{6,5},{7,4},{8,11},{9,10},{10,... | collective-permute-start | bytes 24584 | tf_op jit(solution)/shard_map/ppermute | solution.py:737
  111.6 0.2 collective-permute-start.8
  111.9 0.6 collective-permute-start.9
  112.5 1.3 %convert_element_type.27.refs_0_ = f32[16,200,128]{2,1,0:T(8,128)S(1)} convert(f16[16,200,128]{2,1,0:T(8,128)(2,1)} %all-to-all-done.2) | non-fusion elementwise | flops 409600 | bytes 2457600 | tf_op jit(solution)/shard_map/convert_element_type | solution.py:784
  113.8 2.1 %token_back.1 = bf16[128,768]{1,0:T(8,128)(2,1)S(1)} custom-call(f32[16,200,128]{2,1,0:T(8,128)S(1)} %convert_element_type.27.refs_0_, f32[768,128]{1,0:T(8,128)S(1)} %copy-done.10, f32[768,128]{1,0:T(8,128)S(1)} %copy-done.11, f32[8,128]{1,0:T(8,128)S(1)} %copy-done.13, bf16[768,768]{1,0:T(8,128)(2,1)S(1)} %copy-done.2, bf16[768,768]{1,0:T(8,128)(2,1)S(1)} %copy-done.3, ...), custom_call_target="tpu_custom_call" | custom-call | flops 4000000000 | bytes 8000000 | tf_op jit(solution)/shard_map/token_back/pallas_call | solution.py:603
  115.9 0.0 collective-permute-done.10
  116.0 0.0 collective-permute-done.8
  116.0 0.0 collective-permute-done.9
  116.0 1.6 %collective-permute-start.11 = (bf16[2,64,768]{2,1,0:T(8,128)(2,1)S(1)}, bf16[2,64,768]{2,1,0:T(8,128)(2,1)S(1)}, u32[]{:S(2)}, u32[]{:S(2)}) collective-permute-start(bf16[2,64,768]{2,1,0:T(8,128)(2,1)S(1)} %bitcast.18), channel_id=1, source_target_pairs={{0,8},{8,0},{1,9},{9,1},{2,10},{10,2},{3,11},{11,3},{4,12},{12,4},... | collective-permute-start | bytes 589832 | tf_op jit(solution)/shard_map/ppermute | solution.py:714
  117.6 1.8 %collective-permute-start.12 = (f32[16,128]{1,0:T(8,128)S(1)}, f32[16,128]{1,0:T(8,128)S(1)}, u32[]{:S(2)}, u32[]{:S(2)}) collective-permute-start(f32[16,128]{1,0:T(8,128)S(1)} %add_multiply_fusion), channel_id=1, source_target_pairs={{0,4},{1,5},{2,6},{3,7},{4,0},{5,1},{6,2},{7,3},{8,12},{9,13},{10,... | collective-permute-start | bytes 24584 | tf_op jit(solution)/shard_map/ppermute | solution.py:737
  119.4 3.7 %collective-permute-done.11 = bf16[2,64,768]{2,1,0:T(8,128)(2,1)S(1)} collective-permute-done((bf16[2,64,768]{2,1,0:T(8,128)(2,1)S(1)}, bf16[2,64,768]{2,1,0:T(8,128)(2,1)S(1)}, u32[]{:S(2)}, u32[]{:S(2)}) %collective-permute-start.11) | collective-permute-done | bytes 196640 | tf_op jit(solution)/shard_map/ppermute | solution.py:714
  123.1 0.8 pad_maximum_fusion.1
  123.9 0.0 collective-permute-done.12
  123.9 0.6 add_bitcast_fusion
  (26 shorter events, 0.1 us)
Async XLA Ops:
  0.6 10.0 %copy-start.1 = (bf16[256,64,128]{2,1,0:T(8,128)(2,1)S(1)}, bf16[256,64,128]{2,1,0:T(8,128)(2,1)}, u32[]{:S(2)}) copy-start(bf16[256,64,128]{2,1,0:T(8,128)(2,1)} %param.15) | copy-start | bytes 12582916
  0.6 9.9 %copy-start.6 = (bf16[128,16]{0,1:T(8,128)(2,1)S(1)}, bf16[128,16]{0,1:T(8,128)(2,1)}, u32[]{:S(2)}) copy-start(bf16[128,16]{0,1:T(8,128)(2,1)} %param.16) | copy-start | bytes 12292
  0.7 9.9 %copy-start.7 = (s32[64]{0:T(128)S(1)}, s32[64]{0:T(128)}, u32[]{:S(2)}) copy-start(s32[64]{0:T(128)} %param.14) | copy-start | bytes 772
  5.0 14.7 %collective-permute-start = (bf16[2,4,48,256]{3,2,1,0:T(8,128)(2,1)}, bf16[2,4,48,256]{3,2,1,0:T(8,128)(2,1)S(1)}, u32[]{:S(2)}, u32[]{:S(2)}) collective-permute-start(bf16[2,4,48,256]{3,2,1,0:T(8,128)(2,1)} %get-tuple-element.44), channel_id=1, source_target_pairs={{0,2},{1,3},{2,0},{3,1},{4,6},{5,7},{6,4},{7,5},{8,10},{9,11},{10,... | collective-permute-start | bytes 589832 | tf_op jit(solution)/shard_map/ppermute | solution.py:737
  8.0 17.4 %collective-permute-start.1 = (bf16[2,4,48,256]{3,2,1,0:T(8,128)(2,1)}, bf16[2,4,48,256]{3,2,1,0:T(8,128)(2,1)S(1)}, u32[]{:S(2)}, u32[]{:S(2)}) collective-permute-start(bf16[2,4,48,256]{3,2,1,0:T(8,128)(2,1)} %get-tuple-element.45), channel_id=1, source_target_pairs={{0,4},{1,5},{2,6},{3,7},{4,0},{5,1},{6,2},{7,3},{8,12},{9,13},{10,... | collective-permute-start | bytes 589832 | tf_op jit(solution)/shard_map/ppermute | solution.py:737
  10.6 14.8 %collective-permute-start.2 = (bf16[2,4,48,256]{3,2,1,0:T(8,128)(2,1)}, bf16[2,4,48,256]{3,2,1,0:T(8,128)(2,1)S(1)}, u32[]{:S(2)}, u32[]{:S(2)}) collective-permute-start(bf16[2,4,48,256]{3,2,1,0:T(8,128)(2,1)} %get-tuple-element.46), channel_id=1, source_target_pairs={{0,6},{1,7},{2,4},{3,5},{4,2},{5,3},{6,0},{7,1},{8,14},{9,15},{10,... | collective-permute-start | bytes 589832 | tf_op jit(solution)/shard_map/ppermute | solution.py:737
  18.7 13.3 %copy-start = (bf16[2,4,48,256]{3,2,1,0:T(8,128)(2,1)S(1)}, bf16[2,4,48,256]{3,2,1,0:T(8,128)(2,1)}, u32[]{:S(2)}) copy-start(bf16[2,4,48,256]{3,2,1,0:T(8,128)(2,1)} %get-tuple-element.47.refs_0_) | copy-start | bytes 589828
  25.4 20.9 %all-to-all-start = ((f16[16,64,256]{2,1,0:T(8,128)(2,1)}), f16[16,64,256]{2,1,0:T(8,128)(2,1)S(1)}, u32[]{:S(2)}, u32[]{:S(2)}) async-start(f16[16,64,256]{2,1,0:T(8,128)(2,1)} %convert_element_type.21), calls=%async_computation | async-start | bytes 1048576 | tf_op jit(solution)/shard_map/all_to_all | solution.py:754
  32.2 3.5 %collective-permute-start.3 = (bf16[4,4,48,256]{3,2,1,0:T(8,128)(2,1)S(1)}, bf16[4,4,48,256]{3,2,1,0:T(8,128)(2,1)S(1)}, u32[]{:S(2)}, u32[]{:S(2)}) collective-permute-start(bf16[4,4,48,256]{3,2,1,0:T(8,128)(2,1)S(1)} %pad_maximum_fusion), channel_id=1, source_target_pairs={{0,1},{1,0},{2,3},{3,2},{4,5},{5,4},{6,7},{7,6},{8,9},{9,8},{10,11... | collective-permute-start | bytes 1179656 | tf_op jit(solution)/shard_map/ppermute | solution.py:737
  55.0 18.8 %all-to-all-start.1 = ((f16[16,136,128]{2,1,0:T(8,128)(2,1)}), f16[16,136,128]{2,1,0:T(8,128)(2,1)S(1)}, u32[]{:S(2)}, u32[]{:S(2)}) async-start(f16[16,136,128]{2,1,0:T(8,128)(2,1)} %convert_element_type.24), calls=%async_computation.1 | async-start | bytes 1114112 | tf_op jit(solution)/shard_map/all_to_all | solution.py:759
  73.8 16.4 %collective-permute-start.4 = (f16[16,136,128]{2,1,0:T(8,128)(2,1)S(1)}, f16[16,136,128]{2,1,0:T(8,128)(2,1)S(1)}, u32[]{:S(2)}, u32[]{:S(2)}) collective-permute-start(f16[16,136,128]{2,1,0:T(8,128)(2,1)S(1)} %all-to-all-done.1), channel_id=1, source_target_pairs={{0,16},{16,0},{1,17},{17,1},{2,18},{18,2},{3,19},{19,3},{4,20},{20... | collective-permute-start | bytes 1671176 | tf_op jit(solution)/shard_map/ppermute | solution.py:714
  75.5 3.4 %copy-start.8 = (bf16[32,256,512]{2,1,0:T(8,128)(2,1)S(1)}, bf16[32,256,512]{2,1,0:T(8,128)(2,1)}, u32[]{:S(2)}) copy-start(bf16[32,256,512]{2,1,0:T(8,128)(2,1)} %get-tuple-element.63.normed_ref.refs_0_) | copy-start | bytes 25165828
  82.2 18.1 %collective-permute-start.5 = (f32[16,128]{1,0:T(8,128)S(1)}, f32[16,128]{1,0:T(8,128)S(1)}, u32[]{:S(2)}, u32[]{:S(2)}) collective-permute-start(f32[16,128]{1,0:T(8,128)S(1)} %pair_weight.1), channel_id=1, source_target_pairs={{0,16},{16,0},{1,17},{17,1},{2,18},{18,2},{3,19},{19,3},{4,20},{20... | collective-permute-start | bytes 24584 | tf_op jit(solution)/shard_map/ppermute | solution.py:714
  82.7 17.5 %collective-permute-start.6 = (f32[16,128]{1,0:T(8,128)S(1)}, f32[16,128]{1,0:T(8,128)S(1)}, u32[]{:S(2)}, u32[]{:S(2)}) collective-permute-start(f32[16,128]{1,0:T(8,128)S(1)} %pair_weight.1), channel_id=1, source_target_pairs={{0,8},{8,0},{1,9},{9,1},{2,10},{10,2},{3,11},{11,3},{4,12},{12,4},... | collective-permute-start | bytes 24584 | tf_op jit(solution)/shard_map/ppermute | solution.py:714
  84.2 16.1 %collective-permute-start.7 = (f32[16,128]{1,0:T(8,128)S(1)}, f32[16,128]{1,0:T(8,128)S(1)}, u32[]{:S(2)}, u32[]{:S(2)}) collective-permute-start(f32[16,128]{1,0:T(8,128)S(1)} %pair_weight.1), channel_id=1, source_target_pairs={{0,24},{8,16},{16,8},{24,0},{1,25},{9,17},{17,9},{25,1},{2,26},{10... | collective-permute-start | bytes 24584 | tf_op jit(solution)/shard_map/ppermute | solution.py:772
  85.7 24.3 %all-to-all-start.2 = ((f16[16,200,128]{2,1,0:T(8,128)(2,1)}), f16[16,200,128]{2,1,0:T(8,128)(2,1)}, u32[]{:S(2)}, u32[]{:S(2)}) async-start(f16[16,200,128]{2,1,0:T(8,128)(2,1)} %convert_element_type.23), calls=%async_computation.2 | async-start | bytes 1638400 | tf_op jit(solution)/shard_map/all_to_all | solution.py:765
  90.4 1.0 copy-start.12
  91.5 3.4 %copy-start.9 = (bf16[32,256,512]{2,1,0:T(8,128)(2,1)S(1)}, bf16[32,256,512]{2,1,0:T(8,128)(2,1)}, u32[]{:S(2)}) copy-start(bf16[32,256,512]{2,1,0:T(8,128)(2,1)} %get-tuple-element.63.normed_ref.refs_0_) | copy-start | bytes 25165828
  94.9 18.9 %copy-start.4 = (bf16[768,768]{1,0:T(8,128)(2,1)S(1)}, bf16[768,768]{1,0:T(8,128)(2,1)}, u32[]{:S(2)}) copy-start(bf16[768,768]{1,0:T(8,128)(2,1)} %refs_6_.1) | copy-start | bytes 3538948
  94.9 18.9 %copy-start.5 = (bf16[768,768]{1,0:T(8,128)(2,1)S(1)}, bf16[768,768]{1,0:T(8,128)(2,1)}, u32[]{:S(2)}) copy-start(bf16[768,768]{1,0:T(8,128)(2,1)} %refs_7_.1) | copy-start | bytes 3538948
  94.9 18.9 %copy-start.10 = (f32[768,128]{1,0:T(8,128)S(1)}, f32[768,128]{1,0:T(8,128)}, u32[]{:S(2)}) copy-start(f32[768,128]{1,0:T(8,128)} %get-tuple-element.69.refs_1_) | copy-start | bytes 1179652
  94.9 18.9 %copy-start.11 = (f32[768,128]{1,0:T(8,128)S(1)}, f32[768,128]{1,0:T(8,128)}, u32[]{:S(2)}) copy-start(f32[768,128]{1,0:T(8,128)} %get-tuple-element.70.refs_2_) | copy-start | bytes 1179652
  110.0 3.8 %copy-start.2 = (bf16[768,768]{1,0:T(8,128)(2,1)S(1)}, bf16[768,768]{1,0:T(8,128)(2,1)}, u32[]{:S(2)}) copy-start(bf16[768,768]{1,0:T(8,128)(2,1)} %refs_4_.3) | copy-start | bytes 3538948
  110.0 3.8 %copy-start.3 = (bf16[768,768]{1,0:T(8,128)(2,1)S(1)}, bf16[768,768]{1,0:T(8,128)(2,1)}, u32[]{:S(2)}) copy-start(bf16[768,768]{1,0:T(8,128)(2,1)} %refs_5_.1) | copy-start | bytes 3538948
  110.0 3.8 %copy-start.13 = (f32[8,128]{1,0:T(8,128)S(1)}, f32[8,128]{1,0:T(8,128)}, u32[]{:S(2)}) copy-start(f32[8,128]{1,0:T(8,128)} %get-tuple-element.71.refs_3_) | copy-start | bytes 12292
  110.0 5.9 %collective-permute-start.10 = (f32[16,128]{1,0:T(8,128)S(1)}, f32[16,128]{1,0:T(8,128)S(1)}, u32[]{:S(2)}, u32[]{:S(2)}) collective-permute-start(f32[16,128]{1,0:T(8,128)S(1)} %add_add_fusion), channel_id=1, source_target_pairs={{0,3},{1,2},{2,1},{3,0},{4,7},{5,6},{6,5},{7,4},{8,11},{9,10},{10,... | collective-permute-start | bytes 24584 | tf_op jit(solution)/shard_map/ppermute | solution.py:737
  111.6 4.3 %collective-permute-start.8 = (f32[16,128]{1,0:T(8,128)S(1)}, f32[16,128]{1,0:T(8,128)S(1)}, u32[]{:S(2)}, u32[]{:S(2)}) collective-permute-start(f32[16,128]{1,0:T(8,128)S(1)} %add_add_fusion), channel_id=1, source_target_pairs={{0,1},{1,0},{2,3},{3,2},{4,5},{5,4},{6,7},{7,6},{8,9},{9,8},{10,11... | collective-permute-start | bytes 24584 | tf_op jit(solution)/shard_map/ppermute | solution.py:737
  111.9 4.1 %collective-permute-start.9 = (f32[16,128]{1,0:T(8,128)S(1)}, f32[16,128]{1,0:T(8,128)S(1)}, u32[]{:S(2)}, u32[]{:S(2)}) collective-permute-start(f32[16,128]{1,0:T(8,128)S(1)} %add_add_fusion), channel_id=1, source_target_pairs={{0,2},{1,3},{2,0},{3,1},{4,6},{5,7},{6,4},{7,5},{8,10},{9,11},{10,... | collective-permute-start | bytes 24584 | tf_op jit(solution)/shard_map/ppermute | solution.py:737
  116.0 7.1 %collective-permute-start.11 = (bf16[2,64,768]{2,1,0:T(8,128)(2,1)S(1)}, bf16[2,64,768]{2,1,0:T(8,128)(2,1)S(1)}, u32[]{:S(2)}, u32[]{:S(2)}) collective-permute-start(bf16[2,64,768]{2,1,0:T(8,128)(2,1)S(1)} %bitcast.18), channel_id=1, source_target_pairs={{0,8},{8,0},{1,9},{9,1},{2,10},{10,2},{3,11},{11,3},{4,12},{12,4},... | collective-permute-start | bytes 589832 | tf_op jit(solution)/shard_map/ppermute | solution.py:714
  117.6 6.3 %collective-permute-start.12 = (f32[16,128]{1,0:T(8,128)S(1)}, f32[16,128]{1,0:T(8,128)S(1)}, u32[]{:S(2)}, u32[]{:S(2)}) collective-permute-start(f32[16,128]{1,0:T(8,128)S(1)} %add_multiply_fusion), channel_id=1, source_target_pairs={{0,4},{1,5},{2,6},{3,7},{4,0},{5,1},{6,2},{7,3},{8,12},{9,13},{10,... | collective-permute-start | bytes 24584 | tf_op jit(solution)/shard_map/ppermute | solution.py:737

commit v9 on v8

--- a/solution.py
+++ b/solution.py
@@ -675,7 +675,7 @@
         out_specs=whole_spec(part_shape),
         compiler_params=params(24),
         cost_estimate=pl.CostEstimate(
-            flops=5_000_000_000, bytes_accessed=100_000, transcendentals=0
+            flops=1_000_000, bytes_accessed=100_000, transcendentals=0
         ),
         name="pair_weight",
     )(normed, grads)
@@ -697,7 +697,7 @@
         out_specs=pl.BlockSpec((2, whole // STEPS, tok_col, width), lambda i: (0, i, 0, 0)),
         compiler_params=params(24),
         cost_estimate=pl.CostEstimate(
-            flops=8_000_000_000, bytes_accessed=100_000, transcendentals=0
+            flops=1_000_000, bytes_accessed=100_000, transcendentals=0
         ),
         name="pair_backward",
     )(normed, inv_std, grads, weight_t)

time: 125 us -> 122 us (0.976)
  local copies, waits for them, and re-layouts: 7.74 us -> 4.36 us
    all_to_all x1, waiting for transfers between devices: 6.28 us -> 13.7 us  [body_heads(): lax.all_to_all(grad_bias.astype(jnp.float16), ('row', 'col'), 0, 0, tiled...]
    all_to_all x1, waiting for transfers between devices: 9.72 us -> 2.6 us  [body_heads(): back = lax.all_to_all(back, ('row', 'col'), 0, 0, tiled=True)]
    unnamed x28, local copies, waits for them, and re-layouts: 7.71 us -> 4.32 us
where the time goes in v9:
time: 122 us; the launch traced here: 121 us
  Pallas kernels  41.5 us (34%)
  waiting for transfers between devices  36.3 us (30%)
  starting transfers between devices  32.2 us (26%)
  other arithmetic  6.16 us (5%)
  local copies, waits for them, and re-layouts  4.36 us (4%)
    all_to_all x1, waiting for transfers between devices, body_heads(): lax.all_to_all(grad_bias.astype(jnp.float16), ('row', 'col'), 0, 0, tiled...  13.7 us
    all_to_all x1, waiting for transfers between devices, body_heads(): bias = lax.all_to_all(bias, ('row', 'col'), 0, 0, tiled=True)  10.6 us
    ppermute x8, starting transfers between devices, send(): return lax.ppermute(block, 'col', [(c, c ^ offset) for c in range(n_col)])  10.4 us
    pallas_call x1, Pallas kernels, pair_bias(): pl.pallas_call(bias_kernel, out_shape=jax.ShapeDtypeStruct((H, tok_col, r...  8.12 us
    pallas_call x1, Pallas kernels, attention(): pl.pallas_call(attention_kernel, out_shape=[jax.ShapeDtypeStruct(back_sha...  7.67 us
    pallas_call x1, Pallas kernels, pair_units(): pl.pallas_call(norm_kernel, out_shape=[jax.ShapeDtypeStruct(shapes[0], jn...  7.45 us
    all_to_all x1, starting transfers between devices, body_heads(): bias = lax.all_to_all(bias, ('row', 'col'), 0, 0, tiled=True)  6.67 us
    ppermute x8, waiting for transfers between devices, send(): return lax.ppermute(block, 'col', [(c, c ^ offset) for c in range(n_col)])  5.74 us
  transfers between devices with their start and end apart: 16, of which 5 were waited for; matrix products, arithmetic and copies ran while one was open for 4% of the time, Pallas kernels for 24%

profile of v9, /device:TPU:0, one launch (start us, length us, event | category | flops | bytes accessed | tf_op | source)
XLA Modules:
  0.0 121.5 jit_solution(4611387746295828227)
XLA Ops:
  0.6 0.0 copy-start.4
  0.6 0.0 copy-start.5
  0.7 0.0 copy-start.10
  0.7 4.3 %token_messages.1 = (bf16[2,4,48,256]{3,2,1,0:T(8,128)(2,1)}, bf16[2,4,48,256]{3,2,1,0:T(8,128)(2,1)}, bf16[2,4,48,256]{3,2,1,0:T(8,128)(2,1)}, bf16[2,4,48,256]{3,2,1,0:T(8,128)(2,1)}) custom-call(s32[1]{0:T(128)} %bitcast.4.row_ref, s32[1]{0:T(128)} %bitcast.col_ref, bf16[4,64,768]{2,1,0:T(8,128)(2,1)} %tokens_ref.3, s32[1,64]{1,0:T(1,128)} %bitcast.28, ...), custom_call_target="tpu_custom_call" | custom-call | flops 4000000000 | bytes 4000000 | tf_op jit(solution)/shard_map/token_messages/pallas_call | solution.py:245
  5.0 3.0 %collective-permute-start = (bf16[2,4,48,256]{3,2,1,0:T(8,128)(2,1)}, bf16[2,4,48,256]{3,2,1,0:T(8,128)(2,1)S(1)}, u32[]{:S(2)}, u32[]{:S(2)}) collective-permute-start(bf16[2,4,48,256]{3,2,1,0:T(8,128)(2,1)} %get-tuple-element.44), channel_id=1, source_target_pairs={{0,2},{1,3},{2,0},{3,1},{4,6},{5,7},{6,4},{7,5},{8,10},{9,11},{10,... | collective-permute-start | bytes 589832 | tf_op jit(solution)/shard_map/ppermute | solution.py:737
  8.0 2.6 %collective-permute-start.1 = (bf16[2,4,48,256]{3,2,1,0:T(8,128)(2,1)}, bf16[2,4,48,256]{3,2,1,0:T(8,128)(2,1)S(1)}, u32[]{:S(2)}, u32[]{:S(2)}) collective-permute-start(bf16[2,4,48,256]{3,2,1,0:T(8,128)(2,1)} %get-tuple-element.45), channel_id=1, source_target_pairs={{0,4},{1,5},{2,6},{3,7},{4,0},{5,1},{6,2},{7,3},{8,12},{9,13},{10,... | collective-permute-start | bytes 589832 | tf_op jit(solution)/shard_map/ppermute | solution.py:737
  10.6 0.0 collective-permute-start.2
  10.6 0.0 copy-done.5
  10.6 0.0 copy-done.10
  10.6 8.1 %pair_bias.1 = f32[16,64,256]{2,1,0:T(8,128)S(1)} custom-call(bf16[2,128,64,128]{3,2,1,0:T(8,128)(2,1)S(1)} %bitcast.23, bf16[16,128]{1,0:T(8,128)(2,1)S(1)} %bitcast.20, s32[1,64]{1,0:T(1,128)S(1)} %bitcast.24), custom_call_target="tpu_custom_call" | custom-call | flops 6000000000 | bytes 5000000 | tf_op jit(solution)/shard_map/pair_bias/pallas_call | solution.py:383
  18.7 0.0 copy-start.3
  18.7 0.9 convert_element_type.21
  19.6 0.0 collective-permute-done.refs_1_
  19.6 5.7 %collective-permute-done.1.refs_2_ = bf16[2,4,48,256]{3,2,1,0:T(8,128)(2,1)S(1)} collective-permute-done((bf16[2,4,48,256]{3,2,1,0:T(8,128)(2,1)}, bf16[2,4,48,256]{3,2,1,0:T(8,128)(2,1)S(1)}, u32[]{:S(2)}, u32[]{:S(2)}) %collective-permute-start.1) | collective-permute-done | bytes 196640 | tf_op jit(solution)/shard_map/ppermute | solution.py:737
  25.4 0.0 collective-permute-done.2.refs_3_
  25.4 6.7 %all-to-all-start = ((f16[16,64,256]{2,1,0:T(8,128)(2,1)}), f16[16,64,256]{2,1,0:T(8,128)(2,1)S(1)}, u32[]{:S(2)}, u32[]{:S(2)}) async-start(f16[16,64,256]{2,1,0:T(8,128)(2,1)} %convert_element_type.21), calls=%async_computation | async-start | bytes 1048576 | tf_op jit(solution)/shard_map/all_to_all | solution.py:754
  32.1 0.1 pad_maximum_fusion
  32.2 0.5 collective-permute-start.3
  32.7 3.1 %own_rows.1 = (f32[768,128]{1,0:T(8,128)}, f32[768,128]{1,0:T(8,128)}, f32[8,128]{1,0:T(8,128)}) custom-call(s32[1]{0:T(128)} %bitcast.4.row_ref, bf16[4,64,768]{2,1,0:T(8,128)(2,1)} %tokens_ref.3, s32[1,64]{1,0:T(1,128)} %bitcast.29, bf16[32,768]{1,0:T(8,128)(2,1)} %table_ref.3, bf16[768,768]{1,0:T(8,128)(2,1)} %refs_7_.1, bf16[4,64,768]{2,1,0:T(8,128)(2,1)} %cot_ref.1), custom_call_target="tpu_custom_call" | custom-call | flops 3000000000 | bytes 3000000 | tf_op jit(solution)/shard_map/own_rows/pallas_call | solution.py:289
  35.7 0.0 collective-permute-done.3.refs_4_
  35.7 10.6 %all-to-all-done = f16[16,64,256]{2,1,0:T(8,128)(2,1)S(1)} async-done(((f16[16,64,256]{2,1,0:T(8,128)(2,1)}), f16[16,64,256]{2,1,0:T(8,128)(2,1)S(1)}, u32[]{:S(2)}, u32[]{:S(2)}) %all-to-all-start) | async-done | bytes 524320 | tf_op jit(solution)/shard_map/all_to_all | solution.py:754
  46.3 0.1 convert_element_type.22.refs_5_
  46.4 7.7 %attention.1 = (f32[16,200,128]{2,1,0:T(8,128)S(1)}, f32[16,136,128]{2,1,0:T(8,128)S(1)}) custom-call(s32[1]{0:T(128)} %bitcast.col_ref, bf16[2,4,48,256]{3,2,1,0:T(8,128)(2,1)S(1)} %copy-done.3, bf16[2,4,48,256]{3,2,1,0:T(8,128)(2,1)S(1)} %collective-permute-done.refs_1_, bf16[2,4,48,256]{3,2,1,0:T(8,128)(2,1)S(1)} %collective-permute-done.1.refs_2_, ...), custom_call_target="tpu_custom_call" | custom-call | flops 8000000000 | bytes 6000000 | tf_op jit(solution)/shard_map/attention/pallas_call | solution.py:530
  54.1 0.9 convert_element_type.24
  55.0 4.0 %all-to-all-start.1 = ((f16[16,136,128]{2,1,0:T(8,128)(2,1)}), f16[16,136,128]{2,1,0:T(8,128)(2,1)S(1)}, u32[]{:S(2)}, u32[]{:S(2)}) async-start(f16[16,136,128]{2,1,0:T(8,128)(2,1)} %convert_element_type.24), calls=%async_computation.1 | async-start | bytes 1114112 | tf_op jit(solution)/shard_map/all_to_all | solution.py:759
  59.0 1.0 convert_element_type.23
  60.0 13.7 %all-to-all-done.1 = f16[16,136,128]{2,1,0:T(8,128)(2,1)S(1)} async-done(((f16[16,136,128]{2,1,0:T(8,128)(2,1)}), f16[16,136,128]{2,1,0:T(8,128)(2,1)S(1)}, u32[]{:S(2)}, u32[]{:S(2)}) %all-to-all-start.1) | async-done | bytes 557088 | tf_op jit(solution)/shard_map/all_to_all | solution.py:759
  73.7 1.5 %collective-permute-start.4 = (f16[16,136,128]{2,1,0:T(8,128)(2,1)S(1)}, f16[16,136,128]{2,1,0:T(8,128)(2,1)S(1)}, u32[]{:S(2)}, u32[]{:S(2)}) collective-permute-start(f16[16,136,128]{2,1,0:T(8,128)(2,1)S(1)} %all-to-all-done.1), channel_id=1, source_target_pairs={{0,16},{16,0},{1,17},{17,1},{2,18},{18,2},{3,19},{19,3},{4,20},{20... | collective-permute-start | bytes 1671176 | tf_op jit(solution)/shard_map/ppermute | solution.py:714
  75.3 7.4 %pair_units.1 = (bf16[32,256,512]{2,1,0:T(8,128)(2,1)}, f32[32,8,512]{2,1,0:T(8,128)}) custom-call(bf16[2,128,64,128]{3,2,1,0:T(8,128)(2,1)} %bitcast.22), custom_call_target="tpu_custom_call" | custom-call | flops 6000000000 | bytes 12000000 | tf_op jit(solution)/shard_map/pair_units/pallas_call | solution.py:413
  82.7 4.5 %all-to-all-start.2 = ((f16[16,200,128]{2,1,0:T(8,128)(2,1)}), f16[16,200,128]{2,1,0:T(8,128)(2,1)}, u32[]{:S(2)}, u32[]{:S(2)}) async-start(f16[16,200,128]{2,1,0:T(8,128)(2,1)} %convert_element_type.23), calls=%async_computation.2 | async-start | bytes 1638400 | tf_op jit(solution)/shard_map/all_to_all | solution.py:765
  87.2 0.1 convert_element_type.25
  87.3 0.1 slice_multiply_fusion.1
  87.4 3.4 %copy-done = bf16[32,256,512]{2,1,0:T(8,128)(2,1)S(1)} copy-done((bf16[32,256,512]{2,1,0:T(8,128)(2,1)S(1)}, bf16[32,256,512]{2,1,0:T(8,128)(2,1)}, u32[]{:S(2)}) %copy-start) | copy-done | bytes 8388632
  90.8 3.3 %pair_weight.1 = f32[16,128]{1,0:T(8,128)S(1)} custom-call(bf16[32,256,512]{2,1,0:T(8,128)(2,1)S(1)} %copy-done, f32[2048,128]{1,0:T(8,128)S(1)} %bitcast.17), custom_call_target="tpu_custom_call" | custom-call | flops 1000000 | bytes 100000 | tf_op jit(solution)/shard_map/pair_weight/pallas_call | solution.py:670
  94.1 0.6 collective-permute-start.5
  94.6 1.6 %collective-permute-start.6 = (f32[16,128]{1,0:T(8,128)S(1)}, f32[16,128]{1,0:T(8,128)S(1)}, u32[]{:S(2)}, u32[]{:S(2)}) collective-permute-start(f32[16,128]{1,0:T(8,128)S(1)} %pair_weight.1), channel_id=1, source_target_pairs={{0,8},{8,0},{1,9},{9,1},{2,10},{10,2},{3,11},{11,3},{4,12},{12,4},... | collective-permute-start | bytes 24584 | tf_op jit(solution)/shard_map/ppermute | solution.py:714
  96.2 1.4 %collective-permute-start.7 = (f32[16,128]{1,0:T(8,128)S(1)}, f32[16,128]{1,0:T(8,128)S(1)}, u32[]{:S(2)}, u32[]{:S(2)}) collective-permute-start(f32[16,128]{1,0:T(8,128)S(1)} %pair_weight.1), channel_id=1, source_target_pairs={{0,24},{8,16},{16,8},{24,0},{1,25},{9,17},{17,9},{25,1},{2,26},{10... | collective-permute-start | bytes 24584 | tf_op jit(solution)/shard_map/ppermute | solution.py:772
  97.6 0.0 collective-permute-done.4
  97.6 0.1 convert_element_type.26
  97.7 0.1 slice_multiply_fusion
  97.8 0.0 copy-start.2
  97.8 0.1 bitcast_add_fusion.refs_2_
  98.0 0.0 copy-done.1
  98.0 0.9 copy-done.2
  98.9 5.5 %pair_backward.1 = bf16[2,128,64,128]{3,2,1,0:T(8,128)(2,1)} custom-call(bf16[32,256,512]{2,1,0:T(8,128)(2,1)S(1)} %copy-done.1, f32[32,8,512]{2,1,0:T(8,128)S(1)} %copy-done.2, f32[2048,128]{1,0:T(8,128)S(1)} %bitcast_add_fusion.refs_2_, bf16[16,128]{1,0:T(8,128)(2,1)S(1)} %bitcast.21), custom_call_target="tpu_custom_call" | custom-call | flops 1000000 | bytes 100000 | tf_op jit(solution)/shard_map/pair_backward/pallas_call | solution.py:687
  104.3 0.0 collective-permute-done.5
  104.4 0.0 collective-permute-done.6
  104.4 0.0 collective-permute-done.7
  104.4 2.6 %all-to-all-done.2 = f16[16,200,128]{2,1,0:T(8,128)(2,1)} async-done(((f16[16,200,128]{2,1,0:T(8,128)(2,1)}), f16[16,200,128]{2,1,0:T(8,128)(2,1)}, u32[]{:S(2)}, u32[]{:S(2)}) %all-to-all-start.2) | async-done | bytes 819232 | tf_op jit(solution)/shard_map/all_to_all | solution.py:765
  107.0 0.0 copy-start.13
  107.0 1.6 %collective-permute-start.10 = (f32[16,128]{1,0:T(8,128)S(1)}, f32[16,128]{1,0:T(8,128)S(1)}, u32[]{:S(2)}, u32[]{:S(2)}) collective-permute-start(f32[16,128]{1,0:T(8,128)S(1)} %add_add_fusion), channel_id=1, source_target_pairs={{0,3},{1,2},{2,1},{3,0},{4,7},{5,6},{6,5},{7,4},{8,11},{9,10},{10,... | collective-permute-start | bytes 24584 | tf_op jit(solution)/shard_map/ppermute | solution.py:737
  108.6 0.2 collective-permute-start.8
  108.8 0.6 collective-permute-start.9
  109.5 1.3 %convert_element_type.27.refs_0_ = f32[16,200,128]{2,1,0:T(8,128)S(1)} convert(f16[16,200,128]{2,1,0:T(8,128)(2,1)} %all-to-all-done.2) | non-fusion elementwise | flops 409600 | bytes 2457600 | tf_op jit(solution)/shard_map/convert_element_type | solution.py:784
  110.8 2.1 %token_back.1 = bf16[128,768]{1,0:T(8,128)(2,1)S(1)} custom-call(f32[16,200,128]{2,1,0:T(8,128)S(1)} %convert_element_type.27.refs_0_, f32[768,128]{1,0:T(8,128)S(1)} %copy-done.11, f32[768,128]{1,0:T(8,128)S(1)} %copy-done.12, f32[8,128]{1,0:T(8,128)S(1)} %copy-done.13, bf16[768,768]{1,0:T(8,128)(2,1)S(1)} %copy-done.6, bf16[768,768]{1,0:T(8,128)(2,1)S(1)} %copy-done.7, ...), custom_call_target="tpu_custom_call" | custom-call | flops 4000000000 | bytes 8000000 | tf_op jit(solution)/shard_map/token_back/pallas_call | solution.py:603
  112.9 0.0 collective-permute-done.10
  112.9 0.0 collective-permute-done.8
  113.0 0.0 collective-permute-done.9
  113.0 1.6 %collective-permute-start.11 = (bf16[2,64,768]{2,1,0:T(8,128)(2,1)S(1)}, bf16[2,64,768]{2,1,0:T(8,128)(2,1)S(1)}, u32[]{:S(2)}, u32[]{:S(2)}) collective-permute-start(bf16[2,64,768]{2,1,0:T(8,128)(2,1)S(1)} %bitcast.18), channel_id=1, source_target_pairs={{0,8},{8,0},{1,9},{9,1},{2,10},{10,2},{3,11},{11,3},{4,12},{12,4},... | collective-permute-start | bytes 589832 | tf_op jit(solution)/shard_map/ppermute | solution.py:714
  114.5 1.9 %collective-permute-start.12 = (f32[16,128]{1,0:T(8,128)S(1)}, f32[16,128]{1,0:T(8,128)S(1)}, u32[]{:S(2)}, u32[]{:S(2)}) collective-permute-start(f32[16,128]{1,0:T(8,128)S(1)} %add_multiply_fusion), channel_id=1, source_target_pairs={{0,4},{1,5},{2,6},{3,7},{4,0},{5,1},{6,2},{7,3},{8,12},{9,13},{10,... | collective-permute-start | bytes 24584 | tf_op jit(solution)/shard_map/ppermute | solution.py:737
  116.4 3.7 %collective-permute-done.11 = bf16[2,64,768]{2,1,0:T(8,128)(2,1)S(1)} collective-permute-done((bf16[2,64,768]{2,1,0:T(8,128)(2,1)S(1)}, bf16[2,64,768]{2,1,0:T(8,128)(2,1)S(1)}, u32[]{:S(2)}, u32[]{:S(2)}) %collective-permute-start.11) | collective-permute-done | bytes 196640 | tf_op jit(solution)/shard_map/ppermute | solution.py:714
  120.1 0.8 pad_maximum_fusion.1
  120.9 0.0 collective-permute-done.12
  120.9 0.6 add_bitcast_fusion
  (26 shorter events, 0.1 us)
Async XLA Ops:
  0.6 10.0 %copy-start.4 = (bf16[128,16]{0,1:T(8,128)(2,1)S(1)}, bf16[128,16]{0,1:T(8,128)(2,1)}, u32[]{:S(2)}) copy-start(bf16[128,16]{0,1:T(8,128)(2,1)} %param.16) | copy-start | bytes 12292
  0.6 9.9 %copy-start.5 = (bf16[256,64,128]{2,1,0:T(8,128)(2,1)S(1)}, bf16[256,64,128]{2,1,0:T(8,128)(2,1)}, u32[]{:S(2)}) copy-start(bf16[256,64,128]{2,1,0:T(8,128)(2,1)} %param.15) | copy-start | bytes 12582916
  0.7 9.9 %copy-start.10 = (s32[64]{0:T(128)S(1)}, s32[64]{0:T(128)}, u32[]{:S(2)}) copy-start(s32[64]{0:T(128)} %param.14) | copy-start | bytes 772
  5.0 14.7 %collective-permute-start = (bf16[2,4,48,256]{3,2,1,0:T(8,128)(2,1)}, bf16[2,4,48,256]{3,2,1,0:T(8,128)(2,1)S(1)}, u32[]{:S(2)}, u32[]{:S(2)}) collective-permute-start(bf16[2,4,48,256]{3,2,1,0:T(8,128)(2,1)} %get-tuple-element.44), channel_id=1, source_target_pairs={{0,2},{1,3},{2,0},{3,1},{4,6},{5,7},{6,4},{7,5},{8,10},{9,11},{10,... | collective-permute-start | bytes 589832 | tf_op jit(solution)/shard_map/ppermute | solution.py:737
  8.0 17.4 %collective-permute-start.1 = (bf16[2,4,48,256]{3,2,1,0:T(8,128)(2,1)}, bf16[2,4,48,256]{3,2,1,0:T(8,128)(2,1)S(1)}, u32[]{:S(2)}, u32[]{:S(2)}) collective-permute-start(bf16[2,4,48,256]{3,2,1,0:T(8,128)(2,1)} %get-tuple-element.45), channel_id=1, source_target_pairs={{0,4},{1,5},{2,6},{3,7},{4,0},{5,1},{6,2},{7,3},{8,12},{9,13},{10,... | collective-permute-start | bytes 589832 | tf_op jit(solution)/shard_map/ppermute | solution.py:737
  10.6 14.8 %collective-permute-start.2 = (bf16[2,4,48,256]{3,2,1,0:T(8,128)(2,1)}, bf16[2,4,48,256]{3,2,1,0:T(8,128)(2,1)S(1)}, u32[]{:S(2)}, u32[]{:S(2)}) collective-permute-start(bf16[2,4,48,256]{3,2,1,0:T(8,128)(2,1)} %get-tuple-element.46), channel_id=1, source_target_pairs={{0,6},{1,7},{2,4},{3,5},{4,2},{5,3},{6,0},{7,1},{8,14},{9,15},{10,... | collective-permute-start | bytes 589832 | tf_op jit(solution)/shard_map/ppermute | solution.py:737
  18.7 13.3 %copy-start.3 = (bf16[2,4,48,256]{3,2,1,0:T(8,128)(2,1)S(1)}, bf16[2,4,48,256]{3,2,1,0:T(8,128)(2,1)}, u32[]{:S(2)}) copy-start(bf16[2,4,48,256]{3,2,1,0:T(8,128)(2,1)} %get-tuple-element.47.refs_0_) | copy-start | bytes 589828
  25.4 20.9 %all-to-all-start = ((f16[16,64,256]{2,1,0:T(8,128)(2,1)}), f16[16,64,256]{2,1,0:T(8,128)(2,1)S(1)}, u32[]{:S(2)}, u32[]{:S(2)}) async-start(f16[16,64,256]{2,1,0:T(8,128)(2,1)} %convert_element_type.21), calls=%async_computation | async-start | bytes 1048576 | tf_op jit(solution)/shard_map/all_to_all | solution.py:754
  32.2 3.5 %collective-permute-start.3 = (bf16[4,4,48,256]{3,2,1,0:T(8,128)(2,1)S(1)}, bf16[4,4,48,256]{3,2,1,0:T(8,128)(2,1)S(1)}, u32[]{:S(2)}, u32[]{:S(2)}) collective-permute-start(bf16[4,4,48,256]{3,2,1,0:T(8,128)(2,1)S(1)} %pad_maximum_fusion), channel_id=1, source_target_pairs={{0,1},{1,0},{2,3},{3,2},{4,5},{5,4},{6,7},{7,6},{8,9},{9,8},{10,11... | collective-permute-start | bytes 1179656 | tf_op jit(solution)/shard_map/ppermute | solution.py:737
  55.0 18.8 %all-to-all-start.1 = ((f16[16,136,128]{2,1,0:T(8,128)(2,1)}), f16[16,136,128]{2,1,0:T(8,128)(2,1)S(1)}, u32[]{:S(2)}, u32[]{:S(2)}) async-start(f16[16,136,128]{2,1,0:T(8,128)(2,1)} %convert_element_type.24), calls=%async_computation.1 | async-start | bytes 1114112 | tf_op jit(solution)/shard_map/all_to_all | solution.py:759
  73.7 23.9 %collective-permute-start.4 = (f16[16,136,128]{2,1,0:T(8,128)(2,1)S(1)}, f16[16,136,128]{2,1,0:T(8,128)(2,1)S(1)}, u32[]{:S(2)}, u32[]{:S(2)}) collective-permute-start(f16[16,136,128]{2,1,0:T(8,128)(2,1)S(1)} %all-to-all-done.1), channel_id=1, source_target_pairs={{0,16},{16,0},{1,17},{17,1},{2,18},{18,2},{3,19},{19,3},{4,20},{20... | collective-permute-start | bytes 1671176 | tf_op jit(solution)/shard_map/ppermute | solution.py:714
  82.7 24.3 %all-to-all-start.2 = ((f16[16,200,128]{2,1,0:T(8,128)(2,1)}), f16[16,200,128]{2,1,0:T(8,128)(2,1)}, u32[]{:S(2)}, u32[]{:S(2)}) async-start(f16[16,200,128]{2,1,0:T(8,128)(2,1)} %convert_element_type.23), calls=%async_computation.2 | async-start | bytes 1638400 | tf_op jit(solution)/shard_map/all_to_all | solution.py:765
  87.4 3.4 %copy-start = (bf16[32,256,512]{2,1,0:T(8,128)(2,1)S(1)}, bf16[32,256,512]{2,1,0:T(8,128)(2,1)}, u32[]{:S(2)}) copy-start(bf16[32,256,512]{2,1,0:T(8,128)(2,1)} %get-tuple-element.63.normed_ref.refs_0_) | copy-start | bytes 25165828
  90.8 7.2 %copy-start.1 = (bf16[32,256,512]{2,1,0:T(8,128)(2,1)S(1)}, bf16[32,256,512]{2,1,0:T(8,128)(2,1)}, u32[]{:S(2)}) copy-start(bf16[32,256,512]{2,1,0:T(8,128)(2,1)} %get-tuple-element.63.normed_ref.refs_0_) | copy-start | bytes 25165828
  94.1 10.3 %collective-permute-start.5 = (f32[16,128]{1,0:T(8,128)S(1)}, f32[16,128]{1,0:T(8,128)S(1)}, u32[]{:S(2)}, u32[]{:S(2)}) collective-permute-start(f32[16,128]{1,0:T(8,128)S(1)} %pair_weight.1), channel_id=1, source_target_pairs={{0,16},{16,0},{1,17},{17,1},{2,18},{18,2},{3,19},{19,3},{4,20},{20... | collective-permute-start | bytes 24584 | tf_op jit(solution)/shard_map/ppermute | solution.py:714
  94.6 9.7 %collective-permute-start.6 = (f32[16,128]{1,0:T(8,128)S(1)}, f32[16,128]{1,0:T(8,128)S(1)}, u32[]{:S(2)}, u32[]{:S(2)}) collective-permute-start(f32[16,128]{1,0:T(8,128)S(1)} %pair_weight.1), channel_id=1, source_target_pairs={{0,8},{8,0},{1,9},{9,1},{2,10},{10,2},{3,11},{11,3},{4,12},{12,4},... | collective-permute-start | bytes 24584 | tf_op jit(solution)/shard_map/ppermute | solution.py:714
  96.2 8.1 %collective-permute-start.7 = (f32[16,128]{1,0:T(8,128)S(1)}, f32[16,128]{1,0:T(8,128)S(1)}, u32[]{:S(2)}, u32[]{:S(2)}) collective-permute-start(f32[16,128]{1,0:T(8,128)S(1)} %pair_weight.1), channel_id=1, source_target_pairs={{0,24},{8,16},{16,8},{24,0},{1,25},{9,17},{17,9},{25,1},{2,26},{10... | collective-permute-start | bytes 24584 | tf_op jit(solution)/shard_map/ppermute | solution.py:772
  97.8 1.0 copy-start.2
  98.9 11.8 %copy-start.8 = (bf16[768,768]{1,0:T(8,128)(2,1)S(1)}, bf16[768,768]{1,0:T(8,128)(2,1)}, u32[]{:S(2)}) copy-start(bf16[768,768]{1,0:T(8,128)(2,1)} %refs_6_.1) | copy-start | bytes 3538948
  98.9 11.8 %copy-start.9 = (bf16[768,768]{1,0:T(8,128)(2,1)S(1)}, bf16[768,768]{1,0:T(8,128)(2,1)}, u32[]{:S(2)}) copy-start(bf16[768,768]{1,0:T(8,128)(2,1)} %refs_7_.1) | copy-start | bytes 3538948
  98.9 11.9 %copy-start.11 = (f32[768,128]{1,0:T(8,128)S(1)}, f32[768,128]{1,0:T(8,128)}, u32[]{:S(2)}) copy-start(f32[768,128]{1,0:T(8,128)} %get-tuple-element.69.refs_1_) | copy-start | bytes 1179652
  98.9 11.9 %copy-start.12 = (f32[768,128]{1,0:T(8,128)S(1)}, f32[768,128]{1,0:T(8,128)}, u32[]{:S(2)}) copy-start(f32[768,128]{1,0:T(8,128)} %get-tuple-element.70.refs_2_) | copy-start | bytes 1179652
  107.0 3.8 %copy-start.6 = (bf16[768,768]{1,0:T(8,128)(2,1)S(1)}, bf16[768,768]{1,0:T(8,128)(2,1)}, u32[]{:S(2)}) copy-start(bf16[768,768]{1,0:T(8,128)(2,1)} %refs_4_.3) | copy-start | bytes 3538948
  107.0 3.8 %copy-start.7 = (bf16[768,768]{1,0:T(8,128)(2,1)S(1)}, bf16[768,768]{1,0:T(8,128)(2,1)}, u32[]{:S(2)}) copy-start(bf16[768,768]{1,0:T(8,128)(2,1)} %refs_5_.1) | copy-start | bytes 3538948
  107.0 3.8 %copy-start.13 = (f32[8,128]{1,0:T(8,128)S(1)}, f32[8,128]{1,0:T(8,128)}, u32[]{:S(2)}) copy-start(f32[8,128]{1,0:T(8,128)} %get-tuple-element.71.refs_3_) | copy-start | bytes 12292
  107.0 5.9 %collective-permute-start.10 = (f32[16,128]{1,0:T(8,128)S(1)}, f32[16,128]{1,0:T(8,128)S(1)}, u32[]{:S(2)}, u32[]{:S(2)}) collective-permute-start(f32[16,128]{1,0:T(8,128)S(1)} %add_add_fusion), channel_id=1, source_target_pairs={{0,3},{1,2},{2,1},{3,0},{4,7},{5,6},{6,5},{7,4},{8,11},{9,10},{10,... | collective-permute-start | bytes 24584 | tf_op jit(solution)/shard_map/ppermute | solution.py:737
  108.6 4.3 %collective-permute-start.8 = (f32[16,128]{1,0:T(8,128)S(1)}, f32[16,128]{1,0:T(8,128)S(1)}, u32[]{:S(2)}, u32[]{:S(2)}) collective-permute-start(f32[16,128]{1,0:T(8,128)S(1)} %add_add_fusion), channel_id=1, source_target_pairs={{0,1},{1,0},{2,3},{3,2},{4,5},{5,4},{6,7},{7,6},{8,9},{9,8},{10,11... | collective-permute-start | bytes 24584 | tf_op jit(solution)/shard_map/ppermute | solution.py:737
  108.8 4.1 %collective-permute-start.9 = (f32[16,128]{1,0:T(8,128)S(1)}, f32[16,128]{1,0:T(8,128)S(1)}, u32[]{:S(2)}, u32[]{:S(2)}) collective-permute-start(f32[16,128]{1,0:T(8,128)S(1)} %add_add_fusion), channel_id=1, source_target_pairs={{0,2},{1,3},{2,0},{3,1},{4,6},{5,7},{6,4},{7,5},{8,10},{9,11},{10,... | collective-permute-start | bytes 24584 | tf_op jit(solution)/shard_map/ppermute | solution.py:737
  113.0 7.1 %collective-permute-start.11 = (bf16[2,64,768]{2,1,0:T(8,128)(2,1)S(1)}, bf16[2,64,768]{2,1,0:T(8,128)(2,1)S(1)}, u32[]{:S(2)}, u32[]{:S(2)}) collective-permute-start(bf16[2,64,768]{2,1,0:T(8,128)(2,1)S(1)} %bitcast.18), channel_id=1, source_target_pairs={{0,8},{8,0},{1,9},{9,1},{2,10},{10,2},{3,11},{11,3},{4,12},{12,4},... | collective-permute-start | bytes 589832 | tf_op jit(solution)/shard_map/ppermute | solution.py:714
  114.5 6.3 %collective-permute-start.12 = (f32[16,128]{1,0:T(8,128)S(1)}, f32[16,128]{1,0:T(8,128)S(1)}, u32[]{:S(2)}, u32[]{:S(2)}) collective-permute-start(f32[16,128]{1,0:T(8,128)S(1)} %add_multiply_fusion), channel_id=1, source_target_pairs={{0,4},{1,5},{2,6},{3,7},{4,0},{5,1},{6,2},{7,3},{8,12},{9,13},{10,... | collective-permute-start | bytes 24584 | tf_op jit(solution)/shard_map/ppermute | solution.py:737

commit v10 on v9

--- a/solution.py
+++ b/solution.py
@@ -761,7 +761,7 @@
     )
     back, late_pair = lax.optimization_barrier((back.astype(jnp.float16), pair))
     pair_normed, pair_inv = pair_units(late_pair)
-    back, _, pair_normed = lax.optimization_barrier((back, grad_bias, pair_normed))
+    back, grad_bias, pair_normed = lax.optimization_barrier((back, grad_bias, pair_normed))
     back = lax.all_to_all(back, ("row", "col"), 0, 0, tiled=True)
 
     other_bias = swap(grad_bias, "samp")

time: 122 us -> 115 us (0.943)
  waiting for transfers between devices: 36.3 us -> 28.9 us
    all_to_all x1, waiting for transfers between devices: 13.7 us -> 6.29 us  [body_heads(): lax.all_to_all(grad_bias.astype(jnp.float16), ('row', 'col'), 0, 0, tiled...]
  transfers between devices with their start and end apart: 16 -> 16, of which waited for: 5 -> 5; matrix products, arithmetic and copies ran while one was open for 4% -> 4% of each run, Pallas kernels for 24% -> 26%
where the time goes in v10:
time: 115 us; the launch traced here: 114 us
  Pallas kernels  41.4 us (36%)
  starting transfers between devices  32.2 us (28%)
  waiting for transfers between devices  28.9 us (25%)
  other arithmetic  6.16 us (5%)
  local copies, waits for them, and re-layouts  4.36 us (4%)
    all_to_all x1, waiting for transfers between devices, body_heads(): bias = lax.all_to_all(bias, ('row', 'col'), 0, 0, tiled=True)  10.6 us
    ppermute x8, starting transfers between devices, send(): return lax.ppermute(block, 'col', [(c, c ^ offset) for c in range(n_col)])  10.4 us
    pallas_call x1, Pallas kernels, pair_bias(): pl.pallas_call(bias_kernel, out_shape=jax.ShapeDtypeStruct((H, tok_col, r...  8.12 us
    pallas_call x1, Pallas kernels, attention(): pl.pallas_call(attention_kernel, out_shape=[jax.ShapeDtypeStruct(back_sha...  7.67 us
    pallas_call x1, Pallas kernels, pair_units(): pl.pallas_call(norm_kernel, out_shape=[jax.ShapeDtypeStruct(shapes[0], jn...  7.45 us
    all_to_all x1, starting transfers between devices, body_heads(): bias = lax.all_to_all(bias, ('row', 'col'), 0, 0, tiled=True)  6.67 us
    all_to_all x1, waiting for transfers between devices, body_heads(): lax.all_to_all(grad_bias.astype(jnp.float16), ('row', 'col'), 0, 0, tiled...  6.29 us
    ppermute x8, waiting for transfers between devices, send(): return lax.ppermute(block, 'col', [(c, c ^ offset) for c in range(n_col)])  5.74 us
  transfers between devices with their start and end apart: 16, of which 5 were waited for; matrix products, arithmetic and copies ran while one was open for 4% of the time, Pallas kernels for 26%

profile of v10, /device:TPU:0, one launch (start us, length us, event | category | flops | bytes accessed | tf_op | source)
XLA Modules:
  0.0 114.0 jit_solution(15012417544872049456)
XLA Ops:
  0.6 0.0 copy-start.4
  0.6 0.0 copy-start.5
  0.7 0.0 copy-start.10
  0.7 4.3 %token_messages.1 = (bf16[2,4,48,256]{3,2,1,0:T(8,128)(2,1)}, bf16[2,4,48,256]{3,2,1,0:T(8,128)(2,1)}, bf16[2,4,48,256]{3,2,1,0:T(8,128)(2,1)}, bf16[2,4,48,256]{3,2,1,0:T(8,128)(2,1)}) custom-call(s32[1]{0:T(128)} %bitcast.4.row_ref, s32[1]{0:T(128)} %bitcast.col_ref, bf16[4,64,768]{2,1,0:T(8,128)(2,1)} %tokens_ref.3, s32[1,64]{1,0:T(1,128)} %bitcast.28, ...), custom_call_target="tpu_custom_call" | custom-call | flops 4000000000 | bytes 4000000 | tf_op jit(solution)/shard_map/token_messages/pallas_call | solution.py:245
  5.0 3.0 %collective-permute-start = (bf16[2,4,48,256]{3,2,1,0:T(8,128)(2,1)}, bf16[2,4,48,256]{3,2,1,0:T(8,128)(2,1)S(1)}, u32[]{:S(2)}, u32[]{:S(2)}) collective-permute-start(bf16[2,4,48,256]{3,2,1,0:T(8,128)(2,1)} %get-tuple-element.45), channel_id=1, source_target_pairs={{0,2},{1,3},{2,0},{3,1},{4,6},{5,7},{6,4},{7,5},{8,10},{9,11},{10,... | collective-permute-start | bytes 589832 | tf_op jit(solution)/shard_map/ppermute | solution.py:737
  8.0 2.6 %collective-permute-start.1 = (bf16[2,4,48,256]{3,2,1,0:T(8,128)(2,1)}, bf16[2,4,48,256]{3,2,1,0:T(8,128)(2,1)S(1)}, u32[]{:S(2)}, u32[]{:S(2)}) collective-permute-start(bf16[2,4,48,256]{3,2,1,0:T(8,128)(2,1)} %get-tuple-element.46), channel_id=1, source_target_pairs={{0,4},{1,5},{2,6},{3,7},{4,0},{5,1},{6,2},{7,3},{8,12},{9,13},{10,... | collective-permute-start | bytes 589832 | tf_op jit(solution)/shard_map/ppermute | solution.py:737
  10.6 0.0 collective-permute-start.2
  10.6 0.0 copy-done.4
  10.6 0.0 copy-done.5
  10.6 0.0 copy-done.10
  10.6 8.1 %pair_bias.1 = f32[16,64,256]{2,1,0:T(8,128)S(1)} custom-call(bf16[2,128,64,128]{3,2,1,0:T(8,128)(2,1)S(1)} %bitcast.23, bf16[16,128]{1,0:T(8,128)(2,1)S(1)} %bitcast.20, s32[1,64]{1,0:T(1,128)S(1)} %bitcast.24), custom_call_target="tpu_custom_call" | custom-call | flops 6000000000 | bytes 5000000 | tf_op jit(solution)/shard_map/pair_bias/pallas_call | solution.py:383
  18.7 0.0 copy-start.3
  18.7 0.9 convert_element_type.21
  19.6 0.0 collective-permute-done.refs_1_
  19.6 5.7 %collective-permute-done.1.refs_2_ = bf16[2,4,48,256]{3,2,1,0:T(8,128)(2,1)S(1)} collective-permute-done((bf16[2,4,48,256]{3,2,1,0:T(8,128)(2,1)}, bf16[2,4,48,256]{3,2,1,0:T(8,128)(2,1)S(1)}, u32[]{:S(2)}, u32[]{:S(2)}) %collective-permute-start.1) | collective-permute-done | bytes 196640 | tf_op jit(solution)/shard_map/ppermute | solution.py:737
  25.4 0.0 collective-permute-done.2.refs_3_
  25.4 6.7 %all-to-all-start = ((f16[16,64,256]{2,1,0:T(8,128)(2,1)}), f16[16,64,256]{2,1,0:T(8,128)(2,1)S(1)}, u32[]{:S(2)}, u32[]{:S(2)}) async-start(f16[16,64,256]{2,1,0:T(8,128)(2,1)} %convert_element_type.21), calls=%async_computation | async-start | bytes 1048576 | tf_op jit(solution)/shard_map/all_to_all | solution.py:754
  32.0 0.0 copy-done.3
  32.1 0.1 pad_maximum_fusion
  32.2 0.5 collective-permute-start.3
  32.7 3.0 %own_rows.1 = (f32[768,128]{1,0:T(8,128)}, f32[768,128]{1,0:T(8,128)}, f32[8,128]{1,0:T(8,128)}) custom-call(s32[1]{0:T(128)} %bitcast.4.row_ref, bf16[4,64,768]{2,1,0:T(8,128)(2,1)} %tokens_ref.3, s32[1,64]{1,0:T(1,128)} %bitcast.29, bf16[32,768]{1,0:T(8,128)(2,1)} %table_ref.3, bf16[768,768]{1,0:T(8,128)(2,1)} %refs_7_.1, bf16[4,64,768]{2,1,0:T(8,128)(2,1)} %cot_ref.1), custom_call_target="tpu_custom_call" | custom-call | flops 3000000000 | bytes 3000000 | tf_op jit(solution)/shard_map/own_rows/pallas_call | solution.py:289
  35.7 0.0 collective-permute-done.3.refs_4_
  35.7 10.6 %all-to-all-done = f16[16,64,256]{2,1,0:T(8,128)(2,1)S(1)} async-done(((f16[16,64,256]{2,1,0:T(8,128)(2,1)}), f16[16,64,256]{2,1,0:T(8,128)(2,1)S(1)}, u32[]{:S(2)}, u32[]{:S(2)}) %all-to-all-start) | async-done | bytes 524320 | tf_op jit(solution)/shard_map/all_to_all | solution.py:754
  46.3 0.1 convert_element_type.22.refs_5_
  46.4 7.7 %attention.1 = (f32[16,200,128]{2,1,0:T(8,128)S(1)}, f32[16,136,128]{2,1,0:T(8,128)S(1)}) custom-call(s32[1]{0:T(128)} %bitcast.col_ref, bf16[2,4,48,256]{3,2,1,0:T(8,128)(2,1)S(1)} %copy-done.3, bf16[2,4,48,256]{3,2,1,0:T(8,128)(2,1)S(1)} %collective-permute-done.refs_1_, bf16[2,4,48,256]{3,2,1,0:T(8,128)(2,1)S(1)} %collective-permute-done.1.refs_2_, ...), custom_call_target="tpu_custom_call" | custom-call | flops 8000000000 | bytes 6000000 | tf_op jit(solution)/shard_map/attention/pallas_call | solution.py:530
  54.1 0.9 convert_element_type.24
  55.0 4.0 %all-to-all-start.1 = ((f16[16,136,128]{2,1,0:T(8,128)(2,1)}), f16[16,136,128]{2,1,0:T(8,128)(2,1)S(1)}, u32[]{:S(2)}, u32[]{:S(2)}) async-start(f16[16,136,128]{2,1,0:T(8,128)(2,1)} %convert_element_type.24), calls=%async_computation.1 | async-start | bytes 1114112 | tf_op jit(solution)/shard_map/all_to_all | solution.py:759
  59.0 1.0 convert_element_type.23
  60.0 7.4 %pair_units.1 = (bf16[32,256,512]{2,1,0:T(8,128)(2,1)}, f32[32,8,512]{2,1,0:T(8,128)}) custom-call(bf16[2,128,64,128]{3,2,1,0:T(8,128)(2,1)} %bitcast.22), custom_call_target="tpu_custom_call" | custom-call | flops 6000000000 | bytes 12000000 | tf_op jit(solution)/shard_map/pair_units/pallas_call | solution.py:413
  67.5 6.3 %all-to-all-done.1 = f16[16,136,128]{2,1,0:T(8,128)(2,1)S(1)} async-done(((f16[16,136,128]{2,1,0:T(8,128)(2,1)}), f16[16,136,128]{2,1,0:T(8,128)(2,1)S(1)}, u32[]{:S(2)}, u32[]{:S(2)}) %all-to-all-start.1) | async-done | bytes 557088 | tf_op jit(solution)/shard_map/all_to_all | solution.py:759
  73.7 1.5 %collective-permute-start.4 = (f16[16,136,128]{2,1,0:T(8,128)(2,1)S(1)}, f16[16,136,128]{2,1,0:T(8,128)(2,1)S(1)}, u32[]{:S(2)}, u32[]{:S(2)}) collective-permute-start(f16[16,136,128]{2,1,0:T(8,128)(2,1)S(1)} %all-to-all-done.1), channel_id=1, source_target_pairs={{0,16},{16,0},{1,17},{17,1},{2,18},{18,2},{3,19},{19,3},{4,20},{20... | collective-permute-start | bytes 1671176 | tf_op jit(solution)/shard_map/ppermute | solution.py:714
  75.3 4.5 %all-to-all-start.2 = ((f16[16,200,128]{2,1,0:T(8,128)(2,1)}), f16[16,200,128]{2,1,0:T(8,128)(2,1)}, u32[]{:S(2)}, u32[]{:S(2)}) async-start(f16[16,200,128]{2,1,0:T(8,128)(2,1)} %convert_element_type.23), calls=%async_computation.2 | async-start | bytes 1638400 | tf_op jit(solution)/shard_map/all_to_all | solution.py:765
  79.7 0.1 convert_element_type.25
  79.9 0.1 slice_multiply_fusion.1
  80.0 3.4 %copy-done = bf16[32,256,512]{2,1,0:T(8,128)(2,1)S(1)} copy-done((bf16[32,256,512]{2,1,0:T(8,128)(2,1)S(1)}, bf16[32,256,512]{2,1,0:T(8,128)(2,1)}, u32[]{:S(2)}) %copy-start) | copy-done | bytes 8388632
  83.4 3.3 %pair_weight.1 = f32[16,128]{1,0:T(8,128)S(1)} custom-call(bf16[32,256,512]{2,1,0:T(8,128)(2,1)S(1)} %copy-done, f32[2048,128]{1,0:T(8,128)S(1)} %bitcast.17), custom_call_target="tpu_custom_call" | custom-call | flops 1000000 | bytes 100000 | tf_op jit(solution)/shard_map/pair_weight/pallas_call | solution.py:670
  86.6 0.6 collective-permute-start.5
  87.2 1.6 %collective-permute-start.6 = (f32[16,128]{1,0:T(8,128)S(1)}, f32[16,128]{1,0:T(8,128)S(1)}, u32[]{:S(2)}, u32[]{:S(2)}) collective-permute-start(f32[16,128]{1,0:T(8,128)S(1)} %pair_weight.1), channel_id=1, source_target_pairs={{0,8},{8,0},{1,9},{9,1},{2,10},{10,2},{3,11},{11,3},{4,12},{12,4},... | collective-permute-start | bytes 24584 | tf_op jit(solution)/shard_map/ppermute | solution.py:714
  88.8 1.4 %collective-permute-start.7 = (f32[16,128]{1,0:T(8,128)S(1)}, f32[16,128]{1,0:T(8,128)S(1)}, u32[]{:S(2)}, u32[]{:S(2)}) collective-permute-start(f32[16,128]{1,0:T(8,128)S(1)} %pair_weight.1), channel_id=1, source_target_pairs={{0,24},{8,16},{16,8},{24,0},{1,25},{9,17},{17,9},{25,1},{2,26},{10... | collective-permute-start | bytes 24584 | tf_op jit(solution)/shard_map/ppermute | solution.py:772
  90.2 0.0 collective-permute-done.4
  90.2 0.1 convert_element_type.26
  90.3 0.1 slice_multiply_fusion
  90.4 0.1 bitcast_add_fusion.refs_2_
  90.5 0.9 copy-done.2
  91.4 5.5 %pair_backward.1 = bf16[2,128,64,128]{3,2,1,0:T(8,128)(2,1)} custom-call(bf16[32,256,512]{2,1,0:T(8,128)(2,1)S(1)} %copy-done.1, f32[32,8,512]{2,1,0:T(8,128)S(1)} %copy-done.2, f32[2048,128]{1,0:T(8,128)S(1)} %bitcast_add_fusion.refs_2_, bf16[16,128]{1,0:T(8,128)(2,1)S(1)} %bitcast.21), custom_call_target="tpu_custom_call" | custom-call | flops 1000000 | bytes 100000 | tf_op jit(solution)/shard_map/pair_backward/pallas_call | solution.py:687
  96.9 0.0 collective-permute-done.5
  96.9 0.0 collective-permute-done.6
  96.9 0.0 collective-permute-done.7
  96.9 2.6 %all-to-all-done.2 = f16[16,200,128]{2,1,0:T(8,128)(2,1)} async-done(((f16[16,200,128]{2,1,0:T(8,128)(2,1)}), f16[16,200,128]{2,1,0:T(8,128)(2,1)}, u32[]{:S(2)}, u32[]{:S(2)}) %all-to-all-start.2) | async-done | bytes 819232 | tf_op jit(solution)/shard_map/all_to_all | solution.py:765
  99.5 0.0 copy-start.13
  99.5 1.6 %collective-permute-start.10 = (f32[16,128]{1,0:T(8,128)S(1)}, f32[16,128]{1,0:T(8,128)S(1)}, u32[]{:S(2)}, u32[]{:S(2)}) collective-permute-start(f32[16,128]{1,0:T(8,128)S(1)} %add_add_fusion), channel_id=1, source_target_pairs={{0,3},{1,2},{2,1},{3,0},{4,7},{5,6},{6,5},{7,4},{8,11},{9,10},{10,... | collective-permute-start | bytes 24584 | tf_op jit(solution)/shard_map/ppermute | solution.py:737
  101.2 0.2 collective-permute-start.8
  101.4 0.6 collective-permute-start.9
  102.0 1.3 %convert_element_type.27.refs_0_ = f32[16,200,128]{2,1,0:T(8,128)S(1)} convert(f16[16,200,128]{2,1,0:T(8,128)(2,1)} %all-to-all-done.2) | non-fusion elementwise | flops 409600 | bytes 2457600 | tf_op jit(solution)/shard_map/convert_element_type | solution.py:784
  103.3 2.1 %token_back.1 = bf16[128,768]{1,0:T(8,128)(2,1)S(1)} custom-call(f32[16,200,128]{2,1,0:T(8,128)S(1)} %convert_element_type.27.refs_0_, f32[768,128]{1,0:T(8,128)S(1)} %copy-done.11, f32[768,128]{1,0:T(8,128)S(1)} %copy-done.12, f32[8,128]{1,0:T(8,128)S(1)} %copy-done.13, bf16[768,768]{1,0:T(8,128)(2,1)S(1)} %copy-done.6, bf16[768,768]{1,0:T(8,128)(2,1)S(1)} %copy-done.7, ...), custom_call_target="tpu_custom_call" | custom-call | flops 4000000000 | bytes 8000000 | tf_op jit(solution)/shard_map/token_back/pallas_call | solution.py:603
  105.5 0.0 collective-permute-done.10
  105.5 0.0 collective-permute-done.8
  105.5 0.0 collective-permute-done.9
  105.5 1.6 %collective-permute-start.11 = (bf16[2,64,768]{2,1,0:T(8,128)(2,1)S(1)}, bf16[2,64,768]{2,1,0:T(8,128)(2,1)S(1)}, u32[]{:S(2)}, u32[]{:S(2)}) collective-permute-start(bf16[2,64,768]{2,1,0:T(8,128)(2,1)S(1)} %bitcast.18), channel_id=1, source_target_pairs={{0,8},{8,0},{1,9},{9,1},{2,10},{10,2},{3,11},{11,3},{4,12},{12,4},... | collective-permute-start | bytes 589832 | tf_op jit(solution)/shard_map/ppermute | solution.py:714
  107.1 1.8 %collective-permute-start.12 = (f32[16,128]{1,0:T(8,128)S(1)}, f32[16,128]{1,0:T(8,128)S(1)}, u32[]{:S(2)}, u32[]{:S(2)}) collective-permute-start(f32[16,128]{1,0:T(8,128)S(1)} %add_multiply_fusion), channel_id=1, source_target_pairs={{0,4},{1,5},{2,6},{3,7},{4,0},{5,1},{6,2},{7,3},{8,12},{9,13},{10,... | collective-permute-start | bytes 24584 | tf_op jit(solution)/shard_map/ppermute | solution.py:737
  108.9 3.7 %collective-permute-done.11 = bf16[2,64,768]{2,1,0:T(8,128)(2,1)S(1)} collective-permute-done((bf16[2,64,768]{2,1,0:T(8,128)(2,1)S(1)}, bf16[2,64,768]{2,1,0:T(8,128)(2,1)S(1)}, u32[]{:S(2)}, u32[]{:S(2)}) %collective-permute-start.11) | collective-permute-done | bytes 196640 | tf_op jit(solution)/shard_map/ppermute | solution.py:714
  112.6 0.8 pad_maximum_fusion.1
  113.4 0.0 collective-permute-done.12
  113.4 0.6 add_bitcast_fusion
  (26 shorter events, 0.1 us)
Async XLA Ops:
  0.6 10.0 %copy-start.4 = (bf16[128,16]{0,1:T(8,128)(2,1)S(1)}, bf16[128,16]{0,1:T(8,128)(2,1)}, u32[]{:S(2)}) copy-start(bf16[128,16]{0,1:T(8,128)(2,1)} %param.16) | copy-start | bytes 12292
  0.6 9.9 %copy-start.5 = (bf16[256,64,128]{2,1,0:T(8,128)(2,1)S(1)}, bf16[256,64,128]{2,1,0:T(8,128)(2,1)}, u32[]{:S(2)}) copy-start(bf16[256,64,128]{2,1,0:T(8,128)(2,1)} %param.15) | copy-start | bytes 12582916
  0.7 9.9 %copy-start.10 = (s32[64]{0:T(128)S(1)}, s32[64]{0:T(128)}, u32[]{:S(2)}) copy-start(s32[64]{0:T(128)} %param.14) | copy-start | bytes 772
  5.0 14.7 %collective-permute-start = (bf16[2,4,48,256]{3,2,1,0:T(8,128)(2,1)}, bf16[2,4,48,256]{3,2,1,0:T(8,128)(2,1)S(1)}, u32[]{:S(2)}, u32[]{:S(2)}) collective-permute-start(bf16[2,4,48,256]{3,2,1,0:T(8,128)(2,1)} %get-tuple-element.45), channel_id=1, source_target_pairs={{0,2},{1,3},{2,0},{3,1},{4,6},{5,7},{6,4},{7,5},{8,10},{9,11},{10,... | collective-permute-start | bytes 589832 | tf_op jit(solution)/shard_map/ppermute | solution.py:737
  8.0 17.4 %collective-permute-start.1 = (bf16[2,4,48,256]{3,2,1,0:T(8,128)(2,1)}, bf16[2,4,48,256]{3,2,1,0:T(8,128)(2,1)S(1)}, u32[]{:S(2)}, u32[]{:S(2)}) collective-permute-start(bf16[2,4,48,256]{3,2,1,0:T(8,128)(2,1)} %get-tuple-element.46), channel_id=1, source_target_pairs={{0,4},{1,5},{2,6},{3,7},{4,0},{5,1},{6,2},{7,3},{8,12},{9,13},{10,... | collective-permute-start | bytes 589832 | tf_op jit(solution)/shard_map/ppermute | solution.py:737
  10.6 14.8 %collective-permute-start.2 = (bf16[2,4,48,256]{3,2,1,0:T(8,128)(2,1)}, bf16[2,4,48,256]{3,2,1,0:T(8,128)(2,1)S(1)}, u32[]{:S(2)}, u32[]{:S(2)}) collective-permute-start(bf16[2,4,48,256]{3,2,1,0:T(8,128)(2,1)} %get-tuple-element.47), channel_id=1, source_target_pairs={{0,6},{1,7},{2,4},{3,5},{4,2},{5,3},{6,0},{7,1},{8,14},{9,15},{10,... | collective-permute-start | bytes 589832 | tf_op jit(solution)/shard_map/ppermute | solution.py:737
  18.7 13.3 %copy-start.3 = (bf16[2,4,48,256]{3,2,1,0:T(8,128)(2,1)S(1)}, bf16[2,4,48,256]{3,2,1,0:T(8,128)(2,1)}, u32[]{:S(2)}) copy-start(bf16[2,4,48,256]{3,2,1,0:T(8,128)(2,1)} %get-tuple-element.48.refs_0_) | copy-start | bytes 589828
  25.4 20.9 %all-to-all-start = ((f16[16,64,256]{2,1,0:T(8,128)(2,1)}), f16[16,64,256]{2,1,0:T(8,128)(2,1)S(1)}, u32[]{:S(2)}, u32[]{:S(2)}) async-start(f16[16,64,256]{2,1,0:T(8,128)(2,1)} %convert_element_type.21), calls=%async_computation | async-start | bytes 1048576 | tf_op jit(solution)/shard_map/all_to_all | solution.py:754
  32.2 3.5 %collective-permute-start.3 = (bf16[4,4,48,256]{3,2,1,0:T(8,128)(2,1)S(1)}, bf16[4,4,48,256]{3,2,1,0:T(8,128)(2,1)S(1)}, u32[]{:S(2)}, u32[]{:S(2)}) collective-permute-start(bf16[4,4,48,256]{3,2,1,0:T(8,128)(2,1)S(1)} %pad_maximum_fusion), channel_id=1, source_target_pairs={{0,1},{1,0},{2,3},{3,2},{4,5},{5,4},{6,7},{7,6},{8,9},{9,8},{10,11... | collective-permute-start | bytes 1179656 | tf_op jit(solution)/shard_map/ppermute | solution.py:737
  55.0 18.8 %all-to-all-start.1 = ((f16[16,136,128]{2,1,0:T(8,128)(2,1)}), f16[16,136,128]{2,1,0:T(8,128)(2,1)S(1)}, u32[]{:S(2)}, u32[]{:S(2)}) async-start(f16[16,136,128]{2,1,0:T(8,128)(2,1)} %convert_element_type.24), calls=%async_computation.1 | async-start | bytes 1114112 | tf_op jit(solution)/shard_map/all_to_all | solution.py:759
  73.7 16.4 %collective-permute-start.4 = (f16[16,136,128]{2,1,0:T(8,128)(2,1)S(1)}, f16[16,136,128]{2,1,0:T(8,128)(2,1)S(1)}, u32[]{:S(2)}, u32[]{:S(2)}) collective-permute-start(f16[16,136,128]{2,1,0:T(8,128)(2,1)S(1)} %all-to-all-done.1), channel_id=1, source_target_pairs={{0,16},{16,0},{1,17},{17,1},{2,18},{18,2},{3,19},{19,3},{4,20},{20... | collective-permute-start | bytes 1671176 | tf_op jit(solution)/shard_map/ppermute | solution.py:714
  75.3 24.3 %all-to-all-start.2 = ((f16[16,200,128]{2,1,0:T(8,128)(2,1)}), f16[16,200,128]{2,1,0:T(8,128)(2,1)}, u32[]{:S(2)}, u32[]{:S(2)}) async-start(f16[16,200,128]{2,1,0:T(8,128)(2,1)} %convert_element_type.23), calls=%async_computation.2 | async-start | bytes 1638400 | tf_op jit(solution)/shard_map/all_to_all | solution.py:765
  80.0 3.4 %copy-start = (bf16[32,256,512]{2,1,0:T(8,128)(2,1)S(1)}, bf16[32,256,512]{2,1,0:T(8,128)(2,1)}, u32[]{:S(2)}) copy-start(bf16[32,256,512]{2,1,0:T(8,128)(2,1)} %get-tuple-element.64.normed_ref.refs_0_) | copy-start | bytes 25165828
  83.3 7.2 %copy-start.1 = (bf16[32,256,512]{2,1,0:T(8,128)(2,1)S(1)}, bf16[32,256,512]{2,1,0:T(8,128)(2,1)}, u32[]{:S(2)}) copy-start(bf16[32,256,512]{2,1,0:T(8,128)(2,1)} %get-tuple-element.64.normed_ref.refs_0_) | copy-start | bytes 25165828
  86.6 10.3 %collective-permute-start.5 = (f32[16,128]{1,0:T(8,128)S(1)}, f32[16,128]{1,0:T(8,128)S(1)}, u32[]{:S(2)}, u32[]{:S(2)}) collective-permute-start(f32[16,128]{1,0:T(8,128)S(1)} %pair_weight.1), channel_id=1, source_target_pairs={{0,16},{16,0},{1,17},{17,1},{2,18},{18,2},{3,19},{19,3},{4,20},{20... | collective-permute-start | bytes 24584 | tf_op jit(solution)/shard_map/ppermute | solution.py:714
  87.2 9.7 %collective-permute-start.6 = (f32[16,128]{1,0:T(8,128)S(1)}, f32[16,128]{1,0:T(8,128)S(1)}, u32[]{:S(2)}, u32[]{:S(2)}) collective-permute-start(f32[16,128]{1,0:T(8,128)S(1)} %pair_weight.1), channel_id=1, source_target_pairs={{0,8},{8,0},{1,9},{9,1},{2,10},{10,2},{3,11},{11,3},{4,12},{12,4},... | collective-permute-start | bytes 24584 | tf_op jit(solution)/shard_map/ppermute | solution.py:714
  88.8 8.1 %collective-permute-start.7 = (f32[16,128]{1,0:T(8,128)S(1)}, f32[16,128]{1,0:T(8,128)S(1)}, u32[]{:S(2)}, u32[]{:S(2)}) collective-permute-start(f32[16,128]{1,0:T(8,128)S(1)} %pair_weight.1), channel_id=1, source_target_pairs={{0,24},{8,16},{16,8},{24,0},{1,25},{9,17},{17,9},{25,1},{2,26},{10... | collective-permute-start | bytes 24584 | tf_op jit(solution)/shard_map/ppermute | solution.py:772
  90.4 1.0 copy-start.2
  91.4 11.8 %copy-start.8 = (bf16[768,768]{1,0:T(8,128)(2,1)S(1)}, bf16[768,768]{1,0:T(8,128)(2,1)}, u32[]{:S(2)}) copy-start(bf16[768,768]{1,0:T(8,128)(2,1)} %refs_6_.1) | copy-start | bytes 3538948
  91.4 11.8 %copy-start.9 = (bf16[768,768]{1,0:T(8,128)(2,1)S(1)}, bf16[768,768]{1,0:T(8,128)(2,1)}, u32[]{:S(2)}) copy-start(bf16[768,768]{1,0:T(8,128)(2,1)} %refs_7_.1) | copy-start | bytes 3538948
  91.4 11.8 %copy-start.11 = (f32[768,128]{1,0:T(8,128)S(1)}, f32[768,128]{1,0:T(8,128)}, u32[]{:S(2)}) copy-start(f32[768,128]{1,0:T(8,128)} %get-tuple-element.71.refs_1_) | copy-start | bytes 1179652
  91.4 11.9 %copy-start.12 = (f32[768,128]{1,0:T(8,128)S(1)}, f32[768,128]{1,0:T(8,128)}, u32[]{:S(2)}) copy-start(f32[768,128]{1,0:T(8,128)} %get-tuple-element.72.refs_2_) | copy-start | bytes 1179652
  99.5 3.8 %copy-start.6 = (bf16[768,768]{1,0:T(8,128)(2,1)S(1)}, bf16[768,768]{1,0:T(8,128)(2,1)}, u32[]{:S(2)}) copy-start(bf16[768,768]{1,0:T(8,128)(2,1)} %refs_4_.3) | copy-start | bytes 3538948
  99.5 3.8 %copy-start.7 = (bf16[768,768]{1,0:T(8,128)(2,1)S(1)}, bf16[768,768]{1,0:T(8,128)(2,1)}, u32[]{:S(2)}) copy-start(bf16[768,768]{1,0:T(8,128)(2,1)} %refs_5_.1) | copy-start | bytes 3538948
  99.5 3.8 %copy-start.13 = (f32[8,128]{1,0:T(8,128)S(1)}, f32[8,128]{1,0:T(8,128)}, u32[]{:S(2)}) copy-start(f32[8,128]{1,0:T(8,128)} %get-tuple-element.73.refs_3_) | copy-start | bytes 12292
  99.5 5.9 %collective-permute-start.10 = (f32[16,128]{1,0:T(8,128)S(1)}, f32[16,128]{1,0:T(8,128)S(1)}, u32[]{:S(2)}, u32[]{:S(2)}) collective-permute-start(f32[16,128]{1,0:T(8,128)S(1)} %add_add_fusion), channel_id=1, source_target_pairs={{0,3},{1,2},{2,1},{3,0},{4,7},{5,6},{6,5},{7,4},{8,11},{9,10},{10,... | collective-permute-start | bytes 24584 | tf_op jit(solution)/shard_map/ppermute | solution.py:737
  101.2 4.3 %collective-permute-start.8 = (f32[16,128]{1,0:T(8,128)S(1)}, f32[16,128]{1,0:T(8,128)S(1)}, u32[]{:S(2)}, u32[]{:S(2)}) collective-permute-start(f32[16,128]{1,0:T(8,128)S(1)} %add_add_fusion), channel_id=1, source_target_pairs={{0,1},{1,0},{2,3},{3,2},{4,5},{5,4},{6,7},{7,6},{8,9},{9,8},{10,11... | collective-permute-start | bytes 24584 | tf_op jit(solution)/shard_map/ppermute | solution.py:737
  101.4 4.1 %collective-permute-start.9 = (f32[16,128]{1,0:T(8,128)S(1)}, f32[16,128]{1,0:T(8,128)S(1)}, u32[]{:S(2)}, u32[]{:S(2)}) collective-permute-start(f32[16,128]{1,0:T(8,128)S(1)} %add_add_fusion), channel_id=1, source_target_pairs={{0,2},{1,3},{2,0},{3,1},{4,6},{5,7},{6,4},{7,5},{8,10},{9,11},{10,... | collective-permute-start | bytes 24584 | tf_op jit(solution)/shard_map/ppermute | solution.py:737
  105.5 7.1 %collective-permute-start.11 = (bf16[2,64,768]{2,1,0:T(8,128)(2,1)S(1)}, bf16[2,64,768]{2,1,0:T(8,128)(2,1)S(1)}, u32[]{:S(2)}, u32[]{:S(2)}) collective-permute-start(bf16[2,64,768]{2,1,0:T(8,128)(2,1)S(1)} %bitcast.18), channel_id=1, source_target_pairs={{0,8},{8,0},{1,9},{9,1},{2,10},{10,2},{3,11},{11,3},{4,12},{12,4},... | collective-permute-start | bytes 589832 | tf_op jit(solution)/shard_map/ppermute | solution.py:714
  107.1 6.3 %collective-permute-start.12 = (f32[16,128]{1,0:T(8,128)S(1)}, f32[16,128]{1,0:T(8,128)S(1)}, u32[]{:S(2)}, u32[]{:S(2)}) collective-permute-start(f32[16,128]{1,0:T(8,128)S(1)} %add_multiply_fusion), channel_id=1, source_target_pairs={{0,4},{1,5},{2,6},{3,7},{4,0},{5,1},{6,2},{7,3},{8,12},{9,13},{10,... | collective-permute-start | bytes 24584 | tf_op jit(solution)/shard_map/ppermute | solution.py:737

commit v11 on v10

--- a/solution.py
+++ b/solution.py
@@ -776,14 +776,15 @@
         pair.shape, pair_normed, pair_inv, grads, weight_t, total_tokens / samples
     )
 
-    pair_grad, back, sums = lax.optimization_barrier(
-        (pair_grad, back, (part, samp_part, row_part, both_part))
+    pair_grad, sums = lax.optimization_barrier(
+        (pair_grad, (part, samp_part, row_part, both_part))
     )
     part = (sums[0] + sums[1]) + (sums[2] + sums[3])
-    sums = (send(part, 1), send(part, 2), send(part, 3))
+    sums = (part, send(part, 1), send(part, 2), send(part, 3))
+    back, sums = lax.optimization_barrier((back, sums))
+    part = ((sums[0] + sums[1]) + (sums[2] + sums[3])) / samples
     token_half = token_back(back.astype(jnp.float32), *own, weights)
-    token_half, sums = lax.optimization_barrier((token_half, sums))
-    part = ((part + sums[0]) + (sums[1] + sums[2])) / samples
+    token_half, part = lax.optimization_barrier((token_half, part))
     last = send(part, 4)
     token_half = token_half.reshape(half, tok_col, D)
     other_half = swap(token_half, "row")

time: 115 us -> 117 us (1.017)
  local copies, waits for them, and re-layouts: 4.36 us -> 6.91 us
    ppermute x8, waiting for transfers between devices: 5.74 us -> 8.58 us  [send(): return lax.ppermute(block, 'col', [(c, c ^ offset) for c in range(n_col)])]
    all_to_all x1, waiting for transfers between devices: 2.6 us -> 0.01 us  [body_heads(): back = lax.all_to_all(back, ('row', 'col'), 0, 0, tiled=True)]
    unnamed x28, local copies, waits for them, and re-layouts: 4.32 us -> 6.87 us
  transfers between devices with their start and end apart: 16 -> 16, of which waited for: 5 -> 6; matrix products, arithmetic and copies ran while one was open for 4% -> 3% of each run, Pallas kernels for 26% -> 24%
where the time goes in v11:
time: 117 us; the launch traced here: 116 us
  Pallas kernels  41.4 us (35%)
  starting transfers between devices  32.2 us (28%)
  waiting for transfers between devices  28.6 us (24%)
  local copies, waits for them, and re-layouts  6.91 us (6%)
  other arithmetic  6.15 us (5%)
    all_to_all x1, waiting for transfers between devices, body_heads(): bias = lax.all_to_all(bias, ('row', 'col'), 0, 0, tiled=True)  10.6 us
    ppermute x8, starting transfers between devices, send(): return lax.ppermute(block, 'col', [(c, c ^ offset) for c in range(n_col)])  10.4 us
    ppermute x8, waiting for transfers between devices, send(): return lax.ppermute(block, 'col', [(c, c ^ offset) for c in range(n_col)])  8.58 us
    pallas_call x1, Pallas kernels, pair_bias(): pl.pallas_call(bias_kernel, out_shape=jax.ShapeDtypeStruct((H, tok_col, r...  8.12 us
    pallas_call x1, Pallas kernels, attention(): pl.pallas_call(attention_kernel, out_shape=[jax.ShapeDtypeStruct(back_sha...  7.67 us
    pallas_call x1, Pallas kernels, pair_units(): pl.pallas_call(norm_kernel, out_shape=[jax.ShapeDtypeStruct(shapes[0], jn...  7.45 us
    unnamed x28, local copies, waits for them, and re-layouts  6.87 us
    all_to_all x1, starting transfers between devices, body_heads(): bias = lax.all_to_all(bias, ('row', 'col'), 0, 0, tiled=True)  6.67 us
  transfers between devices with their start and end apart: 16, of which 6 were waited for; matrix products, arithmetic and copies ran while one was open for 3% of the time, Pallas kernels for 24%

profile of v11, /device:TPU:0, one launch (start us, length us, event | category | flops | bytes accessed | tf_op | source)
XLA Modules:
  0.0 116.2 jit_solution(9495417418230673730)
XLA Ops:
  0.6 0.0 copy-start.5
  0.7 0.0 copy-start.10
  0.7 4.3 %token_messages.1 = (bf16[2,4,48,256]{3,2,1,0:T(8,128)(2,1)}, bf16[2,4,48,256]{3,2,1,0:T(8,128)(2,1)}, bf16[2,4,48,256]{3,2,1,0:T(8,128)(2,1)}, bf16[2,4,48,256]{3,2,1,0:T(8,128)(2,1)}) custom-call(s32[1]{0:T(128)} %bitcast.4.row_ref, s32[1]{0:T(128)} %bitcast.col_ref, bf16[4,64,768]{2,1,0:T(8,128)(2,1)} %tokens_ref.3, s32[1,64]{1,0:T(1,128)} %bitcast.28, ...), custom_call_target="tpu_custom_call" | custom-call | flops 4000000000 | bytes 4000000 | tf_op jit(solution)/shard_map/token_messages/pallas_call | solution.py:245
  5.0 3.0 %collective-permute-start = (bf16[2,4,48,256]{3,2,1,0:T(8,128)(2,1)}, bf16[2,4,48,256]{3,2,1,0:T(8,128)(2,1)S(1)}, u32[]{:S(2)}, u32[]{:S(2)}) collective-permute-start(bf16[2,4,48,256]{3,2,1,0:T(8,128)(2,1)} %get-tuple-element.47), channel_id=1, source_target_pairs={{0,2},{1,3},{2,0},{3,1},{4,6},{5,7},{6,4},{7,5},{8,10},{9,11},{10,... | collective-permute-start | bytes 589832 | tf_op jit(solution)/shard_map/ppermute | solution.py:737
  8.0 2.6 %collective-permute-start.1 = (bf16[2,4,48,256]{3,2,1,0:T(8,128)(2,1)}, bf16[2,4,48,256]{3,2,1,0:T(8,128)(2,1)S(1)}, u32[]{:S(2)}, u32[]{:S(2)}) collective-permute-start(bf16[2,4,48,256]{3,2,1,0:T(8,128)(2,1)} %get-tuple-element.48), channel_id=1, source_target_pairs={{0,4},{1,5},{2,6},{3,7},{4,0},{5,1},{6,2},{7,3},{8,12},{9,13},{10,... | collective-permute-start | bytes 589832 | tf_op jit(solution)/shard_map/ppermute | solution.py:737
  10.6 0.0 collective-permute-start.2
  10.6 0.0 copy-done.5
  10.6 8.1 %pair_bias.1 = f32[16,64,256]{2,1,0:T(8,128)S(1)} custom-call(bf16[2,128,64,128]{3,2,1,0:T(8,128)(2,1)S(1)} %bitcast.23, bf16[16,128]{1,0:T(8,128)(2,1)S(1)} %bitcast.20, s32[1,64]{1,0:T(1,128)S(1)} %bitcast.24), custom_call_target="tpu_custom_call" | custom-call | flops 6000000000 | bytes 5000000 | tf_op jit(solution)/shard_map/pair_bias/pallas_call | solution.py:383
  18.7 0.9 convert_element_type.21
  19.6 0.0 collective-permute-done.refs_1_
  19.6 5.7 %collective-permute-done.1.refs_2_ = bf16[2,4,48,256]{3,2,1,0:T(8,128)(2,1)S(1)} collective-permute-done((bf16[2,4,48,256]{3,2,1,0:T(8,128)(2,1)}, bf16[2,4,48,256]{3,2,1,0:T(8,128)(2,1)S(1)}, u32[]{:S(2)}, u32[]{:S(2)}) %collective-permute-start.1) | collective-permute-done | bytes 196640 | tf_op jit(solution)/shard_map/ppermute | solution.py:737
  25.4 0.0 collective-permute-done.2.refs_3_
  25.4 6.7 %all-to-all-start = ((f16[16,64,256]{2,1,0:T(8,128)(2,1)}), f16[16,64,256]{2,1,0:T(8,128)(2,1)S(1)}, u32[]{:S(2)}, u32[]{:S(2)}) async-start(f16[16,64,256]{2,1,0:T(8,128)(2,1)} %convert_element_type.21), calls=%async_computation | async-start | bytes 1048576 | tf_op jit(solution)/shard_map/all_to_all | solution.py:754
  32.1 0.1 pad_maximum_fusion
  32.2 0.5 collective-permute-start.3
  32.7 3.0 %own_rows.1 = (f32[768,128]{1,0:T(8,128)}, f32[768,128]{1,0:T(8,128)}, f32[8,128]{1,0:T(8,128)}) custom-call(s32[1]{0:T(128)} %bitcast.4.row_ref, bf16[4,64,768]{2,1,0:T(8,128)(2,1)} %tokens_ref.3, s32[1,64]{1,0:T(1,128)} %bitcast.29, bf16[32,768]{1,0:T(8,128)(2,1)} %table_ref.3, bf16[768,768]{1,0:T(8,128)(2,1)} %refs_7_.1, bf16[4,64,768]{2,1,0:T(8,128)(2,1)} %cot_ref.1), custom_call_target="tpu_custom_call" | custom-call | flops 3000000000 | bytes 3000000 | tf_op jit(solution)/shard_map/own_rows/pallas_call | solution.py:289
  35.7 0.0 collective-permute-done.3.refs_4_
  35.7 10.6 %all-to-all-done = f16[16,64,256]{2,1,0:T(8,128)(2,1)S(1)} async-done(((f16[16,64,256]{2,1,0:T(8,128)(2,1)}), f16[16,64,256]{2,1,0:T(8,128)(2,1)S(1)}, u32[]{:S(2)}, u32[]{:S(2)}) %all-to-all-start) | async-done | bytes 524320 | tf_op jit(solution)/shard_map/all_to_all | solution.py:754
  46.3 0.1 convert_element_type.22.refs_5_
  46.4 7.7 %attention.1 = (f32[16,200,128]{2,1,0:T(8,128)S(1)}, f32[16,136,128]{2,1,0:T(8,128)S(1)}) custom-call(s32[1]{0:T(128)} %bitcast.col_ref, bf16[2,4,48,256]{3,2,1,0:T(8,128)(2,1)S(1)} %copy-done.3, bf16[2,4,48,256]{3,2,1,0:T(8,128)(2,1)S(1)} %collective-permute-done.refs_1_, bf16[2,4,48,256]{3,2,1,0:T(8,128)(2,1)S(1)} %collective-permute-done.1.refs_2_, ...), custom_call_target="tpu_custom_call" | custom-call | flops 8000000000 | bytes 6000000 | tf_op jit(solution)/shard_map/attention/pallas_call | solution.py:530
  54.1 0.9 convert_element_type.24
  55.0 4.0 %all-to-all-start.1 = ((f16[16,136,128]{2,1,0:T(8,128)(2,1)}), f16[16,136,128]{2,1,0:T(8,128)(2,1)S(1)}, u32[]{:S(2)}, u32[]{:S(2)}) async-start(f16[16,136,128]{2,1,0:T(8,128)(2,1)} %convert_element_type.24), calls=%async_computation.1 | async-start | bytes 1114112 | tf_op jit(solution)/shard_map/all_to_all | solution.py:759
  59.0 1.0 convert_element_type.23
  60.0 7.4 %pair_units.1 = (bf16[32,256,512]{2,1,0:T(8,128)(2,1)}, f32[32,8,512]{2,1,0:T(8,128)}) custom-call(bf16[2,128,64,128]{3,2,1,0:T(8,128)(2,1)} %bitcast.22), custom_call_target="tpu_custom_call" | custom-call | flops 6000000000 | bytes 12000000 | tf_op jit(solution)/shard_map/pair_units/pallas_call | solution.py:413
  67.5 6.3 %all-to-all-done.1 = f16[16,136,128]{2,1,0:T(8,128)(2,1)S(1)} async-done(((f16[16,136,128]{2,1,0:T(8,128)(2,1)}), f16[16,136,128]{2,1,0:T(8,128)(2,1)S(1)}, u32[]{:S(2)}, u32[]{:S(2)}) %all-to-all-start.1) | async-done | bytes 557088 | tf_op jit(solution)/shard_map/all_to_all | solution.py:759
  73.7 1.5 %collective-permute-start.4 = (f16[16,136,128]{2,1,0:T(8,128)(2,1)S(1)}, f16[16,136,128]{2,1,0:T(8,128)(2,1)S(1)}, u32[]{:S(2)}, u32[]{:S(2)}) collective-permute-start(f16[16,136,128]{2,1,0:T(8,128)(2,1)S(1)} %all-to-all-done.1), channel_id=1, source_target_pairs={{0,16},{16,0},{1,17},{17,1},{2,18},{18,2},{3,19},{19,3},{4,20},{20... | collective-permute-start | bytes 1671176 | tf_op jit(solution)/shard_map/ppermute | solution.py:714
  75.3 0.1 convert_element_type.25
  75.3 4.5 %all-to-all-start.2 = ((f16[16,200,128]{2,1,0:T(8,128)(2,1)}), f16[16,200,128]{2,1,0:T(8,128)(2,1)}, u32[]{:S(2)}, u32[]{:S(2)}) async-start(f16[16,200,128]{2,1,0:T(8,128)(2,1)} %convert_element_type.23), calls=%async_computation.2 | async-start | bytes 1638400 | tf_op jit(solution)/shard_map/all_to_all | solution.py:765
  79.9 0.1 slice_multiply_fusion.1
  80.0 3.4 %copy-done = bf16[32,256,512]{2,1,0:T(8,128)(2,1)S(1)} copy-done((bf16[32,256,512]{2,1,0:T(8,128)(2,1)S(1)}, bf16[32,256,512]{2,1,0:T(8,128)(2,1)}, u32[]{:S(2)}) %copy-start) | copy-done | bytes 8388632
  83.4 3.3 %pair_weight.1 = f32[16,128]{1,0:T(8,128)S(1)} custom-call(bf16[32,256,512]{2,1,0:T(8,128)(2,1)S(1)} %copy-done, f32[2048,128]{1,0:T(8,128)S(1)} %bitcast.17), custom_call_target="tpu_custom_call" | custom-call | flops 1000000 | bytes 100000 | tf_op jit(solution)/shard_map/pair_weight/pallas_call | solution.py:670
  86.6 0.6 collective-permute-start.5
  87.2 1.6 %collective-permute-start.6 = (f32[16,128]{1,0:T(8,128)S(1)}, f32[16,128]{1,0:T(8,128)S(1)}, u32[]{:S(2)}, u32[]{:S(2)}) collective-permute-start(f32[16,128]{1,0:T(8,128)S(1)} %pair_weight.1), channel_id=1, source_target_pairs={{0,8},{8,0},{1,9},{9,1},{2,10},{10,2},{3,11},{11,3},{4,12},{12,4},... | collective-permute-start | bytes 24584 | tf_op jit(solution)/shard_map/ppermute | solution.py:714
  88.8 1.4 %collective-permute-start.7 = (f32[16,128]{1,0:T(8,128)S(1)}, f32[16,128]{1,0:T(8,128)S(1)}, u32[]{:S(2)}, u32[]{:S(2)}) collective-permute-start(f32[16,128]{1,0:T(8,128)S(1)} %pair_weight.1), channel_id=1, source_target_pairs={{0,24},{8,16},{16,8},{24,0},{1,25},{9,17},{17,9},{25,1},{2,26},{10... | collective-permute-start | bytes 24584 | tf_op jit(solution)/shard_map/ppermute | solution.py:772
  90.2 0.0 collective-permute-done.4
  90.2 0.1 convert_element_type.26
  90.3 0.1 slice_multiply_fusion
  90.4 0.1 bitcast_add_fusion.refs_2_
  90.5 0.9 copy-done.2
  91.4 5.4 %pair_backward.1 = bf16[2,128,64,128]{3,2,1,0:T(8,128)(2,1)} custom-call(bf16[32,256,512]{2,1,0:T(8,128)(2,1)S(1)} %copy-done.1, f32[32,8,512]{2,1,0:T(8,128)S(1)} %copy-done.2, f32[2048,128]{1,0:T(8,128)S(1)} %bitcast_add_fusion.refs_2_, bf16[16,128]{1,0:T(8,128)(2,1)S(1)} %bitcast.21), custom_call_target="tpu_custom_call" | custom-call | flops 1000000 | bytes 100000 | tf_op jit(solution)/shard_map/pair_backward/pallas_call | solution.py:687
  96.9 0.0 collective-permute-done.5
  96.9 0.0 collective-permute-done.6
  96.9 0.0 collective-permute-done.7
  96.9 0.0 copy-start.6
  96.9 0.0 copy-start.7
  96.9 0.0 copy-start.13
  97.0 0.1 collective-permute-start.8
  97.0 1.6 %collective-permute-start.9 = (f32[16,128]{1,0:T(8,128)S(1)}, f32[16,128]{1,0:T(8,128)S(1)}, u32[]{:S(2)}, u32[]{:S(2)}) collective-permute-start(f32[16,128]{1,0:T(8,128)S(1)} %add_add_fusion), channel_id=1, source_target_pairs={{0,2},{1,3},{2,0},{3,1},{4,6},{5,7},{6,4},{7,5},{8,10},{9,11},{10,... | collective-permute-start | bytes 24584 | tf_op jit(solution)/shard_map/ppermute | solution.py:737
  98.7 0.2 collective-permute-start.10
  98.9 0.0 collective-permute-done.8
  98.9 1.9 %collective-permute-done.9 = f32[16,128]{1,0:T(8,128)S(1)} collective-permute-done((f32[16,128]{1,0:T(8,128)S(1)}, f32[16,128]{1,0:T(8,128)S(1)}, u32[]{:S(2)}, u32[]{:S(2)}) %collective-permute-start.9) | collective-permute-done | bytes 8224 | tf_op jit(solution)/shard_map/ppermute | solution.py:737
  100.7 1.0 collective-permute-done.10
  101.7 0.0 all-to-all-done.2
  101.7 1.3 %convert_element_type.27.refs_0_ = f32[16,200,128]{2,1,0:T(8,128)S(1)} convert(f16[16,200,128]{2,1,0:T(8,128)(2,1)} %all-to-all-done.2) | non-fusion elementwise | flops 409600 | bytes 2457600 | tf_op jit(solution)/shard_map/convert_element_type | solution.py:786
  103.0 0.0 copy-start.8
  103.1 1.3 %copy-done.8 = bf16[768,768]{1,0:T(8,128)(2,1)S(1)} copy-done((bf16[768,768]{1,0:T(8,128)(2,1)S(1)}, bf16[768,768]{1,0:T(8,128)(2,1)}, u32[]{:S(2)}) %copy-start.8) | copy-done | bytes 1179672
  104.3 1.3 %copy-done.9 = bf16[768,768]{1,0:T(8,128)(2,1)S(1)} copy-done((bf16[768,768]{1,0:T(8,128)(2,1)S(1)}, bf16[768,768]{1,0:T(8,128)(2,1)}, u32[]{:S(2)}) %copy-start.9) | copy-done | bytes 1179672
  105.6 2.1 %token_back.1 = bf16[128,768]{1,0:T(8,128)(2,1)S(1)} custom-call(f32[16,200,128]{2,1,0:T(8,128)S(1)} %convert_element_type.27.refs_0_, f32[768,128]{1,0:T(8,128)S(1)} %copy-done.11, f32[768,128]{1,0:T(8,128)S(1)} %copy-done.12, f32[8,128]{1,0:T(8,128)S(1)} %copy-done.13, bf16[768,768]{1,0:T(8,128)(2,1)S(1)} %copy-done.6, bf16[768,768]{1,0:T(8,128)(2,1)S(1)} %copy-done.7, ...), custom_call_target="tpu_custom_call" | custom-call | flops 4000000000 | bytes 8000000 | tf_op jit(solution)/shard_map/token_back/pallas_call | solution.py:603
  107.7 1.6 %collective-permute-start.11 = (bf16[2,64,768]{2,1,0:T(8,128)(2,1)S(1)}, bf16[2,64,768]{2,1,0:T(8,128)(2,1)S(1)}, u32[]{:S(2)}, u32[]{:S(2)}) collective-permute-start(bf16[2,64,768]{2,1,0:T(8,128)(2,1)S(1)} %bitcast.18), channel_id=1, source_target_pairs={{0,8},{8,0},{1,9},{9,1},{2,10},{10,2},{3,11},{11,3},{4,12},{12,4},... | collective-permute-start | bytes 589832 | tf_op jit(solution)/shard_map/ppermute | solution.py:714
  109.3 2.4 %collective-permute-start.12 = (f32[16,128]{1,0:T(8,128)S(1)}, f32[16,128]{1,0:T(8,128)S(1)}, u32[]{:S(2)}, u32[]{:S(2)}) collective-permute-start(f32[16,128]{1,0:T(8,128)S(1)} %add_multiply_fusion), channel_id=1, source_target_pairs={{0,4},{1,5},{2,6},{3,7},{4,0},{5,1},{6,2},{7,3},{8,12},{9,13},{10,... | collective-permute-start | bytes 24584 | tf_op jit(solution)/shard_map/ppermute | solution.py:737
  111.7 3.1 %collective-permute-done.11 = bf16[2,64,768]{2,1,0:T(8,128)(2,1)S(1)} collective-permute-done((bf16[2,64,768]{2,1,0:T(8,128)(2,1)S(1)}, bf16[2,64,768]{2,1,0:T(8,128)(2,1)S(1)}, u32[]{:S(2)}, u32[]{:S(2)}) %collective-permute-start.11) | collective-permute-done | bytes 196640 | tf_op jit(solution)/shard_map/ppermute | solution.py:714
  114.8 0.8 pad_maximum_fusion.1
  115.6 0.0 collective-permute-done.12
  115.6 0.6 add_bitcast_fusion
  (26 shorter events, 0.1 us)
Async XLA Ops:
  0.6 10.0 %copy-start.4 = (bf16[128,16]{0,1:T(8,128)(2,1)S(1)}, bf16[128,16]{0,1:T(8,128)(2,1)}, u32[]{:S(2)}) copy-start(bf16[128,16]{0,1:T(8,128)(2,1)} %param.16) | copy-start | bytes 12292
  0.6 9.9 %copy-start.5 = (bf16[256,64,128]{2,1,0:T(8,128)(2,1)S(1)}, bf16[256,64,128]{2,1,0:T(8,128)(2,1)}, u32[]{:S(2)}) copy-start(bf16[256,64,128]{2,1,0:T(8,128)(2,1)} %param.15) | copy-start | bytes 12582916
  0.7 9.9 %copy-start.10 = (s32[64]{0:T(128)S(1)}, s32[64]{0:T(128)}, u32[]{:S(2)}) copy-start(s32[64]{0:T(128)} %param.14) | copy-start | bytes 772
  5.0 14.7 %collective-permute-start = (bf16[2,4,48,256]{3,2,1,0:T(8,128)(2,1)}, bf16[2,4,48,256]{3,2,1,0:T(8,128)(2,1)S(1)}, u32[]{:S(2)}, u32[]{:S(2)}) collective-permute-start(bf16[2,4,48,256]{3,2,1,0:T(8,128)(2,1)} %get-tuple-element.47), channel_id=1, source_target_pairs={{0,2},{1,3},{2,0},{3,1},{4,6},{5,7},{6,4},{7,5},{8,10},{9,11},{10,... | collective-permute-start | bytes 589832 | tf_op jit(solution)/shard_map/ppermute | solution.py:737
  8.0 17.4 %collective-permute-start.1 = (bf16[2,4,48,256]{3,2,1,0:T(8,128)(2,1)}, bf16[2,4,48,256]{3,2,1,0:T(8,128)(2,1)S(1)}, u32[]{:S(2)}, u32[]{:S(2)}) collective-permute-start(bf16[2,4,48,256]{3,2,1,0:T(8,128)(2,1)} %get-tuple-element.48), channel_id=1, source_target_pairs={{0,4},{1,5},{2,6},{3,7},{4,0},{5,1},{6,2},{7,3},{8,12},{9,13},{10,... | collective-permute-start | bytes 589832 | tf_op jit(solution)/shard_map/ppermute | solution.py:737
  10.6 14.8 %collective-permute-start.2 = (bf16[2,4,48,256]{3,2,1,0:T(8,128)(2,1)}, bf16[2,4,48,256]{3,2,1,0:T(8,128)(2,1)S(1)}, u32[]{:S(2)}, u32[]{:S(2)}) collective-permute-start(bf16[2,4,48,256]{3,2,1,0:T(8,128)(2,1)} %get-tuple-element.49), channel_id=1, source_target_pairs={{0,6},{1,7},{2,4},{3,5},{4,2},{5,3},{6,0},{7,1},{8,14},{9,15},{10,... | collective-permute-start | bytes 589832 | tf_op jit(solution)/shard_map/ppermute | solution.py:737
  19.6 12.5 %copy-start.3 = (bf16[2,4,48,256]{3,2,1,0:T(8,128)(2,1)S(1)}, bf16[2,4,48,256]{3,2,1,0:T(8,128)(2,1)}, u32[]{:S(2)}) copy-start(bf16[2,4,48,256]{3,2,1,0:T(8,128)(2,1)} %get-tuple-element.50.refs_0_) | copy-start | bytes 589828
  25.4 20.9 %all-to-all-start = ((f16[16,64,256]{2,1,0:T(8,128)(2,1)}), f16[16,64,256]{2,1,0:T(8,128)(2,1)S(1)}, u32[]{:S(2)}, u32[]{:S(2)}) async-start(f16[16,64,256]{2,1,0:T(8,128)(2,1)} %convert_element_type.21), calls=%async_computation | async-start | bytes 1048576 | tf_op jit(solution)/shard_map/all_to_all | solution.py:754
  32.2 3.5 %collective-permute-start.3 = (bf16[4,4,48,256]{3,2,1,0:T(8,128)(2,1)S(1)}, bf16[4,4,48,256]{3,2,1,0:T(8,128)(2,1)S(1)}, u32[]{:S(2)}, u32[]{:S(2)}) collective-permute-start(bf16[4,4,48,256]{3,2,1,0:T(8,128)(2,1)S(1)} %pad_maximum_fusion), channel_id=1, source_target_pairs={{0,1},{1,0},{2,3},{3,2},{4,5},{5,4},{6,7},{7,6},{8,9},{9,8},{10,11... | collective-permute-start | bytes 1179656 | tf_op jit(solution)/shard_map/ppermute | solution.py:737
  55.0 18.8 %all-to-all-start.1 = ((f16[16,136,128]{2,1,0:T(8,128)(2,1)}), f16[16,136,128]{2,1,0:T(8,128)(2,1)S(1)}, u32[]{:S(2)}, u32[]{:S(2)}) async-start(f16[16,136,128]{2,1,0:T(8,128)(2,1)} %convert_element_type.24), calls=%async_computation.1 | async-start | bytes 1114112 | tf_op jit(solution)/shard_map/all_to_all | solution.py:759
  73.7 16.4 %collective-permute-start.4 = (f16[16,136,128]{2,1,0:T(8,128)(2,1)S(1)}, f16[16,136,128]{2,1,0:T(8,128)(2,1)S(1)}, u32[]{:S(2)}, u32[]{:S(2)}) collective-permute-start(f16[16,136,128]{2,1,0:T(8,128)(2,1)S(1)} %all-to-all-done.1), channel_id=1, source_target_pairs={{0,16},{16,0},{1,17},{17,1},{2,18},{18,2},{3,19},{19,3},{4,20},{20... | collective-permute-start | bytes 1671176 | tf_op jit(solution)/shard_map/ppermute | solution.py:714
  75.3 26.4 %all-to-all-start.2 = ((f16[16,200,128]{2,1,0:T(8,128)(2,1)}), f16[16,200,128]{2,1,0:T(8,128)(2,1)}, u32[]{:S(2)}, u32[]{:S(2)}) async-start(f16[16,200,128]{2,1,0:T(8,128)(2,1)} %convert_element_type.23), calls=%async_computation.2 | async-start | bytes 1638400 | tf_op jit(solution)/shard_map/all_to_all | solution.py:765
  80.0 3.4 %copy-start = (bf16[32,256,512]{2,1,0:T(8,128)(2,1)S(1)}, bf16[32,256,512]{2,1,0:T(8,128)(2,1)}, u32[]{:S(2)}) copy-start(bf16[32,256,512]{2,1,0:T(8,128)(2,1)} %get-tuple-element.67.normed_ref.refs_0_) | copy-start | bytes 25165828
  83.4 7.2 %copy-start.1 = (bf16[32,256,512]{2,1,0:T(8,128)(2,1)S(1)}, bf16[32,256,512]{2,1,0:T(8,128)(2,1)}, u32[]{:S(2)}) copy-start(bf16[32,256,512]{2,1,0:T(8,128)(2,1)} %get-tuple-element.67.normed_ref.refs_0_) | copy-start | bytes 25165828
  86.6 10.3 %collective-permute-start.5 = (f32[16,128]{1,0:T(8,128)S(1)}, f32[16,128]{1,0:T(8,128)S(1)}, u32[]{:S(2)}, u32[]{:S(2)}) collective-permute-start(f32[16,128]{1,0:T(8,128)S(1)} %pair_weight.1), channel_id=1, source_target_pairs={{0,16},{16,0},{1,17},{17,1},{2,18},{18,2},{3,19},{19,3},{4,20},{20... | collective-permute-start | bytes 24584 | tf_op jit(solution)/shard_map/ppermute | solution.py:714
  87.2 9.7 %collective-permute-start.6 = (f32[16,128]{1,0:T(8,128)S(1)}, f32[16,128]{1,0:T(8,128)S(1)}, u32[]{:S(2)}, u32[]{:S(2)}) collective-permute-start(f32[16,128]{1,0:T(8,128)S(1)} %pair_weight.1), channel_id=1, source_target_pairs={{0,8},{8,0},{1,9},{9,1},{2,10},{10,2},{3,11},{11,3},{4,12},{12,4},... | collective-permute-start | bytes 24584 | tf_op jit(solution)/shard_map/ppermute | solution.py:714
  88.8 8.1 %collective-permute-start.7 = (f32[16,128]{1,0:T(8,128)S(1)}, f32[16,128]{1,0:T(8,128)S(1)}, u32[]{:S(2)}, u32[]{:S(2)}) collective-permute-start(f32[16,128]{1,0:T(8,128)S(1)} %pair_weight.1), channel_id=1, source_target_pairs={{0,24},{8,16},{16,8},{24,0},{1,25},{9,17},{17,9},{25,1},{2,26},{10... | collective-permute-start | bytes 24584 | tf_op jit(solution)/shard_map/ppermute | solution.py:772
  90.4 1.0 copy-start.2
  91.4 11.6 %copy-start.11 = (f32[768,128]{1,0:T(8,128)S(1)}, f32[768,128]{1,0:T(8,128)}, u32[]{:S(2)}) copy-start(f32[768,128]{1,0:T(8,128)} %get-tuple-element.77.refs_1_) | copy-start | bytes 1179652
  91.4 11.6 %copy-start.12 = (f32[768,128]{1,0:T(8,128)S(1)}, f32[768,128]{1,0:T(8,128)}, u32[]{:S(2)}) copy-start(f32[768,128]{1,0:T(8,128)} %get-tuple-element.78.refs_2_) | copy-start | bytes 1179652
  96.9 6.1 %copy-start.6 = (bf16[768,768]{1,0:T(8,128)(2,1)S(1)}, bf16[768,768]{1,0:T(8,128)(2,1)}, u32[]{:S(2)}) copy-start(bf16[768,768]{1,0:T(8,128)(2,1)} %refs_4_.3) | copy-start | bytes 3538948
  96.9 6.1 %copy-start.7 = (bf16[768,768]{1,0:T(8,128)(2,1)S(1)}, bf16[768,768]{1,0:T(8,128)(2,1)}, u32[]{:S(2)}) copy-start(bf16[768,768]{1,0:T(8,128)(2,1)} %refs_5_.1) | copy-start | bytes 3538948
  96.9 6.1 %copy-start.13 = (f32[8,128]{1,0:T(8,128)S(1)}, f32[8,128]{1,0:T(8,128)}, u32[]{:S(2)}) copy-start(f32[8,128]{1,0:T(8,128)} %get-tuple-element.79.refs_3_) | copy-start | bytes 12292
  97.0 1.9 %collective-permute-start.8 = (f32[16,128]{1,0:T(8,128)S(1)}, f32[16,128]{1,0:T(8,128)S(1)}, u32[]{:S(2)}, u32[]{:S(2)}) collective-permute-start(f32[16,128]{1,0:T(8,128)S(1)} %add_add_fusion), channel_id=1, source_target_pairs={{0,1},{1,0},{2,3},{3,2},{4,5},{5,4},{6,7},{7,6},{8,9},{9,8},{10,11... | collective-permute-start | bytes 24584 | tf_op jit(solution)/shard_map/ppermute | solution.py:737
  97.0 3.7 %collective-permute-start.9 = (f32[16,128]{1,0:T(8,128)S(1)}, f32[16,128]{1,0:T(8,128)S(1)}, u32[]{:S(2)}, u32[]{:S(2)}) collective-permute-start(f32[16,128]{1,0:T(8,128)S(1)} %add_add_fusion), channel_id=1, source_target_pairs={{0,2},{1,3},{2,0},{3,1},{4,6},{5,7},{6,4},{7,5},{8,10},{9,11},{10,... | collective-permute-start | bytes 24584 | tf_op jit(solution)/shard_map/ppermute | solution.py:737
  98.7 3.1 %collective-permute-start.10 = (f32[16,128]{1,0:T(8,128)S(1)}, f32[16,128]{1,0:T(8,128)S(1)}, u32[]{:S(2)}, u32[]{:S(2)}) collective-permute-start(f32[16,128]{1,0:T(8,128)S(1)} %add_add_fusion), channel_id=1, source_target_pairs={{0,3},{1,2},{2,1},{3,0},{4,7},{5,6},{6,5},{7,4},{8,11},{9,10},{10,... | collective-permute-start | bytes 24584 | tf_op jit(solution)/shard_map/ppermute | solution.py:737
  103.0 1.3 %copy-start.8 = (bf16[768,768]{1,0:T(8,128)(2,1)S(1)}, bf16[768,768]{1,0:T(8,128)(2,1)}, u32[]{:S(2)}) copy-start(bf16[768,768]{1,0:T(8,128)(2,1)} %refs_6_.1) | copy-start | bytes 3538948
  104.3 1.3 %copy-start.9 = (bf16[768,768]{1,0:T(8,128)(2,1)S(1)}, bf16[768,768]{1,0:T(8,128)(2,1)}, u32[]{:S(2)}) copy-start(bf16[768,768]{1,0:T(8,128)(2,1)} %refs_7_.1) | copy-start | bytes 3538948
  107.7 7.0 %collective-permute-start.11 = (bf16[2,64,768]{2,1,0:T(8,128)(2,1)S(1)}, bf16[2,64,768]{2,1,0:T(8,128)(2,1)S(1)}, u32[]{:S(2)}, u32[]{:S(2)}) collective-permute-start(bf16[2,64,768]{2,1,0:T(8,128)(2,1)S(1)} %bitcast.18), channel_id=1, source_target_pairs={{0,8},{8,0},{1,9},{9,1},{2,10},{10,2},{3,11},{11,3},{4,12},{12,4},... | collective-permute-start | bytes 589832 | tf_op jit(solution)/shard_map/ppermute | solution.py:714
  109.3 6.3 %collective-permute-start.12 = (f32[16,128]{1,0:T(8,128)S(1)}, f32[16,128]{1,0:T(8,128)S(1)}, u32[]{:S(2)}, u32[]{:S(2)}) collective-permute-start(f32[16,128]{1,0:T(8,128)S(1)} %add_multiply_fusion), channel_id=1, source_target_pairs={{0,4},{1,5},{2,6},{3,7},{4,0},{5,1},{6,2},{7,3},{8,12},{9,13},{10,... | collective-permute-start | bytes 24584 | tf_op jit(solution)/shard_map/ppermute | solution.py:737

commit v12 on v11

--- a/solution.py
+++ b/solution.py
@@ -697,7 +697,7 @@
         out_specs=pl.BlockSpec((2, whole // STEPS, tok_col, width), lambda i: (0, i, 0, 0)),
         compiler_params=params(24),
         cost_estimate=pl.CostEstimate(
-            flops=1_000_000, bytes_accessed=100_000, transcendentals=0
+            flops=3_000_000_000, bytes_accessed=100_000, transcendentals=0
         ),
         name="pair_backward",
     )(normed, inv_std, grads, weight_t)

time: 117 us -> 126 us (1.077)
  waiting for transfers between devices: 28.6 us -> 34.3 us
  local copies, waits for them, and re-layouts: 6.91 us -> 10.3 us
    all_to_all x1, waiting for transfers between devices: 0.01 us -> 4.72 us  [body_heads(): back = lax.all_to_all(back, ('row', 'col'), 0, 0, tiled=True)]
    unnamed x28, local copies, waits for them, and re-layouts: 6.87 us -> 10.3 us
  transfers between devices with their start and end apart: 16 -> 16, of which waited for: 6 -> 7; matrix products, arithmetic and copies ran while one was open for 3% -> 3% of each run, Pallas kernels for 24% -> 22%
where the time goes in v12:
time: 126 us; the launch traced here: 125 us
  Pallas kernels  41.4 us (33%)
  waiting for transfers between devices  34.3 us (27%)
  starting transfers between devices  31.9 us (25%)
  local copies, waits for them, and re-layouts  10.3 us (8%)
  other arithmetic  6.15 us (5%)
    all_to_all x1, waiting for transfers between devices, body_heads(): bias = lax.all_to_all(bias, ('row', 'col'), 0, 0, tiled=True)  10.6 us
    unnamed x28, local copies, waits for them, and re-layouts  10.3 us
    ppermute x8, starting transfers between devices, send(): return lax.ppermute(block, 'col', [(c, c ^ offset) for c in range(n_col)])  10.1 us
    ppermute x8, waiting for transfers between devices, send(): return lax.ppermute(block, 'col', [(c, c ^ offset) for c in range(n_col)])  8.68 us
    pallas_call x1, Pallas kernels, pair_bias(): pl.pallas_call(bias_kernel, out_shape=jax.ShapeDtypeStruct((H, tok_col, r...  8.12 us
    pallas_call x1, Pallas kernels, attention(): pl.pallas_call(attention_kernel, out_shape=[jax.ShapeDtypeStruct(back_sha...  7.67 us
    pallas_call x1, Pallas kernels, pair_units(): pl.pallas_call(norm_kernel, out_shape=[jax.ShapeDtypeStruct(shapes[0], jn...  7.45 us
    all_to_all x1, starting transfers between devices, body_heads(): bias = lax.all_to_all(bias, ('row', 'col'), 0, 0, tiled=True)  6.67 us
  transfers between devices with their start and end apart: 16, of which 7 were waited for; matrix products, arithmetic and copies ran while one was open for 3% of the time, Pallas kernels for 22%

profile of v12, /device:TPU:0, one launch (start us, length us, event | category | flops | bytes accessed | tf_op | source)
XLA Modules:
  0.0 125.0 jit_solution(12813643094030348072)
XLA Ops:
  0.6 0.0 copy-start.5
  0.7 4.3 %token_messages.1 = (bf16[2,4,48,256]{3,2,1,0:T(8,128)(2,1)}, bf16[2,4,48,256]{3,2,1,0:T(8,128)(2,1)}, bf16[2,4,48,256]{3,2,1,0:T(8,128)(2,1)}, bf16[2,4,48,256]{3,2,1,0:T(8,128)(2,1)}) custom-call(s32[1]{0:T(128)} %bitcast.4.row_ref, s32[1]{0:T(128)} %bitcast.col_ref, bf16[4,64,768]{2,1,0:T(8,128)(2,1)} %tokens_ref.3, s32[1,64]{1,0:T(1,128)} %bitcast.28, ...), custom_call_target="tpu_custom_call" | custom-call | flops 4000000000 | bytes 4000000 | tf_op jit(solution)/shard_map/token_messages/pallas_call | solution.py:245
  5.0 3.0 %collective-permute-start = (bf16[2,4,48,256]{3,2,1,0:T(8,128)(2,1)}, bf16[2,4,48,256]{3,2,1,0:T(8,128)(2,1)S(1)}, u32[]{:S(2)}, u32[]{:S(2)}) collective-permute-start(bf16[2,4,48,256]{3,2,1,0:T(8,128)(2,1)} %get-tuple-element.47), channel_id=1, source_target_pairs={{0,2},{1,3},{2,0},{3,1},{4,6},{5,7},{6,4},{7,5},{8,10},{9,11},{10,... | collective-permute-start | bytes 589832 | tf_op jit(solution)/shard_map/ppermute | solution.py:737
  8.0 2.6 %collective-permute-start.1 = (bf16[2,4,48,256]{3,2,1,0:T(8,128)(2,1)}, bf16[2,4,48,256]{3,2,1,0:T(8,128)(2,1)S(1)}, u32[]{:S(2)}, u32[]{:S(2)}) collective-permute-start(bf16[2,4,48,256]{3,2,1,0:T(8,128)(2,1)} %get-tuple-element.48), channel_id=1, source_target_pairs={{0,4},{1,5},{2,6},{3,7},{4,0},{5,1},{6,2},{7,3},{8,12},{9,13},{10,... | collective-permute-start | bytes 589832 | tf_op jit(solution)/shard_map/ppermute | solution.py:737
  10.6 0.0 collective-permute-start.2
  10.6 0.0 copy-done.10
  10.6 8.1 %pair_bias.1 = f32[16,64,256]{2,1,0:T(8,128)S(1)} custom-call(bf16[2,128,64,128]{3,2,1,0:T(8,128)(2,1)S(1)} %bitcast.23, bf16[16,128]{1,0:T(8,128)(2,1)S(1)} %bitcast.20, s32[1,64]{1,0:T(1,128)S(1)} %bitcast.24), custom_call_target="tpu_custom_call" | custom-call | flops 6000000000 | bytes 5000000 | tf_op jit(solution)/shard_map/pair_bias/pallas_call | solution.py:383
  18.7 0.9 convert_element_type.21
  19.6 0.0 collective-permute-done.refs_1_
  19.6 5.7 %collective-permute-done.1.refs_2_ = bf16[2,4,48,256]{3,2,1,0:T(8,128)(2,1)S(1)} collective-permute-done((bf16[2,4,48,256]{3,2,1,0:T(8,128)(2,1)}, bf16[2,4,48,256]{3,2,1,0:T(8,128)(2,1)S(1)}, u32[]{:S(2)}, u32[]{:S(2)}) %collective-permute-start.1) | collective-permute-done | bytes 196640 | tf_op jit(solution)/shard_map/ppermute | solution.py:737
  25.4 0.0 collective-permute-done.2.refs_3_
  25.4 6.7 %all-to-all-start = ((f16[16,64,256]{2,1,0:T(8,128)(2,1)}), f16[16,64,256]{2,1,0:T(8,128)(2,1)S(1)}, u32[]{:S(2)}, u32[]{:S(2)}) async-start(f16[16,64,256]{2,1,0:T(8,128)(2,1)} %convert_element_type.21), calls=%async_computation | async-start | bytes 1048576 | tf_op jit(solution)/shard_map/all_to_all | solution.py:754
  32.1 0.1 pad_maximum_fusion
  32.2 0.5 collective-permute-start.3
  32.7 3.0 %own_rows.1 = (f32[768,128]{1,0:T(8,128)}, f32[768,128]{1,0:T(8,128)}, f32[8,128]{1,0:T(8,128)}) custom-call(s32[1]{0:T(128)} %bitcast.4.row_ref, bf16[4,64,768]{2,1,0:T(8,128)(2,1)} %tokens_ref.3, s32[1,64]{1,0:T(1,128)} %bitcast.29, bf16[32,768]{1,0:T(8,128)(2,1)} %table_ref.3, bf16[768,768]{1,0:T(8,128)(2,1)} %refs_7_.1, bf16[4,64,768]{2,1,0:T(8,128)(2,1)} %cot_ref.1), custom_call_target="tpu_custom_call" | custom-call | flops 3000000000 | bytes 3000000 | tf_op jit(solution)/shard_map/own_rows/pallas_call | solution.py:289
  35.7 0.0 collective-permute-done.3.refs_4_
  35.7 10.6 %all-to-all-done = f16[16,64,256]{2,1,0:T(8,128)(2,1)S(1)} async-done(((f16[16,64,256]{2,1,0:T(8,128)(2,1)}), f16[16,64,256]{2,1,0:T(8,128)(2,1)S(1)}, u32[]{:S(2)}, u32[]{:S(2)}) %all-to-all-start) | async-done | bytes 524320 | tf_op jit(solution)/shard_map/all_to_all | solution.py:754
  46.3 0.1 convert_element_type.22.refs_5_
  46.4 7.7 %attention.1 = (f32[16,200,128]{2,1,0:T(8,128)S(1)}, f32[16,136,128]{2,1,0:T(8,128)S(1)}) custom-call(s32[1]{0:T(128)} %bitcast.col_ref, bf16[2,4,48,256]{3,2,1,0:T(8,128)(2,1)S(1)} %copy-done.3, bf16[2,4,48,256]{3,2,1,0:T(8,128)(2,1)S(1)} %collective-permute-done.refs_1_, bf16[2,4,48,256]{3,2,1,0:T(8,128)(2,1)S(1)} %collective-permute-done.1.refs_2_, ...), custom_call_target="tpu_custom_call" | custom-call | flops 8000000000 | bytes 6000000 | tf_op jit(solution)/shard_map/attention/pallas_call | solution.py:530
  54.1 0.9 convert_element_type.24
  55.0 4.0 %all-to-all-start.1 = ((f16[16,136,128]{2,1,0:T(8,128)(2,1)}), f16[16,136,128]{2,1,0:T(8,128)(2,1)S(1)}, u32[]{:S(2)}, u32[]{:S(2)}) async-start(f16[16,136,128]{2,1,0:T(8,128)(2,1)} %convert_element_type.24), calls=%async_computation.1 | async-start | bytes 1114112 | tf_op jit(solution)/shard_map/all_to_all | solution.py:759
  59.0 1.0 convert_element_type.23
  60.0 7.4 %pair_units.1 = (bf16[32,256,512]{2,1,0:T(8,128)(2,1)}, f32[32,8,512]{2,1,0:T(8,128)}) custom-call(bf16[2,128,64,128]{3,2,1,0:T(8,128)(2,1)} %bitcast.22), custom_call_target="tpu_custom_call" | custom-call | flops 6000000000 | bytes 12000000 | tf_op jit(solution)/shard_map/pair_units/pallas_call | solution.py:413
  67.5 6.3 %all-to-all-done.1 = f16[16,136,128]{2,1,0:T(8,128)(2,1)S(1)} async-done(((f16[16,136,128]{2,1,0:T(8,128)(2,1)}), f16[16,136,128]{2,1,0:T(8,128)(2,1)S(1)}, u32[]{:S(2)}, u32[]{:S(2)}) %all-to-all-start.1) | async-done | bytes 557088 | tf_op jit(solution)/shard_map/all_to_all | solution.py:759
  73.7 1.5 %collective-permute-start.4 = (f16[16,136,128]{2,1,0:T(8,128)(2,1)S(1)}, f16[16,136,128]{2,1,0:T(8,128)(2,1)S(1)}, u32[]{:S(2)}, u32[]{:S(2)}) collective-permute-start(f16[16,136,128]{2,1,0:T(8,128)(2,1)S(1)} %all-to-all-done.1), channel_id=1, source_target_pairs={{0,16},{16,0},{1,17},{17,1},{2,18},{18,2},{3,19},{19,3},{4,20},{20... | collective-permute-start | bytes 1671176 | tf_op jit(solution)/shard_map/ppermute | solution.py:714
  75.3 0.1 convert_element_type.25
  75.4 0.1 slice_multiply_fusion.1
  75.5 3.4 %copy-done = bf16[32,256,512]{2,1,0:T(8,128)(2,1)S(1)} copy-done((bf16[32,256,512]{2,1,0:T(8,128)(2,1)S(1)}, bf16[32,256,512]{2,1,0:T(8,128)(2,1)}, u32[]{:S(2)}) %copy-start) | copy-done | bytes 8388632
  78.9 3.3 %pair_weight.1 = f32[16,128]{1,0:T(8,128)S(1)} custom-call(bf16[32,256,512]{2,1,0:T(8,128)(2,1)S(1)} %copy-done, f32[2048,128]{1,0:T(8,128)S(1)} %bitcast.17), custom_call_target="tpu_custom_call" | custom-call | flops 1000000 | bytes 100000 | tf_op jit(solution)/shard_map/pair_weight/pallas_call | solution.py:670
  82.1 0.6 collective-permute-start.5
  82.7 1.5 %collective-permute-start.6 = (f32[16,128]{1,0:T(8,128)S(1)}, f32[16,128]{1,0:T(8,128)S(1)}, u32[]{:S(2)}, u32[]{:S(2)}) collective-permute-start(f32[16,128]{1,0:T(8,128)S(1)} %pair_weight.1), channel_id=1, source_target_pairs={{0,8},{8,0},{1,9},{9,1},{2,10},{10,2},{3,11},{11,3},{4,12},{12,4},... | collective-permute-start | bytes 24584 | tf_op jit(solution)/shard_map/ppermute | solution.py:714
  84.1 1.5 %collective-permute-start.7 = (f32[16,128]{1,0:T(8,128)S(1)}, f32[16,128]{1,0:T(8,128)S(1)}, u32[]{:S(2)}, u32[]{:S(2)}) collective-permute-start(f32[16,128]{1,0:T(8,128)S(1)} %pair_weight.1), channel_id=1, source_target_pairs={{0,24},{8,16},{16,8},{24,0},{1,25},{9,17},{17,9},{25,1},{2,26},{10... | collective-permute-start | bytes 24584 | tf_op jit(solution)/shard_map/ppermute | solution.py:772
  85.7 4.5 %all-to-all-start.2 = ((f16[16,200,128]{2,1,0:T(8,128)(2,1)}), f16[16,200,128]{2,1,0:T(8,128)(2,1)}, u32[]{:S(2)}, u32[]{:S(2)}) async-start(f16[16,200,128]{2,1,0:T(8,128)(2,1)} %convert_element_type.23), calls=%async_computation.2 | async-start | bytes 1638400 | tf_op jit(solution)/shard_map/all_to_all | solution.py:765
  90.1 0.0 collective-permute-done.4
  90.2 0.1 convert_element_type.26
  90.3 0.1 slice_multiply_fusion
  90.4 0.1 bitcast_add_fusion.refs_2_
  90.5 0.9 copy-done.2
  91.4 3.4 %copy-done.1 = bf16[32,256,512]{2,1,0:T(8,128)(2,1)S(1)} copy-done((bf16[32,256,512]{2,1,0:T(8,128)(2,1)S(1)}, bf16[32,256,512]{2,1,0:T(8,128)(2,1)}, u32[]{:S(2)}) %copy-start.1) | copy-done | bytes 8388632
  94.8 5.4 %pair_backward.1 = bf16[2,128,64,128]{3,2,1,0:T(8,128)(2,1)} custom-call(bf16[32,256,512]{2,1,0:T(8,128)(2,1)S(1)} %copy-done.1, f32[32,8,512]{2,1,0:T(8,128)S(1)} %copy-done.2, f32[2048,128]{1,0:T(8,128)S(1)} %bitcast_add_fusion.refs_2_, bf16[16,128]{1,0:T(8,128)(2,1)S(1)} %bitcast.21), custom_call_target="tpu_custom_call" | custom-call | flops 3000000000 | bytes 100000 | tf_op jit(solution)/shard_map/pair_backward/pallas_call | solution.py:687
  100.2 0.0 collective-permute-done.5
  100.2 0.0 collective-permute-done.6
  100.2 0.0 collective-permute-done.7
  100.3 0.0 copy-start.6
  100.3 0.0 copy-start.7
  100.3 0.0 copy-start.13
  100.3 0.1 collective-permute-start.8
  100.4 1.7 %collective-permute-start.9 = (f32[16,128]{1,0:T(8,128)S(1)}, f32[16,128]{1,0:T(8,128)S(1)}, u32[]{:S(2)}, u32[]{:S(2)}) collective-permute-start(f32[16,128]{1,0:T(8,128)S(1)} %add_add_fusion), channel_id=1, source_target_pairs={{0,2},{1,3},{2,0},{3,1},{4,6},{5,7},{6,4},{7,5},{8,10},{9,11},{10,... | collective-permute-start | bytes 24584 | tf_op jit(solution)/shard_map/ppermute | solution.py:737
  102.1 0.1 collective-permute-start.10
  102.2 0.0 collective-permute-done.8
  102.3 2.1 %collective-permute-done.9 = f32[16,128]{1,0:T(8,128)S(1)} collective-permute-done((f32[16,128]{1,0:T(8,128)S(1)}, f32[16,128]{1,0:T(8,128)S(1)}, u32[]{:S(2)}, u32[]{:S(2)}) %collective-permute-start.9) | collective-permute-done | bytes 8224 | tf_op jit(solution)/shard_map/ppermute | solution.py:737
  104.3 0.9 collective-permute-done.10
  105.2 4.7 %all-to-all-done.2 = f16[16,200,128]{2,1,0:T(8,128)(2,1)} async-done(((f16[16,200,128]{2,1,0:T(8,128)(2,1)}), f16[16,200,128]{2,1,0:T(8,128)(2,1)}, u32[]{:S(2)}, u32[]{:S(2)}) %all-to-all-start.2) | async-done | bytes 819232 | tf_op jit(solution)/shard_map/all_to_all | solution.py:765
  109.9 1.3 %convert_element_type.27.refs_0_ = f32[16,200,128]{2,1,0:T(8,128)S(1)} convert(f16[16,200,128]{2,1,0:T(8,128)(2,1)} %all-to-all-done.2) | non-fusion elementwise | flops 409600 | bytes 2457600 | tf_op jit(solution)/shard_map/convert_element_type | solution.py:786
  111.2 0.0 copy-start.8
  111.2 1.3 %copy-done.8 = bf16[768,768]{1,0:T(8,128)(2,1)S(1)} copy-done((bf16[768,768]{1,0:T(8,128)(2,1)S(1)}, bf16[768,768]{1,0:T(8,128)(2,1)}, u32[]{:S(2)}) %copy-start.8) | copy-done | bytes 1179672
  112.5 1.3 %copy-done.9 = bf16[768,768]{1,0:T(8,128)(2,1)S(1)} copy-done((bf16[768,768]{1,0:T(8,128)(2,1)S(1)}, bf16[768,768]{1,0:T(8,128)(2,1)}, u32[]{:S(2)}) %copy-start.9) | copy-done | bytes 1179672
  113.8 2.1 %token_back.1 = bf16[128,768]{1,0:T(8,128)(2,1)S(1)} custom-call(f32[16,200,128]{2,1,0:T(8,128)S(1)} %convert_element_type.27.refs_0_, f32[768,128]{1,0:T(8,128)S(1)} %copy-done.11, f32[768,128]{1,0:T(8,128)S(1)} %copy-done.12, f32[8,128]{1,0:T(8,128)S(1)} %copy-done.13, bf16[768,768]{1,0:T(8,128)(2,1)S(1)} %copy-done.6, bf16[768,768]{1,0:T(8,128)(2,1)S(1)} %copy-done.7, ...), custom_call_target="tpu_custom_call" | custom-call | flops 4000000000 | bytes 8000000 | tf_op jit(solution)/shard_map/token_back/pallas_call | solution.py:603
  115.9 1.6 %collective-permute-start.11 = (bf16[2,64,768]{2,1,0:T(8,128)(2,1)S(1)}, bf16[2,64,768]{2,1,0:T(8,128)(2,1)S(1)}, u32[]{:S(2)}, u32[]{:S(2)}) collective-permute-start(bf16[2,64,768]{2,1,0:T(8,128)(2,1)S(1)} %bitcast.18), channel_id=1, source_target_pairs={{0,8},{8,0},{1,9},{9,1},{2,10},{10,2},{3,11},{11,3},{4,12},{12,4},... | collective-permute-start | bytes 589832 | tf_op jit(solution)/shard_map/ppermute | solution.py:714
  117.5 2.1 %collective-permute-start.12 = (f32[16,128]{1,0:T(8,128)S(1)}, f32[16,128]{1,0:T(8,128)S(1)}, u32[]{:S(2)}, u32[]{:S(2)}) collective-permute-start(f32[16,128]{1,0:T(8,128)S(1)} %add_multiply_fusion), channel_id=1, source_target_pairs={{0,4},{1,5},{2,6},{3,7},{4,0},{5,1},{6,2},{7,3},{8,12},{9,13},{10,... | collective-permute-start | bytes 24584 | tf_op jit(solution)/shard_map/ppermute | solution.py:737
  119.6 3.9 %collective-permute-done.11 = bf16[2,64,768]{2,1,0:T(8,128)(2,1)S(1)} collective-permute-done((bf16[2,64,768]{2,1,0:T(8,128)(2,1)S(1)}, bf16[2,64,768]{2,1,0:T(8,128)(2,1)S(1)}, u32[]{:S(2)}, u32[]{:S(2)}) %collective-permute-start.11) | collective-permute-done | bytes 196640 | tf_op jit(solution)/shard_map/ppermute | solution.py:714
  123.6 0.8 pad_maximum_fusion.1
  124.4 0.0 collective-permute-done.12
  124.4 0.6 add_bitcast_fusion
  (26 shorter events, 0.1 us)
Async XLA Ops:
  0.6 10.0 %copy-start.4 = (bf16[128,16]{0,1:T(8,128)(2,1)S(1)}, bf16[128,16]{0,1:T(8,128)(2,1)}, u32[]{:S(2)}) copy-start(bf16[128,16]{0,1:T(8,128)(2,1)} %param.16) | copy-start | bytes 12292
  0.6 9.9 %copy-start.5 = (bf16[256,64,128]{2,1,0:T(8,128)(2,1)S(1)}, bf16[256,64,128]{2,1,0:T(8,128)(2,1)}, u32[]{:S(2)}) copy-start(bf16[256,64,128]{2,1,0:T(8,128)(2,1)} %param.15) | copy-start | bytes 12582916
  0.7 9.9 %copy-start.10 = (s32[64]{0:T(128)S(1)}, s32[64]{0:T(128)}, u32[]{:S(2)}) copy-start(s32[64]{0:T(128)} %param.14) | copy-start | bytes 772
  5.0 14.7 %collective-permute-start = (bf16[2,4,48,256]{3,2,1,0:T(8,128)(2,1)}, bf16[2,4,48,256]{3,2,1,0:T(8,128)(2,1)S(1)}, u32[]{:S(2)}, u32[]{:S(2)}) collective-permute-start(bf16[2,4,48,256]{3,2,1,0:T(8,128)(2,1)} %get-tuple-element.47), channel_id=1, source_target_pairs={{0,2},{1,3},{2,0},{3,1},{4,6},{5,7},{6,4},{7,5},{8,10},{9,11},{10,... | collective-permute-start | bytes 589832 | tf_op jit(solution)/shard_map/ppermute | solution.py:737
  8.0 17.4 %collective-permute-start.1 = (bf16[2,4,48,256]{3,2,1,0:T(8,128)(2,1)}, bf16[2,4,48,256]{3,2,1,0:T(8,128)(2,1)S(1)}, u32[]{:S(2)}, u32[]{:S(2)}) collective-permute-start(bf16[2,4,48,256]{3,2,1,0:T(8,128)(2,1)} %get-tuple-element.48), channel_id=1, source_target_pairs={{0,4},{1,5},{2,6},{3,7},{4,0},{5,1},{6,2},{7,3},{8,12},{9,13},{10,... | collective-permute-start | bytes 589832 | tf_op jit(solution)/shard_map/ppermute | solution.py:737
  10.6 14.8 %collective-permute-start.2 = (bf16[2,4,48,256]{3,2,1,0:T(8,128)(2,1)}, bf16[2,4,48,256]{3,2,1,0:T(8,128)(2,1)S(1)}, u32[]{:S(2)}, u32[]{:S(2)}) collective-permute-start(bf16[2,4,48,256]{3,2,1,0:T(8,128)(2,1)} %get-tuple-element.49), channel_id=1, source_target_pairs={{0,6},{1,7},{2,4},{3,5},{4,2},{5,3},{6,0},{7,1},{8,14},{9,15},{10,... | collective-permute-start | bytes 589832 | tf_op jit(solution)/shard_map/ppermute | solution.py:737
  19.6 12.5 %copy-start.3 = (bf16[2,4,48,256]{3,2,1,0:T(8,128)(2,1)S(1)}, bf16[2,4,48,256]{3,2,1,0:T(8,128)(2,1)}, u32[]{:S(2)}) copy-start(bf16[2,4,48,256]{3,2,1,0:T(8,128)(2,1)} %get-tuple-element.50.refs_0_) | copy-start | bytes 589828
  25.4 20.9 %all-to-all-start = ((f16[16,64,256]{2,1,0:T(8,128)(2,1)}), f16[16,64,256]{2,1,0:T(8,128)(2,1)S(1)}, u32[]{:S(2)}, u32[]{:S(2)}) async-start(f16[16,64,256]{2,1,0:T(8,128)(2,1)} %convert_element_type.21), calls=%async_computation | async-start | bytes 1048576 | tf_op jit(solution)/shard_map/all_to_all | solution.py:754
  32.2 3.5 %collective-permute-start.3 = (bf16[4,4,48,256]{3,2,1,0:T(8,128)(2,1)S(1)}, bf16[4,4,48,256]{3,2,1,0:T(8,128)(2,1)S(1)}, u32[]{:S(2)}, u32[]{:S(2)}) collective-permute-start(bf16[4,4,48,256]{3,2,1,0:T(8,128)(2,1)S(1)} %pad_maximum_fusion), channel_id=1, source_target_pairs={{0,1},{1,0},{2,3},{3,2},{4,5},{5,4},{6,7},{7,6},{8,9},{9,8},{10,11... | collective-permute-start | bytes 1179656 | tf_op jit(solution)/shard_map/ppermute | solution.py:737
  55.0 18.8 %all-to-all-start.1 = ((f16[16,136,128]{2,1,0:T(8,128)(2,1)}), f16[16,136,128]{2,1,0:T(8,128)(2,1)S(1)}, u32[]{:S(2)}, u32[]{:S(2)}) async-start(f16[16,136,128]{2,1,0:T(8,128)(2,1)} %convert_element_type.24), calls=%async_computation.1 | async-start | bytes 1114112 | tf_op jit(solution)/shard_map/all_to_all | solution.py:759
  73.7 16.4 %collective-permute-start.4 = (f16[16,136,128]{2,1,0:T(8,128)(2,1)S(1)}, f16[16,136,128]{2,1,0:T(8,128)(2,1)S(1)}, u32[]{:S(2)}, u32[]{:S(2)}) collective-permute-start(f16[16,136,128]{2,1,0:T(8,128)(2,1)S(1)} %all-to-all-done.1), channel_id=1, source_target_pairs={{0,16},{16,0},{1,17},{17,1},{2,18},{18,2},{3,19},{19,3},{4,20},{20... | collective-permute-start | bytes 1671176 | tf_op jit(solution)/shard_map/ppermute | solution.py:714
  75.5 3.4 %copy-start = (bf16[32,256,512]{2,1,0:T(8,128)(2,1)S(1)}, bf16[32,256,512]{2,1,0:T(8,128)(2,1)}, u32[]{:S(2)}) copy-start(bf16[32,256,512]{2,1,0:T(8,128)(2,1)} %get-tuple-element.67.normed_ref.refs_0_) | copy-start | bytes 25165828
  82.1 18.1 %collective-permute-start.5 = (f32[16,128]{1,0:T(8,128)S(1)}, f32[16,128]{1,0:T(8,128)S(1)}, u32[]{:S(2)}, u32[]{:S(2)}) collective-permute-start(f32[16,128]{1,0:T(8,128)S(1)} %pair_weight.1), channel_id=1, source_target_pairs={{0,16},{16,0},{1,17},{17,1},{2,18},{18,2},{3,19},{19,3},{4,20},{20... | collective-permute-start | bytes 24584 | tf_op jit(solution)/shard_map/ppermute | solution.py:714
  82.7 17.6 %collective-permute-start.6 = (f32[16,128]{1,0:T(8,128)S(1)}, f32[16,128]{1,0:T(8,128)S(1)}, u32[]{:S(2)}, u32[]{:S(2)}) collective-permute-start(f32[16,128]{1,0:T(8,128)S(1)} %pair_weight.1), channel_id=1, source_target_pairs={{0,8},{8,0},{1,9},{9,1},{2,10},{10,2},{3,11},{11,3},{4,12},{12,4},... | collective-permute-start | bytes 24584 | tf_op jit(solution)/shard_map/ppermute | solution.py:714
  84.1 16.1 %collective-permute-start.7 = (f32[16,128]{1,0:T(8,128)S(1)}, f32[16,128]{1,0:T(8,128)S(1)}, u32[]{:S(2)}, u32[]{:S(2)}) collective-permute-start(f32[16,128]{1,0:T(8,128)S(1)} %pair_weight.1), channel_id=1, source_target_pairs={{0,24},{8,16},{16,8},{24,0},{1,25},{9,17},{17,9},{25,1},{2,26},{10... | collective-permute-start | bytes 24584 | tf_op jit(solution)/shard_map/ppermute | solution.py:772
  85.7 24.3 %all-to-all-start.2 = ((f16[16,200,128]{2,1,0:T(8,128)(2,1)}), f16[16,200,128]{2,1,0:T(8,128)(2,1)}, u32[]{:S(2)}, u32[]{:S(2)}) async-start(f16[16,200,128]{2,1,0:T(8,128)(2,1)} %convert_element_type.23), calls=%async_computation.2 | async-start | bytes 1638400 | tf_op jit(solution)/shard_map/all_to_all | solution.py:765
  90.4 1.0 copy-start.2
  91.4 3.4 %copy-start.1 = (bf16[32,256,512]{2,1,0:T(8,128)(2,1)S(1)}, bf16[32,256,512]{2,1,0:T(8,128)(2,1)}, u32[]{:S(2)}) copy-start(bf16[32,256,512]{2,1,0:T(8,128)(2,1)} %get-tuple-element.67.normed_ref.refs_0_) | copy-start | bytes 25165828
  94.8 16.4 %copy-start.11 = (f32[768,128]{1,0:T(8,128)S(1)}, f32[768,128]{1,0:T(8,128)}, u32[]{:S(2)}) copy-start(f32[768,128]{1,0:T(8,128)} %get-tuple-element.77.refs_1_) | copy-start | bytes 1179652
  94.8 16.4 %copy-start.12 = (f32[768,128]{1,0:T(8,128)S(1)}, f32[768,128]{1,0:T(8,128)}, u32[]{:S(2)}) copy-start(f32[768,128]{1,0:T(8,128)} %get-tuple-element.78.refs_2_) | copy-start | bytes 1179652
  100.3 10.9 %copy-start.6 = (bf16[768,768]{1,0:T(8,128)(2,1)S(1)}, bf16[768,768]{1,0:T(8,128)(2,1)}, u32[]{:S(2)}) copy-start(bf16[768,768]{1,0:T(8,128)(2,1)} %refs_4_.3) | copy-start | bytes 3538948
  100.3 10.9 %copy-start.7 = (bf16[768,768]{1,0:T(8,128)(2,1)S(1)}, bf16[768,768]{1,0:T(8,128)(2,1)}, u32[]{:S(2)}) copy-start(bf16[768,768]{1,0:T(8,128)(2,1)} %refs_5_.1) | copy-start | bytes 3538948
  100.3 10.9 %copy-start.13 = (f32[8,128]{1,0:T(8,128)S(1)}, f32[8,128]{1,0:T(8,128)}, u32[]{:S(2)}) copy-start(f32[8,128]{1,0:T(8,128)} %get-tuple-element.79.refs_3_) | copy-start | bytes 12292
  100.3 1.9 %collective-permute-start.8 = (f32[16,128]{1,0:T(8,128)S(1)}, f32[16,128]{1,0:T(8,128)S(1)}, u32[]{:S(2)}, u32[]{:S(2)}) collective-permute-start(f32[16,128]{1,0:T(8,128)S(1)} %add_add_fusion), channel_id=1, source_target_pairs={{0,1},{1,0},{2,3},{3,2},{4,5},{5,4},{6,7},{7,6},{8,9},{9,8},{10,11... | collective-permute-start | bytes 24584 | tf_op jit(solution)/shard_map/ppermute | solution.py:737
  100.4 3.9 %collective-permute-start.9 = (f32[16,128]{1,0:T(8,128)S(1)}, f32[16,128]{1,0:T(8,128)S(1)}, u32[]{:S(2)}, u32[]{:S(2)}) collective-permute-start(f32[16,128]{1,0:T(8,128)S(1)} %add_add_fusion), channel_id=1, source_target_pairs={{0,2},{1,3},{2,0},{3,1},{4,6},{5,7},{6,4},{7,5},{8,10},{9,11},{10,... | collective-permute-start | bytes 24584 | tf_op jit(solution)/shard_map/ppermute | solution.py:737
  102.1 3.1 %collective-permute-start.10 = (f32[16,128]{1,0:T(8,128)S(1)}, f32[16,128]{1,0:T(8,128)S(1)}, u32[]{:S(2)}, u32[]{:S(2)}) collective-permute-start(f32[16,128]{1,0:T(8,128)S(1)} %add_add_fusion), channel_id=1, source_target_pairs={{0,3},{1,2},{2,1},{3,0},{4,7},{5,6},{6,5},{7,4},{8,11},{9,10},{10,... | collective-permute-start | bytes 24584 | tf_op jit(solution)/shard_map/ppermute | solution.py:737
  111.2 1.3 %copy-start.8 = (bf16[768,768]{1,0:T(8,128)(2,1)S(1)}, bf16[768,768]{1,0:T(8,128)(2,1)}, u32[]{:S(2)}) copy-start(bf16[768,768]{1,0:T(8,128)(2,1)} %refs_6_.1) | copy-start | bytes 3538948
  112.5 1.3 %copy-start.9 = (bf16[768,768]{1,0:T(8,128)(2,1)S(1)}, bf16[768,768]{1,0:T(8,128)(2,1)}, u32[]{:S(2)}) copy-start(bf16[768,768]{1,0:T(8,128)(2,1)} %refs_7_.1) | copy-start | bytes 3538948
  115.9 7.6 %collective-permute-start.11 = (bf16[2,64,768]{2,1,0:T(8,128)(2,1)S(1)}, bf16[2,64,768]{2,1,0:T(8,128)(2,1)S(1)}, u32[]{:S(2)}, u32[]{:S(2)}) collective-permute-start(bf16[2,64,768]{2,1,0:T(8,128)(2,1)S(1)} %bitcast.18), channel_id=1, source_target_pairs={{0,8},{8,0},{1,9},{9,1},{2,10},{10,2},{3,11},{11,3},{4,12},{12,4},... | collective-permute-start | bytes 589832 | tf_op jit(solution)/shard_map/ppermute | solution.py:714
  117.5 6.9 %collective-permute-start.12 = (f32[16,128]{1,0:T(8,128)S(1)}, f32[16,128]{1,0:T(8,128)S(1)}, u32[]{:S(2)}, u32[]{:S(2)}) collective-permute-start(f32[16,128]{1,0:T(8,128)S(1)} %add_multiply_fusion), channel_id=1, source_target_pairs={{0,4},{1,5},{2,6},{3,7},{4,0},{5,1},{6,2},{7,3},{8,12},{9,13},{10,... | collective-permute-start | bytes 24584 | tf_op jit(solution)/shard_map/ppermute | solution.py:737

commit v13 on v10

--- a/solution.py
+++ b/solution.py
@@ -776,9 +776,10 @@
         pair.shape, pair_normed, pair_inv, grads, weight_t, total_tokens / samples
     )
 
-    pair_grad, back, sums = lax.optimization_barrier(
-        (pair_grad, back, (part, samp_part, row_part, both_part))
-    )
+    pair_grad, sums = lax.optimization_barrier(
+        (pair_grad, (part, samp_part, row_part, both_part))
+    )
+    back, _ = lax.optimization_barrier((back, pair_grad))
     part = (sums[0] + sums[1]) + (sums[2] + sums[3])
     sums = (send(part, 1), send(part, 2), send(part, 3))
     token_half = token_back(back.astype(jnp.float32), *own, weights)

time: 115 us -> 115 us (level)
  local copies, waits for them, and re-layouts: 4.36 us -> 6.91 us
  waiting for transfers between devices: 28.9 us -> 27.3 us
    unnamed x28, local copies, waits for them, and re-layouts: 4.32 us -> 6.87 us
    all_to_all x1, waiting for transfers between devices: 2.6 us -> 0.71 us  [body_heads(): back = lax.all_to_all(back, ('row', 'col'), 0, 0, tiled=True)]
where the time goes in v13:
time: 115 us
  Pallas kernels  41.4 us (36%)
  starting transfers between devices  31.9 us (28%)
  waiting for transfers between devices  27.3 us (24%)
  local copies, waits for them, and re-layouts  6.91 us (6%)
  other arithmetic  6.15 us (5%)
    all_to_all x1, waiting for transfers between devices, body_heads(): bias = lax.all_to_all(bias, ('row', 'col'), 0, 0, tiled=True)  10.6 us
    ppermute x8, starting transfers between devices, send(): return lax.ppermute(block, 'col', [(c, c ^ offset) for c in range(n_col)])  10.1 us
    pallas_call x1, Pallas kernels, pair_bias(): pl.pallas_call(bias_kernel, out_shape=jax.ShapeDtypeStruct((H, tok_col, r...  8.12 us
    pallas_call x1, Pallas kernels, attention(): pl.pallas_call(attention_kernel, out_shape=[jax.ShapeDtypeStruct(back_sha...  7.67 us
    pallas_call x1, Pallas kernels, pair_units(): pl.pallas_call(norm_kernel, out_shape=[jax.ShapeDtypeStruct(shapes[0], jn...  7.45 us
    unnamed x28, local copies, waits for them, and re-layouts  6.87 us
    all_to_all x1, starting transfers between devices, body_heads(): bias = lax.all_to_all(bias, ('row', 'col'), 0, 0, tiled=True)  6.67 us
    all_to_all x1, waiting for transfers between devices, body_heads(): lax.all_to_all(grad_bias.astype(jnp.float16), ('row', 'col'), 0, 0, tiled...  6.29 us
  transfers between devices with their start and end apart: 16, of which 5 were waited for; matrix products, arithmetic and copies ran while one was open for 4% of the time, Pallas kernels for 26%

profile of v13, /device:TPU:0, one launch (start us, length us, event | category | flops | bytes accessed | tf_op | source)
XLA Modules:
  0.0 114.7 jit_solution(12955928037688428270)
XLA Ops:
  0.6 0.0 copy-start.4
  0.6 0.0 copy-start.5
  0.7 4.3 %token_messages.1 = (bf16[2,4,48,256]{3,2,1,0:T(8,128)(2,1)}, bf16[2,4,48,256]{3,2,1,0:T(8,128)(2,1)}, bf16[2,4,48,256]{3,2,1,0:T(8,128)(2,1)}, bf16[2,4,48,256]{3,2,1,0:T(8,128)(2,1)}) custom-call(s32[1]{0:T(128)} %bitcast.4.row_ref, s32[1]{0:T(128)} %bitcast.col_ref, bf16[4,64,768]{2,1,0:T(8,128)(2,1)} %tokens_ref.3, s32[1,64]{1,0:T(1,128)} %bitcast.28, ...), custom_call_target="tpu_custom_call" | custom-call | flops 4000000000 | bytes 4000000 | tf_op jit(solution)/shard_map/token_messages/pallas_call | solution.py:245
  5.0 3.0 %collective-permute-start = (bf16[2,4,48,256]{3,2,1,0:T(8,128)(2,1)}, bf16[2,4,48,256]{3,2,1,0:T(8,128)(2,1)S(1)}, u32[]{:S(2)}, u32[]{:S(2)}) collective-permute-start(bf16[2,4,48,256]{3,2,1,0:T(8,128)(2,1)} %get-tuple-element.45), channel_id=1, source_target_pairs={{0,2},{1,3},{2,0},{3,1},{4,6},{5,7},{6,4},{7,5},{8,10},{9,11},{10,... | collective-permute-start | bytes 589832 | tf_op jit(solution)/shard_map/ppermute | solution.py:737
  8.0 2.6 %collective-permute-start.1 = (bf16[2,4,48,256]{3,2,1,0:T(8,128)(2,1)}, bf16[2,4,48,256]{3,2,1,0:T(8,128)(2,1)S(1)}, u32[]{:S(2)}, u32[]{:S(2)}) collective-permute-start(bf16[2,4,48,256]{3,2,1,0:T(8,128)(2,1)} %get-tuple-element.46), channel_id=1, source_target_pairs={{0,4},{1,5},{2,6},{3,7},{4,0},{5,1},{6,2},{7,3},{8,12},{9,13},{10,... | collective-permute-start | bytes 589832 | tf_op jit(solution)/shard_map/ppermute | solution.py:737
  10.6 0.0 collective-permute-start.2
  10.6 8.1 %pair_bias.1 = f32[16,64,256]{2,1,0:T(8,128)S(1)} custom-call(bf16[2,128,64,128]{3,2,1,0:T(8,128)(2,1)S(1)} %bitcast.23, bf16[16,128]{1,0:T(8,128)(2,1)S(1)} %bitcast.20, s32[1,64]{1,0:T(1,128)S(1)} %bitcast.24), custom_call_target="tpu_custom_call" | custom-call | flops 6000000000 | bytes 5000000 | tf_op jit(solution)/shard_map/pair_bias/pallas_call | solution.py:383
  18.7 0.9 convert_element_type.21
  19.6 0.0 collective-permute-done.refs_1_
  19.6 5.7 %collective-permute-done.1.refs_2_ = bf16[2,4,48,256]{3,2,1,0:T(8,128)(2,1)S(1)} collective-permute-done((bf16[2,4,48,256]{3,2,1,0:T(8,128)(2,1)}, bf16[2,4,48,256]{3,2,1,0:T(8,128)(2,1)S(1)}, u32[]{:S(2)}, u32[]{:S(2)}) %collective-permute-start.1) | collective-permute-done | bytes 196640 | tf_op jit(solution)/shard_map/ppermute | solution.py:737
  25.4 0.0 collective-permute-done.2.refs_3_
  25.4 6.7 %all-to-all-start = ((f16[16,64,256]{2,1,0:T(8,128)(2,1)}), f16[16,64,256]{2,1,0:T(8,128)(2,1)S(1)}, u32[]{:S(2)}, u32[]{:S(2)}) async-start(f16[16,64,256]{2,1,0:T(8,128)(2,1)} %convert_element_type.21), calls=%async_computation | async-start | bytes 1048576 | tf_op jit(solution)/shard_map/all_to_all | solution.py:754
  32.1 0.0 copy-done.3
  32.1 0.1 pad_maximum_fusion
  32.2 0.5 collective-permute-start.3
  32.7 3.0 %own_rows.1 = (f32[768,128]{1,0:T(8,128)}, f32[768,128]{1,0:T(8,128)}, f32[8,128]{1,0:T(8,128)}) custom-call(s32[1]{0:T(128)} %bitcast.4.row_ref, bf16[4,64,768]{2,1,0:T(8,128)(2,1)} %tokens_ref.3, s32[1,64]{1,0:T(1,128)} %bitcast.29, bf16[32,768]{1,0:T(8,128)(2,1)} %table_ref.3, bf16[768,768]{1,0:T(8,128)(2,1)} %refs_7_.1, bf16[4,64,768]{2,1,0:T(8,128)(2,1)} %cot_ref.1), custom_call_target="tpu_custom_call" | custom-call | flops 3000000000 | bytes 3000000 | tf_op jit(solution)/shard_map/own_rows/pallas_call | solution.py:289
  35.7 0.0 collective-permute-done.3.refs_4_
  35.7 10.6 %all-to-all-done = f16[16,64,256]{2,1,0:T(8,128)(2,1)S(1)} async-done(((f16[16,64,256]{2,1,0:T(8,128)(2,1)}), f16[16,64,256]{2,1,0:T(8,128)(2,1)S(1)}, u32[]{:S(2)}, u32[]{:S(2)}) %all-to-all-start) | async-done | bytes 524320 | tf_op jit(solution)/shard_map/all_to_all | solution.py:754
  46.3 0.1 convert_element_type.22.refs_5_
  46.4 7.7 %attention.1 = (f32[16,200,128]{2,1,0:T(8,128)S(1)}, f32[16,136,128]{2,1,0:T(8,128)S(1)}) custom-call(s32[1]{0:T(128)} %bitcast.col_ref, bf16[2,4,48,256]{3,2,1,0:T(8,128)(2,1)S(1)} %copy-done.3, bf16[2,4,48,256]{3,2,1,0:T(8,128)(2,1)S(1)} %collective-permute-done.refs_1_, bf16[2,4,48,256]{3,2,1,0:T(8,128)(2,1)S(1)} %collective-permute-done.1.refs_2_, ...), custom_call_target="tpu_custom_call" | custom-call | flops 8000000000 | bytes 6000000 | tf_op jit(solution)/shard_map/attention/pallas_call | solution.py:530
  54.1 0.9 convert_element_type.24
  55.0 4.0 %all-to-all-start.1 = ((f16[16,136,128]{2,1,0:T(8,128)(2,1)}), f16[16,136,128]{2,1,0:T(8,128)(2,1)S(1)}, u32[]{:S(2)}, u32[]{:S(2)}) async-start(f16[16,136,128]{2,1,0:T(8,128)(2,1)} %convert_element_type.24), calls=%async_computation.1 | async-start | bytes 1114112 | tf_op jit(solution)/shard_map/all_to_all | solution.py:759
  59.0 1.0 convert_element_type.23
  60.0 7.4 %pair_units.1 = (bf16[32,256,512]{2,1,0:T(8,128)(2,1)}, f32[32,8,512]{2,1,0:T(8,128)}) custom-call(bf16[2,128,64,128]{3,2,1,0:T(8,128)(2,1)} %bitcast.22), custom_call_target="tpu_custom_call" | custom-call | flops 6000000000 | bytes 12000000 | tf_op jit(solution)/shard_map/pair_units/pallas_call | solution.py:413
  67.5 6.3 %all-to-all-done.1 = f16[16,136,128]{2,1,0:T(8,128)(2,1)S(1)} async-done(((f16[16,136,128]{2,1,0:T(8,128)(2,1)}), f16[16,136,128]{2,1,0:T(8,128)(2,1)S(1)}, u32[]{:S(2)}, u32[]{:S(2)}) %all-to-all-start.1) | async-done | bytes 557088 | tf_op jit(solution)/shard_map/all_to_all | solution.py:759
  73.7 1.5 %collective-permute-start.4 = (f16[16,136,128]{2,1,0:T(8,128)(2,1)S(1)}, f16[16,136,128]{2,1,0:T(8,128)(2,1)S(1)}, u32[]{:S(2)}, u32[]{:S(2)}) collective-permute-start(f16[16,136,128]{2,1,0:T(8,128)(2,1)S(1)} %all-to-all-done.1), channel_id=1, source_target_pairs={{0,16},{16,0},{1,17},{17,1},{2,18},{18,2},{3,19},{19,3},{4,20},{20... | collective-permute-start | bytes 1671176 | tf_op jit(solution)/shard_map/ppermute | solution.py:714
  75.3 0.1 convert_element_type.25
  75.3 4.5 %all-to-all-start.2 = ((f16[16,200,128]{2,1,0:T(8,128)(2,1)}), f16[16,200,128]{2,1,0:T(8,128)(2,1)}, u32[]{:S(2)}, u32[]{:S(2)}) async-start(f16[16,200,128]{2,1,0:T(8,128)(2,1)} %convert_element_type.23), calls=%async_computation.2 | async-start | bytes 1638400 | tf_op jit(solution)/shard_map/all_to_all | solution.py:765
  79.9 0.1 slice_multiply_fusion.1
  80.0 3.4 %copy-done = bf16[32,256,512]{2,1,0:T(8,128)(2,1)S(1)} copy-done((bf16[32,256,512]{2,1,0:T(8,128)(2,1)S(1)}, bf16[32,256,512]{2,1,0:T(8,128)(2,1)}, u32[]{:S(2)}) %copy-start) | copy-done | bytes 8388632
  83.4 3.3 %pair_weight.1 = f32[16,128]{1,0:T(8,128)S(1)} custom-call(bf16[32,256,512]{2,1,0:T(8,128)(2,1)S(1)} %copy-done, f32[2048,128]{1,0:T(8,128)S(1)} %bitcast.17), custom_call_target="tpu_custom_call" | custom-call | flops 1000000 | bytes 100000 | tf_op jit(solution)/shard_map/pair_weight/pallas_call | solution.py:670
  86.6 0.6 collective-permute-start.5
  87.2 1.6 %collective-permute-start.6 = (f32[16,128]{1,0:T(8,128)S(1)}, f32[16,128]{1,0:T(8,128)S(1)}, u32[]{:S(2)}, u32[]{:S(2)}) collective-permute-start(f32[16,128]{1,0:T(8,128)S(1)} %pair_weight.1), channel_id=1, source_target_pairs={{0,8},{8,0},{1,9},{9,1},{2,10},{10,2},{3,11},{11,3},{4,12},{12,4},... | collective-permute-start | bytes 24584 | tf_op jit(solution)/shard_map/ppermute | solution.py:714
  88.8 1.4 %collective-permute-start.7 = (f32[16,128]{1,0:T(8,128)S(1)}, f32[16,128]{1,0:T(8,128)S(1)}, u32[]{:S(2)}, u32[]{:S(2)}) collective-permute-start(f32[16,128]{1,0:T(8,128)S(1)} %pair_weight.1), channel_id=1, source_target_pairs={{0,24},{8,16},{16,8},{24,0},{1,25},{9,17},{17,9},{25,1},{2,26},{10... | collective-permute-start | bytes 24584 | tf_op jit(solution)/shard_map/ppermute | solution.py:772
  90.2 0.0 collective-permute-done.4
  90.2 0.1 convert_element_type.26
  90.3 0.1 slice_multiply_fusion
  90.4 0.1 bitcast_add_fusion.refs_2_
  90.5 0.9 copy-done.2
  91.4 5.4 %pair_backward.1 = bf16[2,128,64,128]{3,2,1,0:T(8,128)(2,1)} custom-call(bf16[32,256,512]{2,1,0:T(8,128)(2,1)S(1)} %copy-done.1, f32[32,8,512]{2,1,0:T(8,128)S(1)} %copy-done.2, f32[2048,128]{1,0:T(8,128)S(1)} %bitcast_add_fusion.refs_2_, bf16[16,128]{1,0:T(8,128)(2,1)S(1)} %bitcast.21), custom_call_target="tpu_custom_call" | custom-call | flops 1000000 | bytes 100000 | tf_op jit(solution)/shard_map/pair_backward/pallas_call | solution.py:687
  96.9 0.0 collective-permute-done.5
  96.9 0.0 collective-permute-done.6
  96.9 0.0 collective-permute-done.7
  96.9 0.0 copy-start.6
  96.9 0.0 copy-start.7
  96.9 0.0 copy-start.13
  97.0 0.1 collective-permute-start.8
  97.0 1.6 %collective-permute-start.9 = (f32[16,128]{1,0:T(8,128)S(1)}, f32[16,128]{1,0:T(8,128)S(1)}, u32[]{:S(2)}, u32[]{:S(2)}) collective-permute-start(f32[16,128]{1,0:T(8,128)S(1)} %add_add_fusion), channel_id=1, source_target_pairs={{0,2},{1,3},{2,0},{3,1},{4,6},{5,7},{6,4},{7,5},{8,10},{9,11},{10,... | collective-permute-start | bytes 24584 | tf_op jit(solution)/shard_map/ppermute | solution.py:737
  98.7 0.2 collective-permute-start.10
  98.9 0.7 all-to-all-done.2
  99.6 1.3 %convert_element_type.27.refs_0_ = f32[16,200,128]{2,1,0:T(8,128)S(1)} convert(f16[16,200,128]{2,1,0:T(8,128)(2,1)} %all-to-all-done.2) | non-fusion elementwise | flops 409600 | bytes 2457600 | tf_op jit(solution)/shard_map/convert_element_type | solution.py:785
  100.9 0.0 copy-start.8
  100.9 1.3 %copy-done.8 = bf16[768,768]{1,0:T(8,128)(2,1)S(1)} copy-done((bf16[768,768]{1,0:T(8,128)(2,1)S(1)}, bf16[768,768]{1,0:T(8,128)(2,1)}, u32[]{:S(2)}) %copy-start.8) | copy-done | bytes 1179672
  102.2 1.3 %copy-done.9 = bf16[768,768]{1,0:T(8,128)(2,1)S(1)} copy-done((bf16[768,768]{1,0:T(8,128)(2,1)S(1)}, bf16[768,768]{1,0:T(8,128)(2,1)}, u32[]{:S(2)}) %copy-start.9) | copy-done | bytes 1179672
  103.5 2.1 %token_back.1 = bf16[128,768]{1,0:T(8,128)(2,1)S(1)} custom-call(f32[16,200,128]{2,1,0:T(8,128)S(1)} %convert_element_type.27.refs_0_, f32[768,128]{1,0:T(8,128)S(1)} %copy-done.11, f32[768,128]{1,0:T(8,128)S(1)} %copy-done.12, f32[8,128]{1,0:T(8,128)S(1)} %copy-done.13, bf16[768,768]{1,0:T(8,128)(2,1)S(1)} %copy-done.6, bf16[768,768]{1,0:T(8,128)(2,1)S(1)} %copy-done.7, ...), custom_call_target="tpu_custom_call" | custom-call | flops 4000000000 | bytes 8000000 | tf_op jit(solution)/shard_map/token_back/pallas_call | solution.py:603
  105.6 0.0 collective-permute-done.8
  105.6 0.0 collective-permute-done.9
  105.6 0.0 collective-permute-done.10
  105.6 1.6 %collective-permute-start.11 = (bf16[2,64,768]{2,1,0:T(8,128)(2,1)S(1)}, bf16[2,64,768]{2,1,0:T(8,128)(2,1)S(1)}, u32[]{:S(2)}, u32[]{:S(2)}) collective-permute-start(bf16[2,64,768]{2,1,0:T(8,128)(2,1)S(1)} %bitcast.18), channel_id=1, source_target_pairs={{0,8},{8,0},{1,9},{9,1},{2,10},{10,2},{3,11},{11,3},{4,12},{12,4},... | collective-permute-start | bytes 589832 | tf_op jit(solution)/shard_map/ppermute | solution.py:714
  107.2 2.1 %collective-permute-start.12 = (f32[16,128]{1,0:T(8,128)S(1)}, f32[16,128]{1,0:T(8,128)S(1)}, u32[]{:S(2)}, u32[]{:S(2)}) collective-permute-start(f32[16,128]{1,0:T(8,128)S(1)} %add_multiply_fusion), channel_id=1, source_target_pairs={{0,4},{1,5},{2,6},{3,7},{4,0},{5,1},{6,2},{7,3},{8,12},{9,13},{10,... | collective-permute-start | bytes 24584 | tf_op jit(solution)/shard_map/ppermute | solution.py:737
  109.3 3.9 %collective-permute-done.11 = bf16[2,64,768]{2,1,0:T(8,128)(2,1)S(1)} collective-permute-done((bf16[2,64,768]{2,1,0:T(8,128)(2,1)S(1)}, bf16[2,64,768]{2,1,0:T(8,128)(2,1)S(1)}, u32[]{:S(2)}, u32[]{:S(2)}) %collective-permute-start.11) | collective-permute-done | bytes 196640 | tf_op jit(solution)/shard_map/ppermute | solution.py:714
  113.3 0.8 pad_maximum_fusion.1
  114.1 0.0 collective-permute-done.12
  114.1 0.6 add_bitcast_fusion
  (26 shorter events, 0.1 us)
Async XLA Ops:
  0.6 10.0 %copy-start.4 = (bf16[128,16]{0,1:T(8,128)(2,1)S(1)}, bf16[128,16]{0,1:T(8,128)(2,1)}, u32[]{:S(2)}) copy-start(bf16[128,16]{0,1:T(8,128)(2,1)} %param.16) | copy-start | bytes 12292
  0.6 9.9 %copy-start.5 = (bf16[256,64,128]{2,1,0:T(8,128)(2,1)S(1)}, bf16[256,64,128]{2,1,0:T(8,128)(2,1)}, u32[]{:S(2)}) copy-start(bf16[256,64,128]{2,1,0:T(8,128)(2,1)} %param.15) | copy-start | bytes 12582916
  0.7 9.9 %copy-start.10 = (s32[64]{0:T(128)S(1)}, s32[64]{0:T(128)}, u32[]{:S(2)}) copy-start(s32[64]{0:T(128)} %param.14) | copy-start | bytes 772
  5.0 14.7 %collective-permute-start = (bf16[2,4,48,256]{3,2,1,0:T(8,128)(2,1)}, bf16[2,4,48,256]{3,2,1,0:T(8,128)(2,1)S(1)}, u32[]{:S(2)}, u32[]{:S(2)}) collective-permute-start(bf16[2,4,48,256]{3,2,1,0:T(8,128)(2,1)} %get-tuple-element.45), channel_id=1, source_target_pairs={{0,2},{1,3},{2,0},{3,1},{4,6},{5,7},{6,4},{7,5},{8,10},{9,11},{10,... | collective-permute-start | bytes 589832 | tf_op jit(solution)/shard_map/ppermute | solution.py:737
  8.0 17.4 %collective-permute-start.1 = (bf16[2,4,48,256]{3,2,1,0:T(8,128)(2,1)}, bf16[2,4,48,256]{3,2,1,0:T(8,128)(2,1)S(1)}, u32[]{:S(2)}, u32[]{:S(2)}) collective-permute-start(bf16[2,4,48,256]{3,2,1,0:T(8,128)(2,1)} %get-tuple-element.46), channel_id=1, source_target_pairs={{0,4},{1,5},{2,6},{3,7},{4,0},{5,1},{6,2},{7,3},{8,12},{9,13},{10,... | collective-permute-start | bytes 589832 | tf_op jit(solution)/shard_map/ppermute | solution.py:737
  10.6 14.8 %collective-permute-start.2 = (bf16[2,4,48,256]{3,2,1,0:T(8,128)(2,1)}, bf16[2,4,48,256]{3,2,1,0:T(8,128)(2,1)S(1)}, u32[]{:S(2)}, u32[]{:S(2)}) collective-permute-start(bf16[2,4,48,256]{3,2,1,0:T(8,128)(2,1)} %get-tuple-element.47), channel_id=1, source_target_pairs={{0,6},{1,7},{2,4},{3,5},{4,2},{5,3},{6,0},{7,1},{8,14},{9,15},{10,... | collective-permute-start | bytes 589832 | tf_op jit(solution)/shard_map/ppermute | solution.py:737
  19.6 12.5 %copy-start.3 = (bf16[2,4,48,256]{3,2,1,0:T(8,128)(2,1)S(1)}, bf16[2,4,48,256]{3,2,1,0:T(8,128)(2,1)}, u32[]{:S(2)}) copy-start(bf16[2,4,48,256]{3,2,1,0:T(8,128)(2,1)} %get-tuple-element.48.refs_0_) | copy-start | bytes 589828
  25.4 20.9 %all-to-all-start = ((f16[16,64,256]{2,1,0:T(8,128)(2,1)}), f16[16,64,256]{2,1,0:T(8,128)(2,1)S(1)}, u32[]{:S(2)}, u32[]{:S(2)}) async-start(f16[16,64,256]{2,1,0:T(8,128)(2,1)} %convert_element_type.21), calls=%async_computation | async-start | bytes 1048576 | tf_op jit(solution)/shard_map/all_to_all | solution.py:754
  32.2 3.5 %collective-permute-start.3 = (bf16[4,4,48,256]{3,2,1,0:T(8,128)(2,1)S(1)}, bf16[4,4,48,256]{3,2,1,0:T(8,128)(2,1)S(1)}, u32[]{:S(2)}, u32[]{:S(2)}) collective-permute-start(bf16[4,4,48,256]{3,2,1,0:T(8,128)(2,1)S(1)} %pad_maximum_fusion), channel_id=1, source_target_pairs={{0,1},{1,0},{2,3},{3,2},{4,5},{5,4},{6,7},{7,6},{8,9},{9,8},{10,11... | collective-permute-start | bytes 1179656 | tf_op jit(solution)/shard_map/ppermute | solution.py:737
  55.0 18.8 %all-to-all-start.1 = ((f16[16,136,128]{2,1,0:T(8,128)(2,1)}), f16[16,136,128]{2,1,0:T(8,128)(2,1)S(1)}, u32[]{:S(2)}, u32[]{:S(2)}) async-start(f16[16,136,128]{2,1,0:T(8,128)(2,1)} %convert_element_type.24), calls=%async_computation.1 | async-start | bytes 1114112 | tf_op jit(solution)/shard_map/all_to_all | solution.py:759
  73.7 16.4 %collective-permute-start.4 = (f16[16,136,128]{2,1,0:T(8,128)(2,1)S(1)}, f16[16,136,128]{2,1,0:T(8,128)(2,1)S(1)}, u32[]{:S(2)}, u32[]{:S(2)}) collective-permute-start(f16[16,136,128]{2,1,0:T(8,128)(2,1)S(1)} %all-to-all-done.1), channel_id=1, source_target_pairs={{0,16},{16,0},{1,17},{17,1},{2,18},{18,2},{3,19},{19,3},{4,20},{20... | collective-permute-start | bytes 1671176 | tf_op jit(solution)/shard_map/ppermute | solution.py:714
  75.3 24.3 %all-to-all-start.2 = ((f16[16,200,128]{2,1,0:T(8,128)(2,1)}), f16[16,200,128]{2,1,0:T(8,128)(2,1)}, u32[]{:S(2)}, u32[]{:S(2)}) async-start(f16[16,200,128]{2,1,0:T(8,128)(2,1)} %convert_element_type.23), calls=%async_computation.2 | async-start | bytes 1638400 | tf_op jit(solution)/shard_map/all_to_all | solution.py:765
  80.0 3.4 %copy-start = (bf16[32,256,512]{2,1,0:T(8,128)(2,1)S(1)}, bf16[32,256,512]{2,1,0:T(8,128)(2,1)}, u32[]{:S(2)}) copy-start(bf16[32,256,512]{2,1,0:T(8,128)(2,1)} %get-tuple-element.65.normed_ref.refs_0_) | copy-start | bytes 25165828
  83.4 7.2 %copy-start.1 = (bf16[32,256,512]{2,1,0:T(8,128)(2,1)S(1)}, bf16[32,256,512]{2,1,0:T(8,128)(2,1)}, u32[]{:S(2)}) copy-start(bf16[32,256,512]{2,1,0:T(8,128)(2,1)} %get-tuple-element.65.normed_ref.refs_0_) | copy-start | bytes 25165828
  86.6 10.3 %collective-permute-start.5 = (f32[16,128]{1,0:T(8,128)S(1)}, f32[16,128]{1,0:T(8,128)S(1)}, u32[]{:S(2)}, u32[]{:S(2)}) collective-permute-start(f32[16,128]{1,0:T(8,128)S(1)} %pair_weight.1), channel_id=1, source_target_pairs={{0,16},{16,0},{1,17},{17,1},{2,18},{18,2},{3,19},{19,3},{4,20},{20... | collective-permute-start | bytes 24584 | tf_op jit(solution)/shard_map/ppermute | solution.py:714
  87.2 9.7 %collective-permute-start.6 = (f32[16,128]{1,0:T(8,128)S(1)}, f32[16,128]{1,0:T(8,128)S(1)}, u32[]{:S(2)}, u32[]{:S(2)}) collective-permute-start(f32[16,128]{1,0:T(8,128)S(1)} %pair_weight.1), channel_id=1, source_target_pairs={{0,8},{8,0},{1,9},{9,1},{2,10},{10,2},{3,11},{11,3},{4,12},{12,4},... | collective-permute-start | bytes 24584 | tf_op jit(solution)/shard_map/ppermute | solution.py:714
  88.8 8.1 %collective-permute-start.7 = (f32[16,128]{1,0:T(8,128)S(1)}, f32[16,128]{1,0:T(8,128)S(1)}, u32[]{:S(2)}, u32[]{:S(2)}) collective-permute-start(f32[16,128]{1,0:T(8,128)S(1)} %pair_weight.1), channel_id=1, source_target_pairs={{0,24},{8,16},{16,8},{24,0},{1,25},{9,17},{17,9},{25,1},{2,26},{10... | collective-permute-start | bytes 24584 | tf_op jit(solution)/shard_map/ppermute | solution.py:772
  90.4 1.0 copy-start.2
  91.4 9.4 %copy-start.11 = (f32[768,128]{1,0:T(8,128)S(1)}, f32[768,128]{1,0:T(8,128)}, u32[]{:S(2)}) copy-start(f32[768,128]{1,0:T(8,128)} %get-tuple-element.72.refs_1_) | copy-start | bytes 1179652
  91.4 9.4 %copy-start.12 = (f32[768,128]{1,0:T(8,128)S(1)}, f32[768,128]{1,0:T(8,128)}, u32[]{:S(2)}) copy-start(f32[768,128]{1,0:T(8,128)} %get-tuple-element.73.refs_2_) | copy-start | bytes 1179652
  96.9 4.0 %copy-start.6 = (bf16[768,768]{1,0:T(8,128)(2,1)S(1)}, bf16[768,768]{1,0:T(8,128)(2,1)}, u32[]{:S(2)}) copy-start(bf16[768,768]{1,0:T(8,128)(2,1)} %refs_4_.3) | copy-start | bytes 3538948
  96.9 4.0 %copy-start.7 = (bf16[768,768]{1,0:T(8,128)(2,1)S(1)}, bf16[768,768]{1,0:T(8,128)(2,1)}, u32[]{:S(2)}) copy-start(bf16[768,768]{1,0:T(8,128)(2,1)} %refs_5_.1) | copy-start | bytes 3538948
  96.9 4.0 %copy-start.13 = (f32[8,128]{1,0:T(8,128)S(1)}, f32[8,128]{1,0:T(8,128)}, u32[]{:S(2)}) copy-start(f32[8,128]{1,0:T(8,128)} %get-tuple-element.74.refs_3_) | copy-start | bytes 12292
  97.0 8.6 %collective-permute-start.8 = (f32[16,128]{1,0:T(8,128)S(1)}, f32[16,128]{1,0:T(8,128)S(1)}, u32[]{:S(2)}, u32[]{:S(2)}) collective-permute-start(f32[16,128]{1,0:T(8,128)S(1)} %add_add_fusion), channel_id=1, source_target_pairs={{0,1},{1,0},{2,3},{3,2},{4,5},{5,4},{6,7},{7,6},{8,9},{9,8},{10,11... | collective-permute-start | bytes 24584 | tf_op jit(solution)/shard_map/ppermute | solution.py:737
  97.0 8.5 %collective-permute-start.9 = (f32[16,128]{1,0:T(8,128)S(1)}, f32[16,128]{1,0:T(8,128)S(1)}, u32[]{:S(2)}, u32[]{:S(2)}) collective-permute-start(f32[16,128]{1,0:T(8,128)S(1)} %add_add_fusion), channel_id=1, source_target_pairs={{0,2},{1,3},{2,0},{3,1},{4,6},{5,7},{6,4},{7,5},{8,10},{9,11},{10,... | collective-permute-start | bytes 24584 | tf_op jit(solution)/shard_map/ppermute | solution.py:737
  98.7 6.9 %collective-permute-start.10 = (f32[16,128]{1,0:T(8,128)S(1)}, f32[16,128]{1,0:T(8,128)S(1)}, u32[]{:S(2)}, u32[]{:S(2)}) collective-permute-start(f32[16,128]{1,0:T(8,128)S(1)} %add_add_fusion), channel_id=1, source_target_pairs={{0,3},{1,2},{2,1},{3,0},{4,7},{5,6},{6,5},{7,4},{8,11},{9,10},{10,... | collective-permute-start | bytes 24584 | tf_op jit(solution)/shard_map/ppermute | solution.py:737
  100.9 1.3 %copy-start.8 = (bf16[768,768]{1,0:T(8,128)(2,1)S(1)}, bf16[768,768]{1,0:T(8,128)(2,1)}, u32[]{:S(2)}) copy-start(bf16[768,768]{1,0:T(8,128)(2,1)} %refs_6_.1) | copy-start | bytes 3538948
  102.2 1.3 %copy-start.9 = (bf16[768,768]{1,0:T(8,128)(2,1)S(1)}, bf16[768,768]{1,0:T(8,128)(2,1)}, u32[]{:S(2)}) copy-start(bf16[768,768]{1,0:T(8,128)(2,1)} %refs_7_.1) | copy-start | bytes 3538948
  105.6 7.6 %collective-permute-start.11 = (bf16[2,64,768]{2,1,0:T(8,128)(2,1)S(1)}, bf16[2,64,768]{2,1,0:T(8,128)(2,1)S(1)}, u32[]{:S(2)}, u32[]{:S(2)}) collective-permute-start(bf16[2,64,768]{2,1,0:T(8,128)(2,1)S(1)} %bitcast.18), channel_id=1, source_target_pairs={{0,8},{8,0},{1,9},{9,1},{2,10},{10,2},{3,11},{11,3},{4,12},{12,4},... | collective-permute-start | bytes 589832 | tf_op jit(solution)/shard_map/ppermute | solution.py:714
  107.2 6.9 %collective-permute-start.12 = (f32[16,128]{1,0:T(8,128)S(1)}, f32[16,128]{1,0:T(8,128)S(1)}, u32[]{:S(2)}, u32[]{:S(2)}) collective-permute-start(f32[16,128]{1,0:T(8,128)S(1)} %add_multiply_fusion), channel_id=1, source_target_pairs={{0,4},{1,5},{2,6},{3,7},{4,0},{5,1},{6,2},{7,3},{8,12},{9,13},{10,... | collective-permute-start | bytes 24584 | tf_op jit(solution)/shard_map/ppermute | solution.py:737
